TPU v7x, 32 devices: a whole 2x2x4 slice. The times are simulated.
32 devices in a mesh: gx: 4 (over z), gy: 4 (over y, x), gz: 2 (over core).
Axes of the slice: x: 2, y: 2, z: 4, core: 2. Of those that a mesh axis runs over, the one named last changes fastest.
Arguments:
- orbitals: float32 [32, 32, 32, 256], P(None, 'gx', 'gy', 'gz'), may hold values from -6 to 6
- potential: float32 [32, 32, 256], P('gx', 'gy', 'gz'), may hold values from -2 to 0
- projectors: float32 [256, 4, 512], P(('gx', 'gy', 'gz')), may hold values from -0.5 to 0.5
- owner_rank: int32 [256], replicated, may hold values from 0 to 31, as said below
- box_anchor: int32 [3, 256], replicated, may hold values from 0 to 120, as said below
- box_extent: int32 [256], replicated, may hold values from 4 to 8
- coupling: float32 [256, 4], replicated, may hold values from 0.5 to 3
Outputs:
- filtered: float32 [32, 32, 32, 256], P(None, 'gx', 'gy', 'gz')
- intersection: float32 [32, 32], replicated
Inputs may be any that keep to these rules, and one draw needn't show every extreme that they name: owner_rank[a] is (ix * 4 + iy) * 2 + iz for the domain (ix, iy, iz) that holds all of atom a's box; every device holds at most 24 atoms, an eighth of the devices exactly 24. box_anchor[0, a] is at most 0, box_anchor[1, a] at most 0, box_anchor[2, a] at most 120, so each box lies inside its owner's domain.
All inputs are finite; a program needn't handle non-finite values.
Results may differ from a plain program's by a relative error of at most 0.00013.
Values sent between devices are 32-bit elements; how exact they have to be, the bound alone decides.
No kernel may reach another device: no remote copies, remote signals or barrier semaphores. Data moves between devices by JAX's collectives and lax.ppermute only.
A program may use at most 128 MiB of HBM per device.

v0:
```python
import jax
import jax.numpy as jnp
from jax import lax
from jax.sharding import PartitionSpec as P

B = 8
DEGREE = 4
ATOM_DEV = 8


STENCIL = (
    -5369.0 / 1800.0,
    12.0 / 7.0,
    -15.0 / 56.0,
    10.0 / 189.0,
    -1.0 / 112.0,
    2.0 / 1925.0,
    -1.0 / 16632.0,
)
SPACING = 0.5
LOW_EDGE = -2.5
CUTOFF = 4.0
UPPER = 60.0


def extended(cells, sides, width):
    for axis, dim in sides:
        count = lax.axis_size(axis)
        head = lax.slice_in_dim(cells, 0, width, axis=dim)
        tail = lax.slice_in_dim(cells, cells.shape[dim] - width, cells.shape[dim], axis=dim)
        cells = jnp.concatenate(
            [
                lax.ppermute(tail, axis, [(i, (i + 1) % count) for i in range(count)]),
                cells,
                lax.ppermute(head, axis, [((i + 1) % count, i) for i in range(count)]),
            ],
            axis=dim,
        )
    return cells


def laplace_padded(padded, shape):
    span_x, span_y, span_z = (shape[1], shape[2], shape[3])
    summed = 3.0 * STENCIL[0] * padded[:, 6 : 6 + span_x, 6 : 6 + span_y, 6 : 6 + span_z]
    for offset in range(1, 7):
        weight = STENCIL[offset]
        summed = summed + weight * (
            padded[:, 6 + offset : 6 + offset + span_x, 6 : 6 + span_y, 6 : 6 + span_z]
            + padded[:, 6 - offset : 6 - offset + span_x, 6 : 6 + span_y, 6 : 6 + span_z]
        )
        summed = summed + weight * (
            padded[:, 6 : 6 + span_x, 6 + offset : 6 + offset + span_y, 6 : 6 + span_z]
            + padded[:, 6 : 6 + span_x, 6 - offset : 6 - offset + span_y, 6 : 6 + span_z]
        )
        summed = summed + weight * (
            padded[:, 6 : 6 + span_x, 6 : 6 + span_y, 6 + offset : 6 + offset + span_z]
            + padded[:, 6 : 6 + span_x, 6 : 6 + span_y, 6 - offset : 6 - offset + span_z]
        )
    return summed / (SPACING * SPACING)


def collect_boxes(projectors, member, box_anchor, box_extent, coupling, capacity):
    member_int = member.astype(jnp.int32)
    slot_all = jnp.cumsum(member_int) - 1
    count = jnp.sum(member_int)
    slot_ids = jnp.arange(capacity, dtype=jnp.int32)
    onehot = ((slot_all[None, :] == slot_ids[:, None]) & member[None, :]).astype(jnp.float32)
    buffer = jnp.einsum(
        "cp,pkf->ckf",
        onehot,
        lax.all_gather(projectors, ("gx", "gy", "gz"), axis=0, tiled=True),
        precision=lax.Precision.HIGHEST,
    )
    hot_all = (slot_all[None, :] == slot_ids[:, None]) & member[None, :]
    slot_anchor = jnp.sum(jnp.where(hot_all[None, :, :], box_anchor[:, None, :], 0), axis=2)
    slot_extent = jnp.sum(jnp.where(hot_all, box_extent[None, :], 0), axis=1)
    slot_coupling = jnp.sum(jnp.where(hot_all[:, :, None], coupling[None, :, :], 0.0), axis=1)
    cell_offsets = jnp.arange(B, dtype=jnp.int32)
    limit = slot_extent[:, None, None, None]
    inside = (
        (cell_offsets[None, :, None, None] < limit)
        & (cell_offsets[None, None, :, None] < limit)
        & (cell_offsets[None, None, None, :] < limit)
    )
    buffer = buffer * inside.reshape(capacity, 1, B * B * B).astype(jnp.float32)
    return (buffer, slot_anchor, slot_coupling, count)


def nonlocal_term(field, buffer, slot_anchor, slot_coupling, count, domain_start):
    states = field.shape[0]

    def add_slot(slot_index, nonlocal_sum):
        corner = slot_anchor[:, slot_index] - domain_start
        start_cell = (0, corner[0], corner[1], corner[2])
        box_cells = lax.dynamic_slice(field, start_cell, (states, B, B, B)).reshape(
            states, B * B * B
        )
        proj_box = buffer[slot_index]
        coeffs = (
            jnp.dot(box_cells, proj_box.T, precision=lax.Precision.HIGHEST)
            * slot_coupling[slot_index][None, :]
        )
        addition = jnp.dot(coeffs, proj_box, precision=lax.Precision.HIGHEST).reshape(
            states, B, B, B
        )
        current = lax.dynamic_slice(nonlocal_sum, start_cell, (states, B, B, B))
        return lax.dynamic_update_slice(nonlocal_sum, current + addition, start_cell)

    return lax.fori_loop(0, count, add_slot, jnp.zeros_like(field))


def run_filter(field, apply_h):
    half_width = (UPPER - CUTOFF) / 2.0
    middle = (UPPER + CUTOFF) / 2.0
    sigma_one = half_width / (LOW_EDGE - middle)
    sigma_now = sigma_one
    result = (apply_h(field) - middle * field) * (sigma_one / half_width)
    previous = field
    for degree_step in range(1, DEGREE):
        sigma_next = 1.0 / (2.0 / sigma_one - sigma_now)
        next_state = (apply_h(result) - middle * result) * (
            2.0 * sigma_next / half_width
        ) - sigma_now * sigma_next * previous
        previous = result
        result = next_state
        sigma_now = sigma_next
    return result


def body(orbitals, potential, projectors, owner_rank, box_anchor, box_extent, coupling):
    groups_y = lax.axis_size("gy")
    groups_z = lax.axis_size("gz")
    own_x = owner_rank // (groups_y * groups_z)
    own_y = owner_rank // groups_z % groups_y
    own_z = owner_rank % groups_z
    index_x = lax.axis_index("gx")
    index_y = lax.axis_index("gy")
    index_z = lax.axis_index("gz")
    span_x, span_y, span_z = (orbitals.shape[1], orbitals.shape[2], orbitals.shape[3])
    grid_anchor = jnp.stack([own_x * span_x, own_y * span_y, own_z * span_z]) + box_anchor
    member = (own_x == index_x) & (own_y == index_y) & (own_z == index_z)
    buffer, slot_anchor, slot_coupling, count = collect_boxes(
        projectors, member, grid_anchor, box_extent, coupling, 3 * ATOM_DEV
    )
    domain_start = jnp.stack([index_x * span_x, index_y * span_y, index_z * span_z])

    def apply_cube(field):
        padded = extended(field, (("gx", 1), ("gy", 2), ("gz", 3)), 6)
        return (
            -0.5 * laplace_padded(padded, field.shape)
            + potential[None] * field
            + nonlocal_term(field, buffer, slot_anchor, slot_coupling, count, domain_start)
        )

    filtered = run_filter(orbitals, apply_cube)
    flattened = filtered.reshape(filtered.shape[0], -1)
    partial_value = jnp.dot(flattened, flattened.T, precision=lax.Precision.HIGHEST)
    cells_total = span_x * span_y * span_z * lax.axis_size("gx") * groups_y * groups_z
    intersection = lax.psum(partial_value, ("gx", "gy", "gz")) / cells_total
    return (filtered, intersection)


def solution(mesh):
    return jax.shard_map(
        body,
        mesh=mesh,
        in_specs=(
            P(None, "gx", "gy", "gz"),
            P("gx", "gy", "gz"),
            P(("gx", "gy", "gz"), None, None),
            P(),
            P(),
            P(),
            P(),
        ),
        out_specs=(P(None, "gx", "gy", "gz"), P()),
        check_vma=False,
    )
```

profile of v0, /device:TPU:0, one launch (start us, length us, event | category | flops | bytes accessed | tf_op | source)
XLA Modules:
  0.0 1548.0 jit_solution(1369140399157276029)
XLA Ops:
  9.1 3.1 collective-permute-start.1
  15.2 2.7 copy.105
  18.4 15.3 collective-permute-done.1
  36.9 13.1 collective-permute-done
  52.5 2.7 fusion.278
  58.3 47.0 %collective-permute-done.2 = f32[32,20,6,128]{3,0,2,1:T(8,128)} collective-permute-done((f32[32,20,6,128]{3,0,2,1:T(8,128)}, f32[32,20,6,128]{3,0,2,1:T(8,128)}, u32[]{:S(2)}, u32[]{:S(2)}) %collective-permute-start.2) | collective-permute-done | bytes 1966112 | tf_op jit(solution)/shard_map/ppermute | solution.py:35
  105.3 42.7 %collective-permute-done.3 = f32[32,20,6,128]{3,0,2,1:T(8,128)} collective-permute-done((f32[32,20,6,128]{3,0,2,1:T(8,128)}, f32[32,20,6,128]{3,0,2,1:T(8,128)}, u32[]{:S(2)}, u32[]{:S(2)}) %collective-permute-start.3) | collective-permute-done | bytes 1966112 | tf_op jit(solution)/shard_map/ppermute | solution.py:33
  148.0 6.0 pad_maximum_fusion
  154.0 11.4 fusion.274
  165.3 6.1 copy.99
  171.6 6.5 copy.97
  179.5 5.2 copy.100
  184.8 5.7 copy.98
  196.1 51.8 %while.40 = (s32[]{:T(128)}, f32[32,8,8,128]{0,3,2,1:T(8,128)}, s32[]{:T(128)}, s32[3,24]{0,1:T(8,128)S(1)}, s32[3]{0:T(128)S(1)}, /*index=5*/f32[32,8,8,128]{0,...) while((s32[]{:T(128)}, f32[32,8,8,128]{0,3,2,1:T(8,128)}, ...), condition=%wide.region_7.8_spmd, body=%wide.region_6.7_spmd.sunk | while | flops 1589387 | bytes 509233 | solution.py:109
  248.0 2.9 copy.108
  250.9 25.1 %broadcast_multiply_fusion = (f32[32,8,8,128]{3,0,2,1:T(8,128)S(1)}, f32[32,8,8,128]{3,0,2,1:T(8,128)}) fusion(f32[32,8,8,128]{3,0,2,1:T(8,128)S(1)} %copy.108, f32[8,8,128]{2,1,0:T(8,128)S(1)} %copy-done.11, f32[32,20,6,128]{3,0,2,1:T(8,128)} %collective-permute-done.2, f32[32,20,8,128]{3,0,2,1:T(8,128)} %copy-done, ...), kind=kLoop, calls=%fused_computation.473 | loop fusion | flops 28835840 | bytes 23977984 | tf_op jit(solution)/shard_map/mul | solution.py:117
  277.4 194.4 %collective-permute-start.6 = (f32[32,6,8,128]{3,0,2,1:T(8,128)}, f32[32,6,8,128]{3,0,2,1:T(8,128)S(1)}, u32[]{:S(2)}, u32[]{:S(2)}) collective-permute-start(f32[32,6,8,128]{3,0,2,1:T(8,128)} %get-tuple-element.405), channel_id=1, source_target_pairs={{8,0},{16,8},{24,16},{0,24},{9,1},{17,9},{25,17},{1,25},{10,2},{18... | collective-permute-start | bytes 2359304 | tf_op jit(solution)/shard_map/ppermute | solution.py:35
  471.8 2.7 copy.115
  474.5 7.1 collective-permute-done.6
  481.6 8.9 collective-permute-done.7
  499.0 40.1 %while.41 = (s32[]{:T(128)}, f32[32,8,8,128]{0,3,2,1:T(8,128)}, s32[]{:T(128)}, s32[3,24]{0,1:T(8,128)S(1)}, s32[3]{0:T(128)S(1)}, /*index=5*/f32[32,8,8,128]{0,...) while((s32[]{:T(128)}, f32[32,8,8,128]{0,3,2,1:T(8,128)}, ...), condition=%wide.region_9.10_spmd, body=%wide.region_8.9_spmd.sunk | while | flops 1589387 | bytes 509233 | solution.py:109
  539.1 3.7 copy.118
  542.8 51.5 %collective-permute-done.9 = f32[32,20,6,128]{3,0,2,1:T(8,128)} collective-permute-done((f32[32,20,6,128]{3,0,2,1:T(8,128)}, f32[32,20,6,128]{3,0,2,1:T(8,128)}, u32[]{:S(2)}, u32[]{:S(2)}) %collective-permute-start.9) | collective-permute-done | bytes 1966112 | tf_op jit(solution)/shard_map/ppermute | solution.py:33
  594.3 4.8 pad_maximum_fusion.1
  599.1 11.4 fusion.273
  610.5 6.5 copy.110
  617.0 6.5 copy.112
  624.0 5.9 pad_maximum_fusion.4
  629.8 5.5 copy.111
  635.4 5.7 copy.113
  641.1 15.7 %fusion.134 = f32[32,8,8,128]{3,0,2,1:T(8,128)S(1)} fusion(f32[32,8,8,128]{3,0,2,1:T(8,128)} %copy.118, f32[32,8,8,128]{3,0,2,1:T(8,128)S(1)} %get-tuple-element.374, f32[32,6,8,128]{3,0,2,1:T(8,128)} %collective-permute-done.7, f32[32,6,8,128]{3,0,2,1:T(8,128)} %copy-done.9, f32[32,20,20,6]{3,0,2,1:T(8,128)} %copy.113, ...), kind=kLoop, calls=%fused_computation.253 | loop fusion | flops 35651584 | bytes 23977984 | tf_op jit(solution)/shard_map/sub | solution.py:121
  657.9 148.0 %collective-permute-start.12 = (f32[32,6,8,128]{3,0,2,1:T(8,128)}, f32[32,6,8,128]{3,0,2,1:T(8,128)S(1)}, u32[]{:S(2)}, u32[]{:S(2)}) collective-permute-start(f32[32,6,8,128]{3,0,2,1:T(8,128)} %get-tuple-element.403), channel_id=1, source_target_pairs={{8,0},{16,8},{24,16},{0,24},{9,1},{17,9},{25,17},{1,25},{10,2},{18... | collective-permute-start | bytes 2359304 | tf_op jit(solution)/shard_map/ppermute | solution.py:35
  805.9 2.7 copy.125
  808.6 15.6 %collective-permute-done.12 = f32[32,6,8,128]{3,0,2,1:T(8,128)S(1)} collective-permute-done((f32[32,6,8,128]{3,0,2,1:T(8,128)}, f32[32,6,8,128]{3,0,2,1:T(8,128)S(1)}, u32[]{:S(2)}, u32[]{:S(2)}) %collective-permute-start.12) | collective-permute-done | bytes 786464 | tf_op jit(solution)/shard_map/ppermute | solution.py:35
  824.2 16.5 %collective-permute-done.13 = f32[32,6,8,128]{3,0,2,1:T(8,128)S(1)} collective-permute-done((f32[32,6,8,128]{3,0,2,1:T(8,128)S(1)}, f32[32,6,8,128]{3,0,2,1:T(8,128)S(1)}, u32[]{:S(2)}, u32[]{:S(2)}) %collective-permute-start.13) | collective-permute-done | bytes 786464 | tf_op jit(solution)/shard_map/ppermute | solution.py:33
  843.4 7.7 collective-permute-start.15
  853.7 39.4 %while.42 = (s32[]{:T(128)}, f32[32,8,8,128]{0,3,2,1:T(8,128)}, s32[]{:T(128)}, s32[3,24]{0,1:T(8,128)S(1)}, s32[3]{0:T(128)S(1)}, /*index=5*/f32[32,8,8,128]{0,...) while((s32[]{:T(128)}, f32[32,8,8,128]{0,3,2,1:T(8,128)}, ...), condition=%wide.region_11.12_spmd, body=%wide.region_10.11_spmd.sunk | while | flops 1589387 | bytes 509233 | solution.py:109
  893.1 3.6 copy.128
  896.7 45.6 %collective-permute-done.15 = f32[32,20,6,128]{3,0,2,1:T(8,128)} collective-permute-done((f32[32,20,6,128]{3,0,2,1:T(8,128)}, f32[32,20,6,128]{3,0,2,1:T(8,128)}, u32[]{:S(2)}, u32[]{:S(2)}) %collective-permute-start.15) | collective-permute-done | bytes 1966112 | tf_op jit(solution)/shard_map/ppermute | solution.py:33
  942.3 4.6 pad_maximum_fusion.2
  946.9 11.4 fusion.272
  958.3 6.5 copy.120
  964.8 6.5 copy.122
  971.8 5.8 pad_maximum_fusion.5
  977.6 5.5 copy.121
  983.2 5.7 copy.123
  988.9 15.1 fusion.90
  1005.4 146.8 %collective-permute-start.18 = (f32[32,6,8,128]{3,0,2,1:T(8,128)}, f32[32,6,8,128]{3,0,2,1:T(8,128)S(1)}, u32[]{:S(2)}, u32[]{:S(2)}) collective-permute-start(f32[32,6,8,128]{3,0,2,1:T(8,128)} %get-tuple-element.401), channel_id=1, source_target_pairs={{8,0},{16,8},{24,16},{0,24},{9,1},{17,9},{25,17},{1,25},{10,2},{18... | collective-permute-start | bytes 2359304 | tf_op jit(solution)/shard_map/ppermute | solution.py:35
  1152.2 2.7 copy.134
  1154.9 15.6 %collective-permute-done.18 = f32[32,6,8,128]{3,0,2,1:T(8,128)S(1)} collective-permute-done((f32[32,6,8,128]{3,0,2,1:T(8,128)}, f32[32,6,8,128]{3,0,2,1:T(8,128)S(1)}, u32[]{:S(2)}, u32[]{:S(2)}) %collective-permute-start.18) | collective-permute-done | bytes 786464 | tf_op jit(solution)/shard_map/ppermute | solution.py:35
  1170.4 16.6 %collective-permute-done.19 = f32[32,6,8,128]{3,0,2,1:T(8,128)} collective-permute-done((f32[32,6,8,128]{3,0,2,1:T(8,128)}, f32[32,6,8,128]{3,0,2,1:T(8,128)}, u32[]{:S(2)}, u32[]{:S(2)}) %collective-permute-start.19) | collective-permute-done | bytes 786464 | tf_op jit(solution)/shard_map/ppermute | solution.py:33
  1190.9 9.2 collective-permute-start.21
  1202.7 39.4 %while.43 = (s32[]{:T(128)}, f32[32,8,8,128]{0,3,2,1:T(8,128)}, s32[]{:T(128)}, s32[3,24]{0,1:T(8,128)S(1)}, s32[3]{0:T(128)S(1)}, /*index=5*/f32[32,8,8,128]{0,...) while((s32[]{:T(128)}, f32[32,8,8,128]{0,3,2,1:T(8,128)}, ...), condition=%wide.region_13.14_spmd, body=%wide.region_12.13_spmd.sunk | while | flops 1589387 | bytes 509233 | solution.py:109
  1242.1 3.6 copy.137
  1245.7 39.7 %collective-permute-done.21 = f32[32,20,6,128]{3,0,2,1:T(8,128)} collective-permute-done((f32[32,20,6,128]{3,0,2,1:T(8,128)}, f32[32,20,6,128]{3,0,2,1:T(8,128)}, u32[]{:S(2)}, u32[]{:S(2)}) %collective-permute-start.21) | collective-permute-done | bytes 1966112 | tf_op jit(solution)/shard_map/ppermute | solution.py:33
  1285.4 4.8 pad_maximum_fusion.3
  1290.1 11.4 fusion.271
  1301.5 6.5 copy.129
  1308.0 6.5 copy.131
  1315.1 5.9 pad_maximum_fusion.6
  1320.9 5.5 copy.130
  1326.5 5.7 copy.132
  1332.1 14.9 fusion.46
  1349.6 190.8 %psum.7 = f32[32,32]{1,0:T(8,128)S(1)} all-reduce(f32[32,32]{1,0:T(8,128)S(1)} %convolution_bitcast_fusion), channel_id=1, replica_groups=mesh['gx'=4,'gy'=4,'gz'=2] {'gx','gy','gz'}, use_global_device_ids=true, to_apply=%region_14.15 | all-reduce | flops 1024 | bytes 8192 | tf_op jit(solution)/shard_map/psum | solution.py:159
  (257 shorter events, 162.7 us)
Async XLA Ops:
  7.2 8.0 copy-start.1
  7.2 5.0 copy-start.12
  7.2 183.2 %all-gather.2.cloned.1.call-start = ((), (), s32[]{:S(2)}) async-start(), calls=%async_computation | async-start | bytes 2162688 | tf_op jit(solution)/shard_map/all_gather | solution.py:71
  8.8 9.1 copy-start.14
  9.1 24.7 %collective-permute-start.1 = (f32[32,6,8,128]{3,0,2,1:T(8,128)S(1)}, f32[32,6,8,128]{3,0,2,1:T(8,128)}, u32[]{:S(2)}, u32[]{:S(2)}) collective-permute-start(f32[32,6,8,128]{3,0,2,1:T(8,128)S(1)} %copy.157), channel_id=1, source_target_pairs={{0,8},{8,16},{16,24},{24,0},{1,9},{9,17},{17,25},{25,1},{2,10},{10... | collective-permute-start | bytes 2359304 | tf_op jit(solution)/shard_map/ppermute | solution.py:33
  13.1 36.9 %collective-permute-start = (f32[32,6,8,128]{3,0,2,1:T(8,128)S(1)}, f32[32,6,8,128]{3,0,2,1:T(8,128)}, u32[]{:S(2)}, u32[]{:S(2)}) collective-permute-start(f32[32,6,8,128]{3,0,2,1:T(8,128)S(1)} %copy.158), channel_id=1, source_target_pairs={{8,0},{16,8},{24,16},{0,24},{9,1},{17,9},{25,17},{1,25},{10,2},{18... | collective-permute-start | bytes 2359304 | tf_op jit(solution)/shard_map/ppermute | solution.py:35
  36.9 14.3 copy-start.4
  51.3 1.2 copy-start.3
  52.5 95.5 %copy-start = (f32[32,20,8,128]{3,0,2,1:T(8,128)}, f32[32,20,8,128]{3,0,2,1:T(8,128)S(1)}, u32[]{:S(2)}) copy-start(f32[32,20,8,128]{3,0,2,1:T(8,128)S(1)} %get-tuple-element.413) | copy-start | bytes 7864324
  52.5 5.2 copy-start.16
  52.5 5.6 copy-start.15
  55.2 50.1 %collective-permute-start.2 = (f32[32,20,6,128]{3,0,2,1:T(8,128)}, f32[32,20,6,128]{3,0,2,1:T(8,128)}, u32[]{:S(2)}, u32[]{:S(2)}) collective-permute-start(f32[32,20,6,128]{3,0,2,1:T(8,128)} %get-tuple-element.400), channel_id=1, source_target_pairs={{2,0},{4,2},{6,4},{0,6},{3,1},{5,3},{7,5},{1,7},{10,8},{12,10},{14... | collective-permute-start | bytes 5898248 | tf_op jit(solution)/shard_map/ppermute | solution.py:35
  57.6 90.3 %collective-permute-start.3 = (f32[32,20,6,128]{3,0,2,1:T(8,128)}, f32[32,20,6,128]{3,0,2,1:T(8,128)}, u32[]{:S(2)}, u32[]{:S(2)}) collective-permute-start(f32[32,20,6,128]{3,0,2,1:T(8,128)} %get-tuple-element.399), channel_id=1, source_target_pairs={{0,2},{2,4},{4,6},{6,0},{1,3},{3,5},{5,7},{7,1},{8,10},{10,12},{12... | collective-permute-start | bytes 5898248 | tf_op jit(solution)/shard_map/ppermute | solution.py:33
  171.5 7.1 copy-start.13
  171.5 8.0 collective-permute-start.5
  178.1 6.6 collective-permute-start.4
  247.9 2.9 copy-start.2
  247.9 2.9 copy-start.11
  277.4 204.2 %collective-permute-start.6 = (f32[32,6,8,128]{3,0,2,1:T(8,128)}, f32[32,6,8,128]{3,0,2,1:T(8,128)S(1)}, u32[]{:S(2)}, u32[]{:S(2)}) collective-permute-start(f32[32,6,8,128]{3,0,2,1:T(8,128)} %get-tuple-element.405), channel_id=1, source_target_pairs={{8,0},{16,8},{24,16},{0,24},{9,1},{17,9},{25,17},{1,25},{10,2},{18... | collective-permute-start | bytes 2359304 | tf_op jit(solution)/shard_map/ppermute | solution.py:35
  471.8 18.7 %collective-permute-start.7 = (f32[32,6,8,128]{3,0,2,1:T(8,128)}, f32[32,6,8,128]{3,0,2,1:T(8,128)}, u32[]{:S(2)}, u32[]{:S(2)}) collective-permute-start(f32[32,6,8,128]{3,0,2,1:T(8,128)} %get-tuple-element.406), channel_id=1, source_target_pairs={{0,8},{8,16},{16,24},{24,0},{1,9},{9,17},{17,25},{25,1},{2,10},{10... | collective-permute-start | bytes 2359304 | tf_op jit(solution)/shard_map/ppermute | solution.py:33
  481.6 12.7 copy-start.9
  494.3 48.4 %collective-permute-start.8 = (f32[32,20,6,128]{3,0,2,1:T(8,128)}, f32[32,20,6,128]{3,0,2,1:T(8,128)}, u32[]{:S(2)}, u32[]{:S(2)}) collective-permute-start(f32[32,20,6,128]{3,0,2,1:T(8,128)} %get-tuple-element.398), channel_id=1, source_target_pairs={{2,0},{4,2},{6,4},{0,6},{3,1},{5,3},{7,5},{1,7},{10,8},{12,10},{14... | collective-permute-start | bytes 5898248 | tf_op jit(solution)/shard_map/ppermute | solution.py:35
  494.3 100.0 %collective-permute-start.9 = (f32[32,20,6,128]{3,0,2,1:T(8,128)}, f32[32,20,6,128]{3,0,2,1:T(8,128)}, u32[]{:S(2)}, u32[]{:S(2)}) collective-permute-start(f32[32,20,6,128]{3,0,2,1:T(8,128)} %get-tuple-element.397), channel_id=1, source_target_pairs={{0,2},{2,4},{4,6},{6,0},{1,3},{3,5},{5,7},{7,1},{8,10},{10,12},{12... | collective-permute-start | bytes 5898248 | tf_op jit(solution)/shard_map/ppermute | solution.py:33
  539.1 55.2 %copy-start.10 = (f32[32,6,8,128]{3,0,2,1:T(8,128)S(1)}, f32[32,6,8,128]{3,0,2,1:T(8,128)}, u32[]{:S(2)}) copy-start(f32[32,6,8,128]{3,0,2,1:T(8,128)} %copy-done.9) | copy-start | bytes 2359300
  617.0 12.9 collective-permute-start.10
  623.5 11.9 collective-permute-start.11
  657.9 166.3 %collective-permute-start.12 = (f32[32,6,8,128]{3,0,2,1:T(8,128)}, f32[32,6,8,128]{3,0,2,1:T(8,128)S(1)}, u32[]{:S(2)}, u32[]{:S(2)}) collective-permute-start(f32[32,6,8,128]{3,0,2,1:T(8,128)} %get-tuple-element.403), channel_id=1, source_target_pairs={{8,0},{16,8},{24,16},{0,24},{9,1},{17,9},{25,17},{1,25},{10,2},{18... | collective-permute-start | bytes 2359304 | tf_op jit(solution)/shard_map/ppermute | solution.py:35
  805.9 34.8 %collective-permute-start.13 = (f32[32,6,8,128]{3,0,2,1:T(8,128)S(1)}, f32[32,6,8,128]{3,0,2,1:T(8,128)S(1)}, u32[]{:S(2)}, u32[]{:S(2)}) collective-permute-start(f32[32,6,8,128]{3,0,2,1:T(8,128)S(1)} %get-tuple-element.404), channel_id=1, source_target_pairs={{0,8},{8,16},{16,24},{24,0},{1,9},{9,17},{17,25},{25,1},{2,10},{10... | collective-permute-start | bytes 2359304 | tf_op jit(solution)/shard_map/ppermute | solution.py:33
  824.2 19.2 %copy-start.6 = (f32[32,6,8,128]{3,0,2,1:T(8,128)}, f32[32,6,8,128]{3,0,2,1:T(8,128)S(1)}, u32[]{:S(2)}) copy-start(f32[32,6,8,128]{3,0,2,1:T(8,128)S(1)} %collective-permute-done.12) | copy-start | bytes 2359300
  840.7 2.7 copy-start.8
  843.4 53.2 %collective-permute-start.14 = (f32[32,20,6,128]{3,0,2,1:T(8,128)}, f32[32,20,6,128]{3,0,2,1:T(8,128)S(1)}, u32[]{:S(2)}, u32[]{:S(2)}) collective-permute-start(f32[32,20,6,128]{3,0,2,1:T(8,128)} %get-tuple-element.394), channel_id=1, source_target_pairs={{2,0},{4,2},{6,4},{0,6},{3,1},{5,3},{7,5},{1,7},{10,8},{12,10},{14... | collective-permute-start | bytes 5898248 | tf_op jit(solution)/shard_map/ppermute | solution.py:35
  843.4 98.8 %collective-permute-start.15 = (f32[32,20,6,128]{3,0,2,1:T(8,128)}, f32[32,20,6,128]{3,0,2,1:T(8,128)}, u32[]{:S(2)}, u32[]{:S(2)}) collective-permute-start(f32[32,20,6,128]{3,0,2,1:T(8,128)} %get-tuple-element.393), channel_id=1, source_target_pairs={{0,2},{2,4},{4,6},{6,0},{1,3},{3,5},{5,7},{7,1},{8,10},{10,12},{12... | collective-permute-start | bytes 5898248 | tf_op jit(solution)/shard_map/ppermute | solution.py:33
  896.7 75.1 %copy-start.5 = (f32[32,20,6,128]{3,0,2,1:T(8,128)}, f32[32,20,6,128]{3,0,2,1:T(8,128)S(1)}, u32[]{:S(2)}) copy-start(f32[32,20,6,128]{3,0,2,1:T(8,128)S(1)} %collective-permute-done.14) | copy-start | bytes 5898244
  964.7 12.9 collective-permute-start.16
  971.3 11.9 collective-permute-start.17
  983.2 5.8 copy-start.7
  1005.4 165.0 %collective-permute-start.18 = (f32[32,6,8,128]{3,0,2,1:T(8,128)}, f32[32,6,8,128]{3,0,2,1:T(8,128)S(1)}, u32[]{:S(2)}, u32[]{:S(2)}) collective-permute-start(f32[32,6,8,128]{3,0,2,1:T(8,128)} %get-tuple-element.401), channel_id=1, source_target_pairs={{8,0},{16,8},{24,16},{0,24},{9,1},{17,9},{25,17},{1,25},{10,2},{18... | collective-permute-start | bytes 2359304 | tf_op jit(solution)/shard_map/ppermute | solution.py:35
  1152.2 34.9 %collective-permute-start.19 = (f32[32,6,8,128]{3,0,2,1:T(8,128)}, f32[32,6,8,128]{3,0,2,1:T(8,128)}, u32[]{:S(2)}, u32[]{:S(2)}) collective-permute-start(f32[32,6,8,128]{3,0,2,1:T(8,128)} %get-tuple-element.402), channel_id=1, source_target_pairs={{0,8},{8,16},{16,24},{24,0},{1,9},{9,17},{17,25},{25,1},{2,10},{10... | collective-permute-start | bytes 2359304 | tf_op jit(solution)/shard_map/ppermute | solution.py:33
  1190.9 54.8 %collective-permute-start.20 = (f32[32,20,6,128]{3,0,2,1:T(8,128)}, f32[32,20,6,128]{3,0,2,1:T(8,128)}, u32[]{:S(2)}, u32[]{:S(2)}) collective-permute-start(f32[32,20,6,128]{3,0,2,1:T(8,128)} %get-tuple-element.390), channel_id=1, source_target_pairs={{2,0},{4,2},{6,4},{0,6},{3,1},{5,3},{7,5},{1,7},{10,8},{12,10},{14... | collective-permute-start | bytes 5898248 | tf_op jit(solution)/shard_map/ppermute | solution.py:35
  1190.9 94.4 %collective-permute-start.21 = (f32[32,20,6,128]{3,0,2,1:T(8,128)}, f32[32,20,6,128]{3,0,2,1:T(8,128)}, u32[]{:S(2)}, u32[]{:S(2)}) collective-permute-start(f32[32,20,6,128]{3,0,2,1:T(8,128)} %get-tuple-element.389), channel_id=1, source_target_pairs={{0,2},{2,4},{4,6},{6,0},{1,3},{3,5},{5,7},{7,1},{8,10},{10,12},{12... | collective-permute-start | bytes 5898248 | tf_op jit(solution)/shard_map/ppermute | solution.py:33
  1308.0 12.9 collective-permute-start.22
  1314.5 11.9 collective-permute-start.23
Sparse Core Ops, SparseCore 0:
  12.9 77.6 all-gather.1
where the time goes:
time: 1570 us; the launch traced here: 1550 us
  starting transfers between devices  518 us (33%)
  waiting for transfers between devices  335 us (21%)
  local copies, waits for them, and re-layouts  272 us (17%)
  blocking collectives  191 us (12%)
  other arithmetic  114 us (7%)
  loops' own time  58 us (4%)
  matrix products  45.5 us (3%)
    ppermute x12, starting transfers between devices, extended(): lax.ppermute(head, axis, [((i + 1) % count, i) for i in range(count)])  494 us
    ppermute x12, waiting for transfers between devices, extended(): lax.ppermute(tail, axis, [(i, (i + 1) % count) for i in range(count)])  237 us
    psum x1, blocking collectives, body(): intersection = lax.psum(partial_value, ('gx', 'gy', 'gz')) / cells_total  191 us
    ppermute x12, waiting for transfers between devices, extended(): lax.ppermute(head, axis, [((i + 1) % count, i) for i in range(count)])  98.4 us
    slice x12, local copies, waits for them, and re-layouts, extended(): head = lax.slice_in_dim(cells, 0, width, axis=dim)  77 us
    another operation x4, loops' own time, nonlocal_term(): return lax.fori_loop(0, count, add_slot, jnp.zeros_like(field))  58 us
    sub x3, other arithmetic, run_filter(): (apply_h(result) - middle * result) * (2.0 * sigma_next / half_width)  45.7 us
    concatenate x10, other arithmetic, extended(): jnp.concatenate([lax.ppermute(tail, axis, [(i, (i + 1) % count) for i in...  40.8 us
  transfers between devices with their start and end apart: 25, of which 13 were waited for; matrix products, arithmetic and copies ran while one was open for 14% of the time, Pallas kernels for 0%

commit v1 on v0

--- a/solution.py
+++ b/solution.py
@@ -1,6 +1,11 @@
+import functools
 import jax
 import jax.numpy as jnp
 from jax import lax
+from jax.experimental import pallas as pl
+from jax.experimental.pallas import tpu as pltpu
+import ml_dtypes
+import numpy as np
 from jax.sharding import PartitionSpec as P
 
 B = 8
@@ -127,7 +132,7 @@
     return result
 
 
-def body(orbitals, potential, projectors, owner_rank, box_anchor, box_extent, coupling):
+def domain_body(orbitals, potential, projectors, owner_rank, box_anchor, box_extent, coupling):
     groups_y = lax.axis_size("gy")
     groups_z = lax.axis_size("gz")
     own_x = owner_rank // (groups_y * groups_z)
@@ -158,6 +163,330 @@
     cells_total = span_x * span_y * span_z * lax.axis_size("gx") * groups_y * groups_z
     intersection = lax.psum(partial_value, ("gx", "gy", "gz")) / cells_total
     return (filtered, intersection)
+
+
+SUB = 8
+LANE = 128
+NPROJ = 4
+
+
+def split_terms(matrix):
+    high = matrix.astype(ml_dtypes.bfloat16)
+    low = (matrix - high.astype(np.float64)).astype(ml_dtypes.bfloat16)
+    return np.concatenate([high, low], axis=0)
+
+
+def ring_matrix(length):
+    matrix = np.zeros((length, length))
+    for offset in range(1, 7):
+        weight = -0.5 * STENCIL[offset] / (SPACING * SPACING)
+        for row in range(length):
+            matrix[row, (row + offset) % length] += weight
+            matrix[row, (row - offset) % length] += weight
+    return matrix
+
+
+def z_weights(groups_z):
+    return split_terms(ring_matrix(groups_z * LANE))
+
+
+def y_weights(groups_y):
+    ring = ring_matrix(groups_y * SUB).reshape(groups_y, SUB, groups_y, SUB)
+    full = np.einsum("aibj,xy->axibyj", ring, np.eye(SUB))
+    return split_terms(full.reshape(groups_y * SUB * SUB, groups_y * SUB * SUB))
+
+
+def split_pair(value):
+    high = value.astype(jnp.bfloat16)
+    low = (value - high.astype(jnp.float32)).astype(jnp.bfloat16)
+    return high, low
+
+
+def mxu(left, right):
+    return jnp.dot(left, right, preferred_element_type=jnp.float32)
+
+
+def box_window(anchor):
+    lane = lax.broadcasted_iota(jnp.int32, (SUB, LANE), 1)
+    return (lane - anchor) & (LANE - 1)
+
+
+def filter_kernel(
+    groups,
+    owner,
+    anchor,
+    start,
+    pack,
+    coupling,
+    zmat,
+    ymat,
+    out,
+    state_a,
+    state_b,
+    rolled,
+    added,
+    boxes,
+    coeffs,
+    high_buf,
+    low_buf,
+    near,
+):
+    groups_x, groups_y, groups_z = groups
+    domains = groups_x * groups_y * groups_z
+    plane = groups_y * groups_z
+    atom_groups = coupling.shape[0] // (2 * SUB)
+    per_domain = atom_groups // domains
+    half_width = (UPPER - CUTOFF) / 2.0
+    middle = (UPPER + CUTOFF) / 2.0
+    edge_z = groups_z * LANE
+    edge_y = groups_y * SUB * SUB
+    weights = [-0.5 * value / (SPACING * SPACING) for value in STENCIL]
+
+    def proj_at(group, kp, row):
+        return pack[group // per_domain, SUB + (group % per_domain) * 2 * SUB + kp * SUB + row]
+
+    def apply_step(cur, prev, new, alpha, beta):
+        def spread(dom, carry):
+            for x in range(SUB):
+                value = cur[dom, x]
+                rolled[dom, x] = value if x == 0 else pltpu.roll(value, SUB * x, 1)
+                added[dom, x] = jnp.zeros((SUB, LANE), jnp.float32)
+            return carry
+
+        lax.fori_loop(0, domains, spread, 0)
+
+        lane = lax.broadcasted_iota(jnp.int32, (SUB, LANE), 1)
+        lower = lane < LANE // 2
+
+        def gather(group, carry):
+            for pair in range(4):
+                halves = []
+                for par in range(2):
+                    atom = group * SUB + pair * 2 + par
+                    dom = owner[atom]
+                    at = anchor[atom]
+                    window = box_window(at)
+                    parts = [rolled[dom, x] for x in range(SUB)]
+                    for bit in (SUB, 2 * SUB, 4 * SUB):
+                        odd = (window & bit) != 0
+                        parts = [
+                            jnp.where(odd, parts[i + 1], parts[i])
+                            for i in range(0, len(parts), 2)
+                        ]
+                    turn = (LANE - at + (LANE // 2) * par) & (LANE - 1)
+                    halves.append(pltpu.roll(parts[0], turn, 1))
+                both = jnp.where(lower, halves[0], halves[1])
+                for kpar in range(2):
+                    boxes[pl.ds(group * SUB * SUB + kpar * 4 + pair, SUB, stride=SUB), :] = both
+            return carry
+
+        lax.fori_loop(0, atom_groups, gather, 0)
+
+        def project(group, carry):
+            base = group * SUB * SUB
+            for kp in range(2):
+                total = boxes[pl.ds(base, SUB), :] * proj_at(group, kp, 0)
+                for row in range(1, SUB):
+                    total = total + boxes[pl.ds(base + row * SUB, SUB), :] * proj_at(group, kp, row)
+                coeffs[pl.ds(group * 2 * SUB + kp * SUB, SUB), :] = total
+            return carry
+
+        lax.fori_loop(0, atom_groups, project, 0)
+
+        same = (
+            lax.broadcasted_iota(jnp.int32, (LANE, LANE), 0) // (LANE // 2)
+            == lax.broadcasted_iota(jnp.int32, (LANE, LANE), 1) // (LANE // 2)
+        ).astype(jnp.float32).astype(jnp.bfloat16)
+        high, low = split_pair(coeffs[...])
+        coeffs[...] = (mxu(high, same) + mxu(low, same)) * coupling[...]
+
+        def expand(group, carry):
+            base = group * SUB * SUB
+            first = coeffs[pl.ds(group * 2 * SUB, SUB), :]
+            second = coeffs[pl.ds(group * 2 * SUB + SUB, SUB), :]
+            for row in range(SUB):
+                boxes[pl.ds(base + row * SUB, SUB), :] = first * proj_at(
+                    group, 0, row
+                ) + second * proj_at(group, 1, row)
+            return carry
+
+        lax.fori_loop(0, atom_groups, expand, 0)
+
+        def scatter(group, carry):
+            for pair in range(4):
+                base = group * SUB * SUB + pair
+                both = (
+                    boxes[pl.ds(base, SUB, stride=SUB), :]
+                    + boxes[pl.ds(base + 4, SUB, stride=SUB), :]
+                )
+                for par in range(2):
+                    atom = group * SUB + pair * 2 + par
+                    dom = owner[atom]
+                    at = anchor[atom]
+                    turned = pltpu.roll(both, (at + (LANE // 2) * par) & (LANE - 1), 1)
+                    slot = box_window(at) >> 3
+                    for x in range(SUB):
+                        added[dom, x] = added[dom, x] + jnp.where(slot == x, turned, 0.0)
+            return carry
+
+        lax.fori_loop(0, atom_groups, scatter, 0)
+
+        def combine(gx, carry):
+            for gy in range(groups_y):
+                for gz in range(groups_z):
+                    dom = gx * plane + gy * groups_z + gz
+                    high, low = split_pair(cur[dom].reshape(SUB * SUB, LANE))
+                    rows = slice(gy * SUB * SUB, (gy + 1) * SUB * SUB)
+                    lanes = slice(gz * LANE, (gz + 1) * LANE)
+                    high_buf[rows, lanes] = high
+                    low_buf[rows, lanes] = low
+            high = high_buf[...]
+            low = low_buf[...]
+            near[...] = (
+                mxu(high, zmat[:edge_z])
+                + mxu(low, zmat[:edge_z])
+                + mxu(high, zmat[edge_z:])
+                + mxu(ymat[:edge_y], high)
+                + mxu(ymat[:edge_y], low)
+                + mxu(ymat[edge_y:], high)
+            )
+            for gy in range(groups_y):
+                for gz in range(groups_z):
+                    column = {}
+                    for t in range(-6, SUB + 6):
+                        away = gx + t // SUB
+                        away = lax.rem(away + groups_x, groups_x)
+                        column[t] = cur[away * plane + gy * groups_z + gz, t % SUB]
+                    dom = gx * plane + gy * groups_z + gz
+                    for x in range(SUB):
+                        value = column[x]
+                        total = near[
+                            pl.ds(gy * SUB * SUB + x * SUB, SUB), pl.ds(gz * LANE, LANE)
+                        ]
+                        extra = added[dom, x]
+                        total = total + (
+                            extra if x == 0 else pltpu.roll(extra, LANE - SUB * x, 1)
+                        )
+                        for offset in range(1, 7):
+                            total = total + weights[offset] * (
+                                column[x + offset] + column[x - offset]
+                            )
+                        total = total + (pack[dom, x] + (3.0 * weights[0] - middle)) * value
+                        total = total * alpha
+                        if beta is not None:
+                            total = total + beta * prev[dom, x]
+                        new[dom, x] = total
+            return carry
+
+        lax.fori_loop(0, groups_x, combine, 0)
+
+    sigma_one = half_width / (LOW_EDGE - middle)
+    sigma_now = sigma_one
+    apply_step(start, None, state_a, sigma_one / half_width, None)
+    prev, cur = start, state_a
+    for degree_step in range(1, DEGREE):
+        sigma_next = 1.0 / (2.0 / sigma_one - sigma_now)
+        if degree_step == DEGREE - 1:
+            new = out
+        else:
+            new = state_b if cur is state_a else state_a
+        apply_step(
+            cur, prev, new, 2.0 * sigma_next / half_width, -sigma_now * sigma_next
+        )
+        prev, cur = cur, new
+        sigma_now = sigma_next
+
+
+def packed_projectors(projectors, extent):
+    atoms = projectors.shape[0]
+    cells = jnp.arange(B, dtype=jnp.int32)
+    limit = extent[:, None, None, None]
+    inside = (
+        (cells[None, :, None, None] < limit)
+        & (cells[None, None, :, None] < limit)
+        & (cells[None, None, None, :] < limit)
+    )
+    masked = jnp.where(inside[:, None], projectors.reshape(atoms, NPROJ, B, B, B), 0.0)
+    masked = masked.reshape(atoms // SUB, 4, 2, 2, 2, B, B, B)
+    return masked.transpose(0, 3, 6, 4, 1, 2, 5, 7).reshape(atoms // SUB * 2 * B, SUB, LANE)
+
+
+def packed_coupling(coupling):
+    atoms = coupling.shape[0]
+    parts = coupling.reshape(atoms // SUB, 4, 2, 2, 2).transpose(0, 3, 4, 1, 2)
+    wide = jnp.broadcast_to(parts[..., None], parts.shape + (LANE // 2,))
+    return wide.reshape(atoms * 2, LANE)
+
+
+def filter_call(groups, owner, anchor, field, pack, coupling, interpret=False):
+    groups_x, groups_y, groups_z = groups
+    domains = groups_x * groups_y * groups_z
+    atoms = owner.shape[0]
+    shape = (domains, SUB, SUB, LANE)
+    rows, lanes = groups_y * SUB * SUB, groups_z * LANE
+    vmem = pl.BlockSpec(memory_space=pltpu.VMEM)
+    smem = pl.BlockSpec(memory_space=pltpu.SMEM)
+    return pl.pallas_call(
+        functools.partial(filter_kernel, groups),
+        out_shape=jax.ShapeDtypeStruct(shape, jnp.float32),
+        in_specs=[smem, smem, vmem, vmem, vmem, vmem, vmem],
+        out_specs=vmem,
+        scratch_shapes=[
+            pltpu.VMEM(shape, jnp.float32),
+            pltpu.VMEM(shape, jnp.float32),
+            pltpu.VMEM(shape, jnp.float32),
+            pltpu.VMEM(shape, jnp.float32),
+            pltpu.VMEM((atoms * SUB, LANE), jnp.float32),
+            pltpu.VMEM((atoms * 2, LANE), jnp.float32),
+            pltpu.VMEM((rows, lanes), jnp.bfloat16),
+            pltpu.VMEM((rows, lanes), jnp.bfloat16),
+            pltpu.VMEM((rows, lanes), jnp.float32),
+        ],
+        compiler_params=pltpu.CompilerParams(vmem_limit_bytes=48 * 1024 * 1024),
+        interpret=interpret,
+    )(
+        owner,
+        anchor,
+        field,
+        pack,
+        coupling,
+        jnp.asarray(z_weights(groups_z)),
+        jnp.asarray(y_weights(groups_y)),
+    )
+
+
+def state_body(orbitals, potential, projectors, owner_rank, box_anchor, box_extent, coupling):
+    axes = ("gx", "gy", "gz")
+    groups = tuple(lax.axis_size(axis) for axis in axes)
+    domains = groups[0] * groups[1] * groups[2]
+    atoms_own = projectors.shape[0]
+    me = (lax.axis_index("gx") * groups[1] + lax.axis_index("gy")) * groups[2] + lax.axis_index("gz")
+    extent = lax.dynamic_slice(box_extent, (me * atoms_own,), (atoms_own,))
+    pack = jnp.concatenate([potential, packed_projectors(projectors, extent)], axis=0)
+    pack = lax.all_gather(pack, axes, axis=0, tiled=False)
+    field = lax.all_to_all(orbitals, axes, split_axis=0, concat_axis=0, tiled=True)
+    result = filter_call(
+        groups, owner_rank, box_anchor[2], field, pack, packed_coupling(coupling)
+    )
+    filtered = lax.all_to_all(result, axes, split_axis=0, concat_axis=0, tiled=True)
+    flattened = filtered.reshape(filtered.shape[0], -1)
+    partial_value = jnp.dot(flattened, flattened.T, precision=lax.Precision.HIGHEST)
+    cells_total = orbitals.shape[1] * orbitals.shape[2] * orbitals.shape[3] * domains
+    intersection = lax.psum(partial_value, axes) / cells_total
+    return (filtered, intersection)
+
+
+def body(orbitals, potential, projectors, owner_rank, box_anchor, box_extent, coupling):
+    domains = lax.axis_size("gx") * lax.axis_size("gy") * lax.axis_size("gz")
+    whole_states = (
+        orbitals.shape == (domains, SUB, SUB, LANE)
+        and projectors.shape[0] % SUB == 0
+        and projectors.shape[1] == NPROJ
+    )
+    chosen = state_body if whole_states else domain_body
+    return chosen(
+        orbitals, potential, projectors, owner_rank, box_anchor, box_extent, coupling
+    )
 
 
 def solution(mesh):

time: 1570 us -> 206 us (0.13); the launches traced: 1550 us -> 205 us
  starting transfers between devices: 518 us -> 7.34 us
  waiting for transfers between devices: 335 us -> 55.8 us
  local copies, waits for them, and re-layouts: 272 us -> 7.75 us
  blocking collectives: 191 us -> 68.1 us
  other arithmetic: 114 us -> 1.84 us
  loops' own time: 58 us -> 0 us
  Pallas kernels: 0 us -> 48.6 us
  matrix products: 45.5 us -> 1.5 us
    ppermute x24 -> x0, starting transfers between devices: 518 us -> none  [the longest x12 494 us: extended(): lax.ppermute(head, axis, [((i + 1) % count, i) for i in range(count)])]
    ppermute x24 -> x0, waiting for transfers between devices: 335 us -> none  [the longest x12 237 us: extended(): lax.ppermute(tail, axis, [(i, (i + 1) % count) for i in range(count)])]
    psum x1, blocking collectives: 191 us -> 38.6 us  [state_body(): intersection = lax.psum(partial_value, axes) / cells_total]
    slice x37 -> x1, local copies, waits for them, and re-layouts: 122 us -> 0.69 us  [state_body(): box_anchor[2]]
    another operation x4 -> x0, loops' own time: 58 us -> none  [nonlocal_term(): return lax.fori_loop(0, count, add_slot, jnp.zeros_like(field))]
    pallas_call x0 -> x1, Pallas kernels: none -> 48.6 us  [filter_call(): pl.pallas_call(functools.partial(filter_kernel, groups), out_shape=jax.Sh...]
    sub x20 -> x0, other arithmetic: 45.9 us -> none  [the longest x3 45.7 us: run_filter(): (apply_h(result) - middle * result) * (2.0 * sigma_next / half_width)]
    ppermute x8 -> x0, local copies, waits for them, and re-layouts: 44.6 us -> none  [the longest x4 22.3 us: extended(): lax.ppermute(head, axis, [((i + 1) % count, i) for i in range(count)])]
  transfers between devices with their start and end apart: 25 -> 2, of which waited for: 13 -> 2; matrix products, arithmetic and copies ran while one was open for 14% -> 1% of each run, Pallas kernels for 0% -> 0%
where the time goes in v1:
time: 206 us; the launch traced here: 205 us
  blocking collectives  68.1 us (33%)
  waiting for transfers between devices  55.8 us (27%)
  Pallas kernels  48.6 us (24%)
  between operations  14.2 us (7%)
  local copies, waits for them, and re-layouts  7.75 us (4%)
  starting transfers between devices  7.34 us (4%)
    pallas_call x1, Pallas kernels, filter_call(): pl.pallas_call(functools.partial(filter_kernel, groups), out_shape=jax.Sh...  48.6 us
    psum x1, blocking collectives, state_body(): intersection = lax.psum(partial_value, axes) / cells_total  38.6 us
    all_to_all x1, blocking collectives, state_body(): lax.all_to_all(result, axes, split_axis=0, concat_axis=0, tiled=True)  29.5 us
    all_gather x1, waiting for transfers between devices, state_body(): pack = lax.all_gather(pack, axes, axis=0, tiled=False)  28 us
    all_to_all x1, waiting for transfers between devices, state_body(): lax.all_to_all(orbitals, axes, split_axis=0, concat_axis=0, tiled=True)  27.8 us
    all_to_all x1, starting transfers between devices, state_body(): lax.all_to_all(orbitals, axes, split_axis=0, concat_axis=0, tiled=True)  7.3 us
  transfers between devices with their start and end apart: 2, of which 2 were waited for; matrix products, arithmetic and copies ran while one was open for 1% of the time, Pallas kernels for 0%

profile of v1, /device:TPU:0, one launch (start us, length us, event | category | flops | bytes accessed | tf_op | source)
XLA Modules:
  0.0 205.1 jit_solution(10021312373986114825)
XLA Ops:
  7.2 0.0 copy-start.4
  7.2 0.0 all-gather.3.cloned.1.call-start
  7.2 0.8 dynamic_slice.3
  8.0 0.1 lt.51
  8.1 0.1 iota_compare_fusion
  8.1 0.1 copy.19
  8.3 0.1 broadcast_and_fusion.1
  8.4 0.1 broadcast_and_fusion
  8.5 0.0 copy-start.5
  8.5 1.4 reshape.120
  10.0 0.3 fusion.1
  10.3 0.0 copy-start.1
  10.3 0.0 copy-start.2
  10.3 0.0 copy-start.3
  10.3 0.5 reshape.121
  10.8 0.0 copy-done.4
  10.8 0.6 pad_maximum_fusion
  11.4 0.0 all-gather.3.cloned.1.call-update
  11.5 7.3 %all-to-all-start = ((f32[32,8,8,128]{3,2,1,0:T(8,128)}), f32[32,8,8,128]{3,2,1,0:T(8,128)S(1)}, u32[]{:S(2)}, u32[]{:S(2)}) async-start(f32[32,8,8,128]{3,2,1,0:T(8,128)} %param.9), calls=%async_computation | async-start | bytes 2097152 | tf_op jit(solution)/shard_map/all_to_all | solution.py:467
  18.8 0.7 slice.3
  19.5 0.0 copy-done.5
  19.5 0.3 reshape.122
  19.9 0.6 broadcast_in_dim.16
  20.5 0.3 reshape.123.coupling
  20.8 27.8 %all-to-all-done.start = f32[32,8,8,128]{3,2,1,0:T(8,128)S(1)} async-done(((f32[32,8,8,128]{3,2,1,0:T(8,128)}), f32[32,8,8,128]{3,2,1,0:T(8,128)S(1)}, u32[]{:S(2)}, u32[]{:S(2)}) %all-to-all-start) | async-done | bytes 1048608 | tf_op jit(solution)/shard_map/all_to_all | solution.py:467
  48.5 28.0 %all-gather.3.cloned.1.call-done = f32[768,8,128]{2,1,0:T(8,128)} async-done(((f32[24,8,128]{2,1,0:T(8,128)}), f32[768,8,128]{2,1,0:T(8,128)}) %all-gather.3.cloned.1.call-update) | async-done | bytes 3145744 | tf_op jit(solution)/shard_map/all_gather | solution.py:466
  76.6 0.0 copy-done.1
  76.6 0.0 copy-done.2
  76.6 0.0 copy-done.3
  76.6 0.0 copy-start
  76.6 1.9 copy-done
  78.5 48.6 %shard_map.104 = f32[32,8,8,128]{3,2,1,0:T(8,128)S(1)} custom-call(s32[256]{0:T(256)S(1)} %copy-done.3, s32[256]{0:T(256)S(1)} %bitcast.14, f32[32,8,8,128]{3,2,1,0:T(8,128)S(1)} %all-to-all-done.start, f32[32,24,8,128]{3,2,1,0:T(8,128)S(1)} %bitcast.13, f32[512,128]{1,0:T(8,128)S(1)} %reshape.123.coupling, bf16[512,256]{1,0:T(8,128)(2,1)S(1)} %copy-done.2, ...), custom_call_target="tpu_custom_call" | custom-call | tf_op jit(solution)/shard_map/pallas_call | solution.py:429
  127.1 29.5 %all_to_all.10 = f32[32,8,8,128]{3,2,1,0:T(8,128)S(1)} all-to-all(f32[32,8,8,128]{3,2,1,0:T(8,128)S(1)} %shard_map.104), channel_id=1, replica_groups=mesh['gx'=4,'gy'=4,'gz'=2] {'gx','gy','gz'}, dimensions={0} | all-to-all | bytes 2097152 | tf_op jit(solution)/shard_map/all_to_all | solution.py:471
  156.6 1.5 convolution_bitcast_fusion
  158.1 38.6 %psum.7 = f32[32,32]{1,0:T(8,128)S(1)} all-reduce(f32[32,32]{1,0:T(8,128)S(1)} %convolution_bitcast_fusion), channel_id=1, replica_groups=mesh['gx'=4,'gy'=4,'gz'=2] {'gx','gy','gz'}, use_global_device_ids=true, to_apply=%region_0.1 | all-reduce | flops 1024 | bytes 8192 | tf_op jit(solution)/shard_map/psum | solution.py:475
  196.7 0.6 broadcast_multiply_fusion
  197.3 1.0 copy.31
  (1 shorter events, 0.0 us)
Async XLA Ops:
  7.2 3.6 %copy-start.4 = (f32[8,8,128]{2,1,0:T(8,128)S(1)}, f32[8,8,128]{2,1,0:T(8,128)}, u32[]{:S(2)}) copy-start(f32[8,8,128]{2,1,0:T(8,128)} %param.10) | copy-start | bytes 98308
  7.2 69.4 %all-gather.3.cloned.1.call-start = ((), (), s32[]{:S(2)}) async-start(), calls=%async_computation.2 | async-start | bytes 3244032 | tf_op jit(solution)/shard_map/all_gather | solution.py:466
  8.5 11.0 %copy-start.5 = (f32[256,4]{0,1:T(4,128)S(1)}, f32[256,4]{0,1:T(4,128)}, u32[]{:S(2)}) copy-start(f32[256,4]{0,1:T(4,128)} %param.15) | copy-start | bytes 12292
  10.3 66.3 %copy-start.1 = (bf16[512,256]{1,0:T(8,128)(2,1)S(1)}, bf16[512,256]{1,0:T(8,128)(2,1)}, u32[]{:S(2)}) copy-start(bf16[512,256]{1,0:T(8,128)(2,1)} %constant.31.clone.ymat) | copy-start | bytes 786436
  10.3 66.3 %copy-start.2 = (bf16[512,256]{1,0:T(8,128)(2,1)S(1)}, bf16[512,256]{1,0:T(8,128)(2,1)}, u32[]{:S(2)}) copy-start(bf16[512,256]{1,0:T(8,128)(2,1)} %constant.30.clone.zmat) | copy-start | bytes 786436
  10.3 66.3 %copy-start.3 = (s32[256]{0:T(256)S(1)}, s32[256]{0:T(256)}, u32[]{:S(2)}) copy-start(s32[256]{0:T(256)} %owner.1) | copy-start | bytes 3076
  11.5 37.1 %all-to-all-start = ((f32[32,8,8,128]{3,2,1,0:T(8,128)}), f32[32,8,8,128]{3,2,1,0:T(8,128)S(1)}, u32[]{:S(2)}, u32[]{:S(2)}) async-start(f32[32,8,8,128]{3,2,1,0:T(8,128)} %param.9), calls=%async_computation | async-start | bytes 2097152 | tf_op jit(solution)/shard_map/all_to_all | solution.py:467
  76.6 1.9 copy-start
Sparse Core Ops, SparseCore 0:
  11.6 64.9 all-gather.2

commit v2 on v0

--- a/solution.py
+++ b/solution.py
@@ -1,6 +1,11 @@
+import functools
 import jax
 import jax.numpy as jnp
 from jax import lax
+from jax.experimental import pallas as pl
+from jax.experimental.pallas import tpu as pltpu
+import ml_dtypes
+import numpy as np
 from jax.sharding import PartitionSpec as P
 
 B = 8
@@ -127,7 +132,7 @@
     return result
 
 
-def body(orbitals, potential, projectors, owner_rank, box_anchor, box_extent, coupling):
+def domain_body(orbitals, potential, projectors, owner_rank, box_anchor, box_extent, coupling):
     groups_y = lax.axis_size("gy")
     groups_z = lax.axis_size("gz")
     own_x = owner_rank // (groups_y * groups_z)
@@ -158,6 +163,387 @@
     cells_total = span_x * span_y * span_z * lax.axis_size("gx") * groups_y * groups_z
     intersection = lax.psum(partial_value, ("gx", "gy", "gz")) / cells_total
     return (filtered, intersection)
+
+
+SUB = 8
+LANE = 128
+HALF = LANE // 2
+NPROJ = 4
+
+
+def split_terms(matrix):
+    high = matrix.astype(ml_dtypes.bfloat16)
+    low = (matrix - high.astype(np.float64)).astype(ml_dtypes.bfloat16)
+    return high, low
+
+
+def stencil_weight(distance):
+    if distance == 0 or abs(distance) > 6:
+        return 0.0
+    return -0.5 * STENCIL[abs(distance)] / (SPACING * SPACING)
+
+
+def ring_matrix(length):
+    matrix = np.zeros((length, length))
+    for offset in range(-6, 7):
+        for row in range(length):
+            matrix[row, (row + offset) % length] += stencil_weight(offset)
+    return matrix
+
+
+def plane_weights(groups_y):
+    slab = groups_y * HALF
+    ring = ring_matrix(groups_y * SUB).reshape(groups_y, SUB, groups_y, SUB)
+    blocks = []
+    for shift in (-SUB, 0, SUB):
+        along_x = np.array(
+            [[stencil_weight(shift + i - o) for o in range(SUB)] for i in range(SUB)]
+        )
+        block = np.einsum("ab,io,jp->aijbop", np.eye(groups_y), along_x, np.eye(SUB))
+        if shift == 0:
+            block = block + np.einsum("ajbp,io->aijbop", ring, np.eye(SUB))
+        blocks.append(block.reshape(slab, slab))
+    high, low = split_terms(np.concatenate(blocks, axis=0))
+    return np.concatenate([high, high, low], axis=0)
+
+
+def depth_weights(groups_z):
+    high, low = split_terms(ring_matrix(groups_z * LANE))
+    return np.concatenate([high, low, high], axis=1)
+
+
+def split_pair(value):
+    high = value.astype(jnp.bfloat16)
+    low = (value - high.astype(jnp.float32)).astype(jnp.bfloat16)
+    return high, low
+
+
+def mxu(left, right):
+    return jnp.dot(left, right, preferred_element_type=jnp.float32)
+
+
+def filter_kernel(groups, atoms, place, half, my_z, start, *refs):
+    groups_x, groups_y, groups_z = groups
+    packs = refs[:groups_z]
+    coupling, plane, depth, out = refs[groups_z : groups_z + 4]
+    field_a, field_b, field_c, local, added, boxes, coeffs, high_buf, low_buf, near = refs[
+        groups_z + 4 :
+    ]
+    columns = groups_x * groups_y
+    domains = columns * groups_z
+    pairs = columns // 2
+    span = groups_z * LANE
+    slab = groups_y * HALF
+    pairs_slab = groups_y // 2
+    per_device = atoms // domains // SUB
+    half_width = (UPPER - CUTOFF) / 2.0
+    middle = (UPPER + CUTOFF) / 2.0
+    diagonal = -0.5 * 3.0 * STENCIL[0] / (SPACING * SPACING) - middle
+    lane = lax.broadcasted_iota(jnp.int32, (SUB, LANE), 1)
+    lower = lane < HALF
+    side = lane // HALF
+    f32 = jnp.float32
+
+    def depth_of(hop):
+        return lax.rem(my_z[0] + (groups_z - hop), groups_z)
+
+    for hop in range(groups_z):
+        base = depth_of(hop) * LANE
+
+        def lay_potential(pair, carry):
+            for row in range(SUB):
+                first = packs[hop][2 * pair, row]
+                second = packs[hop][2 * pair + 1, row]
+                at = pl.multiple_of(pair * span + base + row * SUB, SUB)
+                local[pl.ds(at, SUB), :] = diagonal + jnp.where(
+                    lower, first, pltpu.roll(second, HALF, 1)
+                )
+                at = pl.multiple_of(pair * span + base + HALF + row * SUB, SUB)
+                local[pl.ds(at, SUB), :] = diagonal + jnp.where(
+                    lower, pltpu.roll(first, HALF, 1), second
+                )
+            return carry
+
+        lax.fori_loop(0, pairs, lay_potential, 0)
+
+    def lay_field(pair, carry):
+        for depth_at in range(groups_z):
+            first = start[2 * pair * groups_z + depth_at].reshape(HALF, LANE)
+            second = start[(2 * pair + 1) * groups_z + depth_at].reshape(HALF, LANE)
+            turned = jnp.concatenate([first, second], axis=0).T
+            at = pl.multiple_of(pair * span + depth_at * LANE, LANE)
+            field_a[pl.ds(at, LANE), :] = turned
+            high, low = split_pair(turned)
+            cols = pl.ds(pl.multiple_of(pair * LANE, LANE), LANE)
+            high_buf[depth_at * LANE : (depth_at + 1) * LANE, cols] = high
+            low_buf[depth_at * LANE : (depth_at + 1) * LANE, cols] = low
+            for spare in range(2):
+                added[spare, pl.ds(at, LANE), :] = jnp.zeros((LANE, LANE), f32)
+        return carry
+
+    lax.fori_loop(0, pairs, lay_field, 0)
+
+    ones = (
+        (
+            lax.broadcasted_iota(jnp.int32, (LANE, LANE), 0) // HALF
+            == lax.broadcasted_iota(jnp.int32, (LANE, LANE), 1) // HALF
+        )
+        .astype(f32)
+        .astype(jnp.bfloat16)
+    )
+
+    def each_group(visit):
+        for hop in range(groups_z):
+            depth_at = depth_of(hop)
+
+            def step(column, carry):
+                device = column * groups_z + depth_at
+                for inner in range(per_device):
+                    stored = (hop * columns + column) * per_device + inner
+                    visit(
+                        stored,
+                        device * per_device + inner,
+                        lambda kp, row: packs[hop][column, SUB + (inner * 2 + kp) * SUB + row],
+                    )
+                return carry
+
+            lax.fori_loop(0, columns, step, 0)
+
+    def apply_step(cur, prev, new, alpha, beta, last):
+        def gather(stored, group, proj):
+            for j in range(SUB):
+                atom = group * SUB + j
+                value = cur[pl.ds(place[atom], SUB), :]
+                both = jnp.where(side == half[atom], value, pltpu.roll(value, HALF, 1))
+                boxes[pl.ds(stored * SUB * SUB + j, SUB, stride=SUB), :] = both
+
+        each_group(gather)
+
+        def project(stored, group, proj):
+            base = pl.multiple_of(stored * SUB * SUB, SUB * SUB)
+            values = [boxes[pl.ds(base + row * SUB, SUB), :] for row in range(SUB)]
+            for kp in range(2):
+                terms = [values[row] * proj(kp, row) for row in range(SUB)]
+                while len(terms) > 1:
+                    terms = [terms[i] + terms[i + 1] for i in range(0, len(terms), 2)]
+                at = pl.multiple_of(stored * 2 * SUB + kp * SUB, SUB)
+                coeffs[pl.ds(at, SUB), :] = terms[0]
+
+        each_group(project)
+
+        high, low = split_pair(coeffs[...])
+        coeffs[...] = mxu(high, ones) + mxu(low, ones)
+
+        def expand(stored, group, proj):
+            base = pl.multiple_of(stored * SUB * SUB, SUB * SUB)
+            at = pl.multiple_of(stored * 2 * SUB, 2 * SUB)
+            by = pl.multiple_of(group * 2 * SUB, 2 * SUB)
+            first = coeffs[pl.ds(at, SUB), :] * coupling[pl.ds(by, SUB), :]
+            second = coeffs[pl.ds(at + SUB, SUB), :] * coupling[pl.ds(by + SUB, SUB), :]
+            for row in range(SUB):
+                value = first * proj(0, row) + second * proj(1, row)
+                boxes[pl.ds(base + row * SUB, SUB), :] = value + pltpu.roll(value, HALF, 1)
+
+        each_group(expand)
+
+        def scatter(stored, group, proj):
+            for j in range(SUB):
+                atom = group * SUB + j
+                value = boxes[pl.ds(stored * SUB * SUB + j, SUB, stride=SUB), :]
+                value = jnp.where(side == half[atom], value, 0.0)
+                at = pl.ds(place[atom], SUB)
+                added[j % 2, at, :] = added[j % 2, at, :] + value
+
+        each_group(scatter)
+
+        def product(slab_at, carry):
+            def around(buf, shift):
+                other = lax.rem(slab_at + shift + groups_x, groups_x)
+                return buf[:, pl.ds(pl.multiple_of(other * slab, slab), slab)]
+
+            high = [around(high_buf, shift) for shift in (-1, 0, 1)]
+            low = [around(low_buf, shift) for shift in (-1, 0, 1)]
+            left = jnp.concatenate(high + low + high + [depth[...]], axis=1)
+            right = jnp.concatenate([plane[...], high[1], high[1], low[1]], axis=0)
+            near[:, pl.ds(pl.multiple_of(slab_at * slab, slab), slab)] = mxu(left, right)
+            return carry
+
+        lax.fori_loop(0, groups_x, product, 0)
+
+        def combine(pair, carry):
+            for at_row in range(0, span, SUB):
+                at = pl.multiple_of(pair * span + at_row, SUB)
+                rows = pl.ds(at, SUB)
+                cols = pl.ds(pl.multiple_of(pair * LANE, LANE), LANE)
+                total = near[at_row : at_row + SUB, cols] + local[rows, :] * cur[rows, :]
+                total = (total + (added[0, rows, :] + added[1, rows, :])) * alpha
+                if beta is not None:
+                    total = total + beta * prev[rows, :]
+                new[rows, :] = total
+                if not last:
+                    for spare in range(2):
+                        added[spare, rows, :] = jnp.zeros((SUB, LANE), f32)
+            if not last:
+                for at_row in range(0, span, 2 * SUB):
+                    at = pl.multiple_of(pair * span + at_row, 2 * SUB)
+                    cols = pl.ds(pl.multiple_of(pair * LANE, LANE), LANE)
+                    high, low = split_pair(new[pl.ds(at, 2 * SUB), :])
+                    high_buf[at_row : at_row + 2 * SUB, cols] = high
+                    low_buf[at_row : at_row + 2 * SUB, cols] = low
+            return carry
+
+        lax.fori_loop(0, pairs, combine, 0)
+
+    sigma_one = half_width / (LOW_EDGE - middle)
+    sigma_now = sigma_one
+    apply_step(field_a, None, field_b, sigma_one / half_width, None, DEGREE == 1)
+    prev, cur, new = field_a, field_b, field_c
+    for degree_step in range(1, DEGREE):
+        sigma_next = 1.0 / (2.0 / sigma_one - sigma_now)
+        apply_step(
+            cur,
+            prev,
+            new,
+            2.0 * sigma_next / half_width,
+            -sigma_now * sigma_next,
+            degree_step == DEGREE - 1,
+        )
+        prev, cur, new = cur, new, prev
+        sigma_now = sigma_next
+
+    def hand_back(pair, carry):
+        for depth_at in range(groups_z):
+            at = pl.multiple_of(pair * span + depth_at * LANE, LANE)
+            turned = cur[pl.ds(at, LANE), :].T
+            out[2 * pair * groups_z + depth_at] = turned[:HALF].reshape(SUB, SUB, LANE)
+            out[(2 * pair + 1) * groups_z + depth_at] = turned[HALF:].reshape(SUB, SUB, LANE)
+        return carry
+
+    lax.fori_loop(0, pairs, hand_back, 0)
+
+
+def packed_inputs(potential, projectors, extent):
+    atoms = projectors.shape[0]
+    cells = jnp.arange(B, dtype=jnp.int32)
+    limit = extent[:, None, None, None]
+    inside = (
+        (cells[None, :, None, None] < limit)
+        & (cells[None, None, :, None] < limit)
+        & (cells[None, None, None, :] < limit)
+    )
+    masked = jnp.where(
+        inside.reshape(atoms, 1, B * B * B), projectors, 0.0
+    ).reshape(atoms // SUB, SUB, 2, 2, B * B, B)
+    masked = masked.transpose(0, 2, 5, 1, 3, 4).reshape(atoms // SUB * 2 * B, SUB, LANE)
+    shaped = potential.reshape(HALF, 2, HALF).transpose(2, 1, 0).reshape(SUB, SUB, LANE)
+    return jnp.concatenate([shaped, masked], axis=0)
+
+
+def packed_coupling(coupling):
+    atoms = coupling.shape[0]
+    parts = coupling.reshape(atoms // SUB, SUB, 2, 2).transpose(0, 2, 1, 3)
+    wide = jnp.broadcast_to(parts[..., None], parts.shape + (HALF,))
+    return wide.reshape(atoms * 2, LANE)
+
+
+def box_places(groups, owner, anchor):
+    groups_z = groups[2]
+    column = owner // groups_z
+    place = (column // 2 * groups_z + owner % groups_z) * LANE + anchor
+    return place, column % 2
+
+
+def filter_call(groups, place, half, my_z, field, packs, coupling, interpret=False):
+    groups_x, groups_y, groups_z = groups
+    columns = groups_x * groups_y
+    atoms = place.shape[0]
+    shape = (columns * groups_z, SUB, SUB, LANE)
+    span = groups_z * LANE
+    width = columns * HALF
+    cells = (columns // 2 * span, LANE)
+    vmem = pl.BlockSpec(memory_space=pltpu.VMEM)
+    smem = pl.BlockSpec(memory_space=pltpu.SMEM)
+    return pl.pallas_call(
+        functools.partial(filter_kernel, groups, atoms),
+        out_shape=jax.ShapeDtypeStruct(shape, jnp.float32),
+        in_specs=[smem] * 3 + [vmem] * (groups_z + 4),
+        out_specs=vmem,
+        scratch_shapes=[
+            pltpu.VMEM(cells, jnp.float32),
+            pltpu.VMEM(cells, jnp.float32),
+            pltpu.VMEM(cells, jnp.float32),
+            pltpu.VMEM(cells, jnp.float32),
+            pltpu.VMEM((2,) + cells, jnp.float32),
+            pltpu.VMEM((atoms * SUB, LANE), jnp.float32),
+            pltpu.VMEM((atoms * 2, LANE), jnp.float32),
+            pltpu.VMEM((span, width), jnp.bfloat16),
+            pltpu.VMEM((span, width), jnp.bfloat16),
+            pltpu.VMEM((span, width), jnp.float32),
+        ],
+        compiler_params=pltpu.CompilerParams(vmem_limit_bytes=48 * 1024 * 1024),
+        interpret=interpret,
+    )(
+        place,
+        half,
+        my_z,
+        field,
+        *packs,
+        coupling,
+        jnp.asarray(plane_weights(groups_y)),
+        jnp.asarray(depth_weights(groups_z)),
+    )
+
+
+def state_body(orbitals, potential, projectors, owner_rank, box_anchor, box_extent, coupling):
+    axes = ("gx", "gy", "gz")
+    groups = tuple(lax.axis_size(axis) for axis in axes)
+    groups_z = groups[2]
+    domains = groups[0] * groups[1] * groups_z
+    atoms_own = projectors.shape[0]
+    my_z = lax.axis_index("gz")
+    me = (lax.axis_index("gx") * groups[1] + lax.axis_index("gy")) * groups_z + my_z
+    extent = lax.dynamic_slice(box_extent, (me * atoms_own,), (atoms_own,))
+    pack = packed_inputs(potential, projectors, extent)
+    pack = lax.all_gather(pack, ("gx", "gy"), axis=0, tiled=False)
+    packs = [pack] + [
+        lax.ppermute(pack, "gz", [(i, (i + hop) % groups_z) for i in range(groups_z)])
+        for hop in range(1, groups_z)
+    ]
+    field = lax.all_to_all(orbitals, axes, split_axis=0, concat_axis=0, tiled=True)
+    place, half = box_places(groups, owner_rank, box_anchor[2])
+    result = filter_call(
+        groups, place, half, my_z[None], field, packs, packed_coupling(coupling)
+    )
+    filtered = lax.all_to_all(result, axes, split_axis=0, concat_axis=0, tiled=True)
+    states = filtered.shape[0]
+    flattened = filtered.reshape(states, -1)
+    partial_value = jnp.dot(flattened, flattened.T, precision=lax.Precision.HIGHEST)
+    quarter = partial_value.reshape(-1, SUB, states).transpose(1, 0, 2).reshape(SUB, -1)
+    parts = lax.all_to_all(
+        jnp.broadcast_to(quarter[None], (domains,) + quarter.shape),
+        axes,
+        split_axis=0,
+        concat_axis=0,
+        tiled=True,
+    )
+    summed = jnp.sum(parts, axis=0).reshape(SUB, -1, states).transpose(1, 0, 2)
+    cells_total = orbitals.shape[1] * orbitals.shape[2] * orbitals.shape[3] * domains
+    intersection = summed.reshape(states, states) / cells_total
+    return (filtered, intersection)
+
+
+def body(orbitals, potential, projectors, owner_rank, box_anchor, box_extent, coupling):
+    domains = lax.axis_size("gx") * lax.axis_size("gy") * lax.axis_size("gz")
+    whole_states = (
+        orbitals.shape == (domains, SUB, SUB, LANE)
+        and projectors.shape[0] % SUB == 0
+        and projectors.shape[1] == NPROJ
+        and lax.axis_size("gy") % 2 == 0
+    )
+    chosen = state_body if whole_states else domain_body
+    return chosen(
+        orbitals, potential, projectors, owner_rank, box_anchor, box_extent, coupling
+    )
 
 
 def solution(mesh):

time: 1570 us -> 175 us (0.11); the launches traced: 1550 us -> 174 us
  starting transfers between devices: 518 us -> 7.34 us
  waiting for transfers between devices: 335 us -> 56.7 us
  local copies, waits for them, and re-layouts: 272 us -> 10.6 us
  blocking collectives: 191 us -> 41.1 us
  other arithmetic: 114 us -> 1.88 us
  loops' own time: 58 us -> 0 us
  matrix products: 45.5 us -> 0.97 us
  Pallas kernels: 0 us -> 41.6 us
    ppermute x24 -> x1, starting transfers between devices: 518 us -> 0.01 us  [state_body(): lax.ppermute(pack, 'gz', [(i, (i + hop) % groups_z) for i in range(groups...]
    ppermute x24 -> x1, waiting for transfers between devices: 335 us -> 0.01 us  [state_body(): lax.ppermute(pack, 'gz', [(i, (i + hop) % groups_z) for i in range(groups...]
    psum x1 -> x0, blocking collectives: 191 us -> none  [body(): intersection = lax.psum(partial_value, ('gx', 'gy', 'gz')) / cells_total]
    slice x37 -> x1, local copies, waits for them, and re-layouts: 122 us -> 0.81 us  [state_body(): place, half = box_places(groups, owner_rank, box_anchor[2])]
    another operation x4 -> x0, loops' own time: 58 us -> none  [nonlocal_term(): return lax.fori_loop(0, count, add_slot, jnp.zeros_like(field))]
    all_gather x1, waiting for transfers between devices: 0.01 us -> 56.6 us  [state_body(): pack = lax.all_gather(pack, ('gx', 'gy'), axis=0, tiled=False)]
    sub x20 -> x0, other arithmetic: 45.9 us -> none  [the longest x3 45.7 us: run_filter(): (apply_h(result) - middle * result) * (2.0 * sigma_next / half_width)]
    ppermute x8 -> x0, local copies, waits for them, and re-layouts: 44.6 us -> none  [the longest x4 22.3 us: extended(): lax.ppermute(head, axis, [((i + 1) % count, i) for i in range(count)])]
  transfers between devices with their start and end apart: 25 -> 3, of which waited for: 13 -> 1; matrix products, arithmetic and copies ran while one was open for 14% -> 2% of each run, Pallas kernels for 0% -> 0%
where the time goes in v2:
time: 175 us; the launch traced here: 174 us
  waiting for transfers between devices  56.7 us (32%)
  Pallas kernels  41.6 us (24%)
  blocking collectives  41.1 us (23%)
  between operations  14.2 us (8%)
  local copies, waits for them, and re-layouts  10.6 us (6%)
  starting transfers between devices  7.34 us (4%)
  other arithmetic  1.88 us (1%)
    all_gather x1, waiting for transfers between devices, state_body(): pack = lax.all_gather(pack, ('gx', 'gy'), axis=0, tiled=False)  56.6 us
    pallas_call x1, Pallas kernels, filter_call(): pl.pallas_call(functools.partial(filter_kernel, groups, atoms), out_shape...  41.6 us
    all_to_all x1, blocking collectives, state_body(): lax.all_to_all(result, axes, split_axis=0, concat_axis=0, tiled=True)  29.4 us
    all_to_all x1, blocking collectives, state_body(): lax.all_to_all(jnp.broadcast_to(quarter[None], (domains,) + quarter.shape...  11.7 us
    all_to_all x1, starting transfers between devices, state_body(): lax.all_to_all(orbitals, axes, split_axis=0, concat_axis=0, tiled=True)  7.3 us
  transfers between devices with their start and end apart: 3, of which 1 were waited for; matrix products, arithmetic and copies ran while one was open for 2% of the time, Pallas kernels for 0%

profile of v2, /device:TPU:0, one launch (start us, length us, event | category | flops | bytes accessed | tf_op | source)
XLA Modules:
  0.0 174.3 jit_solution(18251519720877670765)
XLA Ops:
  7.2 0.0 all-gather.3.cloned.1.call-start
  7.2 0.8 dynamic_slice.3
  8.0 0.1 iota_compare_fusion
  8.1 0.1 broadcast_and_fusion.1
  8.1 0.1 broadcast_and_fusion
  8.3 0.2 and.69
  8.5 0.9 broadcast_select_fusion
  9.4 0.9 reshape.125
  10.2 0.1 copy.30
  10.3 0.1 reshape.126
  10.4 0.6 reshape.127
  11.0 0.3 copy.32
  11.4 0.0 copy-start.3
  11.4 0.1 reshape.128
  11.5 0.7 pad_maximum_fusion
  12.2 0.0 all-gather.3.cloned.1.call-update
  12.2 0.0 copy-start.4
  12.2 0.0 copy-start.2
  12.2 7.3 %all-to-all-start = ((f32[32,8,8,128]{3,2,1,0:T(8,128)}), f32[32,8,8,128]{3,2,1,0:T(8,128)S(1)}, u32[]{:S(2)}, u32[]{:S(2)}) async-start(f32[32,8,8,128]{3,2,1,0:T(8,128)} %param.9), calls=%async_computation | async-start | bytes 2097152 | tf_op jit(solution)/shard_map/all_to_all | solution.py:512
  19.5 56.6 %all-gather.3.cloned.1.call-done = f32[384,8,128]{2,1,0:T(8,128)} async-done(((f32[24,8,128]{2,1,0:T(8,128)}), f32[384,8,128]{2,1,0:T(8,128)}) %all-gather.3.cloned.1.call-update) | async-done | bytes 1572880 | tf_op jit(solution)/shard_map/all_gather | solution.py:507
  76.2 0.0 copy-start
  76.2 0.0 collective-permute-start
  76.2 0.8 slice.3
  77.0 0.0 copy-done.3
  77.0 0.1 reshape.129
  77.1 0.4 copy.33
  77.5 1.4 broadcast_in_dim.35
  78.9 1.3 reshape.130.refs_2_
  80.3 0.0 copy-done.4
  80.3 0.0 all-to-all-done.start
  80.3 0.0 collective-permute-done.refs_1_
  80.3 0.0 copy-done.2
  80.3 0.0 copy-done
  80.3 0.0 copy-start.1
  80.4 1.3 copy-done.1
  81.6 41.6 %shard_map.104 = f32[32,8,8,128]{3,2,1,0:T(8,128)S(1)} custom-call(s32[256]{0:T(256)S(1)} %multiply_add_fusion.place, s32[256]{0:T(256)S(1)} %get-tuple-element.2.half, s32[1]{0:T(128)} %bitcast.1.my_z, f32[32,8,8,128]{3,2,1,0:T(8,128)S(1)} %all-to-all-done.start, f32[16,24,8,128]{3,2,1,0:T(8,128)S(1)} %bitcast.25, ...), custom_call_target="tpu_custom_call" | custom-call | tf_op jit(solution)/shard_map/pallas_call | solution.py:466
  123.2 29.4 %all_to_all.15 = f32[32,8,8,128]{3,2,1,0:T(8,128)S(1)} all-to-all(f32[32,8,8,128]{3,2,1,0:T(8,128)S(1)} %shard_map.104), channel_id=1, replica_groups=mesh['gx'=4,'gy'=4,'gz'=2] {'gx','gy','gz'}, dimensions={0} | all-to-all | bytes 2097152 | tf_op jit(solution)/shard_map/all_to_all | solution.py:517
  152.6 0.2 reshape.133
  152.8 0.2 dot_general.5
  153.0 1.0 convolution_bitcast_fusion
  154.0 0.1 broadcast_in_dim.36
  154.1 11.7 %all_to_all.16 = f32[32,8,128]{2,1,0:T(8,128)S(1)} all-to-all(f32[32,8,128]{2,1,0:T(8,128)S(1)} %broadcast_in_dim.37), channel_id=1, replica_groups=mesh['gx'=4,'gy'=4,'gz'=2] {'gx','gy','gz'}, dimensions={0} | all-to-all | bytes 262144 | tf_op jit(solution)/shard_map/all_to_all | solution.py:522
  165.8 0.1 div.38
  165.9 0.6 copy.37
  166.5 1.0 copy.39
  (7 shorter events, 0.1 us)
Async XLA Ops:
  7.2 69.0 %all-gather.3.cloned.1.call-start = ((), (), s32[]{:S(2)}) async-start(), calls=%async_computation.3 | async-start | bytes 1671168 | tf_op jit(solution)/shard_map/all_gather | solution.py:507
  11.4 65.6 %copy-start.3 = (f32[256,4]{0,1:T(4,128)S(1)}, f32[256,4]{0,1:T(4,128)}, u32[]{:S(2)}) copy-start(f32[256,4]{0,1:T(4,128)} %param.15) | copy-start | bytes 12292
  12.2 68.1 %copy-start.4 = (s32[256]{0:T(256)S(1)}, s32[256]{0:T(256)}, u32[]{:S(2)}) copy-start(s32[256]{0:T(256)} %param.12) | copy-start | bytes 3076
  12.2 68.1 %copy-start.2 = (bf16[256,768]{1,0:T(8,128)(2,1)S(1)}, bf16[256,768]{1,0:T(8,128)(2,1)}, u32[]{:S(2)}) copy-start(bf16[256,768]{1,0:T(8,128)(2,1)} %constant.69.clone.refs_4_) | copy-start | bytes 1179652
  12.2 68.1 %all-to-all-start = ((f32[32,8,8,128]{3,2,1,0:T(8,128)}), f32[32,8,8,128]{3,2,1,0:T(8,128)S(1)}, u32[]{:S(2)}, u32[]{:S(2)}) async-start(f32[32,8,8,128]{3,2,1,0:T(8,128)} %param.9), calls=%async_computation | async-start | bytes 2097152 | tf_op jit(solution)/shard_map/all_to_all | solution.py:512
  76.2 4.2 %copy-start = (f32[384,8,128]{2,1,0:T(8,128)S(1)}, f32[384,8,128]{2,1,0:T(8,128)}, u32[]{:S(2)}) copy-start(f32[384,8,128]{2,1,0:T(8,128)} %all-gather.3.cloned.1.call-done) | copy-start | bytes 4718596
  76.2 4.2 %collective-permute-start = (f32[16,24,8,128]{3,2,1,0:T(8,128)}, f32[16,24,8,128]{3,2,1,0:T(8,128)}, u32[]{:S(2)}, u32[]{:S(2)}) collective-permute-start(f32[16,24,8,128]{3,2,1,0:T(8,128)} %bitcast.24), channel_id=1, source_target_pairs={{0,1},{1,0},{2,3},{3,2},{4,5},{5,4},{6,7},{7,6},{8,9},{9,8},{10,11... | collective-permute-start | bytes 4718600 | tf_op jit(solution)/shard_map/ppermute | solution.py:509
  80.3 1.3 copy-start.1
Sparse Core Ops, SparseCore 0:
  12.3 63.8 all-gather.2

commit v3 on v2

--- a/solution.py
+++ b/solution.py
@@ -222,19 +222,49 @@
     return jnp.dot(left, right, preferred_element_type=jnp.float32)
 
 
-def filter_kernel(groups, atoms, place, half, my_z, start, *refs):
+def row_sums(values):
+    row = lax.broadcasted_iota(jnp.int32, (SUB, LANE), 0)
+    for stride in (1, 2, 4):
+        keep = (row & stride) == 0
+        values = [
+            jnp.where(keep, one, two) + pltpu.roll(jnp.where(keep, two, one), stride, 0)
+            for one, two in zip(values[0::2], values[1::2])
+        ]
+    return values[0]
+
+
+SPARES = 2
+
+
+def filter_kernel(groups, atoms, place, half, my_place, *refs):
     groups_x, groups_y, groups_z = groups
-    packs = refs[:groups_z]
-    coupling, plane, depth, out = refs[groups_z : groups_z + 4]
-    field_a, field_b, field_c, local, added, boxes, coeffs, high_buf, low_buf, near = refs[
-        groups_z + 4 :
-    ]
+    pieces = groups_y * groups_z
+    field_in = refs[0]
+    packs_in = refs[1 : 1 + pieces]
+    coupling_in, plane_in, depth_in, out = refs[1 + pieces : 5 + pieces]
+    (
+        field_a,
+        field_b,
+        field_c,
+        local,
+        added,
+        coeffs,
+        high_buf,
+        low_buf,
+        near,
+        packs,
+        coupling,
+        plane,
+        depth,
+        in_sems,
+        pack_sems,
+        out_sems,
+    ) = refs[5 + pieces :]
     columns = groups_x * groups_y
     domains = columns * groups_z
     pairs = columns // 2
     span = groups_z * LANE
     slab = groups_y * HALF
-    pairs_slab = groups_y // 2
     per_device = atoms // domains // SUB
     half_width = (UPPER - CUTOFF) / 2.0
     middle = (UPPER + CUTOFF) / 2.0
@@ -244,44 +274,76 @@
     side = lane // HALF
     f32 = jnp.float32
 
-    def depth_of(hop):
-        return lax.rem(my_z[0] + (groups_z - hop), groups_z)
-
-    for hop in range(groups_z):
-        base = depth_of(hop) * LANE
-
-        def lay_potential(pair, carry):
+    loads = [
+        pltpu.make_async_copy(source, target, in_sems.at[number])
+        for number, (source, target) in enumerate(
+            ((field_in, field_b), (plane_in, plane), (depth_in, depth), (coupling_in, coupling))
+        )
+    ]
+    for load in loads:
+        load.start()
+    pack_loads = []
+    for hop_z in range(groups_z):
+        for hop_y in range(groups_y):
+            source = packs_in[hop_z * groups_y + hop_y]
+            for hop_x in range(groups_x):
+                from_x = lax.rem(my_place[0] + (groups_x - hop_x), groups_x)
+                from_y = lax.rem(my_place[1] + (groups_y - hop_y), groups_y)
+                from_z = lax.rem(my_place[2] + (groups_z - hop_z), groups_z)
+                device = (from_x * groups_y + from_y) * groups_z + from_z
+                number = (hop_z * groups_y + hop_y) * groups_x + hop_x
+                pack_loads.append(
+                    pltpu.make_async_copy(
+                        source.at[hop_x], packs.at[device], pack_sems.at[number]
+                    )
+                )
+    for load in pack_loads:
+        load.start()
+    loads[0].wait()
+
+    def split_rows(source, pair, first_row, rows):
+        cols = pl.ds(pl.multiple_of(pair * LANE, LANE), LANE)
+        for at_row in range(first_row, first_row + rows, 2 * SUB):
+            at = pl.multiple_of(pair * span + at_row, 2 * SUB)
+            high, low = split_pair(source[pl.ds(at, 2 * SUB), :])
+            high_buf[at_row : at_row + 2 * SUB, cols] = high
+            low_buf[at_row : at_row + 2 * SUB, cols] = low
+
+    def block_rows(pair, parity, depth_at):
+        return pl.multiple_of(((2 * pair + parity) * groups_z + depth_at) * HALF, HALF)
+
+    def lay_field(pair, carry):
+        for depth_at in range(groups_z):
+            first = field_b[pl.ds(block_rows(pair, 0, depth_at), HALF), :]
+            second = field_b[pl.ds(block_rows(pair, 1, depth_at), HALF), :]
+            at = pl.multiple_of(pair * span + depth_at * LANE, LANE)
+            field_a[pl.ds(at, LANE), :] = jnp.concatenate([first, second], axis=0).T
+            for spare in range(SPARES):
+                added[spare, pl.ds(at, LANE), :] = jnp.zeros((LANE, LANE), f32)
+        split_rows(field_a, pair, 0, span)
+        return carry
+
+    lax.fori_loop(0, pairs, lay_field, 0)
+
+    for load in loads[1:] + pack_loads:
+        load.wait()
+
+    def lay_potential(pair, carry):
+        for depth_at in range(groups_z):
             for row in range(SUB):
-                first = packs[hop][2 * pair, row]
-                second = packs[hop][2 * pair + 1, row]
-                at = pl.multiple_of(pair * span + base + row * SUB, SUB)
+                first = packs[2 * pair * groups_z + depth_at, row]
+                second = packs[(2 * pair + 1) * groups_z + depth_at, row]
+                at = pl.multiple_of(pair * span + depth_at * LANE + row * SUB, SUB)
                 local[pl.ds(at, SUB), :] = diagonal + jnp.where(
                     lower, first, pltpu.roll(second, HALF, 1)
                 )
-                at = pl.multiple_of(pair * span + base + HALF + row * SUB, SUB)
+                at = pl.multiple_of(at + HALF, SUB)
                 local[pl.ds(at, SUB), :] = diagonal + jnp.where(
                     lower, pltpu.roll(first, HALF, 1), second
                 )
-            return carry
-
-        lax.fori_loop(0, pairs, lay_potential, 0)
-
-    def lay_field(pair, carry):
-        for depth_at in range(groups_z):
-            first = start[2 * pair * groups_z + depth_at].reshape(HALF, LANE)
-            second = start[(2 * pair + 1) * groups_z + depth_at].reshape(HALF, LANE)
-            turned = jnp.concatenate([first, second], axis=0).T
-            at = pl.multiple_of(pair * span + depth_at * LANE, LANE)
-            field_a[pl.ds(at, LANE), :] = turned
-            high, low = split_pair(turned)
-            cols = pl.ds(pl.multiple_of(pair * LANE, LANE), LANE)
-            high_buf[depth_at * LANE : (depth_at + 1) * LANE, cols] = high
-            low_buf[depth_at * LANE : (depth_at + 1) * LANE, cols] = low
-            for spare in range(2):
-                added[spare, pl.ds(at, LANE), :] = jnp.zeros((LANE, LANE), f32)
         return carry
 
-    lax.fori_loop(0, pairs, lay_field, 0)
+    lax.fori_loop(0, pairs, lay_potential, 0)
 
     ones = (
         (
@@ -292,69 +354,14 @@
         .astype(jnp.bfloat16)
     )
 
-    def each_group(visit):
-        for hop in range(groups_z):
-            depth_at = depth_of(hop)
-
-            def step(column, carry):
-                device = column * groups_z + depth_at
-                for inner in range(per_device):
-                    stored = (hop * columns + column) * per_device + inner
-                    visit(
-                        stored,
-                        device * per_device + inner,
-                        lambda kp, row: packs[hop][column, SUB + (inner * 2 + kp) * SUB + row],
-                    )
-                return carry
-
-            lax.fori_loop(0, columns, step, 0)
-
-    def apply_step(cur, prev, new, alpha, beta, last):
-        def gather(stored, group, proj):
-            for j in range(SUB):
-                atom = group * SUB + j
-                value = cur[pl.ds(place[atom], SUB), :]
-                both = jnp.where(side == half[atom], value, pltpu.roll(value, HALF, 1))
-                boxes[pl.ds(stored * SUB * SUB + j, SUB, stride=SUB), :] = both
-
-        each_group(gather)
-
-        def project(stored, group, proj):
-            base = pl.multiple_of(stored * SUB * SUB, SUB * SUB)
-            values = [boxes[pl.ds(base + row * SUB, SUB), :] for row in range(SUB)]
-            for kp in range(2):
-                terms = [values[row] * proj(kp, row) for row in range(SUB)]
-                while len(terms) > 1:
-                    terms = [terms[i] + terms[i + 1] for i in range(0, len(terms), 2)]
-                at = pl.multiple_of(stored * 2 * SUB + kp * SUB, SUB)
-                coeffs[pl.ds(at, SUB), :] = terms[0]
-
-        each_group(project)
-
-        high, low = split_pair(coeffs[...])
-        coeffs[...] = mxu(high, ones) + mxu(low, ones)
-
-        def expand(stored, group, proj):
-            base = pl.multiple_of(stored * SUB * SUB, SUB * SUB)
-            at = pl.multiple_of(stored * 2 * SUB, 2 * SUB)
-            by = pl.multiple_of(group * 2 * SUB, 2 * SUB)
-            first = coeffs[pl.ds(at, SUB), :] * coupling[pl.ds(by, SUB), :]
-            second = coeffs[pl.ds(at + SUB, SUB), :] * coupling[pl.ds(by + SUB, SUB), :]
-            for row in range(SUB):
-                value = first * proj(0, row) + second * proj(1, row)
-                boxes[pl.ds(base + row * SUB, SUB), :] = value + pltpu.roll(value, HALF, 1)
-
-        each_group(expand)
-
-        def scatter(stored, group, proj):
-            for j in range(SUB):
-                atom = group * SUB + j
-                value = boxes[pl.ds(stored * SUB * SUB + j, SUB, stride=SUB), :]
-                value = jnp.where(side == half[atom], value, 0.0)
-                at = pl.ds(place[atom], SUB)
-                added[j % 2, at, :] = added[j % 2, at, :] + value
-
-        each_group(scatter)
+    def slab_groups(slab_at):
+        for number in range(groups_y * groups_z):
+            device = slab_at * (groups_y * groups_z) + number
+            for inner in range(per_device):
+                yield device, inner
+
+    def apply_step(cur, prev, new, alpha, beta, spill):
+        last = spill is not None
 
         def product(slab_at, carry):
             def around(buf, shift):
@@ -366,9 +373,44 @@
             left = jnp.concatenate(high + low + high + [depth[...]], axis=1)
             right = jnp.concatenate([plane[...], high[1], high[1], low[1]], axis=0)
             near[:, pl.ds(pl.multiple_of(slab_at * slab, slab), slab)] = mxu(left, right)
+
+            for device, inner in slab_groups(slab_at):
+                group = device * per_device + inner
+                terms = ([], [])
+                for j in range(SUB):
+                    atom = group * SUB + j
+                    value = cur[pl.ds(place[atom], SUB), :]
+                    both = jnp.where(side == half[atom], value, pltpu.roll(value, HALF, 1))
+                    for kp in range(2):
+                        at = SUB + (inner * 2 + kp) * SUB + j
+                        terms[kp].append(both * packs[device, at])
+                for kp in range(2):
+                    at = pl.multiple_of((group * 2 + kp) * SUB, SUB)
+                    coeffs[pl.ds(at, SUB), :] = row_sums(terms[kp])
             return carry
 
         lax.fori_loop(0, groups_x, product, 0)
+
+        high, low = split_pair(coeffs[...])
+        coeffs[...] = (mxu(high, ones) + mxu(low, ones)) * coupling[...]
+
+        def scatter(slab_at, carry):
+            for device, inner in slab_groups(slab_at):
+                group = device * per_device + inner
+                for j in range(SUB):
+                    atom = group * SUB + j
+                    value = 0.0
+                    for kp in range(2):
+                        at = SUB + (inner * 2 + kp) * SUB + j
+                        row = coeffs[pl.ds((group * 2 + kp) * SUB + j, 1), :]
+                        value = value + jnp.broadcast_to(row, (SUB, LANE)) * packs[device, at]
+                    value = value + pltpu.roll(value, HALF, 1)
+                    value = jnp.where(side == half[atom], value, 0.0)
+                    rows = pl.ds(place[atom], SUB)
+                    added[j % SPARES, rows, :] = added[j % SPARES, rows, :] + value
+            return carry
+
+        lax.fori_loop(0, groups_x, scatter, 0)
 
         def combine(pair, carry):
             for at_row in range(0, span, SUB):
@@ -376,50 +418,54 @@
                 rows = pl.ds(at, SUB)
                 cols = pl.ds(pl.multiple_of(pair * LANE, LANE), LANE)
                 total = near[at_row : at_row + SUB, cols] + local[rows, :] * cur[rows, :]
-                total = (total + (added[0, rows, :] + added[1, rows, :])) * alpha
+                for spare in range(SPARES):
+                    total = total + added[spare, rows, :]
+                    if not last:
+                        added[spare, rows, :] = jnp.zeros((SUB, LANE), f32)
+                total = total * alpha
                 if beta is not None:
                     total = total + beta * prev[rows, :]
                 new[rows, :] = total
-                if not last:
-                    for spare in range(2):
-                        added[spare, rows, :] = jnp.zeros((SUB, LANE), f32)
             if not last:
-                for at_row in range(0, span, 2 * SUB):
-                    at = pl.multiple_of(pair * span + at_row, 2 * SUB)
-                    cols = pl.ds(pl.multiple_of(pair * LANE, LANE), LANE)
-                    high, low = split_pair(new[pl.ds(at, 2 * SUB), :])
-                    high_buf[at_row : at_row + 2 * SUB, cols] = high
-                    low_buf[at_row : at_row + 2 * SUB, cols] = low
+                split_rows(new, pair, 0, span)
+            else:
+                for depth_at in range(groups_z):
+                    at = pl.multiple_of(pair * span + depth_at * LANE, LANE)
+                    turned = new[pl.ds(at, LANE), :].T
+                    spill[pl.ds(block_rows(pair, 0, depth_at), HALF), :] = turned[:HALF]
+                    spill[pl.ds(block_rows(pair, 1, depth_at), HALF), :] = turned[HALF:]
+                rows = pl.ds(pl.multiple_of(pair * span, span), span)
+                pltpu.make_async_copy(spill.at[rows], out.at[rows], out_sems.at[pair]).start()
             return carry
 
         lax.fori_loop(0, pairs, combine, 0)
 
     sigma_one = half_width / (LOW_EDGE - middle)
     sigma_now = sigma_one
-    apply_step(field_a, None, field_b, sigma_one / half_width, None, DEGREE == 1)
+    apply_step(field_a, None, field_b, sigma_one / half_width, None, None)
     prev, cur, new = field_a, field_b, field_c
     for degree_step in range(1, DEGREE):
         sigma_next = 1.0 / (2.0 / sigma_one - sigma_now)
+        last = degree_step == DEGREE - 1
+        target = prev if degree_step > 1 else new
+        spare = new if degree_step > 1 else prev
         apply_step(
             cur,
             prev,
-            new,
+            target,
             2.0 * sigma_next / half_width,
             -sigma_now * sigma_next,
-            degree_step == DEGREE - 1,
-        )
-        prev, cur, new = cur, new, prev
+            spare if last else None,
+        )
+        prev, cur, new = cur, target, spare
         sigma_now = sigma_next
 
-    def hand_back(pair, carry):
-        for depth_at in range(groups_z):
-            at = pl.multiple_of(pair * span + depth_at * LANE, LANE)
-            turned = cur[pl.ds(at, LANE), :].T
-            out[2 * pair * groups_z + depth_at] = turned[:HALF].reshape(SUB, SUB, LANE)
-            out[(2 * pair + 1) * groups_z + depth_at] = turned[HALF:].reshape(SUB, SUB, LANE)
+    def finish(pair, carry):
+        rows = pl.ds(pl.multiple_of(pair * span, span), span)
+        pltpu.make_async_copy(prev.at[rows], out.at[rows], out_sems.at[pair]).wait()
         return carry
 
-    lax.fori_loop(0, pairs, hand_back, 0)
+    lax.fori_loop(0, pairs, finish, 0)
 
 
 def packed_inputs(potential, projectors, extent):
@@ -434,7 +480,7 @@
     masked = jnp.where(
         inside.reshape(atoms, 1, B * B * B), projectors, 0.0
     ).reshape(atoms // SUB, SUB, 2, 2, B * B, B)
-    masked = masked.transpose(0, 2, 5, 1, 3, 4).reshape(atoms // SUB * 2 * B, SUB, LANE)
+    masked = masked.transpose(0, 2, 1, 5, 3, 4).reshape(atoms // SUB * 2 * B, SUB, LANE)
     shaped = potential.reshape(HALF, 2, HALF).transpose(2, 1, 0).reshape(SUB, SUB, LANE)
     return jnp.concatenate([shaped, masked], axis=0)
 
@@ -453,45 +499,52 @@
     return place, column % 2
 
 
-def filter_call(groups, place, half, my_z, field, packs, coupling, interpret=False):
+def filter_call(groups, place, half, my_place, field, packs, coupling, interpret=False):
     groups_x, groups_y, groups_z = groups
     columns = groups_x * groups_y
     atoms = place.shape[0]
-    shape = (columns * groups_z, SUB, SUB, LANE)
     span = groups_z * LANE
     width = columns * HALF
     cells = (columns // 2 * span, LANE)
-    vmem = pl.BlockSpec(memory_space=pltpu.VMEM)
+    plane = jnp.asarray(plane_weights(groups_y))
+    depth = jnp.asarray(depth_weights(groups_z))
+    anywhere = pl.BlockSpec(memory_space=pl.ANY)
     smem = pl.BlockSpec(memory_space=pltpu.SMEM)
-    return pl.pallas_call(
+    out = pl.pallas_call(
         functools.partial(filter_kernel, groups, atoms),
-        out_shape=jax.ShapeDtypeStruct(shape, jnp.float32),
-        in_specs=[smem] * 3 + [vmem] * (groups_z + 4),
-        out_specs=vmem,
+        out_shape=jax.ShapeDtypeStruct(cells, jnp.float32),
+        in_specs=[smem] * 3 + [anywhere] * (len(packs) + 4),
+        out_specs=anywhere,
         scratch_shapes=[
             pltpu.VMEM(cells, jnp.float32),
             pltpu.VMEM(cells, jnp.float32),
             pltpu.VMEM(cells, jnp.float32),
             pltpu.VMEM(cells, jnp.float32),
-            pltpu.VMEM((2,) + cells, jnp.float32),
-            pltpu.VMEM((atoms * SUB, LANE), jnp.float32),
+            pltpu.VMEM((SPARES,) + cells, jnp.float32),
             pltpu.VMEM((atoms * 2, LANE), jnp.float32),
             pltpu.VMEM((span, width), jnp.bfloat16),
             pltpu.VMEM((span, width), jnp.bfloat16),
             pltpu.VMEM((span, width), jnp.float32),
+            pltpu.VMEM((columns * groups_z,) + packs[0].shape[1:], jnp.float32),
+            pltpu.VMEM(coupling.shape, jnp.float32),
+            pltpu.VMEM(plane.shape, plane.dtype),
+            pltpu.VMEM(depth.shape, depth.dtype),
+            pltpu.SemaphoreType.DMA((4,)),
+            pltpu.SemaphoreType.DMA((columns * groups_z,)),
+            pltpu.SemaphoreType.DMA((columns // 2,)),
         ],
         compiler_params=pltpu.CompilerParams(vmem_limit_bytes=48 * 1024 * 1024),
         interpret=interpret,
-    )(
-        place,
-        half,
-        my_z,
-        field,
-        *packs,
-        coupling,
-        jnp.asarray(plane_weights(groups_y)),
-        jnp.asarray(depth_weights(groups_z)),
-    )
+    )(place, half, my_place, field.reshape(cells), *packs, coupling, plane, depth)
+    return out.reshape(field.shape)
+
+
+def hops(value, axis):
+    count = lax.axis_size(axis)
+    return [value] + [
+        lax.ppermute(value, axis, [(i, (i + hop) % count) for i in range(count)])
+        for hop in range(1, count)
+    ]
 
 
 def state_body(orbitals, potential, projectors, owner_rank, box_anchor, box_extent, coupling):
@@ -500,19 +553,18 @@
     groups_z = groups[2]
     domains = groups[0] * groups[1] * groups_z
     atoms_own = projectors.shape[0]
-    my_z = lax.axis_index("gz")
-    me = (lax.axis_index("gx") * groups[1] + lax.axis_index("gy")) * groups_z + my_z
+    my_place = jnp.stack([lax.axis_index(axis) for axis in axes])
+    me = (my_place[0] * groups[1] + my_place[1]) * groups_z + my_place[2]
     extent = lax.dynamic_slice(box_extent, (me * atoms_own,), (atoms_own,))
     pack = packed_inputs(potential, projectors, extent)
-    pack = lax.all_gather(pack, ("gx", "gy"), axis=0, tiled=False)
-    packs = [pack] + [
-        lax.ppermute(pack, "gz", [(i, (i + hop) % groups_z) for i in range(groups_z)])
-        for hop in range(1, groups_z)
-    ]
+    line = jnp.stack(hops(pack, "gx"))
+    plane = hops(line, "gy")
+    crossed = [hops(piece, "gz") for piece in plane]
+    packs = [crossed[hop_y][hop_z] for hop_z in range(groups_z) for hop_y in range(groups[1])]
     field = lax.all_to_all(orbitals, axes, split_axis=0, concat_axis=0, tiled=True)
     place, half = box_places(groups, owner_rank, box_anchor[2])
     result = filter_call(
-        groups, place, half, my_z[None], field, packs, packed_coupling(coupling)
+        groups, place, half, my_place, field, packs, packed_coupling(coupling)
     )
     filtered = lax.all_to_all(result, axes, split_axis=0, concat_axis=0, tiled=True)
     states = filtered.shape[0]

time: 175 us -> 143 us (0.82)
  waiting for transfers between devices: 56.7 us -> 41.5 us
  Pallas kernels: 41.6 us -> 27.8 us
  between operations: 14.2 us -> 0.88 us
  starting transfers between devices: 7.34 us -> 16.1 us
  local copies, waits for them, and re-layouts: 10.6 us -> 14.8 us
    all_gather x1 -> x0, waiting for transfers between devices: 56.6 us -> none  [state_body(): pack = lax.all_gather(pack, ('gx', 'gy'), axis=0, tiled=False)]
    ppermute x1 -> x10, waiting for transfers between devices: 0.01 us -> 41.5 us  [hops(): lax.ppermute(value, axis, [(i, (i + hop) % count) for i in range(count)])]
    pallas_call x1, Pallas kernels: 41.6 us -> 27.8 us  [filter_call(): pl.pallas_call(functools.partial(filter_kernel, groups, atoms), out_shape...]
    ppermute x1 -> x10, starting transfers between devices: 0.01 us -> 8.83 us  [hops(): lax.ppermute(value, axis, [(i, (i + hop) % count) for i in range(count)])]
    unnamed x11 -> x30, local copies, waits for them, and re-layouts: 2.26 us -> 7.99 us
  transfers between devices with their start and end apart: 3 -> 11, of which waited for: 1 -> 4; matrix products, arithmetic and copies ran while one was open for 2% -> 4% of each run, Pallas kernels for 0% -> 0%
where the time goes in v3:
time: 143 us; the launch traced here: 142 us
  waiting for transfers between devices  41.5 us (29%)
  blocking collectives  39.5 us (28%)
  Pallas kernels  27.8 us (19%)
  starting transfers between devices  16.1 us (11%)
  local copies, waits for them, and re-layouts  14.8 us (10%)
    ppermute x10, waiting for transfers between devices, hops(): lax.ppermute(value, axis, [(i, (i + hop) % count) for i in range(count)])  41.5 us
    all_to_all x1, blocking collectives, state_body(): lax.all_to_all(result, axes, split_axis=0, concat_axis=0, tiled=True)  28 us
    pallas_call x1, Pallas kernels, filter_call(): pl.pallas_call(functools.partial(filter_kernel, groups, atoms), out_shape...  27.8 us
    all_to_all x1, blocking collectives, state_body(): lax.all_to_all(jnp.broadcast_to(quarter[None], (domains,) + quarter.shape...  11.6 us
    ppermute x10, starting transfers between devices, hops(): lax.ppermute(value, axis, [(i, (i + hop) % count) for i in range(count)])  8.83 us
    unnamed x30, local copies, waits for them, and re-layouts  7.99 us
    all_to_all x1, starting transfers between devices, state_body(): lax.all_to_all(orbitals, axes, split_axis=0, concat_axis=0, tiled=True)  7.3 us
  transfers between devices with their start and end apart: 11, of which 4 were waited for; matrix products, arithmetic and copies ran while one was open for 4% of the time, Pallas kernels for 0%

profile of v3, /device:TPU:0, one launch (start us, length us, event | category | flops | bytes accessed | tf_op | source)
XLA Modules:
  0.0 142.0 jit_solution(11971165586224020104)
XLA Ops:
  0.6 0.0 copy-start.13
  0.7 7.3 %all-to-all-start = ((f32[32,8,8,128]{3,2,1,0:T(8,128)}), f32[32,8,8,128]{3,2,1,0:T(8,128)S(1)}, u32[]{:S(2)}, u32[]{:S(2)}) async-start(f32[32,8,8,128]{3,2,1,0:T(8,128)} %param.9), calls=%async_computation | async-start | bytes 2097152 | tf_op jit(solution)/shard_map/all_to_all | solution.py:564
  8.0 0.1 dynamic_slice.3
  8.1 0.1 iota_compare_fusion
  8.1 0.1 broadcast_and_fusion.1
  8.2 0.1 broadcast_and_fusion
  8.4 0.2 and.69
  8.6 0.0 copy-done.10
  8.7 0.1 reshape.132
  8.8 0.1 copy.25
  8.9 0.1 reshape.133
  9.0 0.6 reshape.134
  9.5 0.0 copy-start.11
  9.6 0.3 copy.27
  9.9 0.1 reshape.135
  10.0 3.7 %collective-permute-start.2 = (f32[24,8,128]{2,1,0:T(8,128)S(1)}, f32[24,8,128]{2,1,0:T(8,128)S(1)}, u32[]{:S(2)}, u32[]{:S(2)}) collective-permute-start(f32[24,8,128]{2,1,0:T(8,128)S(1)} %constant_dynamic-update-slice_fusion), channel_id=1, source_target_pairs={{0,24},{8,0},{16,8},{24,16},{1,25},{9,1},{17,9},{25,17},{2,26},{10... | collective-permute-start | bytes 294920 | tf_op jit(solution)/shard_map/ppermute | solution.py:545
  13.7 0.0 collective-permute-start.1
  13.7 1.1 collective-permute-start
  14.8 13.2 %collective-permute-done.2 = f32[24,8,128]{2,1,0:T(8,128)S(1)} collective-permute-done((f32[24,8,128]{2,1,0:T(8,128)S(1)}, f32[24,8,128]{2,1,0:T(8,128)S(1)}, u32[]{:S(2)}, u32[]{:S(2)}) %collective-permute-start.2) | collective-permute-done | bytes 98336 | tf_op jit(solution)/shard_map/ppermute | solution.py:545
  28.0 14.6 %collective-permute-done.1 = f32[24,8,128]{2,1,0:T(8,128)S(1)} collective-permute-done((f32[24,8,128]{2,1,0:T(8,128)S(1)}, f32[24,8,128]{2,1,0:T(8,128)S(1)}, u32[]{:S(2)}, u32[]{:S(2)}) %collective-permute-start.1) | collective-permute-done | bytes 98336 | tf_op jit(solution)/shard_map/ppermute | solution.py:545
  42.6 0.0 collective-permute-done
  42.7 0.0 copy-start.12
  42.7 0.0 copy-start
  42.7 2.4 %collective-permute-start.5 = (f32[4,24,8,128]{3,2,1,0:T(8,128)S(1)}, f32[4,24,8,128]{3,2,1,0:T(8,128)S(1)}, u32[]{:S(2)}, u32[]{:S(2)}) collective-permute-start(f32[4,24,8,128]{3,2,1,0:T(8,128)S(1)} %pad_maximum_fusion.refs_1_), channel_id=1, source_target_pairs={{0,6},{2,0},{4,2},{6,4},{1,7},{3,1},{5,3},{7,5},{8,14},{10,8},{12,... | collective-permute-start | bytes 1179656 | tf_op jit(solution)/shard_map/ppermute | solution.py:545
  45.1 0.6 collective-permute-start.4
  45.7 0.5 collective-permute-start.3
  46.2 0.7 slice.3
  46.9 0.1 reshape.136
  47.0 0.4 copy.28
  47.5 1.4 broadcast_in_dim.31
  48.9 1.3 reshape.137.refs_9_
  50.2 0.1 pad_add_fusion.my_place
  50.3 0.0 collective-permute-start.6
  50.3 4.4 %collective-permute-done.5.refs_4_ = f32[4,24,8,128]{3,2,1,0:T(8,128)S(1)} collective-permute-done((f32[4,24,8,128]{3,2,1,0:T(8,128)S(1)}, f32[4,24,8,128]{3,2,1,0:T(8,128)S(1)}, u32[]{:S(2)}, u32[]{:S(2)}) %collective-permute-start.5) | collective-permute-done | bytes 393248 | tf_op jit(solution)/shard_map/ppermute | solution.py:545
  54.8 0.0 collective-permute-start.9
  54.8 9.2 %collective-permute-done.4.refs_3_ = f32[4,24,8,128]{3,2,1,0:T(8,128)S(1)} collective-permute-done((f32[4,24,8,128]{3,2,1,0:T(8,128)S(1)}, f32[4,24,8,128]{3,2,1,0:T(8,128)S(1)}, u32[]{:S(2)}, u32[]{:S(2)}) %collective-permute-start.4) | collective-permute-done | bytes 393248 | tf_op jit(solution)/shard_map/ppermute | solution.py:545
  63.9 0.0 collective-permute-start.8
  63.9 0.0 collective-permute-done.3.refs_2_
  64.0 0.5 collective-permute-start.7
  64.5 0.0 copy-done.12
  64.5 0.0 collective-permute-done.6.refs_5_
  64.5 0.0 copy-start.1
  64.5 0.7 copy-done.1
  65.3 0.0 collective-permute-done.9.refs_8_
  65.3 0.8 copy-done.3
  66.0 0.0 collective-permute-done.8.refs_7_
  66.0 0.7 copy-done.5
  66.8 0.0 collective-permute-done.7.refs_6_
  66.8 0.7 copy-done.7
  67.5 0.0 all-to-all-done
  67.5 1.0 copy-done.2
  68.5 1.0 copy-done.4
  69.5 1.0 copy-done.6
  70.5 1.0 copy-done.8
  71.5 27.8 %shard_map.104 = f32[2048,128]{1,0:T(8,128)S(1)} custom-call(s32[256]{0:T(256)S(1)} %multiply_add_fusion.place, s32[256]{0:T(256)S(1)} %get-tuple-element.2.half, s32[3]{0:T(128)S(1)} %pad_add_fusion.my_place, f32[2048,128]{1,0:T(8,128)S(1)} %bitcast.31, f32[4,24,8,128]{3,2,1,0:T(8,128)S(1)} %pad_maximum_fusion.refs_1_, ...), custom_call_target="tpu_custom_call" | custom-call | tf_op jit(solution)/shard_map/pallas_call | solution.py:513
  99.3 28.0 %all_to_all.15 = f32[32,8,8,128]{3,2,1,0:T(8,128)S(1)} all-to-all(f32[32,8,8,128]{3,2,1,0:T(8,128)S(1)} %bitcast.32), channel_id=1, replica_groups=mesh['gx'=4,'gy'=4,'gz'=2] {'gx','gy','gz'}, dimensions={0} | all-to-all | bytes 2097152 | tf_op jit(solution)/shard_map/all_to_all | solution.py:569
  127.3 0.2 reshape.140
  127.5 0.2 dot_general.5
  127.7 1.0 convolution_bitcast_fusion
  128.6 0.1 broadcast_in_dim.32
  128.7 11.6 %all_to_all.16 = f32[32,8,128]{2,1,0:T(8,128)S(1)} all-to-all(f32[32,8,128]{2,1,0:T(8,128)S(1)} %broadcast_in_dim.33), channel_id=1, replica_groups=mesh['gx'=4,'gy'=4,'gz'=2] {'gx','gy','gz'}, dimensions={0} | all-to-all | bytes 262144 | tf_op jit(solution)/shard_map/all_to_all | solution.py:574
  140.4 0.1 div.38
  140.4 0.6 copy.32
  141.1 1.0 copy.35
  (24 shorter events, 0.2 us)
Async XLA Ops:
  0.6 7.4 %copy-start.13 = (s32[256]{0:T(256)S(1)}, s32[256]{0:T(256)}, u32[]{:S(2)}) copy-start(s32[256]{0:T(256)} %param.14) | copy-start | bytes 3076
  0.6 7.9 %copy-start.9 = (f32[8,4,512]{2,1,0:T(4,128)S(1)}, f32[8,4,512]{2,1,0:T(4,128)}, u32[]{:S(2)}) copy-start(f32[8,4,512]{2,1,0:T(4,128)} %param.11) | copy-start | bytes 196612
  0.7 8.0 %copy-start.10 = (f32[8,8,128]{2,1,0:T(8,128)S(1)}, f32[8,8,128]{2,1,0:T(8,128)}, u32[]{:S(2)}) copy-start(f32[8,8,128]{2,1,0:T(8,128)} %param.10) | copy-start | bytes 98308
  0.7 66.9 %all-to-all-start = ((f32[32,8,8,128]{3,2,1,0:T(8,128)}), f32[32,8,8,128]{3,2,1,0:T(8,128)S(1)}, u32[]{:S(2)}, u32[]{:S(2)}) async-start(f32[32,8,8,128]{3,2,1,0:T(8,128)} %param.9), calls=%async_computation | async-start | bytes 2097152 | tf_op jit(solution)/shard_map/all_to_all | solution.py:564
  9.5 37.4 %copy-start.11 = (f32[256,4]{0,1:T(4,128)S(1)}, f32[256,4]{0,1:T(4,128)}, u32[]{:S(2)}) copy-start(f32[256,4]{0,1:T(4,128)} %param.15) | copy-start | bytes 12292
  10.0 18.0 %collective-permute-start.2 = (f32[24,8,128]{2,1,0:T(8,128)S(1)}, f32[24,8,128]{2,1,0:T(8,128)S(1)}, u32[]{:S(2)}, u32[]{:S(2)}) collective-permute-start(f32[24,8,128]{2,1,0:T(8,128)S(1)} %constant_dynamic-update-slice_fusion), channel_id=1, source_target_pairs={{0,24},{8,0},{16,8},{24,16},{1,25},{9,1},{17,9},{25,17},{2,26},{10... | collective-permute-start | bytes 294920 | tf_op jit(solution)/shard_map/ppermute | solution.py:545
  13.7 28.9 %collective-permute-start.1 = (f32[24,8,128]{2,1,0:T(8,128)S(1)}, f32[24,8,128]{2,1,0:T(8,128)S(1)}, u32[]{:S(2)}, u32[]{:S(2)}) collective-permute-start(f32[24,8,128]{2,1,0:T(8,128)S(1)} %constant_dynamic-update-slice_fusion), channel_id=1, source_target_pairs={{0,16},{8,24},{16,0},{24,8},{1,17},{9,25},{17,1},{25,9},{2,18},{10... | collective-permute-start | bytes 294920 | tf_op jit(solution)/shard_map/ppermute | solution.py:545
  13.7 28.9 %collective-permute-start = (f32[24,8,128]{2,1,0:T(8,128)S(1)}, f32[24,8,128]{2,1,0:T(8,128)S(1)}, u32[]{:S(2)}, u32[]{:S(2)}) collective-permute-start(f32[24,8,128]{2,1,0:T(8,128)S(1)} %constant_dynamic-update-slice_fusion), channel_id=1, source_target_pairs={{0,8},{8,16},{16,24},{24,0},{1,9},{9,17},{17,25},{25,1},{2,10},{10... | collective-permute-start | bytes 294920 | tf_op jit(solution)/shard_map/ppermute | solution.py:545
  42.7 21.8 %copy-start.12 = (s32[256]{0:T(256)S(1)}, s32[256]{0:T(256)}, u32[]{:S(2)}) copy-start(s32[256]{0:T(256)} %param.12) | copy-start | bytes 3076
  42.7 24.9 %copy-start = (bf16[256,768]{1,0:T(8,128)(2,1)S(1)}, bf16[256,768]{1,0:T(8,128)(2,1)}, u32[]{:S(2)}) copy-start(bf16[256,768]{1,0:T(8,128)(2,1)} %constant.69.clone.refs_11_) | copy-start | bytes 1179652
  42.7 12.1 %collective-permute-start.5 = (f32[4,24,8,128]{3,2,1,0:T(8,128)S(1)}, f32[4,24,8,128]{3,2,1,0:T(8,128)S(1)}, u32[]{:S(2)}, u32[]{:S(2)}) collective-permute-start(f32[4,24,8,128]{3,2,1,0:T(8,128)S(1)} %pad_maximum_fusion.refs_1_), channel_id=1, source_target_pairs={{0,6},{2,0},{4,2},{6,4},{1,7},{3,1},{5,3},{7,5},{8,14},{10,8},{12,... | collective-permute-start | bytes 1179656 | tf_op jit(solution)/shard_map/ppermute | solution.py:545
  45.1 18.8 %collective-permute-start.4 = (f32[4,24,8,128]{3,2,1,0:T(8,128)S(1)}, f32[4,24,8,128]{3,2,1,0:T(8,128)S(1)}, u32[]{:S(2)}, u32[]{:S(2)}) collective-permute-start(f32[4,24,8,128]{3,2,1,0:T(8,128)S(1)} %pad_maximum_fusion.refs_1_), channel_id=1, source_target_pairs={{0,4},{2,6},{4,0},{6,2},{1,5},{3,7},{5,1},{7,3},{8,12},{10,14},{12... | collective-permute-start | bytes 1179656 | tf_op jit(solution)/shard_map/ppermute | solution.py:545
  45.7 18.2 %collective-permute-start.3 = (f32[4,24,8,128]{3,2,1,0:T(8,128)S(1)}, f32[4,24,8,128]{3,2,1,0:T(8,128)S(1)}, u32[]{:S(2)}, u32[]{:S(2)}) collective-permute-start(f32[4,24,8,128]{3,2,1,0:T(8,128)S(1)} %pad_maximum_fusion.refs_1_), channel_id=1, source_target_pairs={{0,2},{2,4},{4,6},{6,0},{1,3},{3,5},{5,7},{7,1},{8,10},{10,12},{12... | collective-permute-start | bytes 1179656 | tf_op jit(solution)/shard_map/ppermute | solution.py:545
  50.3 14.2 %collective-permute-start.6 = (f32[4,24,8,128]{3,2,1,0:T(8,128)S(1)}, f32[4,24,8,128]{3,2,1,0:T(8,128)S(1)}, u32[]{:S(2)}, u32[]{:S(2)}) collective-permute-start(f32[4,24,8,128]{3,2,1,0:T(8,128)S(1)} %pad_maximum_fusion.refs_1_), channel_id=1, source_target_pairs={{0,1},{1,0},{2,3},{3,2},{4,5},{5,4},{6,7},{7,6},{8,9},{9,8},{10,11... | collective-permute-start | bytes 1179656 | tf_op jit(solution)/shard_map/ppermute | solution.py:545
  54.8 10.5 %collective-permute-start.9 = (f32[4,24,8,128]{3,2,1,0:T(8,128)S(1)}, f32[4,24,8,128]{3,2,1,0:T(8,128)S(1)}, u32[]{:S(2)}, u32[]{:S(2)}) collective-permute-start(f32[4,24,8,128]{3,2,1,0:T(8,128)S(1)} %collective-permute-done.5.refs_4_), channel_id=1, source_target_pairs={{0,1},{1,0},{2,3},{3,2},{4,5},{5,4},{6,7},{7,6},{8,9},{9,8},{10,11... | collective-permute-start | bytes 1179656 | tf_op jit(solution)/shard_map/ppermute | solution.py:545
  63.9 2.1 %collective-permute-start.8 = (f32[4,24,8,128]{3,2,1,0:T(8,128)S(1)}, f32[4,24,8,128]{3,2,1,0:T(8,128)S(1)}, u32[]{:S(2)}, u32[]{:S(2)}) collective-permute-start(f32[4,24,8,128]{3,2,1,0:T(8,128)S(1)} %collective-permute-done.4.refs_3_), channel_id=1, source_target_pairs={{0,1},{1,0},{2,3},{3,2},{4,5},{5,4},{6,7},{7,6},{8,9},{9,8},{10,11... | collective-permute-start | bytes 1179656 | tf_op jit(solution)/shard_map/ppermute | solution.py:545
  64.0 2.8 %collective-permute-start.7 = (f32[4,24,8,128]{3,2,1,0:T(8,128)S(1)}, f32[4,24,8,128]{3,2,1,0:T(8,128)S(1)}, u32[]{:S(2)}, u32[]{:S(2)}) collective-permute-start(f32[4,24,8,128]{3,2,1,0:T(8,128)S(1)} %collective-permute-done.3.refs_2_), channel_id=1, source_target_pairs={{0,1},{1,0},{2,3},{3,2},{4,5},{5,4},{6,7},{7,6},{8,9},{9,8},{10,11... | collective-permute-start | bytes 1179656 | tf_op jit(solution)/shard_map/ppermute | solution.py:545
  64.5 0.7 copy-start.1
  65.3 0.8 copy-start.3
  66.0 0.7 copy-start.5
  66.8 0.8 copy-start.7
  67.5 1.0 copy-start.2
  68.5 1.0 copy-start.4
  69.5 1.0 copy-start.6
  70.5 1.0 copy-start.8

commit v4 on v3

--- a/solution.py
+++ b/solution.py
@@ -204,7 +204,7 @@
             block = block + np.einsum("ajbp,io->aijbop", ring, np.eye(SUB))
         blocks.append(block.reshape(slab, slab))
     high, low = split_terms(np.concatenate(blocks, axis=0))
-    return np.concatenate([high, high, low], axis=0)
+    return np.concatenate([high, low], axis=0)
 
 
 def depth_weights(groups_z):
@@ -360,18 +360,20 @@
             for inner in range(per_device):
                 yield device, inner
 
+    def slab_of(buf, slab_at):
+        return buf[:, pl.ds(pl.multiple_of(slab_at * slab, slab), slab)]
+
     def apply_step(cur, prev, new, alpha, beta, spill):
         last = spill is not None
 
         def product(slab_at, carry):
             def around(buf, shift):
-                other = lax.rem(slab_at + shift + groups_x, groups_x)
-                return buf[:, pl.ds(pl.multiple_of(other * slab, slab), slab)]
+                return slab_of(buf, lax.rem(slab_at + shift + groups_x, groups_x))
 
             high = [around(high_buf, shift) for shift in (-1, 0, 1)]
             low = [around(low_buf, shift) for shift in (-1, 0, 1)]
-            left = jnp.concatenate(high + low + high + [depth[...]], axis=1)
-            right = jnp.concatenate([plane[...], high[1], high[1], low[1]], axis=0)
+            left = jnp.concatenate(high + low, axis=1)
+            right = jnp.concatenate([plane[: 3 * slab], plane[: 3 * slab]], axis=0)
             near[:, pl.ds(pl.multiple_of(slab_at * slab, slab), slab)] = mxu(left, right)
 
             for device, inner in slab_groups(slab_at):
@@ -395,6 +397,17 @@
         coeffs[...] = (mxu(high, ones) + mxu(low, ones)) * coupling[...]
 
         def scatter(slab_at, carry):
+            high = [
+                slab_of(high_buf, lax.rem(slab_at + shift + groups_x, groups_x))
+                for shift in (-1, 0, 1)
+            ]
+            left = jnp.concatenate(high + [depth[...]], axis=1)
+            right = jnp.concatenate(
+                [plane[3 * slab :], high[1], high[1], slab_of(low_buf, slab_at)], axis=0
+            )
+            at = pl.ds(pl.multiple_of(slab_at * slab, slab), slab)
+            near[:, at] = near[:, at] + mxu(left, right)
+
             for device, inner in slab_groups(slab_at):
                 group = device * per_device + inner
                 for j in range(SUB):
@@ -533,7 +546,7 @@
             pltpu.SemaphoreType.DMA((columns * groups_z,)),
             pltpu.SemaphoreType.DMA((columns // 2,)),
         ],
-        compiler_params=pltpu.CompilerParams(vmem_limit_bytes=48 * 1024 * 1024),
+        compiler_params=pltpu.CompilerParams(vmem_limit_bytes=20 * 1024 * 1024),
         interpret=interpret,
     )(place, half, my_place, field.reshape(cells), *packs, coupling, plane, depth)
     return out.reshape(field.shape)
@@ -559,7 +572,9 @@
     pack = packed_inputs(potential, projectors, extent)
     line = jnp.stack(hops(pack, "gx"))
     plane = hops(line, "gy")
-    crossed = [hops(piece, "gz") for piece in plane]
+    swapped = hops(line, "gz")
+    orbitals, swapped = lax.optimization_barrier((orbitals, swapped))
+    crossed = [swapped] + [hops(piece, "gz") for piece in plane[1:]]
     packs = [crossed[hop_y][hop_z] for hop_z in range(groups_z) for hop_y in range(groups[1])]
     field = lax.all_to_all(orbitals, axes, split_axis=0, concat_axis=0, tiled=True)
     place, half = box_places(groups, owner_rank, box_anchor[2])

time: 143 us -> 133 us (0.930)
  waiting for transfers between devices: 41.5 us -> 33.3 us
  Pallas kernels: 27.8 us -> 24.1 us
  blocking collectives: 39.5 us -> 42.7 us
    ppermute x10, waiting for transfers between devices: 41.5 us -> 33.3 us  [hops(): lax.ppermute(value, axis, [(i, (i + hop) % count) for i in range(count)])]
    pallas_call x1, Pallas kernels: 27.8 us -> 24.1 us  [filter_call(): pl.pallas_call(functools.partial(filter_kernel, groups, atoms), out_shape...]
    all_to_all x1, blocking collectives: 28 us -> 31 us  [state_body(): lax.all_to_all(result, axes, split_axis=0, concat_axis=0, tiled=True)]
    all_to_all x1, starting transfers between devices: 7.3 us -> 4.52 us  [state_body(): lax.all_to_all(orbitals, axes, split_axis=0, concat_axis=0, tiled=True)]
    ppermute x10, starting transfers between devices: 8.83 us -> 10.5 us  [hops(): lax.ppermute(value, axis, [(i, (i + hop) % count) for i in range(count)])]
    unnamed x30 -> x28, local copies, waits for them, and re-layouts: 7.99 us -> 8.12 us
  transfers between devices with their start and end apart: 11 -> 11, of which waited for: 4 -> 6; matrix products, arithmetic and copies ran while one was open for 4% -> 3% of each run, Pallas kernels for 0% -> 0%
where the time goes in v4:
time: 133 us; the launch traced here: 132 us
  blocking collectives  42.7 us (32%)
  waiting for transfers between devices  33.3 us (25%)
  Pallas kernels  24.1 us (18%)
  starting transfers between devices  15.1 us (11%)
  local copies, waits for them, and re-layouts  15 us (11%)
    ppermute x10, waiting for transfers between devices, hops(): lax.ppermute(value, axis, [(i, (i + hop) % count) for i in range(count)])  33.3 us
    all_to_all x1, blocking collectives, state_body(): lax.all_to_all(result, axes, split_axis=0, concat_axis=0, tiled=True)  31 us
    pallas_call x1, Pallas kernels, filter_call(): pl.pallas_call(functools.partial(filter_kernel, groups, atoms), out_shape...  24.1 us
    all_to_all x1, blocking collectives, state_body(): lax.all_to_all(jnp.broadcast_to(quarter[None], (domains,) + quarter.shape...  11.7 us
    ppermute x10, starting transfers between devices, hops(): lax.ppermute(value, axis, [(i, (i + hop) % count) for i in range(count)])  10.5 us
    unnamed x28, local copies, waits for them, and re-layouts  8.12 us
    all_to_all x1, starting transfers between devices, state_body(): lax.all_to_all(orbitals, axes, split_axis=0, concat_axis=0, tiled=True)  4.52 us
  transfers between devices with their start and end apart: 11, of which 6 were waited for; matrix products, arithmetic and copies ran while one was open for 3% of the time, Pallas kernels for 0%

profile of v4, /device:TPU:0, one launch (start us, length us, event | category | flops | bytes accessed | tf_op | source)
XLA Modules:
  0.0 132.4 jit_solution(4346252559190721785)
XLA Ops:
  0.6 0.0 copy-start.12
  0.7 0.7 copy-done.12
  1.3 0.1 dynamic_slice.3
  1.4 0.1 iota_compare_fusion
  1.5 0.1 broadcast_and_fusion.1
  1.6 0.1 broadcast_and_fusion
  1.7 0.2 and.69
  1.9 0.5 copy-done.8
  2.4 0.0 copy-start.9
  2.5 0.7 copy-done.9
  3.2 0.1 reshape.131
  3.3 0.1 copy.25
  3.4 0.1 reshape.132
  3.5 0.6 reshape.133
  4.1 0.3 copy.27
  4.4 0.1 reshape.134
  4.6 5.1 %collective-permute-start.2 = (f32[24,8,128]{2,1,0:T(8,128)S(1)}, f32[24,8,128]{2,1,0:T(8,128)S(1)}, u32[]{:S(2)}, u32[]{:S(2)}) collective-permute-start(f32[24,8,128]{2,1,0:T(8,128)S(1)} %constant_dynamic-update-slice_fusion), channel_id=1, source_target_pairs={{0,24},{8,0},{16,8},{24,16},{1,25},{9,1},{17,9},{25,17},{2,26},{10... | collective-permute-start | bytes 294920 | tf_op jit(solution)/shard_map/ppermute | solution.py:558
  9.7 0.0 collective-permute-start.1
  9.7 1.0 collective-permute-start
  10.7 2.2 %collective-permute-done.2 = f32[24,8,128]{2,1,0:T(8,128)S(1)} collective-permute-done((f32[24,8,128]{2,1,0:T(8,128)S(1)}, f32[24,8,128]{2,1,0:T(8,128)S(1)}, u32[]{:S(2)}, u32[]{:S(2)}) %collective-permute-start.2) | collective-permute-done | bytes 98336 | tf_op jit(solution)/shard_map/ppermute | solution.py:558
  12.9 5.5 %collective-permute-done.1 = f32[24,8,128]{2,1,0:T(8,128)S(1)} collective-permute-done((f32[24,8,128]{2,1,0:T(8,128)S(1)}, f32[24,8,128]{2,1,0:T(8,128)S(1)}, u32[]{:S(2)}, u32[]{:S(2)}) %collective-permute-start.1) | collective-permute-done | bytes 98336 | tf_op jit(solution)/shard_map/ppermute | solution.py:558
  18.4 0.0 collective-permute-done
  18.4 0.1 collective-permute-start.3
  18.5 1.7 %collective-permute-done.3.refs_5_ = f32[4,24,8,128]{3,2,1,0:T(8,128)S(1)} collective-permute-done((f32[4,24,8,128]{3,2,1,0:T(8,128)S(1)}, f32[4,24,8,128]{3,2,1,0:T(8,128)S(1)}, u32[]{:S(2)}, u32[]{:S(2)}) %collective-permute-start.3) | collective-permute-done | bytes 393248 | tf_op jit(solution)/shard_map/ppermute | solution.py:558
  20.2 4.5 %all-to-all-start = ((f32[32,8,8,128]{3,2,1,0:T(8,128)}), f32[32,8,8,128]{3,2,1,0:T(8,128)S(1)}, u32[]{:S(2)}, u32[]{:S(2)}) async-start(f32[32,8,8,128]{3,2,1,0:T(8,128)} %param.9), calls=%async_computation | async-start | bytes 2097152 | tf_op jit(solution)/shard_map/all_to_all | solution.py:579
  24.8 2.7 %collective-permute-start.6 = (f32[4,24,8,128]{3,2,1,0:T(8,128)S(1)}, f32[4,24,8,128]{3,2,1,0:T(8,128)}, u32[]{:S(2)}, u32[]{:S(2)}) collective-permute-start(f32[4,24,8,128]{3,2,1,0:T(8,128)S(1)} %pad_maximum_fusion.refs_1_), channel_id=1, source_target_pairs={{0,6},{2,0},{4,2},{6,4},{1,7},{3,1},{5,3},{7,5},{8,14},{10,8},{12,... | collective-permute-start | bytes 1179656 | tf_op jit(solution)/shard_map/ppermute | solution.py:558
  27.5 0.6 collective-permute-start.5
  28.0 0.6 collective-permute-start.4
  28.6 0.7 slice.3
  29.3 0.0 copy-done.10
  29.3 0.1 reshape.136
  29.4 0.4 copy.28
  29.9 1.4 %broadcast_in_dim.31 = f32[32,2,8,2,64]{4,3,2,1,0:T(2,128)} broadcast(f32[32,2,8,2]{3,2,1,0:T(8,128)S(1)} %copy.28), dimensions={0,1,2,3} | broadcast | bytes 266240 | tf_op jit(solution)/shard_map/broadcast_in_dim | solution.py:504
  31.3 1.4 %reshape.137.refs_9_ = f32[512,128]{1,0:T(8,128)S(1)} reshape(f32[32,2,8,2,64]{4,3,2,1,0:T(2,128)} %broadcast_in_dim.31) | data formatting | bytes 524288 | tf_op jit(solution)/shard_map/reshape | solution.py:505
  32.6 0.0 copy-start.11
  32.7 0.1 pad_add_fusion.my_place
  32.7 13.7 %collective-permute-done.6.refs_4_ = f32[4,24,8,128]{3,2,1,0:T(8,128)} collective-permute-done((f32[4,24,8,128]{3,2,1,0:T(8,128)S(1)}, f32[4,24,8,128]{3,2,1,0:T(8,128)}, u32[]{:S(2)}, u32[]{:S(2)}) %collective-permute-start.6) | collective-permute-done | bytes 393248 | tf_op jit(solution)/shard_map/ppermute | solution.py:558
  46.5 0.0 collective-permute-start.9
  46.5 0.0 collective-permute-done.5.refs_3_
  46.5 0.5 collective-permute-start.8
  47.0 9.7 %collective-permute-done.4.refs_2_ = f32[4,24,8,128]{3,2,1,0:T(8,128)} collective-permute-done((f32[4,24,8,128]{3,2,1,0:T(8,128)S(1)}, f32[4,24,8,128]{3,2,1,0:T(8,128)}, u32[]{:S(2)}, u32[]{:S(2)}) %collective-permute-start.4) | collective-permute-done | bytes 393248 | tf_op jit(solution)/shard_map/ppermute | solution.py:558
  56.7 0.0 collective-permute-start.7
  56.7 0.0 copy-done.11
  56.8 0.0 collective-permute-done.9.refs_8_
  56.8 0.0 copy-start.2
  56.8 0.8 copy-done.2
  57.5 0.0 collective-permute-done.8.refs_7_
  57.6 0.7 copy-done.4
  58.3 0.4 collective-permute-done.7.refs_6_
  58.7 0.7 copy-done.6
  59.4 0.0 all-to-all-done
  59.4 1.0 copy-done.3
  60.4 1.0 copy-done.5
  61.4 1.0 copy-done.7
  62.4 24.1 %shard_map.104 = f32[2048,128]{1,0:T(8,128)S(1)} custom-call(s32[256]{0:T(256)S(1)} %multiply_add_fusion.place, s32[256]{0:T(256)S(1)} %get-tuple-element.8.half, s32[3]{0:T(128)S(1)} %pad_add_fusion.my_place, f32[2048,128]{1,0:T(8,128)S(1)} %bitcast.31, f32[4,24,8,128]{3,2,1,0:T(8,128)S(1)} %pad_maximum_fusion.refs_1_, ...), custom_call_target="tpu_custom_call" | custom-call | tf_op jit(solution)/shard_map/pallas_call | solution.py:526
  86.5 31.0 %all_to_all.15 = f32[32,8,8,128]{3,2,1,0:T(8,128)S(1)} all-to-all(f32[32,8,8,128]{3,2,1,0:T(8,128)S(1)} %bitcast.32), channel_id=1, replica_groups=mesh['gx'=4,'gy'=4,'gz'=2] {'gx','gy','gz'}, dimensions={0} | all-to-all | bytes 2097152 | tf_op jit(solution)/shard_map/all_to_all | solution.py:584
  117.6 0.2 reshape.140
  117.8 0.2 dot_general.5
  118.0 1.0 convolution_bitcast_fusion
  118.9 0.1 broadcast_in_dim.32
  119.0 11.7 %all_to_all.16 = f32[32,8,128]{2,1,0:T(8,128)S(1)} all-to-all(f32[32,8,128]{2,1,0:T(8,128)S(1)} %broadcast_in_dim.33), channel_id=1, replica_groups=mesh['gx'=4,'gy'=4,'gz'=2] {'gx','gy','gz'}, dimensions={0} | all-to-all | bytes 262144 | tf_op jit(solution)/shard_map/all_to_all | solution.py:589
  130.7 0.1 div.38
  130.8 0.6 copy.32
  131.4 1.0 copy.35
  (22 shorter events, 0.2 us)
Async XLA Ops:
  0.6 0.7 copy-start.12
  1.6 0.8 copy-start.8
  2.4 0.8 copy-start.9
  4.6 8.3 %collective-permute-start.2 = (f32[24,8,128]{2,1,0:T(8,128)S(1)}, f32[24,8,128]{2,1,0:T(8,128)S(1)}, u32[]{:S(2)}, u32[]{:S(2)}) collective-permute-start(f32[24,8,128]{2,1,0:T(8,128)S(1)} %constant_dynamic-update-slice_fusion), channel_id=1, source_target_pairs={{0,24},{8,0},{16,8},{24,16},{1,25},{9,1},{17,9},{25,17},{2,26},{10... | collective-permute-start | bytes 294920 | tf_op jit(solution)/shard_map/ppermute | solution.py:558
  9.7 8.7 %collective-permute-start.1 = (f32[24,8,128]{2,1,0:T(8,128)S(1)}, f32[24,8,128]{2,1,0:T(8,128)S(1)}, u32[]{:S(2)}, u32[]{:S(2)}) collective-permute-start(f32[24,8,128]{2,1,0:T(8,128)S(1)} %constant_dynamic-update-slice_fusion), channel_id=1, source_target_pairs={{0,16},{8,24},{16,0},{24,8},{1,17},{9,25},{17,1},{25,9},{2,18},{10... | collective-permute-start | bytes 294920 | tf_op jit(solution)/shard_map/ppermute | solution.py:558
  9.7 8.7 %collective-permute-start = (f32[24,8,128]{2,1,0:T(8,128)S(1)}, f32[24,8,128]{2,1,0:T(8,128)S(1)}, u32[]{:S(2)}, u32[]{:S(2)}) collective-permute-start(f32[24,8,128]{2,1,0:T(8,128)S(1)} %constant_dynamic-update-slice_fusion), channel_id=1, source_target_pairs={{0,8},{8,16},{16,24},{24,0},{1,9},{9,17},{17,25},{25,1},{2,10},{10... | collective-permute-start | bytes 294920 | tf_op jit(solution)/shard_map/ppermute | solution.py:558
  18.4 1.8 %collective-permute-start.3 = (f32[4,24,8,128]{3,2,1,0:T(8,128)S(1)}, f32[4,24,8,128]{3,2,1,0:T(8,128)S(1)}, u32[]{:S(2)}, u32[]{:S(2)}) collective-permute-start(f32[4,24,8,128]{3,2,1,0:T(8,128)S(1)} %pad_maximum_fusion.refs_1_), channel_id=1, source_target_pairs={{0,1},{1,0},{2,3},{3,2},{4,5},{5,4},{6,7},{7,6},{8,9},{9,8},{10,11... | collective-permute-start | bytes 1179656 | tf_op jit(solution)/shard_map/ppermute | solution.py:558
  20.2 9.1 %copy-start.10 = (f32[256,4]{0,1:T(4,128)S(1)}, f32[256,4]{0,1:T(4,128)}, u32[]{:S(2)}) copy-start(f32[256,4]{0,1:T(4,128)} %param.15) | copy-start | bytes 12292
  20.2 39.2 %all-to-all-start = ((f32[32,8,8,128]{3,2,1,0:T(8,128)}), f32[32,8,8,128]{3,2,1,0:T(8,128)S(1)}, u32[]{:S(2)}, u32[]{:S(2)}) async-start(f32[32,8,8,128]{3,2,1,0:T(8,128)} %param.9), calls=%async_computation | async-start | bytes 2097152 | tf_op jit(solution)/shard_map/all_to_all | solution.py:579
  24.8 21.7 %collective-permute-start.6 = (f32[4,24,8,128]{3,2,1,0:T(8,128)S(1)}, f32[4,24,8,128]{3,2,1,0:T(8,128)}, u32[]{:S(2)}, u32[]{:S(2)}) collective-permute-start(f32[4,24,8,128]{3,2,1,0:T(8,128)S(1)} %pad_maximum_fusion.refs_1_), channel_id=1, source_target_pairs={{0,6},{2,0},{4,2},{6,4},{1,7},{3,1},{5,3},{7,5},{8,14},{10,8},{12,... | collective-permute-start | bytes 1179656 | tf_op jit(solution)/shard_map/ppermute | solution.py:558
  27.5 19.0 %collective-permute-start.5 = (f32[4,24,8,128]{3,2,1,0:T(8,128)S(1)}, f32[4,24,8,128]{3,2,1,0:T(8,128)}, u32[]{:S(2)}, u32[]{:S(2)}) collective-permute-start(f32[4,24,8,128]{3,2,1,0:T(8,128)S(1)} %pad_maximum_fusion.refs_1_), channel_id=1, source_target_pairs={{0,4},{2,6},{4,0},{6,2},{1,5},{3,7},{5,1},{7,3},{8,12},{10,14},{12... | collective-permute-start | bytes 1179656 | tf_op jit(solution)/shard_map/ppermute | solution.py:558
  28.0 28.7 %collective-permute-start.4 = (f32[4,24,8,128]{3,2,1,0:T(8,128)S(1)}, f32[4,24,8,128]{3,2,1,0:T(8,128)}, u32[]{:S(2)}, u32[]{:S(2)}) collective-permute-start(f32[4,24,8,128]{3,2,1,0:T(8,128)S(1)} %pad_maximum_fusion.refs_1_), channel_id=1, source_target_pairs={{0,2},{2,4},{4,6},{6,0},{1,3},{3,5},{5,7},{7,1},{8,10},{10,12},{12... | collective-permute-start | bytes 1179656 | tf_op jit(solution)/shard_map/ppermute | solution.py:558
  29.8 29.6 %copy-start = (bf16[1536,256]{1,0:T(8,128)(2,1)S(1)}, bf16[1536,256]{1,0:T(8,128)(2,1)}, u32[]{:S(2)}) copy-start(bf16[1536,256]{1,0:T(8,128)(2,1)} %constant.68.clone.refs_10_) | copy-start | bytes 2359300
  31.2 28.2 %copy-start.1 = (bf16[256,768]{1,0:T(8,128)(2,1)S(1)}, bf16[256,768]{1,0:T(8,128)(2,1)}, u32[]{:S(2)}) copy-start(bf16[256,768]{1,0:T(8,128)(2,1)} %constant.69.clone.refs_11_) | copy-start | bytes 1179652
  32.6 24.1 %copy-start.11 = (s32[256]{0:T(256)S(1)}, s32[256]{0:T(256)}, u32[]{:S(2)}) copy-start(s32[256]{0:T(256)} %param.12) | copy-start | bytes 3076
  46.5 10.3 %collective-permute-start.9 = (f32[4,24,8,128]{3,2,1,0:T(8,128)}, f32[4,24,8,128]{3,2,1,0:T(8,128)S(1)}, u32[]{:S(2)}, u32[]{:S(2)}) collective-permute-start(f32[4,24,8,128]{3,2,1,0:T(8,128)} %collective-permute-done.6.refs_4_), channel_id=1, source_target_pairs={{0,1},{1,0},{2,3},{3,2},{4,5},{5,4},{6,7},{7,6},{8,9},{9,8},{10,11... | collective-permute-start | bytes 1179656 | tf_op jit(solution)/shard_map/ppermute | solution.py:558
  46.5 11.1 %collective-permute-start.8 = (f32[4,24,8,128]{3,2,1,0:T(8,128)}, f32[4,24,8,128]{3,2,1,0:T(8,128)S(1)}, u32[]{:S(2)}, u32[]{:S(2)}) collective-permute-start(f32[4,24,8,128]{3,2,1,0:T(8,128)} %collective-permute-done.5.refs_3_), channel_id=1, source_target_pairs={{0,1},{1,0},{2,3},{3,2},{4,5},{5,4},{6,7},{7,6},{8,9},{9,8},{10,11... | collective-permute-start | bytes 1179656 | tf_op jit(solution)/shard_map/ppermute | solution.py:558
  56.7 1.9 %collective-permute-start.7 = (f32[4,24,8,128]{3,2,1,0:T(8,128)}, f32[4,24,8,128]{3,2,1,0:T(8,128)S(1)}, u32[]{:S(2)}, u32[]{:S(2)}) collective-permute-start(f32[4,24,8,128]{3,2,1,0:T(8,128)} %collective-permute-done.4.refs_2_), channel_id=1, source_target_pairs={{0,1},{1,0},{2,3},{3,2},{4,5},{5,4},{6,7},{7,6},{8,9},{9,8},{10,11... | collective-permute-start | bytes 1179656 | tf_op jit(solution)/shard_map/ppermute | solution.py:558
  56.8 0.8 copy-start.2
  57.6 0.7 copy-start.4
  58.7 0.7 copy-start.6
  59.4 1.0 copy-start.3
  60.4 1.0 copy-start.5
  61.4 1.0 copy-start.7

commit v5 on v4

--- a/solution.py
+++ b/solution.py
@@ -1,4 +1,5 @@
 import functools
+import math
 import jax
 import jax.numpy as jnp
 from jax import lax
@@ -521,7 +522,7 @@
     cells = (columns // 2 * span, LANE)
     plane = jnp.asarray(plane_weights(groups_y))
     depth = jnp.asarray(depth_weights(groups_z))
-    anywhere = pl.BlockSpec(memory_space=pl.ANY)
+    anywhere = pl.BlockSpec(memory_space=pltpu.HBM)
     smem = pl.BlockSpec(memory_space=pltpu.SMEM)
     out = pl.pallas_call(
         functools.partial(filter_kernel, groups, atoms),
@@ -570,33 +571,29 @@
     me = (my_place[0] * groups[1] + my_place[1]) * groups_z + my_place[2]
     extent = lax.dynamic_slice(box_extent, (me * atoms_own,), (atoms_own,))
     pack = packed_inputs(potential, projectors, extent)
-    line = jnp.stack(hops(pack, "gx"))
-    plane = hops(line, "gy")
-    swapped = hops(line, "gz")
-    orbitals, swapped = lax.optimization_barrier((orbitals, swapped))
-    crossed = [swapped] + [hops(piece, "gz") for piece in plane[1:]]
-    packs = [crossed[hop_y][hop_z] for hop_z in range(groups_z) for hop_y in range(groups[1])]
+    line = hops(pack, "gx")
+    if len(line) > 1:
+        orbitals, line[1] = lax.optimization_barrier((orbitals, line[1]))
+    spread = [hops(piece, "gy") for piece in line]
+    packs = []
+    for hop_y in range(groups[1]):
+        packs.append(hops(jnp.stack([pieces[hop_y] for pieces in spread]), "gz"))
+    packs = [packs[hop_y][hop_z] for hop_z in range(groups_z) for hop_y in range(groups[1])]
     field = lax.all_to_all(orbitals, axes, split_axis=0, concat_axis=0, tiled=True)
     place, half = box_places(groups, owner_rank, box_anchor[2])
     result = filter_call(
         groups, place, half, my_place, field, packs, packed_coupling(coupling)
     )
     filtered = lax.all_to_all(result, axes, split_axis=0, concat_axis=0, tiled=True)
-    states = filtered.shape[0]
-    flattened = filtered.reshape(states, -1)
-    partial_value = jnp.dot(flattened, flattened.T, precision=lax.Precision.HIGHEST)
-    quarter = partial_value.reshape(-1, SUB, states).transpose(1, 0, 2).reshape(SUB, -1)
-    parts = lax.all_to_all(
-        jnp.broadcast_to(quarter[None], (domains,) + quarter.shape),
-        axes,
-        split_axis=0,
-        concat_axis=0,
-        tiled=True,
-    )
-    summed = jnp.sum(parts, axis=0).reshape(SUB, -1, states).transpose(1, 0, 2)
+    flattened = filtered.reshape(filtered.shape[0], -1)
+    intersection = jnp.dot(flattened, flattened.T, precision=lax.Precision.HIGHEST)
+    for stage in (("gy", "gz"), ("gx",)):
+        sharers = math.prod(lax.axis_size(axis) for axis in stage)
+        copies = jnp.broadcast_to(intersection[None], (sharers,) + intersection.shape)
+        copies = lax.all_to_all(copies, stage, split_axis=0, concat_axis=0, tiled=True)
+        intersection = jnp.sum(copies, axis=0)
     cells_total = orbitals.shape[1] * orbitals.shape[2] * orbitals.shape[3] * domains
-    intersection = summed.reshape(states, states) / cells_total
-    return (filtered, intersection)
+    return (filtered, intersection / cells_total)
 
 
 def body(orbitals, potential, projectors, owner_rank, box_anchor, box_extent, coupling):

time: 133 us -> 157 us (1.18)
  starting transfers between devices: 15.1 us -> 26.3 us
  blocking collectives: 42.7 us -> 47.6 us
  waiting for transfers between devices: 33.3 us -> 35.8 us
  other arithmetic: 0.49 us -> 2.6 us
  Pallas kernels: 24.1 us -> 26 us
    ppermute x10 -> x19, starting transfers between devices: 10.5 us -> 22.2 us  [hops(): lax.ppermute(value, axis, [(i, (i + hop) % count) for i in range(count)])]
    all_to_all x1 -> x2, blocking collectives: 11.7 us -> 16.4 us  [state_body(): lax.all_to_all(copies, stage, split_axis=0, concat_axis=0, tiled=True)]
    unnamed x28 -> x36, local copies, waits for them, and re-layouts: 8.12 us -> 11.8 us
    ppermute x10 -> x19, waiting for transfers between devices: 33.3 us -> 35.8 us  [hops(): lax.ppermute(value, axis, [(i, (i + hop) % count) for i in range(count)])]
    pallas_call x1, Pallas kernels: 24.1 us -> 26 us  [filter_call(): pl.pallas_call(functools.partial(filter_kernel, groups, atoms), out_shape...]
  transfers between devices with their start and end apart: 11 -> 20, of which waited for: 6 -> 9; matrix products, arithmetic and copies ran while one was open for 3% -> 2% of each run, Pallas kernels for 0% -> 0%
where the time goes in v5:
time: 157 us
  blocking collectives  47.6 us (30%)
  waiting for transfers between devices  35.8 us (23%)
  starting transfers between devices  26.3 us (17%)
  Pallas kernels  26 us (17%)
  local copies, waits for them, and re-layouts  16.1 us (10%)
  other arithmetic  2.6 us (2%)
    ppermute x19, waiting for transfers between devices, hops(): lax.ppermute(value, axis, [(i, (i + hop) % count) for i in range(count)])  35.8 us
    all_to_all x1, blocking collectives, state_body(): lax.all_to_all(result, axes, split_axis=0, concat_axis=0, tiled=True)  31.1 us
    pallas_call x1, Pallas kernels, filter_call(): pl.pallas_call(functools.partial(filter_kernel, groups, atoms), out_shape...  26 us
    ppermute x19, starting transfers between devices, hops(): lax.ppermute(value, axis, [(i, (i + hop) % count) for i in range(count)])  22.2 us
    all_to_all x2, blocking collectives, state_body(): lax.all_to_all(copies, stage, split_axis=0, concat_axis=0, tiled=True)  16.4 us
    unnamed x36, local copies, waits for them, and re-layouts  11.8 us
    all_to_all x1, starting transfers between devices, state_body(): lax.all_to_all(orbitals, axes, split_axis=0, concat_axis=0, tiled=True)  4.07 us
  transfers between devices with their start and end apart: 20, of which 9 were waited for; matrix products, arithmetic and copies ran while one was open for 2% of the time, Pallas kernels for 0%

profile of v5, /device:TPU:0, one launch (start us, length us, event | category | flops | bytes accessed | tf_op | source)
XLA Modules:
  0.0 156.7 jit_solution(6051134119032912596)
XLA Ops:
  0.7 0.7 copy-done.14
  1.6 0.1 broadcast_and_fusion
  1.7 0.2 and.69
  1.9 0.5 copy-done.10
  2.5 0.6 reshape.123
  3.0 0.3 copy.30
  3.4 0.1 reshape.124
  3.5 0.6 copy-done.11
  4.1 0.1 reshape.121
  4.2 0.1 copy.28
  4.3 0.1 reshape.122
  4.5 3.1 %collective-permute-start = (f32[24,8,128]{2,1,0:T(8,128)S(1)}, f32[24,8,128]{2,1,0:T(8,128)S(1)}, u32[]{:S(2)}, u32[]{:S(2)}) collective-permute-start(f32[24,8,128]{2,1,0:T(8,128)S(1)} %constant_dynamic-update-slice_fusion), channel_id=1, source_target_pairs={{0,8},{8,16},{16,24},{24,0},{1,9},{9,17},{17,25},{25,1},{2,10},{10... | collective-permute-start | bytes 294920 | tf_op jit(solution)/shard_map/ppermute | solution.py:559
  7.5 4.8 %collective-permute-done = f32[24,8,128]{2,1,0:T(8,128)S(1)} collective-permute-done((f32[24,8,128]{2,1,0:T(8,128)S(1)}, f32[24,8,128]{2,1,0:T(8,128)S(1)}, u32[]{:S(2)}, u32[]{:S(2)}) %collective-permute-start) | collective-permute-done | bytes 98336 | tf_op jit(solution)/shard_map/ppermute | solution.py:559
  12.4 4.1 %all-to-all-start = ((f32[32,8,8,128]{3,2,1,0:T(8,128)}), f32[32,8,8,128]{3,2,1,0:T(8,128)S(1)}, u32[]{:S(2)}, u32[]{:S(2)}) async-start(f32[32,8,8,128]{3,2,1,0:T(8,128)} %param.9), calls=%async_computation | async-start | bytes 2097152 | tf_op jit(solution)/shard_map/all_to_all | solution.py:582
  16.4 2.7 %collective-permute-start.1 = (f32[24,8,128]{2,1,0:T(8,128)S(1)}, f32[24,8,128]{2,1,0:T(8,128)S(1)}, u32[]{:S(2)}, u32[]{:S(2)}) collective-permute-start(f32[24,8,128]{2,1,0:T(8,128)S(1)} %constant_dynamic-update-slice_fusion), channel_id=1, source_target_pairs={{0,16},{8,24},{16,0},{24,8},{1,17},{9,25},{17,1},{25,9},{2,18},{10... | collective-permute-start | bytes 294920 | tf_op jit(solution)/shard_map/ppermute | solution.py:559
  19.2 1.5 collective-permute-start.2
  20.6 2.4 %collective-permute-start.11 = (f32[24,8,128]{2,1,0:T(8,128)S(1)}, f32[24,8,128]{2,1,0:T(8,128)S(1)}, u32[]{:S(2)}, u32[]{:S(2)}) collective-permute-start(f32[24,8,128]{2,1,0:T(8,128)S(1)} %constant_dynamic-update-slice_fusion), channel_id=1, source_target_pairs={{0,6},{2,0},{4,2},{6,4},{1,7},{3,1},{5,3},{7,5},{8,14},{10,8},{12,... | collective-permute-start | bytes 294920 | tf_op jit(solution)/shard_map/ppermute | solution.py:559
  23.0 0.6 collective-permute-start.7
  23.6 0.7 slice.3
  24.4 0.4 copy.31
  24.8 0.6 broadcast_in_dim.20
  25.4 0.3 reshape.127.refs_9_
  25.8 0.6 collective-permute-start.12
  26.4 21.0 %collective-permute-done.1 = f32[24,8,128]{2,1,0:T(8,128)S(1)} collective-permute-done((f32[24,8,128]{2,1,0:T(8,128)S(1)}, f32[24,8,128]{2,1,0:T(8,128)S(1)}, u32[]{:S(2)}, u32[]{:S(2)}) %collective-permute-start.1) | collective-permute-done | bytes 98336 | tf_op jit(solution)/shard_map/ppermute | solution.py:559
  47.4 2.4 %collective-permute-start.13 = (f32[24,8,128]{2,1,0:T(8,128)S(1)}, f32[24,8,128]{2,1,0:T(8,128)S(1)}, u32[]{:S(2)}, u32[]{:S(2)}) collective-permute-start(f32[24,8,128]{2,1,0:T(8,128)S(1)} %collective-permute-done.1), channel_id=1, source_target_pairs={{0,6},{2,0},{4,2},{6,4},{1,7},{3,1},{5,3},{7,5},{8,14},{10,8},{12,... | collective-permute-start | bytes 294920 | tf_op jit(solution)/shard_map/ppermute | solution.py:559
  49.8 0.6 collective-permute-start.14
  50.4 1.5 collective-permute-start.3
  51.9 0.6 collective-permute-start.8
  52.5 0.5 collective-permute-done.13
  53.0 1.5 collective-permute-start.9
  54.5 0.7 collective-permute-done.14
  55.1 0.9 collective-permute-start.10
  56.1 2.3 %collective-permute-start.4 = (f32[24,8,128]{2,1,0:T(8,128)S(1)}, f32[24,8,128]{2,1,0:T(8,128)S(1)}, u32[]{:S(2)}, u32[]{:S(2)}) collective-permute-start(f32[24,8,128]{2,1,0:T(8,128)S(1)} %collective-permute-done), channel_id=1, source_target_pairs={{0,2},{2,4},{4,6},{6,0},{1,3},{3,5},{5,7},{7,1},{8,10},{10,12},{12... | collective-permute-start | bytes 294920 | tf_op jit(solution)/shard_map/ppermute | solution.py:559
  58.4 1.3 collective-permute-done.8
  59.7 2.6 %collective-permute-done.9 = f32[24,8,128]{2,1,0:T(8,128)S(1)} collective-permute-done((f32[24,8,128]{2,1,0:T(8,128)S(1)}, f32[24,8,128]{2,1,0:T(8,128)S(1)}, u32[]{:S(2)}, u32[]{:S(2)}) %collective-permute-start.9) | collective-permute-done | bytes 98336 | tf_op jit(solution)/shard_map/ppermute | solution.py:559
  62.3 1.1 collective-permute-done.10
  63.3 1.1 collective-permute-start.6
  64.5 0.5 collective-permute-start.17
  65.0 2.8 %collective-permute-done.5 = f32[24,8,128]{2,1,0:T(8,128)S(1)} collective-permute-done((f32[24,8,128]{2,1,0:T(8,128)S(1)}, f32[24,8,128]{2,1,0:T(8,128)S(1)}, u32[]{:S(2)}, u32[]{:S(2)}) %collective-permute-start.5) | collective-permute-done | bytes 98336 | tf_op jit(solution)/shard_map/ppermute | solution.py:559
  67.8 1.1 collective-permute-done.6
  69.0 0.6 copy-done.13
  69.6 0.7 copy-done.2
  70.3 0.8 copy-done.4
  71.1 0.7 copy-done.6
  71.8 0.7 copy-done.8
  72.6 1.1 copy-done
  73.7 1.0 copy-done.3
  74.7 1.0 copy-done.5
  75.7 1.0 copy-done.7
  76.7 1.0 copy-done.9
  77.7 26.0 %shard_map.104 = f32[2048,128]{1,0:T(8,128)S(1)} custom-call(s32[256]{0:T(256)S(1)} %multiply_add_fusion.place, s32[256]{0:T(256)S(1)} %get-tuple-element.10.half, s32[3]{0:T(128)S(1)} %pad_add_fusion.my_place, f32[2048,128]{1,0:T(8,128)S(1)} %bitcast.35, f32[4,24,8,128]{3,2,1,0:T(8,128)S(1)} %pad_maximum_fusion.refs_1_, ...), custom_call_target="tpu_custom_call" | custom-call | tf_op jit(solution)/shard_map/pallas_call | solution.py:527
  103.7 31.1 %all_to_all.20 = f32[32,8,8,128]{3,2,1,0:T(8,128)S(1)} all-to-all(f32[32,8,8,128]{3,2,1,0:T(8,128)S(1)} %bitcast.36), channel_id=1, replica_groups=mesh['gx'=4,'gy'=4,'gz'=2] {'gx','gy','gz'}, dimensions={0} | all-to-all | bytes 2097152 | tf_op jit(solution)/shard_map/all_to_all | solution.py:587
  134.8 1.5 convolution_bitcast_fusion
  136.4 0.1 reshape.130
  136.5 8.3 %all_to_all.21 = f32[8,1,1024]{2,1,0:T(1,128)S(1)} all-to-all(f32[8,1,1024]{2,1,0:T(1,128)S(1)} %reshape.130), channel_id=1, replica_groups=mesh['gx'=4,'gy'=4,'gz'=2] {'gy','gz'}, dimensions={0} | all-to-all | bytes 65536 | tf_op jit(solution)/shard_map/all_to_all | solution.py:593
  144.8 0.5 broadcast.131
  145.3 0.7 reduce
  146.0 0.1 reshape.131
  146.2 0.1 reshape.132
  146.3 8.1 %all_to_all.22 = f32[4,1,1024]{2,1,0:T(1,128)S(1)} all-to-all(f32[4,1,1024]{2,1,0:T(1,128)S(1)} %reshape.132), channel_id=1, replica_groups=mesh['gx'=4,'gy'=4,'gz'=2] {'gx'}, dimensions={0} | all-to-all | bytes 32768 | tf_op jit(solution)/shard_map/all_to_all | solution.py:593
  154.4 0.7 reduce.1
  155.1 0.1 reshape.133
  155.2 0.6 broadcast_multiply_fusion
  155.8 1.0 copy.39
  (51 shorter events, 0.9 us)
Async XLA Ops:
  0.6 0.7 copy-start.14
  1.6 0.8 copy-start.10
  3.4 0.8 copy-start.11
  4.5 7.9 %collective-permute-start = (f32[24,8,128]{2,1,0:T(8,128)S(1)}, f32[24,8,128]{2,1,0:T(8,128)S(1)}, u32[]{:S(2)}, u32[]{:S(2)}) collective-permute-start(f32[24,8,128]{2,1,0:T(8,128)S(1)} %constant_dynamic-update-slice_fusion), channel_id=1, source_target_pairs={{0,8},{8,16},{16,24},{24,0},{1,9},{9,17},{17,25},{25,1},{2,10},{10... | collective-permute-start | bytes 294920 | tf_op jit(solution)/shard_map/ppermute | solution.py:559
  12.4 11.9 %copy-start.12 = (f32[256,4]{0,1:T(4,128)S(1)}, f32[256,4]{0,1:T(4,128)}, u32[]{:S(2)}) copy-start(f32[256,4]{0,1:T(4,128)} %param.15) | copy-start | bytes 12292
  12.4 60.2 %all-to-all-start = ((f32[32,8,8,128]{3,2,1,0:T(8,128)}), f32[32,8,8,128]{3,2,1,0:T(8,128)S(1)}, u32[]{:S(2)}, u32[]{:S(2)}) async-start(f32[32,8,8,128]{3,2,1,0:T(8,128)} %param.9), calls=%async_computation | async-start | bytes 2097152 | tf_op jit(solution)/shard_map/all_to_all | solution.py:582
  16.4 30.9 %collective-permute-start.1 = (f32[24,8,128]{2,1,0:T(8,128)S(1)}, f32[24,8,128]{2,1,0:T(8,128)S(1)}, u32[]{:S(2)}, u32[]{:S(2)}) collective-permute-start(f32[24,8,128]{2,1,0:T(8,128)S(1)} %constant_dynamic-update-slice_fusion), channel_id=1, source_target_pairs={{0,16},{8,24},{16,0},{24,8},{1,17},{9,25},{17,1},{25,9},{2,18},{10... | collective-permute-start | bytes 294920 | tf_op jit(solution)/shard_map/ppermute | solution.py:559
  19.2 30.6 %collective-permute-start.2 = (f32[24,8,128]{2,1,0:T(8,128)S(1)}, f32[24,8,128]{2,1,0:T(8,128)S(1)}, u32[]{:S(2)}, u32[]{:S(2)}) collective-permute-start(f32[24,8,128]{2,1,0:T(8,128)S(1)} %constant_dynamic-update-slice_fusion), channel_id=1, source_target_pairs={{0,24},{8,0},{16,8},{24,16},{1,25},{9,1},{17,9},{25,17},{2,26},{10... | collective-permute-start | bytes 294920 | tf_op jit(solution)/shard_map/ppermute | solution.py:559
  20.6 29.7 %collective-permute-start.11 = (f32[24,8,128]{2,1,0:T(8,128)S(1)}, f32[24,8,128]{2,1,0:T(8,128)S(1)}, u32[]{:S(2)}, u32[]{:S(2)}) collective-permute-start(f32[24,8,128]{2,1,0:T(8,128)S(1)} %constant_dynamic-update-slice_fusion), channel_id=1, source_target_pairs={{0,6},{2,0},{4,2},{6,4},{1,7},{3,1},{5,3},{7,5},{8,14},{10,8},{12,... | collective-permute-start | bytes 294920 | tf_op jit(solution)/shard_map/ppermute | solution.py:559
  23.0 33.1 %collective-permute-start.7 = (f32[24,8,128]{2,1,0:T(8,128)S(1)}, f32[24,8,128]{2,1,0:T(8,128)S(1)}, u32[]{:S(2)}, u32[]{:S(2)}) collective-permute-start(f32[24,8,128]{2,1,0:T(8,128)S(1)} %constant_dynamic-update-slice_fusion), channel_id=1, source_target_pairs={{0,4},{2,6},{4,0},{6,2},{1,5},{3,7},{5,1},{7,3},{8,12},{10,14},{12... | collective-permute-start | bytes 294920 | tf_op jit(solution)/shard_map/ppermute | solution.py:559
  25.8 26.1 %collective-permute-start.12 = (f32[24,8,128]{2,1,0:T(8,128)S(1)}, f32[24,8,128]{2,1,0:T(8,128)S(1)}, u32[]{:S(2)}, u32[]{:S(2)}) collective-permute-start(f32[24,8,128]{2,1,0:T(8,128)S(1)} %collective-permute-done), channel_id=1, source_target_pairs={{0,6},{2,0},{4,2},{6,4},{1,7},{3,1},{5,3},{7,5},{8,14},{10,8},{12,... | collective-permute-start | bytes 294920 | tf_op jit(solution)/shard_map/ppermute | solution.py:559
  47.4 5.6 %collective-permute-start.13 = (f32[24,8,128]{2,1,0:T(8,128)S(1)}, f32[24,8,128]{2,1,0:T(8,128)S(1)}, u32[]{:S(2)}, u32[]{:S(2)}) collective-permute-start(f32[24,8,128]{2,1,0:T(8,128)S(1)} %collective-permute-done.1), channel_id=1, source_target_pairs={{0,6},{2,0},{4,2},{6,4},{1,7},{3,1},{5,3},{7,5},{8,14},{10,8},{12,... | collective-permute-start | bytes 294920 | tf_op jit(solution)/shard_map/ppermute | solution.py:559
  49.8 5.4 %collective-permute-start.14 = (f32[24,8,128]{2,1,0:T(8,128)S(1)}, f32[24,8,128]{2,1,0:T(8,128)S(1)}, u32[]{:S(2)}, u32[]{:S(2)}) collective-permute-start(f32[24,8,128]{2,1,0:T(8,128)S(1)} %collective-permute-done.2), channel_id=1, source_target_pairs={{0,6},{2,0},{4,2},{6,4},{1,7},{3,1},{5,3},{7,5},{8,14},{10,8},{12,... | collective-permute-start | bytes 294920 | tf_op jit(solution)/shard_map/ppermute | solution.py:559
  50.4 14.1 %collective-permute-start.3 = (f32[24,8,128]{2,1,0:T(8,128)S(1)}, f32[24,8,128]{2,1,0:T(8,128)S(1)}, u32[]{:S(2)}, u32[]{:S(2)}) collective-permute-start(f32[24,8,128]{2,1,0:T(8,128)S(1)} %constant_dynamic-update-slice_fusion), channel_id=1, source_target_pairs={{0,2},{2,4},{4,6},{6,0},{1,3},{3,5},{5,7},{7,1},{8,10},{10,12},{12... | collective-permute-start | bytes 294920 | tf_op jit(solution)/shard_map/ppermute | solution.py:559
  51.9 7.8 %collective-permute-start.8 = (f32[24,8,128]{2,1,0:T(8,128)S(1)}, f32[24,8,128]{2,1,0:T(8,128)S(1)}, u32[]{:S(2)}, u32[]{:S(2)}) collective-permute-start(f32[24,8,128]{2,1,0:T(8,128)S(1)} %collective-permute-done), channel_id=1, source_target_pairs={{0,4},{2,6},{4,0},{6,2},{1,5},{3,7},{5,1},{7,3},{8,12},{10,14},{12... | collective-permute-start | bytes 294920 | tf_op jit(solution)/shard_map/ppermute | solution.py:559
  53.0 9.3 %collective-permute-start.9 = (f32[24,8,128]{2,1,0:T(8,128)S(1)}, f32[24,8,128]{2,1,0:T(8,128)S(1)}, u32[]{:S(2)}, u32[]{:S(2)}) collective-permute-start(f32[24,8,128]{2,1,0:T(8,128)S(1)} %collective-permute-done.1), channel_id=1, source_target_pairs={{0,4},{2,6},{4,0},{6,2},{1,5},{3,7},{5,1},{7,3},{8,12},{10,14},{12... | collective-permute-start | bytes 294920 | tf_op jit(solution)/shard_map/ppermute | solution.py:559
  55.1 8.2 %collective-permute-start.10 = (f32[24,8,128]{2,1,0:T(8,128)S(1)}, f32[24,8,128]{2,1,0:T(8,128)S(1)}, u32[]{:S(2)}, u32[]{:S(2)}) collective-permute-start(f32[24,8,128]{2,1,0:T(8,128)S(1)} %collective-permute-done.2), channel_id=1, source_target_pairs={{0,4},{2,6},{4,0},{6,2},{1,5},{3,7},{5,1},{7,3},{8,12},{10,14},{12... | collective-permute-start | bytes 294920 | tf_op jit(solution)/shard_map/ppermute | solution.py:559
  56.1 8.4 %collective-permute-start.4 = (f32[24,8,128]{2,1,0:T(8,128)S(1)}, f32[24,8,128]{2,1,0:T(8,128)S(1)}, u32[]{:S(2)}, u32[]{:S(2)}) collective-permute-start(f32[24,8,128]{2,1,0:T(8,128)S(1)} %collective-permute-done), channel_id=1, source_target_pairs={{0,2},{2,4},{4,6},{6,0},{1,3},{3,5},{5,7},{7,1},{8,10},{10,12},{12... | collective-permute-start | bytes 294920 | tf_op jit(solution)/shard_map/ppermute | solution.py:559
  59.7 9.8 %collective-permute-start.15 = (f32[4,24,8,128]{3,2,1,0:T(8,128)S(1)}, f32[4,24,8,128]{3,2,1,0:T(8,128)S(1)}, u32[]{:S(2)}, u32[]{:S(2)}) collective-permute-start(f32[4,24,8,128]{3,2,1,0:T(8,128)S(1)} %pad_maximum_fusion.refs_1_), channel_id=1, source_target_pairs={{0,1},{1,0},{2,3},{3,2},{4,5},{5,4},{6,7},{7,6},{8,9},{9,8},{10,11... | collective-permute-start | bytes 1179656 | tf_op jit(solution)/shard_map/ppermute | solution.py:559
  62.3 5.5 %collective-permute-start.5 = (f32[24,8,128]{2,1,0:T(8,128)S(1)}, f32[24,8,128]{2,1,0:T(8,128)S(1)}, u32[]{:S(2)}, u32[]{:S(2)}) collective-permute-start(f32[24,8,128]{2,1,0:T(8,128)S(1)} %collective-permute-done.1), channel_id=1, source_target_pairs={{0,2},{2,4},{4,6},{6,0},{1,3},{3,5},{5,7},{7,1},{8,10},{10,12},{12... | collective-permute-start | bytes 294920 | tf_op jit(solution)/shard_map/ppermute | solution.py:559
  63.3 5.5 %collective-permute-start.6 = (f32[24,8,128]{2,1,0:T(8,128)S(1)}, f32[24,8,128]{2,1,0:T(8,128)S(1)}, u32[]{:S(2)}, u32[]{:S(2)}) collective-permute-start(f32[24,8,128]{2,1,0:T(8,128)S(1)} %collective-permute-done.2), channel_id=1, source_target_pairs={{0,2},{2,4},{4,6},{6,0},{1,3},{3,5},{5,7},{7,1},{8,10},{10,12},{12... | collective-permute-start | bytes 294920 | tf_op jit(solution)/shard_map/ppermute | solution.py:559
  64.4 5.9 %collective-permute-start.18 = (f32[4,24,8,128]{3,2,1,0:T(8,128)S(1)}, f32[4,24,8,128]{3,2,1,0:T(8,128)S(1)}, u32[]{:S(2)}, u32[]{:S(2)}) collective-permute-start(f32[4,24,8,128]{3,2,1,0:T(8,128)S(1)} %pad_maximum_fusion.3.refs_4_), channel_id=1, source_target_pairs={{0,1},{1,0},{2,3},{3,2},{4,5},{5,4},{6,7},{7,6},{8,9},{9,8},{10,11... | collective-permute-start | bytes 1179656 | tf_op jit(solution)/shard_map/ppermute | solution.py:559
  64.5 6.6 %collective-permute-start.17 = (f32[4,24,8,128]{3,2,1,0:T(8,128)S(1)}, f32[4,24,8,128]{3,2,1,0:T(8,128)S(1)}, u32[]{:S(2)}, u32[]{:S(2)}) collective-permute-start(f32[4,24,8,128]{3,2,1,0:T(8,128)S(1)} %pad_maximum_fusion.2.refs_3_), channel_id=1, source_target_pairs={{0,1},{1,0},{2,3},{3,2},{4,5},{5,4},{6,7},{7,6},{8,9},{9,8},{10,11... | collective-permute-start | bytes 1179656 | tf_op jit(solution)/shard_map/ppermute | solution.py:559
  68.9 0.7 copy-start.13
  68.9 3.7 %copy-start.1 = (bf16[256,768]{1,0:T(8,128)(2,1)S(1)}, bf16[256,768]{1,0:T(8,128)(2,1)}, u32[]{:S(2)}) copy-start(bf16[256,768]{1,0:T(8,128)(2,1)} %constant.69.clone.refs_11_) | copy-start | bytes 1179652
  68.9 2.9 %collective-permute-start.16 = (f32[4,24,8,128]{3,2,1,0:T(8,128)S(1)}, f32[4,24,8,128]{3,2,1,0:T(8,128)S(1)}, u32[]{:S(2)}, u32[]{:S(2)}) collective-permute-start(f32[4,24,8,128]{3,2,1,0:T(8,128)S(1)} %pad_maximum_fusion.1.refs_2_), channel_id=1, source_target_pairs={{0,1},{1,0},{2,3},{3,2},{4,5},{5,4},{6,7},{7,6},{8,9},{9,8},{10,11... | collective-permute-start | bytes 1179656 | tf_op jit(solution)/shard_map/ppermute | solution.py:559
  69.6 0.7 copy-start.2
  70.3 0.8 copy-start.4
  71.1 0.7 copy-start.6
  71.8 0.7 copy-start.8
  72.6 1.1 copy-start
  73.7 1.0 copy-start.3
  74.7 1.0 copy-start.5
  75.7 1.0 copy-start.7
  76.7 1.0 copy-start.9

commit v6 on v3

--- a/solution.py
+++ b/solution.py
@@ -1,4 +1,5 @@
 import functools
+import math
 import jax
 import jax.numpy as jnp
 from jax import lax
@@ -204,7 +205,7 @@
             block = block + np.einsum("ajbp,io->aijbop", ring, np.eye(SUB))
         blocks.append(block.reshape(slab, slab))
     high, low = split_terms(np.concatenate(blocks, axis=0))
-    return np.concatenate([high, high, low], axis=0)
+    return np.concatenate([high, low], axis=0)
 
 
 def depth_weights(groups_z):
@@ -234,18 +235,106 @@
 
 
 SPARES = 2
+TALL = 2 * SUB
+
+
+def split_store(high_buf, low_buf, rows, cols, value):
+    high, low = split_pair(value)
+    high_buf[rows, cols] = high
+    low_buf[rows, cols] = low
+
+
+def slab_rows(slab_at, span):
+    return pl.ds(pl.multiple_of(slab_at * span, span), span)
+
+
+def plane_product(groups_x, span, high_buf, low_buf, plane, slabs):
+    width = plane.shape[1]
+
+    def around(buf, shift):
+        parts = [
+            buf[slab_rows(lax.rem(at + shift + groups_x, groups_x), span), :] for at in slabs
+        ]
+        return jnp.concatenate(parts, axis=0)
+
+    high = [around(high_buf, shift) for shift in (-1, 0, 1)]
+    low = [around(low_buf, shift) for shift in (-1, 0, 1)]
+    left = jnp.concatenate(high + low + high, axis=1)
+    right = jnp.concatenate([plane[: 3 * width], plane[: 3 * width], plane[3 * width :]], axis=0)
+    return mxu(left, right)
+
+
+def depth_product(span, high_buf, low_buf, depth, slab_at):
+    high = high_buf[slab_rows(slab_at, span), :]
+    low = low_buf[slab_rows(slab_at, span), :]
+    return mxu(depth[...], jnp.concatenate([high, high, low], axis=0))
+
+
+def chunk_of(groups_x):
+    return 2 if groups_x % 2 == 0 else 1
+
+
+def block_rows(groups_z, pair, parity, depth_at):
+    return pl.ds(pl.multiple_of(((2 * pair + parity) * groups_z + depth_at) * HALF, HALF), HALF)
+
+
+def first_kernel(groups, *refs):
+    field_in, plane_in, depth_in, field, near = refs[:5]
+    raw, high_buf, low_buf, plane, depth, sems = refs[5:]
+    groups_x, groups_y, groups_z = groups
+    span = groups_z * LANE
+    pairs_slab = groups_y // 2
+    loads = [
+        pltpu.make_async_copy(source, target, sems.at[number])
+        for number, (source, target) in enumerate(
+            ((field_in, raw), (plane_in, plane), (depth_in, depth))
+        )
+    ]
+    for load in loads:
+        load.start()
+    loads[0].wait()
+
+    def lay_field(slab_at, carry):
+        for tile in range(pairs_slab):
+            pair = slab_at * pairs_slab + tile
+            cols = slice(tile * LANE, (tile + 1) * LANE)
+            for depth_at in range(groups_z):
+                first = raw[block_rows(groups_z, pair, 0, depth_at), :]
+                second = raw[block_rows(groups_z, pair, 1, depth_at), :]
+                turned = jnp.concatenate([first, second], axis=0).T
+                at = pl.multiple_of(pair * span + depth_at * LANE, LANE)
+                field[pl.ds(at, LANE), :] = turned
+                at = pl.multiple_of(slab_at * span + depth_at * LANE, LANE)
+                split_store(high_buf, low_buf, pl.ds(at, LANE), cols, turned)
+        return carry
+
+    lax.fori_loop(0, groups_x, lay_field, 0)
+    for load in loads[1:]:
+        load.wait()
+    chunk = chunk_of(groups_x)
+
+    def product(chunk_at, carry):
+        slabs = [chunk_at * chunk + number for number in range(chunk)]
+        total = plane_product(groups_x, span, high_buf, low_buf, plane, slabs)
+        near[slab_rows(chunk_at, chunk * span), :] = total
+        for slab_at in slabs:
+            rows = slab_rows(slab_at, span)
+            near[rows, :] += depth_product(span, high_buf, low_buf, depth, slab_at)
+        return carry
+
+    lax.fori_loop(0, groups_x // chunk, product, 0)
 
 
 def filter_kernel(groups, atoms, place, half, my_place, *refs):
     groups_x, groups_y, groups_z = groups
     pieces = groups_y * groups_z
-    field_in = refs[0]
-    packs_in = refs[1 : 1 + pieces]
-    coupling_in, plane_in, depth_in, out = refs[1 + pieces : 5 + pieces]
+    field_a, near_a = refs[:2]
+    packs_in = refs[2 : 2 + pieces]
+    coupling_in, plane_in, depth_in, out = refs[2 + pieces : 6 + pieces]
     (
-        field_a,
         field_b,
         field_c,
+        turned_out,
         local,
         added,
         coeffs,
@@ -259,13 +348,14 @@
         in_sems,
         pack_sems,
         out_sems,
-    ) = refs[5 + pieces :]
+    ) = refs[6 + pieces :]
     columns = groups_x * groups_y
     domains = columns * groups_z
     pairs = columns // 2
     span = groups_z * LANE
-    slab = groups_y * HALF
+    pairs_slab = groups_y // 2
     per_device = atoms // domains // SUB
+    chunk = chunk_of(groups_x)
     half_width = (UPPER - CUTOFF) / 2.0
     middle = (UPPER + CUTOFF) / 2.0
     diagonal = -0.5 * 3.0 * STENCIL[0] / (SPACING * SPACING) - middle
@@ -277,11 +367,9 @@
     loads = [
         pltpu.make_async_copy(source, target, in_sems.at[number])
         for number, (source, target) in enumerate(
-            ((field_in, field_b), (plane_in, plane), (depth_in, depth), (coupling_in, coupling))
+            ((coupling_in, coupling), (plane_in, plane), (depth_in, depth))
         )
     ]
-    for load in loads:
-        load.start()
     pack_loads = []
     for hop_z in range(groups_z):
         for hop_y in range(groups_y):
@@ -297,35 +385,10 @@
                         source.at[hop_x], packs.at[device], pack_sems.at[number]
                     )
                 )
-    for load in pack_loads:
+    for load in pack_loads + loads:
         load.start()
-    loads[0].wait()
-
-    def split_rows(source, pair, first_row, rows):
-        cols = pl.ds(pl.multiple_of(pair * LANE, LANE), LANE)
-        for at_row in range(first_row, first_row + rows, 2 * SUB):
-            at = pl.multiple_of(pair * span + at_row, 2 * SUB)
-            high, low = split_pair(source[pl.ds(at, 2 * SUB), :])
-            high_buf[at_row : at_row + 2 * SUB, cols] = high
-            low_buf[at_row : at_row + 2 * SUB, cols] = low
-
-    def block_rows(pair, parity, depth_at):
-        return pl.multiple_of(((2 * pair + parity) * groups_z + depth_at) * HALF, HALF)
-
-    def lay_field(pair, carry):
-        for depth_at in range(groups_z):
-            first = field_b[pl.ds(block_rows(pair, 0, depth_at), HALF), :]
-            second = field_b[pl.ds(block_rows(pair, 1, depth_at), HALF), :]
-            at = pl.multiple_of(pair * span + depth_at * LANE, LANE)
-            field_a[pl.ds(at, LANE), :] = jnp.concatenate([first, second], axis=0).T
-            for spare in range(SPARES):
-                added[spare, pl.ds(at, LANE), :] = jnp.zeros((LANE, LANE), f32)
-        split_rows(field_a, pair, 0, span)
-        return carry
-
-    lax.fori_loop(0, pairs, lay_field, 0)
-
-    for load in loads[1:] + pack_loads:
+    added[...] = jnp.zeros(added.shape, f32)
+    for load in pack_loads + loads:
         load.wait()
 
     def lay_potential(pair, carry):
@@ -360,41 +423,37 @@
             for inner in range(per_device):
                 yield device, inner
 
-    def apply_step(cur, prev, new, alpha, beta, spill):
-        last = spill is not None
-
-        def product(slab_at, carry):
-            def around(buf, shift):
-                other = lax.rem(slab_at + shift + groups_x, groups_x)
-                return buf[:, pl.ds(pl.multiple_of(other * slab, slab), slab)]
-
-            high = [around(high_buf, shift) for shift in (-1, 0, 1)]
-            low = [around(low_buf, shift) for shift in (-1, 0, 1)]
-            left = jnp.concatenate(high + low + high + [depth[...]], axis=1)
-            right = jnp.concatenate([plane[...], high[1], high[1], low[1]], axis=0)
-            near[:, pl.ds(pl.multiple_of(slab_at * slab, slab), slab)] = mxu(left, right)
-
-            for device, inner in slab_groups(slab_at):
-                group = device * per_device + inner
-                terms = ([], [])
-                for j in range(SUB):
-                    atom = group * SUB + j
-                    value = cur[pl.ds(place[atom], SUB), :]
-                    both = jnp.where(side == half[atom], value, pltpu.roll(value, HALF, 1))
+    def apply_step(cur, prev, new, alpha, beta, first, last):
+        def project(chunk_at, carry):
+            slabs = [chunk_at * chunk + number for number in range(chunk)]
+            if not first:
+                total = plane_product(groups_x, span, high_buf, low_buf, plane, slabs)
+                near[slab_rows(chunk_at, chunk * span), :] = total
+            for slab_at in slabs:
+                for device, inner in slab_groups(slab_at):
+                    group = device * per_device + inner
+                    terms = ([], [])
+                    for j in range(SUB):
+                        atom = group * SUB + j
+                        value = cur[pl.ds(place[atom], SUB), :]
+                        both = jnp.where(side == half[atom], value, pltpu.roll(value, HALF, 1))
+                        for kp in range(2):
+                            at = SUB + (inner * 2 + kp) * SUB + j
+                            terms[kp].append(both * packs[device, at])
                     for kp in range(2):
-                        at = SUB + (inner * 2 + kp) * SUB + j
-                        terms[kp].append(both * packs[device, at])
-                for kp in range(2):
-                    at = pl.multiple_of((group * 2 + kp) * SUB, SUB)
-                    coeffs[pl.ds(at, SUB), :] = row_sums(terms[kp])
+                        at = pl.multiple_of((group * 2 + kp) * SUB, SUB)
+                        coeffs[pl.ds(at, SUB), :] = row_sums(terms[kp])
             return carry
 
-        lax.fori_loop(0, groups_x, product, 0)
+        lax.fori_loop(0, groups_x // chunk, project, 0)
 
         high, low = split_pair(coeffs[...])
         coeffs[...] = (mxu(high, ones) + mxu(low, ones)) * coupling[...]
 
         def scatter(slab_at, carry):
+            if not first:
+                rows = slab_rows(slab_at, span)
+                near[rows, :] += depth_product(span, high_buf, low_buf, depth, slab_at)
             for device, inner in slab_groups(slab_at):
                 group = device * per_device + inner
                 for j in range(SUB):
@@ -412,57 +471,63 @@
 
         lax.fori_loop(0, groups_x, scatter, 0)
 
-        def combine(pair, carry):
-            for at_row in range(0, span, SUB):
-                at = pl.multiple_of(pair * span + at_row, SUB)
-                rows = pl.ds(at, SUB)
-                cols = pl.ds(pl.multiple_of(pair * LANE, LANE), LANE)
-                total = near[at_row : at_row + SUB, cols] + local[rows, :] * cur[rows, :]
-                for spare in range(SPARES):
-                    total = total + added[spare, rows, :]
+        kinetic = near_a if first else near
+
+        def combine(slab_at, carry):
+            for tile in range(pairs_slab):
+                pair = slab_at * pairs_slab + tile
+                cols = slice(tile * LANE, (tile + 1) * LANE)
+                for at_row in range(0, span, TALL):
+                    rows = pl.ds(pl.multiple_of(pair * span + at_row, TALL), TALL)
+                    slab_at_row = pl.ds(pl.multiple_of(slab_at * span + at_row, TALL), TALL)
+                    total = kinetic[slab_at_row, cols] + local[rows, :] * cur[rows, :]
+                    for spare in range(SPARES):
+                        total = total + added[spare, rows, :]
+                        if not last:
+                            added[spare, rows, :] = jnp.zeros((TALL, LANE), f32)
+                    total = total * alpha
+                    if beta is not None:
+                        total = total + beta * prev[rows, :]
+                    new[rows, :] = total
                     if not last:
-                        added[spare, rows, :] = jnp.zeros((SUB, LANE), f32)
-                total = total * alpha
-                if beta is not None:
-                    total = total + beta * prev[rows, :]
-                new[rows, :] = total
-            if not last:
-                split_rows(new, pair, 0, span)
-            else:
-                for depth_at in range(groups_z):
-                    at = pl.multiple_of(pair * span + depth_at * LANE, LANE)
-                    turned = new[pl.ds(at, LANE), :].T
-                    spill[pl.ds(block_rows(pair, 0, depth_at), HALF), :] = turned[:HALF]
-                    spill[pl.ds(block_rows(pair, 1, depth_at), HALF), :] = turned[HALF:]
-                rows = pl.ds(pl.multiple_of(pair * span, span), span)
-                pltpu.make_async_copy(spill.at[rows], out.at[rows], out_sems.at[pair]).start()
+                        split_store(high_buf, low_buf, slab_at_row, cols, total)
+                if last:
+                    for depth_at in range(groups_z):
+                        at = pl.multiple_of(pair * span + depth_at * LANE, LANE)
+                        turned = new[pl.ds(at, LANE), :].T
+                        turned_out[block_rows(groups_z, pair, 0, depth_at), :] = turned[:HALF]
+                        turned_out[block_rows(groups_z, pair, 1, depth_at), :] = turned[HALF:]
+                    rows = pl.ds(pl.multiple_of(pair * span, span), span)
+                    pltpu.make_async_copy(
+                        turned_out.at[rows], out.at[rows], out_sems.at[pair]
+                    ).start()
             return carry
 
-        lax.fori_loop(0, pairs, combine, 0)
+        lax.fori_loop(0, groups_x, combine, 0)
 
     sigma_one = half_width / (LOW_EDGE - middle)
     sigma_now = sigma_one
-    apply_step(field_a, None, field_b, sigma_one / half_width, None, None)
+    apply_step(field_a, None, field_b, sigma_one / half_width, None, True, DEGREE == 1)
     prev, cur, new = field_a, field_b, field_c
     for degree_step in range(1, DEGREE):
         sigma_next = 1.0 / (2.0 / sigma_one - sigma_now)
         last = degree_step == DEGREE - 1
         target = prev if degree_step > 1 else new
-        spare = new if degree_step > 1 else prev
         apply_step(
             cur,
             prev,
             target,
             2.0 * sigma_next / half_width,
             -sigma_now * sigma_next,
-            spare if last else None,
-        )
-        prev, cur, new = cur, target, spare
+            False,
+            last,
+        )
+        prev, cur = cur, target
         sigma_now = sigma_next
 
     def finish(pair, carry):
         rows = pl.ds(pl.multiple_of(pair * span, span), span)
-        pltpu.make_async_copy(prev.at[rows], out.at[rows], out_sems.at[pair]).wait()
+        pltpu.make_async_copy(turned_out.at[rows], out.at[rows], out_sems.at[pair]).wait()
         return carry
 
     lax.fori_loop(0, pairs, finish, 0)
@@ -499,44 +564,82 @@
     return place, column % 2
 
 
-def filter_call(groups, place, half, my_place, field, packs, coupling, interpret=False):
+def weights_of(groups):
+    return jnp.asarray(plane_weights(groups[1])), jnp.asarray(depth_weights(groups[2]))
+
+
+def first_call(groups, field, interpret=False):
+    groups_x, groups_y, groups_z = groups
+    span = groups_z * LANE
+    cells = (groups_x * groups_y // 2 * span, LANE)
+    slabs = (groups_x * span, groups_y * HALF)
+    plane, depth = weights_of(groups)
+    vmem = pl.BlockSpec(memory_space=pltpu.VMEM)
+    anywhere = pl.BlockSpec(memory_space=pl.ANY)
+    work = 2 * slabs[0] * slabs[1] * (9 * slabs[1] + 3 * span)
+    return pl.pallas_call(
+        functools.partial(first_kernel, groups),
+        out_shape=[
+            jax.ShapeDtypeStruct(cells, jnp.float32),
+            jax.ShapeDtypeStruct(slabs, jnp.float32),
+        ],
+        in_specs=[anywhere] * 3,
+        out_specs=[vmem] * 2,
+        scratch_shapes=[
+            pltpu.VMEM(cells, jnp.float32),
+            pltpu.VMEM(slabs, jnp.bfloat16),
+            pltpu.VMEM(slabs, jnp.bfloat16),
+            pltpu.VMEM(plane.shape, plane.dtype),
+            pltpu.VMEM(depth.shape, depth.dtype),
+            pltpu.SemaphoreType.DMA((3,)),
+        ],
+        compiler_params=pltpu.CompilerParams(vmem_limit_bytes=16 * 1024 * 1024),
+        cost_estimate=pl.CostEstimate(
+            flops=work, bytes_accessed=4 * field.size * 4, transcendentals=0
+        ),
+        interpret=interpret,
+    )(field.reshape(cells), plane, depth)
+
+
+def filter_call(groups, place, half, my_place, field, near, packs, coupling, interpret=False):
     groups_x, groups_y, groups_z = groups
     columns = groups_x * groups_y
     atoms = place.shape[0]
-    span = groups_z * LANE
-    width = columns * HALF
-    cells = (columns // 2 * span, LANE)
-    plane = jnp.asarray(plane_weights(groups_y))
-    depth = jnp.asarray(depth_weights(groups_z))
+    plane, depth = weights_of(groups)
+    vmem = pl.BlockSpec(memory_space=pltpu.VMEM)
     anywhere = pl.BlockSpec(memory_space=pl.ANY)
     smem = pl.BlockSpec(memory_space=pltpu.SMEM)
+    work = 2 * near.shape[0] * near.shape[1] * (9 * near.shape[1] + 3 * groups_z * LANE)
     out = pl.pallas_call(
         functools.partial(filter_kernel, groups, atoms),
-        out_shape=jax.ShapeDtypeStruct(cells, jnp.float32),
-        in_specs=[smem] * 3 + [anywhere] * (len(packs) + 4),
+        out_shape=jax.ShapeDtypeStruct(field.shape, jnp.float32),
+        in_specs=[smem] * 3 + [vmem] * 2 + [anywhere] * (len(packs) + 3),
         out_specs=anywhere,
         scratch_shapes=[
-            pltpu.VMEM(cells, jnp.float32),
-            pltpu.VMEM(cells, jnp.float32),
-            pltpu.VMEM(cells, jnp.float32),
-            pltpu.VMEM(cells, jnp.float32),
-            pltpu.VMEM((SPARES,) + cells, jnp.float32),
+            pltpu.VMEM(field.shape, jnp.float32),
+            pltpu.VMEM(field.shape, jnp.float32),
+            pltpu.VMEM(field.shape, jnp.float32),
+            pltpu.VMEM(field.shape, jnp.float32),
+            pltpu.VMEM((SPARES,) + field.shape, jnp.float32),
             pltpu.VMEM((atoms * 2, LANE), jnp.float32),
-            pltpu.VMEM((span, width), jnp.bfloat16),
-            pltpu.VMEM((span, width), jnp.bfloat16),
-            pltpu.VMEM((span, width), jnp.float32),
+            pltpu.VMEM(near.shape, jnp.bfloat16),
+            pltpu.VMEM(near.shape, jnp.bfloat16),
+            pltpu.VMEM(near.shape, jnp.float32),
             pltpu.VMEM((columns * groups_z,) + packs[0].shape[1:], jnp.float32),
             pltpu.VMEM(coupling.shape, jnp.float32),
             pltpu.VMEM(plane.shape, plane.dtype),
             pltpu.VMEM(depth.shape, depth.dtype),
-            pltpu.SemaphoreType.DMA((4,)),
+            pltpu.SemaphoreType.DMA((3,)),
             pltpu.SemaphoreType.DMA((columns * groups_z,)),
             pltpu.SemaphoreType.DMA((columns // 2,)),
         ],
-        compiler_params=pltpu.CompilerParams(vmem_limit_bytes=48 * 1024 * 1024),
+        compiler_params=pltpu.CompilerParams(vmem_limit_bytes=20 * 1024 * 1024),
+        cost_estimate=pl.CostEstimate(
+            flops=3 * work, bytes_accessed=8 * field.size * 4, transcendentals=0
+        ),
         interpret=interpret,
-    )(place, half, my_place, field.reshape(cells), *packs, coupling, plane, depth)
-    return out.reshape(field.shape)
+    )(place, half, my_place, field, near, *packs, coupling, plane, depth)
+    return out.reshape(columns * groups_z, SUB, SUB, LANE)
 
 
 def hops(value, axis):
@@ -558,13 +661,14 @@
     extent = lax.dynamic_slice(box_extent, (me * atoms_own,), (atoms_own,))
     pack = packed_inputs(potential, projectors, extent)
     line = jnp.stack(hops(pack, "gx"))
-    plane = hops(line, "gy")
-    crossed = [hops(piece, "gz") for piece in plane]
+    orbitals, line = lax.optimization_barrier((orbitals, line))
+    crossed = [hops(piece, "gz") for piece in hops(line, "gy")]
     packs = [crossed[hop_y][hop_z] for hop_z in range(groups_z) for hop_y in range(groups[1])]
     field = lax.all_to_all(orbitals, axes, split_axis=0, concat_axis=0, tiled=True)
+    field, near = first_call(groups, field)
     place, half = box_places(groups, owner_rank, box_anchor[2])
     result = filter_call(
-        groups, place, half, my_place, field, packs, packed_coupling(coupling)
+        groups, place, half, my_place, field, near, packs, packed_coupling(coupling)
     )
     filtered = lax.all_to_all(result, axes, split_axis=0, concat_axis=0, tiled=True)
     states = filtered.shape[0]

time: 143 us -> 133 us (0.930)
  waiting for transfers between devices: 41.5 us -> 32.1 us
  blocking collectives: 39.5 us -> 43 us
  local copies, waits for them, and re-layouts: 14.8 us -> 11.7 us
  Pallas kernels: 27.8 us -> 25.9 us
  starting transfers between devices: 16.1 us -> 17.7 us
    ppermute x10, waiting for transfers between devices: 41.5 us -> 32.1 us  [hops(): lax.ppermute(value, axis, [(i, (i + hop) % count) for i in range(count)])]
    pallas_call x1, Pallas kernels: 27.8 us -> 23 us  [filter_call(): pl.pallas_call(functools.partial(filter_kernel, groups, atoms), out_shape...]
    all_to_all x1, blocking collectives: 28 us -> 31.3 us  [state_body(): lax.all_to_all(result, axes, split_axis=0, concat_axis=0, tiled=True)]
    unnamed x30 -> x20, local copies, waits for them, and re-layouts: 7.99 us -> 4.92 us
    ppermute x10, starting transfers between devices: 8.83 us -> 11.9 us  [hops(): lax.ppermute(value, axis, [(i, (i + hop) % count) for i in range(count)])]
    pallas_call x0 -> x1, Pallas kernels: none -> 2.92 us  [first_call(): pl.pallas_call(functools.partial(first_kernel, groups), out_shape=[jax.Sh...]
    all_to_all x1, starting transfers between devices: 7.3 us -> 5.85 us  [state_body(): lax.all_to_all(orbitals, axes, split_axis=0, concat_axis=0, tiled=True)]
  transfers between devices with their start and end apart: 11 -> 11, of which waited for: 4 -> 5; matrix products, arithmetic and copies ran while one was open for 4% -> 3% of each run, Pallas kernels for 0% -> 2%
where the time goes in v6:
time: 133 us
  blocking collectives  43 us (32%)
  waiting for transfers between devices  32.1 us (24%)
  Pallas kernels  25.9 us (19%)
  starting transfers between devices  17.7 us (13%)
  local copies, waits for them, and re-layouts  11.7 us (9%)
    ppermute x10, waiting for transfers between devices, hops(): lax.ppermute(value, axis, [(i, (i + hop) % count) for i in range(count)])  32.1 us
    all_to_all x1, blocking collectives, state_body(): lax.all_to_all(result, axes, split_axis=0, concat_axis=0, tiled=True)  31.3 us
    pallas_call x1, Pallas kernels, filter_call(): pl.pallas_call(functools.partial(filter_kernel, groups, atoms), out_shape...  23 us
    ppermute x10, starting transfers between devices, hops(): lax.ppermute(value, axis, [(i, (i + hop) % count) for i in range(count)])  11.9 us
    all_to_all x1, blocking collectives, state_body(): lax.all_to_all(jnp.broadcast_to(quarter[None], (domains,) + quarter.shape...  11.7 us
    all_to_all x1, starting transfers between devices, state_body(): lax.all_to_all(orbitals, axes, split_axis=0, concat_axis=0, tiled=True)  5.85 us
    unnamed x20, local copies, waits for them, and re-layouts  4.92 us
    pallas_call x1, Pallas kernels, first_call(): pl.pallas_call(functools.partial(first_kernel, groups), out_shape=[jax.Sh...  2.92 us
  transfers between devices with their start and end apart: 11, of which 5 were waited for; matrix products, arithmetic and copies ran while one was open for 3% of the time, Pallas kernels for 2%

profile of v6, /device:TPU:0, one launch (start us, length us, event | category | flops | bytes accessed | tf_op | source)
XLA Modules:
  0.0 132.8 jit_solution(9457520682984051938)
XLA Ops:
  0.6 0.0 copy-start.8
  0.7 0.7 copy-done.8
  1.3 0.1 dynamic_slice.3
  1.4 0.1 iota_compare_fusion
  1.5 0.1 broadcast_and_fusion.1
  1.6 0.0 copy-start.4
  1.6 0.1 broadcast_and_fusion
  1.7 0.2 and.69
  1.9 0.5 copy-done.4
  2.5 0.6 reshape.133
  3.0 0.3 copy.29
  3.4 0.0 copy-start.5
  3.4 0.1 reshape.134
  3.5 0.6 copy-done.5
  4.1 0.1 reshape.131
  4.2 0.1 copy.27
  4.3 0.1 reshape.132
  4.5 3.1 %collective-permute-start = (f32[24,8,128]{2,1,0:T(8,128)S(1)}, f32[24,8,128]{2,1,0:T(8,128)S(1)}, u32[]{:S(2)}, u32[]{:S(2)}) collective-permute-start(f32[24,8,128]{2,1,0:T(8,128)S(1)} %constant_dynamic-update-slice_fusion), channel_id=1, source_target_pairs={{0,8},{8,16},{16,24},{24,0},{1,9},{9,17},{17,25},{25,1},{2,10},{10... | collective-permute-start | bytes 294920 | tf_op jit(solution)/shard_map/ppermute | solution.py:648
  7.5 2.6 %collective-permute-start.1 = (f32[24,8,128]{2,1,0:T(8,128)S(1)}, f32[24,8,128]{2,1,0:T(8,128)S(1)}, u32[]{:S(2)}, u32[]{:S(2)}) collective-permute-start(f32[24,8,128]{2,1,0:T(8,128)S(1)} %constant_dynamic-update-slice_fusion), channel_id=1, source_target_pairs={{0,16},{8,24},{16,0},{24,8},{1,17},{9,25},{17,1},{25,9},{2,18},{10... | collective-permute-start | bytes 294920 | tf_op jit(solution)/shard_map/ppermute | solution.py:648
  10.1 1.3 %collective-permute-start.2 = (f32[24,8,128]{2,1,0:T(8,128)S(1)}, f32[24,8,128]{2,1,0:T(8,128)S(1)}, u32[]{:S(2)}, u32[]{:S(2)}) collective-permute-start(f32[24,8,128]{2,1,0:T(8,128)S(1)} %constant_dynamic-update-slice_fusion), channel_id=1, source_target_pairs={{0,24},{8,0},{16,8},{24,16},{1,25},{9,1},{17,9},{25,17},{2,26},{10... | collective-permute-start | bytes 294920 | tf_op jit(solution)/shard_map/ppermute | solution.py:648
  11.5 1.7 %collective-permute-done = f32[24,8,128]{2,1,0:T(8,128)S(1)} collective-permute-done((f32[24,8,128]{2,1,0:T(8,128)S(1)}, f32[24,8,128]{2,1,0:T(8,128)S(1)}, u32[]{:S(2)}, u32[]{:S(2)}) %collective-permute-start) | collective-permute-done | bytes 98336 | tf_op jit(solution)/shard_map/ppermute | solution.py:648
  13.2 3.5 %collective-permute-done.1 = f32[24,8,128]{2,1,0:T(8,128)S(1)} collective-permute-done((f32[24,8,128]{2,1,0:T(8,128)S(1)}, f32[24,8,128]{2,1,0:T(8,128)S(1)}, u32[]{:S(2)}, u32[]{:S(2)}) %collective-permute-start.1) | collective-permute-done | bytes 98336 | tf_op jit(solution)/shard_map/ppermute | solution.py:648
  16.7 0.0 collective-permute-done.2
  16.8 0.0 copy-start.7
  16.8 5.8 %all-to-all-start = ((f32[32,8,8,128]{3,2,1,0:T(8,128)}), f32[32,8,8,128]{3,2,1,0:T(8,128)S(1)}, u32[]{:S(2)}, u32[]{:S(2)}) async-start(f32[32,8,8,128]{3,2,1,0:T(8,128)} %param.11), calls=%async_computation | async-start | bytes 2097152 | tf_op jit(solution)/shard_map/all_to_all | solution.py:667
  22.7 1.8 %collective-permute-start.3 = (f32[4,24,8,128]{3,2,1,0:T(8,128)S(1)}, f32[4,24,8,128]{3,2,1,0:T(8,128)S(1)}, u32[]{:S(2)}, u32[]{:S(2)}) collective-permute-start(f32[4,24,8,128]{3,2,1,0:T(8,128)S(1)} %pad_maximum_fusion.refs_2_), channel_id=1, source_target_pairs={{0,2},{2,4},{4,6},{6,0},{1,3},{3,5},{5,7},{7,1},{8,10},{10,12},{12... | collective-permute-start | bytes 1179656 | tf_op jit(solution)/shard_map/ppermute | solution.py:648
  24.5 1.5 %collective-permute-start.4 = (f32[4,24,8,128]{3,2,1,0:T(8,128)S(1)}, f32[4,24,8,128]{3,2,1,0:T(8,128)S(1)}, u32[]{:S(2)}, u32[]{:S(2)}) collective-permute-start(f32[4,24,8,128]{3,2,1,0:T(8,128)S(1)} %pad_maximum_fusion.refs_2_), channel_id=1, source_target_pairs={{0,4},{2,6},{4,0},{6,2},{1,5},{3,7},{5,1},{7,3},{8,12},{10,14},{12... | collective-permute-start | bytes 1179656 | tf_op jit(solution)/shard_map/ppermute | solution.py:648
  25.9 1.5 %collective-permute-start.5 = (f32[4,24,8,128]{3,2,1,0:T(8,128)S(1)}, f32[4,24,8,128]{3,2,1,0:T(8,128)S(1)}, u32[]{:S(2)}, u32[]{:S(2)}) collective-permute-start(f32[4,24,8,128]{3,2,1,0:T(8,128)S(1)} %pad_maximum_fusion.refs_2_), channel_id=1, source_target_pairs={{0,6},{2,0},{4,2},{6,4},{1,7},{3,1},{5,3},{7,5},{8,14},{10,8},{12,... | collective-permute-start | bytes 1179656 | tf_op jit(solution)/shard_map/ppermute | solution.py:648
  27.4 0.0 copy-done.7
  27.4 0.1 collective-permute-start.6
  27.5 18.5 %collective-permute-done.3.refs_3_ = f32[4,24,8,128]{3,2,1,0:T(8,128)S(1)} collective-permute-done((f32[4,24,8,128]{3,2,1,0:T(8,128)S(1)}, f32[4,24,8,128]{3,2,1,0:T(8,128)S(1)}, u32[]{:S(2)}, u32[]{:S(2)}) %collective-permute-start.3) | collective-permute-done | bytes 393248 | tf_op jit(solution)/shard_map/ppermute | solution.py:648
  46.0 0.0 collective-permute-start.7
  46.0 7.6 %collective-permute-done.4.refs_4_ = f32[4,24,8,128]{3,2,1,0:T(8,128)S(1)} collective-permute-done((f32[4,24,8,128]{3,2,1,0:T(8,128)S(1)}, f32[4,24,8,128]{3,2,1,0:T(8,128)S(1)}, u32[]{:S(2)}, u32[]{:S(2)}) %collective-permute-start.4) | collective-permute-done | bytes 393248 | tf_op jit(solution)/shard_map/ppermute | solution.py:648
  53.6 0.0 collective-permute-start.8
  53.7 0.7 collective-permute-done.5.refs_5_
  54.4 0.0 collective-permute-start.9
  54.4 0.1 pad_add_fusion.my_place
  54.5 0.7 slice.3
  55.2 0.0 copy-done.6
  55.2 0.1 reshape.136
  55.3 0.4 copy.30
  55.7 1.4 %broadcast_in_dim.31 = f32[32,2,8,2,64]{4,3,2,1,0:T(2,128)} broadcast(f32[32,2,8,2]{3,2,1,0:T(8,128)S(1)} %copy.30), dimensions={0,1,2,3} | broadcast | bytes 266240 | tf_op jit(solution)/shard_map/broadcast_in_dim | solution.py:556
  57.1 1.3 %reshape.137.refs_10_ = f32[512,128]{1,0:T(8,128)S(1)} reshape(f32[32,2,8,2,64]{4,3,2,1,0:T(2,128)} %broadcast_in_dim.31) | data formatting | bytes 524288 | tf_op jit(solution)/shard_map/reshape | solution.py:557
  58.5 0.0 all-to-all-done
  58.5 0.0 copy-start
  58.5 1.1 copy-done
  59.6 1.0 copy-done.2
  60.6 2.9 %shard_map.122 = (f32[2048,128]{1,0:T(8,128)S(1)}, f32[1024,256]{1,0:T(8,128)S(1)}) custom-call(f32[2048,128]{1,0:T(8,128)S(1)} %bitcast.31, bf16[1536,256]{1,0:T(8,128)(2,1)S(1)} %copy-done, bf16[256,768]{1,0:T(8,128)(2,1)S(1)} %copy-done.2), custom_call_target="tpu_custom_call" | custom-call | flops 1610612736 | bytes 4194304 | tf_op jit(solution)/shard_map/pallas_call | solution.py:580
  63.6 0.0 collective-permute-done.6.refs_6_
  63.6 0.0 collective-permute-done.7.refs_7_
  63.6 0.0 collective-permute-done.8.refs_8_
  63.6 0.0 collective-permute-done.9.refs_9_
  63.6 0.0 copy-done.1
  63.6 0.0 copy-done.3
  63.6 23.0 %shard_map.123 = f32[2048,128]{1,0:T(8,128)S(1)} custom-call(s32[256]{0:T(256)S(1)} %multiply_add_fusion.place, s32[256]{0:T(256)S(1)} %get-tuple-element.10.half, s32[3]{0:T(128)S(1)} %pad_add_fusion.my_place, f32[2048,128]{1,0:T(8,128)S(1)} %get-tuple-element.7.refs_0_, f32[1024,256]{1,0:T(8,128)S(1)} %get-tuple-element.8.refs_1_, ...), custom_call_target="tpu_custom_call" | custom-call | flops 4831838208 | bytes 8388608 | tf_op jit(solution)/shard_map/pallas_call | solution.py:613
  86.6 31.3 %all_to_all.15 = f32[32,8,8,128]{3,2,1,0:T(8,128)S(1)} all-to-all(f32[32,8,8,128]{3,2,1,0:T(8,128)S(1)} %bitcast.32), channel_id=1, replica_groups=mesh['gx'=4,'gy'=4,'gz'=2] {'gx','gy','gz'}, dimensions={0} | all-to-all | bytes 2097152 | tf_op jit(solution)/shard_map/all_to_all | solution.py:673
  117.9 0.2 dot_general.5
  118.1 0.2 reshape.140
  118.3 1.0 convolution_bitcast_fusion
  119.3 0.1 broadcast_in_dim.32
  119.4 11.7 %all_to_all.16 = f32[32,8,128]{2,1,0:T(8,128)S(1)} all-to-all(f32[32,8,128]{2,1,0:T(8,128)S(1)} %broadcast_in_dim.33), channel_id=1, replica_groups=mesh['gx'=4,'gy'=4,'gz'=2] {'gx','gy','gz'}, dimensions={0} | all-to-all | bytes 262144 | tf_op jit(solution)/shard_map/all_to_all | solution.py:678
  131.1 0.1 div.38
  131.2 0.6 copy.34
  131.8 1.0 copy.37
  (15 shorter events, 0.2 us)
Async XLA Ops:
  0.6 0.7 copy-start.8
  1.6 0.8 copy-start.4
  3.4 0.8 copy-start.5
  4.5 8.8 %collective-permute-start = (f32[24,8,128]{2,1,0:T(8,128)S(1)}, f32[24,8,128]{2,1,0:T(8,128)S(1)}, u32[]{:S(2)}, u32[]{:S(2)}) collective-permute-start(f32[24,8,128]{2,1,0:T(8,128)S(1)} %constant_dynamic-update-slice_fusion), channel_id=1, source_target_pairs={{0,8},{8,16},{16,24},{24,0},{1,9},{9,17},{17,25},{25,1},{2,10},{10... | collective-permute-start | bytes 294920 | tf_op jit(solution)/shard_map/ppermute | solution.py:648
  7.5 9.2 %collective-permute-start.1 = (f32[24,8,128]{2,1,0:T(8,128)S(1)}, f32[24,8,128]{2,1,0:T(8,128)S(1)}, u32[]{:S(2)}, u32[]{:S(2)}) collective-permute-start(f32[24,8,128]{2,1,0:T(8,128)S(1)} %constant_dynamic-update-slice_fusion), channel_id=1, source_target_pairs={{0,16},{8,24},{16,0},{24,8},{1,17},{9,25},{17,1},{25,9},{2,18},{10... | collective-permute-start | bytes 294920 | tf_op jit(solution)/shard_map/ppermute | solution.py:648
  10.1 6.6 %collective-permute-start.2 = (f32[24,8,128]{2,1,0:T(8,128)S(1)}, f32[24,8,128]{2,1,0:T(8,128)S(1)}, u32[]{:S(2)}, u32[]{:S(2)}) collective-permute-start(f32[24,8,128]{2,1,0:T(8,128)S(1)} %constant_dynamic-update-slice_fusion), channel_id=1, source_target_pairs={{0,24},{8,0},{16,8},{24,16},{1,25},{9,1},{17,9},{25,17},{2,26},{10... | collective-permute-start | bytes 294920 | tf_op jit(solution)/shard_map/ppermute | solution.py:648
  16.8 10.6 %copy-start.7 = (s32[256]{0:T(256)S(1)}, s32[256]{0:T(256)}, u32[]{:S(2)}) copy-start(s32[256]{0:T(256)} %param.14) | copy-start | bytes 3076
  16.8 41.7 %all-to-all-start = ((f32[32,8,8,128]{3,2,1,0:T(8,128)}), f32[32,8,8,128]{3,2,1,0:T(8,128)S(1)}, u32[]{:S(2)}, u32[]{:S(2)}) async-start(f32[32,8,8,128]{3,2,1,0:T(8,128)} %param.11), calls=%async_computation | async-start | bytes 2097152 | tf_op jit(solution)/shard_map/all_to_all | solution.py:667
  22.7 23.3 %collective-permute-start.3 = (f32[4,24,8,128]{3,2,1,0:T(8,128)S(1)}, f32[4,24,8,128]{3,2,1,0:T(8,128)S(1)}, u32[]{:S(2)}, u32[]{:S(2)}) collective-permute-start(f32[4,24,8,128]{3,2,1,0:T(8,128)S(1)} %pad_maximum_fusion.refs_2_), channel_id=1, source_target_pairs={{0,2},{2,4},{4,6},{6,0},{1,3},{3,5},{5,7},{7,1},{8,10},{10,12},{12... | collective-permute-start | bytes 1179656 | tf_op jit(solution)/shard_map/ppermute | solution.py:648
  24.5 29.1 %collective-permute-start.4 = (f32[4,24,8,128]{3,2,1,0:T(8,128)S(1)}, f32[4,24,8,128]{3,2,1,0:T(8,128)S(1)}, u32[]{:S(2)}, u32[]{:S(2)}) collective-permute-start(f32[4,24,8,128]{3,2,1,0:T(8,128)S(1)} %pad_maximum_fusion.refs_2_), channel_id=1, source_target_pairs={{0,4},{2,6},{4,0},{6,2},{1,5},{3,7},{5,1},{7,3},{8,12},{10,14},{12... | collective-permute-start | bytes 1179656 | tf_op jit(solution)/shard_map/ppermute | solution.py:648
  25.9 28.5 %collective-permute-start.5 = (f32[4,24,8,128]{3,2,1,0:T(8,128)S(1)}, f32[4,24,8,128]{3,2,1,0:T(8,128)S(1)}, u32[]{:S(2)}, u32[]{:S(2)}) collective-permute-start(f32[4,24,8,128]{3,2,1,0:T(8,128)S(1)} %pad_maximum_fusion.refs_2_), channel_id=1, source_target_pairs={{0,6},{2,0},{4,2},{6,4},{1,7},{3,1},{5,3},{7,5},{8,14},{10,8},{12,... | collective-permute-start | bytes 1179656 | tf_op jit(solution)/shard_map/ppermute | solution.py:648
  27.4 36.1 %collective-permute-start.6 = (f32[4,24,8,128]{3,2,1,0:T(8,128)S(1)}, f32[4,24,8,128]{3,2,1,0:T(8,128)S(1)}, u32[]{:S(2)}, u32[]{:S(2)}) collective-permute-start(f32[4,24,8,128]{3,2,1,0:T(8,128)S(1)} %pad_maximum_fusion.refs_2_), channel_id=1, source_target_pairs={{0,1},{1,0},{2,3},{3,2},{4,5},{5,4},{6,7},{7,6},{8,9},{9,8},{10,11... | collective-permute-start | bytes 1179656 | tf_op jit(solution)/shard_map/ppermute | solution.py:648
  46.0 17.6 %collective-permute-start.7 = (f32[4,24,8,128]{3,2,1,0:T(8,128)S(1)}, f32[4,24,8,128]{3,2,1,0:T(8,128)}, u32[]{:S(2)}, u32[]{:S(2)}) collective-permute-start(f32[4,24,8,128]{3,2,1,0:T(8,128)S(1)} %collective-permute-done.3.refs_3_), channel_id=1, source_target_pairs={{0,1},{1,0},{2,3},{3,2},{4,5},{5,4},{6,7},{7,6},{8,9},{9,8},{10,11... | collective-permute-start | bytes 1179656 | tf_op jit(solution)/shard_map/ppermute | solution.py:648
  53.6 10.0 %collective-permute-start.8 = (f32[4,24,8,128]{3,2,1,0:T(8,128)S(1)}, f32[4,24,8,128]{3,2,1,0:T(8,128)}, u32[]{:S(2)}, u32[]{:S(2)}) collective-permute-start(f32[4,24,8,128]{3,2,1,0:T(8,128)S(1)} %collective-permute-done.4.refs_4_), channel_id=1, source_target_pairs={{0,1},{1,0},{2,3},{3,2},{4,5},{5,4},{6,7},{7,6},{8,9},{9,8},{10,11... | collective-permute-start | bytes 1179656 | tf_op jit(solution)/shard_map/ppermute | solution.py:648
  54.4 9.2 %collective-permute-start.9 = (f32[4,24,8,128]{3,2,1,0:T(8,128)S(1)}, f32[4,24,8,128]{3,2,1,0:T(8,128)}, u32[]{:S(2)}, u32[]{:S(2)}) collective-permute-start(f32[4,24,8,128]{3,2,1,0:T(8,128)S(1)} %collective-permute-done.5.refs_5_), channel_id=1, source_target_pairs={{0,1},{1,0},{2,3},{3,2},{4,5},{5,4},{6,7},{7,6},{8,9},{9,8},{10,11... | collective-permute-start | bytes 1179656 | tf_op jit(solution)/shard_map/ppermute | solution.py:648
  54.4 0.8 copy-start.6
  58.5 1.1 copy-start
  59.6 1.0 copy-start.2
  60.6 3.0 %copy-start.1 = (bf16[1536,256]{1,0:T(8,128)(2,1)S(1)}, bf16[1536,256]{1,0:T(8,128)(2,1)}, u32[]{:S(2)}) copy-start(bf16[1536,256]{1,0:T(8,128)(2,1)} %constant.68.clone.refs_1_.refs_11_) | copy-start | bytes 2359300
  60.6 3.0 %copy-start.3 = (bf16[256,768]{1,0:T(8,128)(2,1)S(1)}, bf16[256,768]{1,0:T(8,128)(2,1)}, u32[]{:S(2)}) copy-start(bf16[256,768]{1,0:T(8,128)(2,1)} %constant.69.clone.refs_2_.refs_12_) | copy-start | bytes 1179652

commit v7 on v6

--- a/solution.py
+++ b/solution.py
@@ -234,7 +234,7 @@
     return values[0]
 
 
-SPARES = 2
+SPARES = 3
 TALL = 2 * SUB
 
 
@@ -268,6 +268,19 @@
     high = high_buf[slab_rows(slab_at, span), :]
     low = low_buf[slab_rows(slab_at, span), :]
     return mxu(depth[...], jnp.concatenate([high, high, low], axis=0))
+
+
+def lay_products(groups, high_buf, low_buf, plane, depth, slabs, near):
+    groups_x, groups_y, groups_z = groups
+    span = groups_z * LANE
+    pairs_slab = groups_y // 2
+    total = plane_product(groups_x, span, high_buf, low_buf, plane, slabs)
+    for number, slab_at in enumerate(slabs):
+        deep = depth_product(span, high_buf, low_buf, depth, slab_at)
+        part = total[number * span : (number + 1) * span] + deep
+        for tile in range(pairs_slab):
+            cols = part[:, tile * LANE : (tile + 1) * LANE]
+            near[slab_rows(slab_at * pairs_slab + tile, span), :] = cols
 
 
 def chunk_of(groups_x):
@@ -315,11 +328,7 @@
 
     def product(chunk_at, carry):
         slabs = [chunk_at * chunk + number for number in range(chunk)]
-        total = plane_product(groups_x, span, high_buf, low_buf, plane, slabs)
-        near[slab_rows(chunk_at, chunk * span), :] = total
-        for slab_at in slabs:
-            rows = slab_rows(slab_at, span)
-            near[rows, :] += depth_product(span, high_buf, low_buf, depth, slab_at)
+        lay_products(groups, high_buf, low_buf, plane, depth, slabs, near)
         return carry
 
     lax.fori_loop(0, groups_x // chunk, product, 0)
@@ -330,25 +339,25 @@
     pieces = groups_y * groups_z
     field_a, near_a = refs[:2]
     packs_in = refs[2 : 2 + pieces]
-    coupling_in, plane_in, depth_in, out = refs[2 + pieces : 6 + pieces]
+    plane_in, depth_in, out = refs[2 + pieces : 5 + pieces]
     (
         field_b,
         field_c,
         turned_out,
         local,
-        added,
         coeffs,
         high_buf,
         low_buf,
         near,
         packs,
-        coupling,
         plane,
         depth,
         in_sems,
         pack_sems,
         out_sems,
-    ) = refs[6 + pieces :]
+    ) = refs[5 + pieces : 5 + pieces + 14]
+    spares = refs[5 + pieces + 14 :]
+    targets = (near,) + tuple(spares)
     columns = groups_x * groups_y
     domains = columns * groups_z
     pairs = columns // 2
@@ -367,7 +376,7 @@
     loads = [
         pltpu.make_async_copy(source, target, in_sems.at[number])
         for number, (source, target) in enumerate(
-            ((coupling_in, coupling), (plane_in, plane), (depth_in, depth))
+            ((near_a, near), (plane_in, plane), (depth_in, depth))
         )
     ]
     pack_loads = []
@@ -387,7 +396,8 @@
                 )
     for load in pack_loads + loads:
         load.start()
-    added[...] = jnp.zeros(added.shape, f32)
+    for spare in spares:
+        spare[...] = jnp.zeros(spare.shape, f32)
     for load in pack_loads + loads:
         load.wait()
 
@@ -427,8 +437,7 @@
         def project(chunk_at, carry):
             slabs = [chunk_at * chunk + number for number in range(chunk)]
             if not first:
-                total = plane_product(groups_x, span, high_buf, low_buf, plane, slabs)
-                near[slab_rows(chunk_at, chunk * span), :] = total
+                lay_products(groups, high_buf, low_buf, plane, depth, slabs, near)
             for slab_at in slabs:
                 for device, inner in slab_groups(slab_at):
                     group = device * per_device + inner
@@ -448,30 +457,31 @@
         lax.fori_loop(0, groups_x // chunk, project, 0)
 
         high, low = split_pair(coeffs[...])
-        coeffs[...] = (mxu(high, ones) + mxu(low, ones)) * coupling[...]
+        coeffs[...] = mxu(high, ones) + mxu(low, ones)
 
         def scatter(slab_at, carry):
-            if not first:
-                rows = slab_rows(slab_at, span)
-                near[rows, :] += depth_product(span, high_buf, low_buf, depth, slab_at)
             for device, inner in slab_groups(slab_at):
                 group = device * per_device + inner
+                weights = [
+                    coeffs[pl.ds(pl.multiple_of((group * 2 + kp) * SUB, SUB), SUB), :]
+                    for kp in range(2)
+                ]
                 for j in range(SUB):
                     atom = group * SUB + j
-                    value = 0.0
-                    for kp in range(2):
-                        at = SUB + (inner * 2 + kp) * SUB + j
-                        row = coeffs[pl.ds((group * 2 + kp) * SUB + j, 1), :]
-                        value = value + jnp.broadcast_to(row, (SUB, LANE)) * packs[device, at]
+                    parts = [
+                        jnp.broadcast_to(weights[kp][j : j + 1], (SUB, LANE))
+                        * packs[device, SUB + (inner * 2 + kp) * SUB + j]
+                        for kp in range(2)
+                    ]
+                    value = parts[0] + parts[1]
                     value = value + pltpu.roll(value, HALF, 1)
                     value = jnp.where(side == half[atom], value, 0.0)
                     rows = pl.ds(place[atom], SUB)
-                    added[j % SPARES, rows, :] = added[j % SPARES, rows, :] + value
+                    target = targets[j % len(targets)]
+                    target[rows, :] = target[rows, :] + value
             return carry
 
         lax.fori_loop(0, groups_x, scatter, 0)
-
-        kinetic = near_a if first else near
 
         def combine(slab_at, carry):
             for tile in range(pairs_slab):
@@ -480,11 +490,12 @@
                 for at_row in range(0, span, TALL):
                     rows = pl.ds(pl.multiple_of(pair * span + at_row, TALL), TALL)
                     slab_at_row = pl.ds(pl.multiple_of(slab_at * span + at_row, TALL), TALL)
-                    total = kinetic[slab_at_row, cols] + local[rows, :] * cur[rows, :]
-                    for spare in range(SPARES):
-                        total = total + added[spare, rows, :]
-                        if not last:
-                            added[spare, rows, :] = jnp.zeros((TALL, LANE), f32)
+                    total = local[rows, :] * cur[rows, :]
+                    for target in targets:
+                        total = total + target[rows, :]
+                    if not last:
+                        for target in targets[1:]:
+                            target[rows, :] = jnp.zeros((TALL, LANE), f32)
                     total = total * alpha
                     if beta is not None:
                         total = total + beta * prev[rows, :]
@@ -533,7 +544,7 @@
     lax.fori_loop(0, pairs, finish, 0)
 
 
-def packed_inputs(potential, projectors, extent):
+def packed_inputs(potential, projectors, extent, coupling):
     atoms = projectors.shape[0]
     cells = jnp.arange(B, dtype=jnp.int32)
     limit = extent[:, None, None, None]
@@ -543,18 +554,11 @@
         & (cells[None, None, None, :] < limit)
     )
     masked = jnp.where(
-        inside.reshape(atoms, 1, B * B * B), projectors, 0.0
+        inside.reshape(atoms, 1, B * B * B), projectors * jnp.sqrt(coupling)[:, :, None], 0.0
     ).reshape(atoms // SUB, SUB, 2, 2, B * B, B)
     masked = masked.transpose(0, 2, 1, 5, 3, 4).reshape(atoms // SUB * 2 * B, SUB, LANE)
     shaped = potential.reshape(HALF, 2, HALF).transpose(2, 1, 0).reshape(SUB, SUB, LANE)
     return jnp.concatenate([shaped, masked], axis=0)
-
-
-def packed_coupling(coupling):
-    atoms = coupling.shape[0]
-    parts = coupling.reshape(atoms // SUB, SUB, 2, 2).transpose(0, 2, 1, 3)
-    wide = jnp.broadcast_to(parts[..., None], parts.shape + (HALF,))
-    return wide.reshape(atoms * 2, LANE)
 
 
 def box_places(groups, owner, anchor):
@@ -576,14 +580,15 @@
     plane, depth = weights_of(groups)
     vmem = pl.BlockSpec(memory_space=pltpu.VMEM)
     anywhere = pl.BlockSpec(memory_space=pl.ANY)
+    in_hbm = pl.BlockSpec(memory_space=pltpu.HBM)
     work = 2 * slabs[0] * slabs[1] * (9 * slabs[1] + 3 * span)
     return pl.pallas_call(
         functools.partial(first_kernel, groups),
         out_shape=[
             jax.ShapeDtypeStruct(cells, jnp.float32),
-            jax.ShapeDtypeStruct(slabs, jnp.float32),
+            jax.ShapeDtypeStruct(cells, jnp.float32),
         ],
-        in_specs=[anywhere] * 3,
+        in_specs=[anywhere, in_hbm, in_hbm],
         out_specs=[vmem] * 2,
         scratch_shapes=[
             pltpu.VMEM(cells, jnp.float32),
@@ -601,7 +606,7 @@
     )(field.reshape(cells), plane, depth)
 
 
-def filter_call(groups, place, half, my_place, field, near, packs, coupling, interpret=False):
+def filter_call(groups, place, half, my_place, field, near, packs, interpret=False):
     groups_x, groups_y, groups_z = groups
     columns = groups_x * groups_y
     atoms = place.shape[0]
@@ -609,36 +614,37 @@
     vmem = pl.BlockSpec(memory_space=pltpu.VMEM)
     anywhere = pl.BlockSpec(memory_space=pl.ANY)
     smem = pl.BlockSpec(memory_space=pltpu.SMEM)
-    work = 2 * near.shape[0] * near.shape[1] * (9 * near.shape[1] + 3 * groups_z * LANE)
+    slabs = (groups_x * groups_z * LANE, groups_y * HALF)
+    work = 2 * slabs[0] * slabs[1] * (9 * slabs[1] + 3 * groups_z * LANE)
+    in_hbm = pl.BlockSpec(memory_space=pltpu.HBM)
     out = pl.pallas_call(
         functools.partial(filter_kernel, groups, atoms),
         out_shape=jax.ShapeDtypeStruct(field.shape, jnp.float32),
-        in_specs=[smem] * 3 + [vmem] * 2 + [anywhere] * (len(packs) + 3),
+        in_specs=[smem] * 3 + [vmem] * 2 + [anywhere] * len(packs) + [in_hbm] * 2,
         out_specs=anywhere,
         scratch_shapes=[
             pltpu.VMEM(field.shape, jnp.float32),
             pltpu.VMEM(field.shape, jnp.float32),
             pltpu.VMEM(field.shape, jnp.float32),
             pltpu.VMEM(field.shape, jnp.float32),
-            pltpu.VMEM((SPARES,) + field.shape, jnp.float32),
             pltpu.VMEM((atoms * 2, LANE), jnp.float32),
-            pltpu.VMEM(near.shape, jnp.bfloat16),
-            pltpu.VMEM(near.shape, jnp.bfloat16),
+            pltpu.VMEM(slabs, jnp.bfloat16),
+            pltpu.VMEM(slabs, jnp.bfloat16),
             pltpu.VMEM(near.shape, jnp.float32),
             pltpu.VMEM((columns * groups_z,) + packs[0].shape[1:], jnp.float32),
-            pltpu.VMEM(coupling.shape, jnp.float32),
             pltpu.VMEM(plane.shape, plane.dtype),
             pltpu.VMEM(depth.shape, depth.dtype),
             pltpu.SemaphoreType.DMA((3,)),
             pltpu.SemaphoreType.DMA((columns * groups_z,)),
             pltpu.SemaphoreType.DMA((columns // 2,)),
-        ],
-        compiler_params=pltpu.CompilerParams(vmem_limit_bytes=20 * 1024 * 1024),
+        ]
+        + [pltpu.VMEM(field.shape, jnp.float32) for _ in range(SPARES)],
+        compiler_params=pltpu.CompilerParams(vmem_limit_bytes=22 * 1024 * 1024),
         cost_estimate=pl.CostEstimate(
             flops=3 * work, bytes_accessed=8 * field.size * 4, transcendentals=0
         ),
         interpret=interpret,
-    )(place, half, my_place, field, near, *packs, coupling, plane, depth)
+    )(place, half, my_place, field, near, *packs, plane, depth)
     return out.reshape(columns * groups_z, SUB, SUB, LANE)
 
 
@@ -659,7 +665,8 @@
     my_place = jnp.stack([lax.axis_index(axis) for axis in axes])
     me = (my_place[0] * groups[1] + my_place[1]) * groups_z + my_place[2]
     extent = lax.dynamic_slice(box_extent, (me * atoms_own,), (atoms_own,))
-    pack = packed_inputs(potential, projectors, extent)
+    own = lax.dynamic_slice(coupling, (me * atoms_own, 0), (atoms_own, NPROJ))
+    pack = packed_inputs(potential, projectors, extent, own)
     line = jnp.stack(hops(pack, "gx"))
     orbitals, line = lax.optimization_barrier((orbitals, line))
     crossed = [hops(piece, "gz") for piece in hops(line, "gy")]
@@ -667,9 +674,7 @@
     field = lax.all_to_all(orbitals, axes, split_axis=0, concat_axis=0, tiled=True)
     field, near = first_call(groups, field)
     place, half = box_places(groups, owner_rank, box_anchor[2])
-    result = filter_call(
-        groups, place, half, my_place, field, near, packs, packed_coupling(coupling)
-    )
+    result = filter_call(groups, place, half, my_place, field, near, packs)
     filtered = lax.all_to_all(result, axes, split_axis=0, concat_axis=0, tiled=True)
     states = filtered.shape[0]
     flattened = filtered.reshape(states, -1)

time: 133 us -> 129 us (0.970)
  local copies, waits for them, and re-layouts: 11.7 us -> 8.58 us
  Pallas kernels: 25.9 us -> 24.2 us
    pallas_call x1, Pallas kernels: 23 us -> 21.3 us  [filter_call(): pl.pallas_call(functools.partial(filter_kernel, groups, atoms), out_shape...]
    reshape x3 -> x1, local copies, waits for them, and re-layouts: 2 us -> 0.58 us  [packed_inputs(): masked = jnp.where(inside.reshape(atoms, 1, B * B * B), projectors * jnp....]
    broadcast_in_dim x1 -> x0, local copies, waits for them, and re-layouts: 1.4 us -> none  [packed_coupling(): wide = jnp.broadcast_to(parts[..., None], parts.shape + (HALF,))]
  transfers between devices with their start and end apart: 11 -> 11, of which waited for: 5 -> 5; matrix products, arithmetic and copies ran while one was open for 3% -> 1% of each run, Pallas kernels for 2% -> 2%
where the time goes in v7:
time: 129 us; the launch traced here: 128 us
  blocking collectives  43 us (33%)
  waiting for transfers between devices  32.1 us (25%)
  Pallas kernels  24.2 us (19%)
  starting transfers between devices  17.7 us (14%)
  local copies, waits for them, and re-layouts  8.58 us (7%)
    ppermute x10, waiting for transfers between devices, hops(): lax.ppermute(value, axis, [(i, (i + hop) % count) for i in range(count)])  32.1 us
    all_to_all x1, blocking collectives, state_body(): lax.all_to_all(result, axes, split_axis=0, concat_axis=0, tiled=True)  31.3 us
    pallas_call x1, Pallas kernels, filter_call(): pl.pallas_call(functools.partial(filter_kernel, groups, atoms), out_shape...  21.3 us
    ppermute x10, starting transfers between devices, hops(): lax.ppermute(value, axis, [(i, (i + hop) % count) for i in range(count)])  11.9 us
    all_to_all x1, blocking collectives, state_body(): lax.all_to_all(jnp.broadcast_to(quarter[None], (domains,) + quarter.shape...  11.7 us
    all_to_all x1, starting transfers between devices, state_body(): lax.all_to_all(orbitals, axes, split_axis=0, concat_axis=0, tiled=True)  5.85 us
    unnamed x20, local copies, waits for them, and re-layouts  4.9 us
    pallas_call x1, Pallas kernels, first_call(): pl.pallas_call(functools.partial(first_kernel, groups), out_shape=[jax.Sh...  2.88 us
  transfers between devices with their start and end apart: 11, of which 5 were waited for; matrix products, arithmetic and copies ran while one was open for 1% of the time, Pallas kernels for 2%

profile of v7, /device:TPU:0, one launch (start us, length us, event | category | flops | bytes accessed | tf_op | source)
XLA Modules:
  0.0 128.0 jit_solution(14109457751719808371)
XLA Ops:
  0.6 0.0 copy-start.8
  0.7 0.7 copy-done.8
  1.3 0.1 dynamic_slice.6
  1.4 0.1 iota_compare_fusion
  1.5 0.1 broadcast_and_fusion.1
  1.6 0.0 copy-start.4
  1.6 0.1 broadcast_and_fusion
  1.7 0.0 copy-start.7
  1.7 0.2 and.69
  1.9 0.5 copy-done.7
  2.4 0.1 dynamic-slice_sqrt_fusion
  2.5 0.1 copy.28
  2.5 0.0 copy-done.4
  2.6 0.1 multiply_select_fusion
  2.7 0.6 reshape.127
  3.3 0.3 copy.30
  3.6 0.0 copy-start.5
  3.6 0.1 reshape.128
  3.7 0.6 copy-done.5
  4.4 0.1 reshape.125
  4.5 0.1 copy.27
  4.6 0.1 reshape.126
  4.7 3.1 %collective-permute-start = (f32[24,8,128]{2,1,0:T(8,128)S(1)}, f32[24,8,128]{2,1,0:T(8,128)S(1)}, u32[]{:S(2)}, u32[]{:S(2)}) collective-permute-start(f32[24,8,128]{2,1,0:T(8,128)S(1)} %constant_dynamic-update-slice_fusion), channel_id=1, source_target_pairs={{0,8},{8,16},{16,24},{24,0},{1,9},{9,17},{17,25},{25,1},{2,10},{10... | collective-permute-start | bytes 294920 | tf_op jit(solution)/shard_map/ppermute | solution.py:654
  7.8 2.6 %collective-permute-start.1 = (f32[24,8,128]{2,1,0:T(8,128)S(1)}, f32[24,8,128]{2,1,0:T(8,128)S(1)}, u32[]{:S(2)}, u32[]{:S(2)}) collective-permute-start(f32[24,8,128]{2,1,0:T(8,128)S(1)} %constant_dynamic-update-slice_fusion), channel_id=1, source_target_pairs={{0,16},{8,24},{16,0},{24,8},{1,17},{9,25},{17,1},{25,9},{2,18},{10... | collective-permute-start | bytes 294920 | tf_op jit(solution)/shard_map/ppermute | solution.py:654
  10.3 1.3 %collective-permute-start.2 = (f32[24,8,128]{2,1,0:T(8,128)S(1)}, f32[24,8,128]{2,1,0:T(8,128)S(1)}, u32[]{:S(2)}, u32[]{:S(2)}) collective-permute-start(f32[24,8,128]{2,1,0:T(8,128)S(1)} %constant_dynamic-update-slice_fusion), channel_id=1, source_target_pairs={{0,24},{8,0},{16,8},{24,16},{1,25},{9,1},{17,9},{25,17},{2,26},{10... | collective-permute-start | bytes 294920 | tf_op jit(solution)/shard_map/ppermute | solution.py:654
  11.7 1.7 %collective-permute-done = f32[24,8,128]{2,1,0:T(8,128)S(1)} collective-permute-done((f32[24,8,128]{2,1,0:T(8,128)S(1)}, f32[24,8,128]{2,1,0:T(8,128)S(1)}, u32[]{:S(2)}, u32[]{:S(2)}) %collective-permute-start) | collective-permute-done | bytes 98336 | tf_op jit(solution)/shard_map/ppermute | solution.py:654
  13.4 3.5 %collective-permute-done.1 = f32[24,8,128]{2,1,0:T(8,128)S(1)} collective-permute-done((f32[24,8,128]{2,1,0:T(8,128)S(1)}, f32[24,8,128]{2,1,0:T(8,128)S(1)}, u32[]{:S(2)}, u32[]{:S(2)}) %collective-permute-start.1) | collective-permute-done | bytes 98336 | tf_op jit(solution)/shard_map/ppermute | solution.py:654
  16.9 0.0 collective-permute-done.2
  17.0 0.0 copy-start.6
  17.0 5.8 %all-to-all-start = ((f32[32,8,8,128]{3,2,1,0:T(8,128)}), f32[32,8,8,128]{3,2,1,0:T(8,128)S(1)}, u32[]{:S(2)}, u32[]{:S(2)}) async-start(f32[32,8,8,128]{3,2,1,0:T(8,128)} %param.11), calls=%async_computation | async-start | bytes 2097152 | tf_op jit(solution)/shard_map/all_to_all | solution.py:674
  22.9 1.8 %collective-permute-start.3 = (f32[4,24,8,128]{3,2,1,0:T(8,128)S(1)}, f32[4,24,8,128]{3,2,1,0:T(8,128)S(1)}, u32[]{:S(2)}, u32[]{:S(2)}) collective-permute-start(f32[4,24,8,128]{3,2,1,0:T(8,128)S(1)} %pad_maximum_fusion.refs_2_), channel_id=1, source_target_pairs={{0,2},{2,4},{4,6},{6,0},{1,3},{3,5},{5,7},{7,1},{8,10},{10,12},{12... | collective-permute-start | bytes 1179656 | tf_op jit(solution)/shard_map/ppermute | solution.py:654
  24.7 1.5 %collective-permute-start.4 = (f32[4,24,8,128]{3,2,1,0:T(8,128)S(1)}, f32[4,24,8,128]{3,2,1,0:T(8,128)S(1)}, u32[]{:S(2)}, u32[]{:S(2)}) collective-permute-start(f32[4,24,8,128]{3,2,1,0:T(8,128)S(1)} %pad_maximum_fusion.refs_2_), channel_id=1, source_target_pairs={{0,4},{2,6},{4,0},{6,2},{1,5},{3,7},{5,1},{7,3},{8,12},{10,14},{12... | collective-permute-start | bytes 1179656 | tf_op jit(solution)/shard_map/ppermute | solution.py:654
  26.2 1.5 %collective-permute-start.5 = (f32[4,24,8,128]{3,2,1,0:T(8,128)S(1)}, f32[4,24,8,128]{3,2,1,0:T(8,128)S(1)}, u32[]{:S(2)}, u32[]{:S(2)}) collective-permute-start(f32[4,24,8,128]{3,2,1,0:T(8,128)S(1)} %pad_maximum_fusion.refs_2_), channel_id=1, source_target_pairs={{0,6},{2,0},{4,2},{6,4},{1,7},{3,1},{5,3},{7,5},{8,14},{10,8},{12,... | collective-permute-start | bytes 1179656 | tf_op jit(solution)/shard_map/ppermute | solution.py:654
  27.6 0.0 copy-done.6
  27.6 0.1 collective-permute-start.6
  27.7 18.5 %collective-permute-done.3.refs_3_ = f32[4,24,8,128]{3,2,1,0:T(8,128)S(1)} collective-permute-done((f32[4,24,8,128]{3,2,1,0:T(8,128)S(1)}, f32[4,24,8,128]{3,2,1,0:T(8,128)S(1)}, u32[]{:S(2)}, u32[]{:S(2)}) %collective-permute-start.3) | collective-permute-done | bytes 393248 | tf_op jit(solution)/shard_map/ppermute | solution.py:654
  46.2 0.0 collective-permute-start.7
  46.2 7.6 %collective-permute-done.4.refs_4_ = f32[4,24,8,128]{3,2,1,0:T(8,128)S(1)} collective-permute-done((f32[4,24,8,128]{3,2,1,0:T(8,128)S(1)}, f32[4,24,8,128]{3,2,1,0:T(8,128)S(1)}, u32[]{:S(2)}, u32[]{:S(2)}) %collective-permute-start.4) | collective-permute-done | bytes 393248 | tf_op jit(solution)/shard_map/ppermute | solution.py:654
  53.8 0.0 collective-permute-start.8
  53.9 0.7 collective-permute-done.5.refs_5_
  54.6 0.0 collective-permute-start.9
  54.6 0.1 pad_add_fusion.my_place
  54.7 0.7 slice.3
  55.4 0.0 all-to-all-done
  55.4 0.0 copy-start
  55.4 1.1 copy-done
  56.6 1.0 copy-done.2
  57.5 2.9 %shard_map.122 = (f32[2048,128]{1,0:T(8,128)S(1)}, f32[2048,128]{1,0:T(8,128)S(1)}) custom-call(f32[2048,128]{1,0:T(8,128)S(1)} %bitcast.28, bf16[1536,256]{1,0:T(8,128)(2,1)S(1)} %copy-done, bf16[256,768]{1,0:T(8,128)(2,1)S(1)} %copy-done.2), custom_call_target="tpu_custom_call" | custom-call | flops 1610612736 | bytes 4194304 | tf_op jit(solution)/shard_map/pallas_call | solution.py:585
  60.4 0.0 collective-permute-done.6.refs_6_
  60.4 0.0 collective-permute-done.7.refs_7_
  60.5 0.0 collective-permute-done.8.refs_8_
  60.5 0.0 collective-permute-done.9.refs_9_
  60.5 0.0 copy-done.1
  60.5 0.0 copy-done.3
  60.5 21.3 %shard_map.123 = f32[2048,128]{1,0:T(8,128)S(1)} custom-call(s32[256]{0:T(256)S(1)} %multiply_add_fusion.place, s32[256]{0:T(256)S(1)} %get-tuple-element.10.half, s32[3]{0:T(128)S(1)} %pad_add_fusion.my_place, f32[2048,128]{1,0:T(8,128)S(1)} %get-tuple-element.7.refs_0_, f32[2048,128]{1,0:T(8,128)S(1)} %get-tuple-element.8.refs_1_, ...), custom_call_target="tpu_custom_call" | custom-call | flops 4831838208 | bytes 8388608 | tf_op jit(solution)/shard_map/pallas_call | solution.py:620
  81.8 31.3 %all_to_all.15 = f32[32,8,8,128]{3,2,1,0:T(8,128)S(1)} all-to-all(f32[32,8,8,128]{3,2,1,0:T(8,128)S(1)} %bitcast.29), channel_id=1, replica_groups=mesh['gx'=4,'gy'=4,'gz'=2] {'gx','gy','gz'}, dimensions={0} | all-to-all | bytes 2097152 | tf_op jit(solution)/shard_map/all_to_all | solution.py:678
  113.1 0.2 dot_general.5
  113.3 0.2 reshape.132
  113.5 1.0 convolution_bitcast_fusion
  114.5 0.1 broadcast_in_dim.26
  114.6 11.7 %all_to_all.16 = f32[32,8,128]{2,1,0:T(8,128)S(1)} all-to-all(f32[32,8,128]{2,1,0:T(8,128)S(1)} %broadcast_in_dim.27), channel_id=1, replica_groups=mesh['gx'=4,'gy'=4,'gz'=2] {'gx','gy','gz'}, dimensions={0} | all-to-all | bytes 262144 | tf_op jit(solution)/shard_map/all_to_all | solution.py:683
  126.3 0.1 div.38
  126.4 0.6 copy.34
  127.0 1.0 copy.37
  (13 shorter events, 0.2 us)
Async XLA Ops:
  0.6 0.7 copy-start.8
  1.6 1.0 copy-start.4
  1.7 0.7 copy-start.7
  3.6 0.8 copy-start.5
  4.7 8.8 %collective-permute-start = (f32[24,8,128]{2,1,0:T(8,128)S(1)}, f32[24,8,128]{2,1,0:T(8,128)S(1)}, u32[]{:S(2)}, u32[]{:S(2)}) collective-permute-start(f32[24,8,128]{2,1,0:T(8,128)S(1)} %constant_dynamic-update-slice_fusion), channel_id=1, source_target_pairs={{0,8},{8,16},{16,24},{24,0},{1,9},{9,17},{17,25},{25,1},{2,10},{10... | collective-permute-start | bytes 294920 | tf_op jit(solution)/shard_map/ppermute | solution.py:654
  7.8 9.2 %collective-permute-start.1 = (f32[24,8,128]{2,1,0:T(8,128)S(1)}, f32[24,8,128]{2,1,0:T(8,128)S(1)}, u32[]{:S(2)}, u32[]{:S(2)}) collective-permute-start(f32[24,8,128]{2,1,0:T(8,128)S(1)} %constant_dynamic-update-slice_fusion), channel_id=1, source_target_pairs={{0,16},{8,24},{16,0},{24,8},{1,17},{9,25},{17,1},{25,9},{2,18},{10... | collective-permute-start | bytes 294920 | tf_op jit(solution)/shard_map/ppermute | solution.py:654
  10.3 6.6 %collective-permute-start.2 = (f32[24,8,128]{2,1,0:T(8,128)S(1)}, f32[24,8,128]{2,1,0:T(8,128)S(1)}, u32[]{:S(2)}, u32[]{:S(2)}) collective-permute-start(f32[24,8,128]{2,1,0:T(8,128)S(1)} %constant_dynamic-update-slice_fusion), channel_id=1, source_target_pairs={{0,24},{8,0},{16,8},{24,16},{1,25},{9,1},{17,9},{25,17},{2,26},{10... | collective-permute-start | bytes 294920 | tf_op jit(solution)/shard_map/ppermute | solution.py:654
  17.0 10.6 %copy-start.6 = (s32[256]{0:T(256)S(1)}, s32[256]{0:T(256)}, u32[]{:S(2)}) copy-start(s32[256]{0:T(256)} %param.14) | copy-start | bytes 3076
  17.0 38.4 %all-to-all-start = ((f32[32,8,8,128]{3,2,1,0:T(8,128)}), f32[32,8,8,128]{3,2,1,0:T(8,128)S(1)}, u32[]{:S(2)}, u32[]{:S(2)}) async-start(f32[32,8,8,128]{3,2,1,0:T(8,128)} %param.11), calls=%async_computation | async-start | bytes 2097152 | tf_op jit(solution)/shard_map/all_to_all | solution.py:674
  22.9 23.3 %collective-permute-start.3 = (f32[4,24,8,128]{3,2,1,0:T(8,128)S(1)}, f32[4,24,8,128]{3,2,1,0:T(8,128)S(1)}, u32[]{:S(2)}, u32[]{:S(2)}) collective-permute-start(f32[4,24,8,128]{3,2,1,0:T(8,128)S(1)} %pad_maximum_fusion.refs_2_), channel_id=1, source_target_pairs={{0,2},{2,4},{4,6},{6,0},{1,3},{3,5},{5,7},{7,1},{8,10},{10,12},{12... | collective-permute-start | bytes 1179656 | tf_op jit(solution)/shard_map/ppermute | solution.py:654
  24.7 29.1 %collective-permute-start.4 = (f32[4,24,8,128]{3,2,1,0:T(8,128)S(1)}, f32[4,24,8,128]{3,2,1,0:T(8,128)S(1)}, u32[]{:S(2)}, u32[]{:S(2)}) collective-permute-start(f32[4,24,8,128]{3,2,1,0:T(8,128)S(1)} %pad_maximum_fusion.refs_2_), channel_id=1, source_target_pairs={{0,4},{2,6},{4,0},{6,2},{1,5},{3,7},{5,1},{7,3},{8,12},{10,14},{12... | collective-permute-start | bytes 1179656 | tf_op jit(solution)/shard_map/ppermute | solution.py:654
  26.2 28.5 %collective-permute-start.5 = (f32[4,24,8,128]{3,2,1,0:T(8,128)S(1)}, f32[4,24,8,128]{3,2,1,0:T(8,128)S(1)}, u32[]{:S(2)}, u32[]{:S(2)}) collective-permute-start(f32[4,24,8,128]{3,2,1,0:T(8,128)S(1)} %pad_maximum_fusion.refs_2_), channel_id=1, source_target_pairs={{0,6},{2,0},{4,2},{6,4},{1,7},{3,1},{5,3},{7,5},{8,14},{10,8},{12,... | collective-permute-start | bytes 1179656 | tf_op jit(solution)/shard_map/ppermute | solution.py:654
  27.6 32.8 %collective-permute-start.6 = (f32[4,24,8,128]{3,2,1,0:T(8,128)S(1)}, f32[4,24,8,128]{3,2,1,0:T(8,128)S(1)}, u32[]{:S(2)}, u32[]{:S(2)}) collective-permute-start(f32[4,24,8,128]{3,2,1,0:T(8,128)S(1)} %pad_maximum_fusion.refs_2_), channel_id=1, source_target_pairs={{0,1},{1,0},{2,3},{3,2},{4,5},{5,4},{6,7},{7,6},{8,9},{9,8},{10,11... | collective-permute-start | bytes 1179656 | tf_op jit(solution)/shard_map/ppermute | solution.py:654
  46.2 14.3 %collective-permute-start.7 = (f32[4,24,8,128]{3,2,1,0:T(8,128)S(1)}, f32[4,24,8,128]{3,2,1,0:T(8,128)S(1)}, u32[]{:S(2)}, u32[]{:S(2)}) collective-permute-start(f32[4,24,8,128]{3,2,1,0:T(8,128)S(1)} %collective-permute-done.3.refs_3_), channel_id=1, source_target_pairs={{0,1},{1,0},{2,3},{3,2},{4,5},{5,4},{6,7},{7,6},{8,9},{9,8},{10,11... | collective-permute-start | bytes 1179656 | tf_op jit(solution)/shard_map/ppermute | solution.py:654
  53.8 6.6 %collective-permute-start.8 = (f32[4,24,8,128]{3,2,1,0:T(8,128)S(1)}, f32[4,24,8,128]{3,2,1,0:T(8,128)}, u32[]{:S(2)}, u32[]{:S(2)}) collective-permute-start(f32[4,24,8,128]{3,2,1,0:T(8,128)S(1)} %collective-permute-done.4.refs_4_), channel_id=1, source_target_pairs={{0,1},{1,0},{2,3},{3,2},{4,5},{5,4},{6,7},{7,6},{8,9},{9,8},{10,11... | collective-permute-start | bytes 1179656 | tf_op jit(solution)/shard_map/ppermute | solution.py:654
  54.6 5.9 %collective-permute-start.9 = (f32[4,24,8,128]{3,2,1,0:T(8,128)S(1)}, f32[4,24,8,128]{3,2,1,0:T(8,128)}, u32[]{:S(2)}, u32[]{:S(2)}) collective-permute-start(f32[4,24,8,128]{3,2,1,0:T(8,128)S(1)} %collective-permute-done.5.refs_5_), channel_id=1, source_target_pairs={{0,1},{1,0},{2,3},{3,2},{4,5},{5,4},{6,7},{7,6},{8,9},{9,8},{10,11... | collective-permute-start | bytes 1179656 | tf_op jit(solution)/shard_map/ppermute | solution.py:654
  55.4 1.1 copy-start
  56.5 1.0 copy-start.2
  57.5 2.9 %copy-start.1 = (bf16[1536,256]{1,0:T(8,128)(2,1)S(1)}, bf16[1536,256]{1,0:T(8,128)(2,1)}, u32[]{:S(2)}) copy-start(bf16[1536,256]{1,0:T(8,128)(2,1)} %constant.68.clone.refs_1_.refs_10_) | copy-start | bytes 2359300
  57.5 2.9 %copy-start.3 = (bf16[256,768]{1,0:T(8,128)(2,1)S(1)}, bf16[256,768]{1,0:T(8,128)(2,1)}, u32[]{:S(2)}) copy-start(bf16[256,768]{1,0:T(8,128)(2,1)} %constant.69.clone.refs_2_.refs_11_) | copy-start | bytes 1179652

commit v8 on v7

--- a/solution.py
+++ b/solution.py
@@ -371,6 +371,7 @@
     lane = lax.broadcasted_iota(jnp.int32, (SUB, LANE), 1)
     lower = lane < HALF
     side = lane // HALF
+    row = lax.broadcasted_iota(jnp.int32, (SUB, LANE), 0)
     f32 = jnp.float32
 
     loads = [
@@ -403,10 +404,10 @@
 
     def lay_potential(pair, carry):
         for depth_at in range(groups_z):
-            for row in range(SUB):
-                first = packs[2 * pair * groups_z + depth_at, row]
-                second = packs[(2 * pair + 1) * groups_z + depth_at, row]
-                at = pl.multiple_of(pair * span + depth_at * LANE + row * SUB, SUB)
+            for tile in range(SUB):
+                first = packs[2 * pair * groups_z + depth_at, tile]
+                second = packs[(2 * pair + 1) * groups_z + depth_at, tile]
+                at = pl.multiple_of(pair * span + depth_at * LANE + tile * SUB, SUB)
                 local[pl.ds(at, SUB), :] = diagonal + jnp.where(
                     lower, first, pltpu.roll(second, HALF, 1)
                 )
@@ -432,6 +433,24 @@
             device = slab_at * (groups_y * groups_z) + number
             for inner in range(per_device):
                 yield device, inner
+
+    def box_tiles(atom):
+        at = place[atom]
+        turn = at & (SUB - 1)
+        base = pl.multiple_of(at - turn, SUB)
+        after = pl.multiple_of(base + jnp.where(turn > 0, SUB, 0), SUB)
+        return turn, pl.ds(base, SUB), pl.ds(after, SUB)
+
+    def turn_projectors(device, carry):
+        for inner in range(per_device):
+            for j in range(SUB):
+                turn = place[(device * per_device + inner) * SUB + j] & (SUB - 1)
+                for kp in range(2):
+                    at = SUB + (inner * 2 + kp) * SUB + j
+                    packs[device, at] = pltpu.roll(packs[device, at], turn, 0)
+        return carry
+
+    lax.fori_loop(0, domains, turn_projectors, 0)
 
     def apply_step(cur, prev, new, alpha, beta, first, last):
         def project(chunk_at, carry):
@@ -444,7 +463,8 @@
                     terms = ([], [])
                     for j in range(SUB):
                         atom = group * SUB + j
-                        value = cur[pl.ds(place[atom], SUB), :]
+                        turn, rows, rows_after = box_tiles(atom)
+                        value = jnp.where(row >= turn, cur[rows, :], cur[rows_after, :])
                         both = jnp.where(side == half[atom], value, pltpu.roll(value, HALF, 1))
                         for kp in range(2):
                             at = SUB + (inner * 2 + kp) * SUB + j
@@ -476,9 +496,12 @@
                     value = parts[0] + parts[1]
                     value = value + pltpu.roll(value, HALF, 1)
                     value = jnp.where(side == half[atom], value, 0.0)
-                    rows = pl.ds(place[atom], SUB)
+                    turn, rows, rows_after = box_tiles(atom)
                     target = targets[j % len(targets)]
-                    target[rows, :] = target[rows, :] + value
+                    target[rows, :] = target[rows, :] + jnp.where(row >= turn, value, 0.0)
+                    target[rows_after, :] = target[rows_after, :] + jnp.where(
+                        row >= turn, 0.0, value
+                    )
             return carry
 
         lax.fori_loop(0, groups_x, scatter, 0)
@@ -668,12 +691,12 @@
     own = lax.dynamic_slice(coupling, (me * atoms_own, 0), (atoms_own, NPROJ))
     pack = packed_inputs(potential, projectors, extent, own)
     line = jnp.stack(hops(pack, "gx"))
-    orbitals, line = lax.optimization_barrier((orbitals, line))
+    place, half = box_places(groups, owner_rank, box_anchor[2])
+    orbitals, line, place, half = lax.optimization_barrier((orbitals, line, place, half))
     crossed = [hops(piece, "gz") for piece in hops(line, "gy")]
     packs = [crossed[hop_y][hop_z] for hop_z in range(groups_z) for hop_y in range(groups[1])]
     field = lax.all_to_all(orbitals, axes, split_axis=0, concat_axis=0, tiled=True)
     field, near = first_call(groups, field)
-    place, half = box_places(groups, owner_rank, box_anchor[2])
     result = filter_call(groups, place, half, my_place, field, near, packs)
     filtered = lax.all_to_all(result, axes, split_axis=0, concat_axis=0, tiled=True)
     states = filtered.shape[0]

time: 129 us -> 131 us (1.016)
  Pallas kernels: 24.2 us -> 27.5 us
    pallas_call x1, Pallas kernels: 21.3 us -> 24.6 us  [filter_call(): pl.pallas_call(functools.partial(filter_kernel, groups, atoms), out_shape...]
where the time goes in v8:
time: 131 us
  blocking collectives  43 us (33%)
  waiting for transfers between devices  31.5 us (24%)
  Pallas kernels  27.5 us (21%)
  starting transfers between devices  17.7 us (14%)
  local copies, waits for them, and re-layouts  8.58 us (7%)
    ppermute x10, waiting for transfers between devices, hops(): lax.ppermute(value, axis, [(i, (i + hop) % count) for i in range(count)])  31.5 us
    all_to_all x1, blocking collectives, state_body(): lax.all_to_all(result, axes, split_axis=0, concat_axis=0, tiled=True)  31.3 us
    pallas_call x1, Pallas kernels, filter_call(): pl.pallas_call(functools.partial(filter_kernel, groups, atoms), out_shape...  24.6 us
    ppermute x10, starting transfers between devices, hops(): lax.ppermute(value, axis, [(i, (i + hop) % count) for i in range(count)])  11.8 us
    all_to_all x1, blocking collectives, state_body(): lax.all_to_all(jnp.broadcast_to(quarter[None], (domains,) + quarter.shape...  11.7 us
    all_to_all x1, starting transfers between devices, state_body(): lax.all_to_all(orbitals, axes, split_axis=0, concat_axis=0, tiled=True)  5.85 us
    unnamed x20, local copies, waits for them, and re-layouts  4.91 us
    pallas_call x1, Pallas kernels, first_call(): pl.pallas_call(functools.partial(first_kernel, groups), out_shape=[jax.Sh...  2.88 us
  transfers between devices with their start and end apart: 11, of which 5 were waited for; matrix products, arithmetic and copies ran while one was open for 1% of the time, Pallas kernels for 2%

profile of v8, /device:TPU:0, one launch (start us, length us, event | category | flops | bytes accessed | tf_op | source)
XLA Modules:
  0.0 130.6 jit_solution(4769203936048684109)
XLA Ops:
  0.6 0.0 copy-start.8
  0.7 0.7 copy-done.8
  1.3 0.1 dynamic_slice.6
  1.4 0.1 iota_compare_fusion
  1.5 0.1 broadcast_and_fusion.1
  1.6 0.0 copy-start.4
  1.6 0.1 broadcast_and_fusion
  1.7 0.0 copy-start.7
  1.7 0.2 and.65
  1.9 0.5 copy-done.7
  2.4 0.1 dynamic-slice_sqrt_fusion
  2.5 0.1 copy.28
  2.5 0.0 copy-done.4
  2.6 0.1 multiply_select_fusion
  2.7 0.6 reshape.127
  3.3 0.3 copy.30
  3.6 0.0 copy-start.5
  3.6 0.1 reshape.128
  3.7 0.6 copy-done.5
  4.4 0.1 reshape.125
  4.5 0.1 copy.27
  4.6 0.1 reshape.126
  4.7 0.0 copy-start.6
  4.7 3.1 %collective-permute-start = (f32[24,8,128]{2,1,0:T(8,128)S(1)}, f32[24,8,128]{2,1,0:T(8,128)S(1)}, u32[]{:S(2)}, u32[]{:S(2)}) collective-permute-start(f32[24,8,128]{2,1,0:T(8,128)S(1)} %constant_dynamic-update-slice_fusion), channel_id=1, source_target_pairs={{0,8},{8,16},{16,24},{24,0},{1,9},{9,17},{17,25},{25,1},{2,10},{10... | collective-permute-start | bytes 294920 | tf_op jit(solution)/shard_map/ppermute | solution.py:677
  7.8 2.6 %collective-permute-start.1 = (f32[24,8,128]{2,1,0:T(8,128)S(1)}, f32[24,8,128]{2,1,0:T(8,128)S(1)}, u32[]{:S(2)}, u32[]{:S(2)}) collective-permute-start(f32[24,8,128]{2,1,0:T(8,128)S(1)} %constant_dynamic-update-slice_fusion), channel_id=1, source_target_pairs={{0,16},{8,24},{16,0},{24,8},{1,17},{9,25},{17,1},{25,9},{2,18},{10... | collective-permute-start | bytes 294920 | tf_op jit(solution)/shard_map/ppermute | solution.py:677
  10.4 1.3 %collective-permute-start.2 = (f32[24,8,128]{2,1,0:T(8,128)S(1)}, f32[24,8,128]{2,1,0:T(8,128)S(1)}, u32[]{:S(2)}, u32[]{:S(2)}) collective-permute-start(f32[24,8,128]{2,1,0:T(8,128)S(1)} %constant_dynamic-update-slice_fusion), channel_id=1, source_target_pairs={{0,24},{8,0},{16,8},{24,16},{1,25},{9,1},{17,9},{25,17},{2,26},{10... | collective-permute-start | bytes 294920 | tf_op jit(solution)/shard_map/ppermute | solution.py:677
  11.7 0.0 copy-done.6
  11.7 0.7 slice.3
  12.4 1.0 collective-permute-done
  13.4 3.5 %collective-permute-done.1 = f32[24,8,128]{2,1,0:T(8,128)S(1)} collective-permute-done((f32[24,8,128]{2,1,0:T(8,128)S(1)}, f32[24,8,128]{2,1,0:T(8,128)S(1)}, u32[]{:S(2)}, u32[]{:S(2)}) %collective-permute-start.1) | collective-permute-done | bytes 98336 | tf_op jit(solution)/shard_map/ppermute | solution.py:677
  16.9 0.0 collective-permute-done.2
  17.0 5.8 %all-to-all-start = ((f32[32,8,8,128]{3,2,1,0:T(8,128)}), f32[32,8,8,128]{3,2,1,0:T(8,128)S(1)}, u32[]{:S(2)}, u32[]{:S(2)}) async-start(f32[32,8,8,128]{3,2,1,0:T(8,128)} %param.11), calls=%async_computation | async-start | bytes 2097152 | tf_op jit(solution)/shard_map/all_to_all | solution.py:698
  22.9 1.8 %collective-permute-start.3 = (f32[4,24,8,128]{3,2,1,0:T(8,128)S(1)}, f32[4,24,8,128]{3,2,1,0:T(8,128)S(1)}, u32[]{:S(2)}, u32[]{:S(2)}) collective-permute-start(f32[4,24,8,128]{3,2,1,0:T(8,128)S(1)} %pad_maximum_fusion.refs_2_), channel_id=1, source_target_pairs={{0,2},{2,4},{4,6},{6,0},{1,3},{3,5},{5,7},{7,1},{8,10},{10,12},{12... | collective-permute-start | bytes 1179656 | tf_op jit(solution)/shard_map/ppermute | solution.py:677
  24.7 1.5 %collective-permute-start.4 = (f32[4,24,8,128]{3,2,1,0:T(8,128)S(1)}, f32[4,24,8,128]{3,2,1,0:T(8,128)S(1)}, u32[]{:S(2)}, u32[]{:S(2)}) collective-permute-start(f32[4,24,8,128]{3,2,1,0:T(8,128)S(1)} %pad_maximum_fusion.refs_2_), channel_id=1, source_target_pairs={{0,4},{2,6},{4,0},{6,2},{1,5},{3,7},{5,1},{7,3},{8,12},{10,14},{12... | collective-permute-start | bytes 1179656 | tf_op jit(solution)/shard_map/ppermute | solution.py:677
  26.2 1.5 %collective-permute-start.5 = (f32[4,24,8,128]{3,2,1,0:T(8,128)S(1)}, f32[4,24,8,128]{3,2,1,0:T(8,128)S(1)}, u32[]{:S(2)}, u32[]{:S(2)}) collective-permute-start(f32[4,24,8,128]{3,2,1,0:T(8,128)S(1)} %pad_maximum_fusion.refs_2_), channel_id=1, source_target_pairs={{0,6},{2,0},{4,2},{6,4},{1,7},{3,1},{5,3},{7,5},{8,14},{10,8},{12,... | collective-permute-start | bytes 1179656 | tf_op jit(solution)/shard_map/ppermute | solution.py:677
  27.6 0.0 collective-permute-start.6
  27.6 18.6 %collective-permute-done.3.refs_3_ = f32[4,24,8,128]{3,2,1,0:T(8,128)S(1)} collective-permute-done((f32[4,24,8,128]{3,2,1,0:T(8,128)S(1)}, f32[4,24,8,128]{3,2,1,0:T(8,128)S(1)}, u32[]{:S(2)}, u32[]{:S(2)}) %collective-permute-start.3) | collective-permute-done | bytes 393248 | tf_op jit(solution)/shard_map/ppermute | solution.py:677
  46.2 0.0 collective-permute-start.7
  46.2 7.6 %collective-permute-done.4.refs_4_ = f32[4,24,8,128]{3,2,1,0:T(8,128)S(1)} collective-permute-done((f32[4,24,8,128]{3,2,1,0:T(8,128)S(1)}, f32[4,24,8,128]{3,2,1,0:T(8,128)S(1)}, u32[]{:S(2)}, u32[]{:S(2)}) %collective-permute-start.4) | collective-permute-done | bytes 393248 | tf_op jit(solution)/shard_map/ppermute | solution.py:677
  53.8 0.0 collective-permute-start.8
  53.9 0.7 collective-permute-done.5.refs_5_
  54.6 0.0 collective-permute-start.9
  54.6 0.1 pad_add_fusion.my_place
  54.7 0.0 all-to-all-done
  54.7 0.0 copy-start
  54.7 1.1 copy-done
  55.8 1.0 copy-done.2
  56.8 2.9 %shard_map.122 = (f32[2048,128]{1,0:T(8,128)S(1)}, f32[2048,128]{1,0:T(8,128)S(1)}) custom-call(f32[2048,128]{1,0:T(8,128)S(1)} %bitcast.28, bf16[1536,256]{1,0:T(8,128)(2,1)S(1)} %copy-done, bf16[256,768]{1,0:T(8,128)(2,1)S(1)} %copy-done.2), custom_call_target="tpu_custom_call" | custom-call | flops 1610612736 | bytes 4194304 | tf_op jit(solution)/shard_map/pallas_call | solution.py:608
  59.7 0.0 collective-permute-done.6.refs_6_
  59.7 0.0 collective-permute-done.7.refs_7_
  59.7 0.0 collective-permute-done.8.refs_8_
  59.7 0.0 collective-permute-done.9.refs_9_
  59.8 0.0 copy-done.1
  59.8 0.0 copy-done.3
  59.8 24.6 %shard_map.123 = f32[2048,128]{1,0:T(8,128)S(1)} custom-call(s32[256]{0:T(256)S(1)} %multiply_add_fusion.place, s32[256]{0:T(256)S(1)} %get-tuple-element.9.half, s32[3]{0:T(128)S(1)} %pad_add_fusion.my_place, f32[2048,128]{1,0:T(8,128)S(1)} %get-tuple-element.11.refs_0_, f32[2048,128]{1,0:T(8,128)S(1)} %get-tuple-element.12.refs_1_, ...), custom_call_target="tpu_custom_call" | custom-call | flops 4831838208 | bytes 8388608 | tf_op jit(solution)/shard_map/pallas_call | solution.py:643
  84.4 31.3 %all_to_all.15 = f32[32,8,8,128]{3,2,1,0:T(8,128)S(1)} all-to-all(f32[32,8,8,128]{3,2,1,0:T(8,128)S(1)} %bitcast.29), channel_id=1, replica_groups=mesh['gx'=4,'gy'=4,'gz'=2] {'gx','gy','gz'}, dimensions={0} | all-to-all | bytes 2097152 | tf_op jit(solution)/shard_map/all_to_all | solution.py:701
  115.7 0.2 dot_general.5
  115.9 0.2 reshape.132
  116.1 1.0 convolution_bitcast_fusion
  117.1 0.1 broadcast_in_dim.26
  117.2 11.7 %all_to_all.16 = f32[32,8,128]{2,1,0:T(8,128)S(1)} all-to-all(f32[32,8,128]{2,1,0:T(8,128)S(1)} %broadcast_in_dim.27), channel_id=1, replica_groups=mesh['gx'=4,'gy'=4,'gz'=2] {'gx','gy','gz'}, dimensions={0} | all-to-all | bytes 262144 | tf_op jit(solution)/shard_map/all_to_all | solution.py:706
  128.9 0.1 div.38
  129.0 0.6 copy.34
  129.6 1.0 copy.37
  (13 shorter events, 0.2 us)
Async XLA Ops:
  0.6 0.7 copy-start.8
  1.6 1.0 copy-start.4
  1.7 0.7 copy-start.7
  3.6 0.8 copy-start.5
  4.7 7.0 %copy-start.6 = (s32[256]{0:T(256)S(1)}, s32[256]{0:T(256)}, u32[]{:S(2)}) copy-start(s32[256]{0:T(256)} %param.14) | copy-start | bytes 3076
  4.7 8.8 %collective-permute-start = (f32[24,8,128]{2,1,0:T(8,128)S(1)}, f32[24,8,128]{2,1,0:T(8,128)S(1)}, u32[]{:S(2)}, u32[]{:S(2)}) collective-permute-start(f32[24,8,128]{2,1,0:T(8,128)S(1)} %constant_dynamic-update-slice_fusion), channel_id=1, source_target_pairs={{0,8},{8,16},{16,24},{24,0},{1,9},{9,17},{17,25},{25,1},{2,10},{10... | collective-permute-start | bytes 294920 | tf_op jit(solution)/shard_map/ppermute | solution.py:677
  7.8 9.2 %collective-permute-start.1 = (f32[24,8,128]{2,1,0:T(8,128)S(1)}, f32[24,8,128]{2,1,0:T(8,128)S(1)}, u32[]{:S(2)}, u32[]{:S(2)}) collective-permute-start(f32[24,8,128]{2,1,0:T(8,128)S(1)} %constant_dynamic-update-slice_fusion), channel_id=1, source_target_pairs={{0,16},{8,24},{16,0},{24,8},{1,17},{9,25},{17,1},{25,9},{2,18},{10... | collective-permute-start | bytes 294920 | tf_op jit(solution)/shard_map/ppermute | solution.py:677
  10.4 6.6 %collective-permute-start.2 = (f32[24,8,128]{2,1,0:T(8,128)S(1)}, f32[24,8,128]{2,1,0:T(8,128)S(1)}, u32[]{:S(2)}, u32[]{:S(2)}) collective-permute-start(f32[24,8,128]{2,1,0:T(8,128)S(1)} %constant_dynamic-update-slice_fusion), channel_id=1, source_target_pairs={{0,24},{8,0},{16,8},{24,16},{1,25},{9,1},{17,9},{25,17},{2,26},{10... | collective-permute-start | bytes 294920 | tf_op jit(solution)/shard_map/ppermute | solution.py:677
  17.0 37.7 %all-to-all-start = ((f32[32,8,8,128]{3,2,1,0:T(8,128)}), f32[32,8,8,128]{3,2,1,0:T(8,128)S(1)}, u32[]{:S(2)}, u32[]{:S(2)}) async-start(f32[32,8,8,128]{3,2,1,0:T(8,128)} %param.11), calls=%async_computation | async-start | bytes 2097152 | tf_op jit(solution)/shard_map/all_to_all | solution.py:698
  22.9 23.3 %collective-permute-start.3 = (f32[4,24,8,128]{3,2,1,0:T(8,128)S(1)}, f32[4,24,8,128]{3,2,1,0:T(8,128)S(1)}, u32[]{:S(2)}, u32[]{:S(2)}) collective-permute-start(f32[4,24,8,128]{3,2,1,0:T(8,128)S(1)} %pad_maximum_fusion.refs_2_), channel_id=1, source_target_pairs={{0,2},{2,4},{4,6},{6,0},{1,3},{3,5},{5,7},{7,1},{8,10},{10,12},{12... | collective-permute-start | bytes 1179656 | tf_op jit(solution)/shard_map/ppermute | solution.py:677
  24.7 29.1 %collective-permute-start.4 = (f32[4,24,8,128]{3,2,1,0:T(8,128)S(1)}, f32[4,24,8,128]{3,2,1,0:T(8,128)S(1)}, u32[]{:S(2)}, u32[]{:S(2)}) collective-permute-start(f32[4,24,8,128]{3,2,1,0:T(8,128)S(1)} %pad_maximum_fusion.refs_2_), channel_id=1, source_target_pairs={{0,4},{2,6},{4,0},{6,2},{1,5},{3,7},{5,1},{7,3},{8,12},{10,14},{12... | collective-permute-start | bytes 1179656 | tf_op jit(solution)/shard_map/ppermute | solution.py:677
  26.2 28.5 %collective-permute-start.5 = (f32[4,24,8,128]{3,2,1,0:T(8,128)S(1)}, f32[4,24,8,128]{3,2,1,0:T(8,128)S(1)}, u32[]{:S(2)}, u32[]{:S(2)}) collective-permute-start(f32[4,24,8,128]{3,2,1,0:T(8,128)S(1)} %pad_maximum_fusion.refs_2_), channel_id=1, source_target_pairs={{0,6},{2,0},{4,2},{6,4},{1,7},{3,1},{5,3},{7,5},{8,14},{10,8},{12,... | collective-permute-start | bytes 1179656 | tf_op jit(solution)/shard_map/ppermute | solution.py:677
  27.6 32.1 %collective-permute-start.6 = (f32[4,24,8,128]{3,2,1,0:T(8,128)S(1)}, f32[4,24,8,128]{3,2,1,0:T(8,128)S(1)}, u32[]{:S(2)}, u32[]{:S(2)}) collective-permute-start(f32[4,24,8,128]{3,2,1,0:T(8,128)S(1)} %pad_maximum_fusion.refs_2_), channel_id=1, source_target_pairs={{0,1},{1,0},{2,3},{3,2},{4,5},{5,4},{6,7},{7,6},{8,9},{9,8},{10,11... | collective-permute-start | bytes 1179656 | tf_op jit(solution)/shard_map/ppermute | solution.py:677
  46.2 13.5 %collective-permute-start.7 = (f32[4,24,8,128]{3,2,1,0:T(8,128)S(1)}, f32[4,24,8,128]{3,2,1,0:T(8,128)S(1)}, u32[]{:S(2)}, u32[]{:S(2)}) collective-permute-start(f32[4,24,8,128]{3,2,1,0:T(8,128)S(1)} %collective-permute-done.3.refs_3_), channel_id=1, source_target_pairs={{0,1},{1,0},{2,3},{3,2},{4,5},{5,4},{6,7},{7,6},{8,9},{9,8},{10,11... | collective-permute-start | bytes 1179656 | tf_op jit(solution)/shard_map/ppermute | solution.py:677
  53.8 5.9 %collective-permute-start.8 = (f32[4,24,8,128]{3,2,1,0:T(8,128)S(1)}, f32[4,24,8,128]{3,2,1,0:T(8,128)}, u32[]{:S(2)}, u32[]{:S(2)}) collective-permute-start(f32[4,24,8,128]{3,2,1,0:T(8,128)S(1)} %collective-permute-done.4.refs_4_), channel_id=1, source_target_pairs={{0,1},{1,0},{2,3},{3,2},{4,5},{5,4},{6,7},{7,6},{8,9},{9,8},{10,11... | collective-permute-start | bytes 1179656 | tf_op jit(solution)/shard_map/ppermute | solution.py:677
  54.6 5.1 %collective-permute-start.9 = (f32[4,24,8,128]{3,2,1,0:T(8,128)S(1)}, f32[4,24,8,128]{3,2,1,0:T(8,128)}, u32[]{:S(2)}, u32[]{:S(2)}) collective-permute-start(f32[4,24,8,128]{3,2,1,0:T(8,128)S(1)} %collective-permute-done.5.refs_5_), channel_id=1, source_target_pairs={{0,1},{1,0},{2,3},{3,2},{4,5},{5,4},{6,7},{7,6},{8,9},{9,8},{10,11... | collective-permute-start | bytes 1179656 | tf_op jit(solution)/shard_map/ppermute | solution.py:677
  54.7 1.1 copy-start
  55.8 1.0 copy-start.2
  56.8 2.9 %copy-start.1 = (bf16[1536,256]{1,0:T(8,128)(2,1)S(1)}, bf16[1536,256]{1,0:T(8,128)(2,1)}, u32[]{:S(2)}) copy-start(bf16[1536,256]{1,0:T(8,128)(2,1)} %constant.68.clone.refs_1_.refs_10_) | copy-start | bytes 2359300
  56.8 2.9 %copy-start.3 = (bf16[256,768]{1,0:T(8,128)(2,1)S(1)}, bf16[256,768]{1,0:T(8,128)(2,1)}, u32[]{:S(2)}) copy-start(bf16[256,768]{1,0:T(8,128)(2,1)} %constant.69.clone.refs_2_.refs_11_) | copy-start | bytes 1179652

commit v9 on v7

--- a/solution.py
+++ b/solution.py
@@ -234,6 +234,10 @@
     return values[0]
 
 
+def spread_row(ref, at):
+    return ref[pl.ds(at, SUB, stride=0), :]
+
+
 SPARES = 3
 TALL = 2 * SUB
 
@@ -292,20 +296,13 @@
 
 
 def first_kernel(groups, *refs):
-    field_in, plane_in, depth_in, field, near = refs[:5]
-    raw, high_buf, low_buf, plane, depth, sems = refs[5:]
+    field_in, plane, depth, field, near, raw, high_buf, low_buf, sems = refs
     groups_x, groups_y, groups_z = groups
     span = groups_z * LANE
     pairs_slab = groups_y // 2
-    loads = [
-        pltpu.make_async_copy(source, target, sems.at[number])
-        for number, (source, target) in enumerate(
-            ((field_in, raw), (plane_in, plane), (depth_in, depth))
-        )
-    ]
-    for load in loads:
-        load.start()
-    loads[0].wait()
+    load = pltpu.make_async_copy(field_in, raw, sems.at[0])
+    load.start()
+    load.wait()
 
     def lay_field(slab_at, carry):
         for tile in range(pairs_slab):
@@ -322,8 +319,6 @@
         return carry
 
     lax.fori_loop(0, groups_x, lay_field, 0)
-    for load in loads[1:]:
-        load.wait()
     chunk = chunk_of(groups_x)
 
     def product(chunk_at, carry):
@@ -339,7 +334,7 @@
     pieces = groups_y * groups_z
     field_a, near_a = refs[:2]
     packs_in = refs[2 : 2 + pieces]
-    plane_in, depth_in, out = refs[2 + pieces : 5 + pieces]
+    plane, depth, out = refs[2 + pieces : 5 + pieces]
     (
         field_b,
         field_c,
@@ -350,13 +345,11 @@
         low_buf,
         near,
         packs,
-        plane,
-        depth,
         in_sems,
         pack_sems,
         out_sems,
-    ) = refs[5 + pieces : 5 + pieces + 14]
-    spares = refs[5 + pieces + 14 :]
+    ) = refs[5 + pieces : 5 + pieces + 12]
+    spares = refs[5 + pieces + 12 :]
     targets = (near,) + tuple(spares)
     columns = groups_x * groups_y
     domains = columns * groups_z
@@ -373,12 +366,7 @@
     side = lane // HALF
     f32 = jnp.float32
 
-    loads = [
-        pltpu.make_async_copy(source, target, in_sems.at[number])
-        for number, (source, target) in enumerate(
-            ((near_a, near), (plane_in, plane), (depth_in, depth))
-        )
-    ]
+    loads = [pltpu.make_async_copy(near_a, near, in_sems.at[0])]
     pack_loads = []
     for hop_z in range(groups_z):
         for hop_y in range(groups_y):
@@ -427,49 +415,52 @@
         .astype(jnp.bfloat16)
     )
 
-    def slab_groups(slab_at):
-        for number in range(groups_y * groups_z):
-            device = slab_at * (groups_y * groups_z) + number
+    share = 4 if domains % 4 == 0 else 1
+    parts = domains // share
+
+    def part_groups(part):
+        for number in range(share):
             for inner in range(per_device):
-                yield device, inner
+                yield part * share + number, inner
 
     def apply_step(cur, prev, new, alpha, beta, first, last):
-        def project(chunk_at, carry):
+        def product(chunk_at, carry):
             slabs = [chunk_at * chunk + number for number in range(chunk)]
-            if not first:
-                lay_products(groups, high_buf, low_buf, plane, depth, slabs, near)
-            for slab_at in slabs:
-                for device, inner in slab_groups(slab_at):
-                    group = device * per_device + inner
-                    terms = ([], [])
-                    for j in range(SUB):
-                        atom = group * SUB + j
-                        value = cur[pl.ds(place[atom], SUB), :]
-                        both = jnp.where(side == half[atom], value, pltpu.roll(value, HALF, 1))
-                        for kp in range(2):
-                            at = SUB + (inner * 2 + kp) * SUB + j
-                            terms[kp].append(both * packs[device, at])
+            lay_products(groups, high_buf, low_buf, plane, depth, slabs, near)
+            return carry
+
+        if not first:
+            lax.fori_loop(0, groups_x // chunk, product, 0)
+
+        def project(part, carry):
+            for device, inner in part_groups(part):
+                group = device * per_device + inner
+                terms = ([], [])
+                for j in range(SUB):
+                    atom = group * SUB + j
+                    value = cur[pl.ds(place[atom], SUB), :]
+                    both = jnp.where(side == half[atom], value, pltpu.roll(value, HALF, 1))
                     for kp in range(2):
-                        at = pl.multiple_of((group * 2 + kp) * SUB, SUB)
-                        coeffs[pl.ds(at, SUB), :] = row_sums(terms[kp])
+                        at = SUB + (inner * 2 + kp) * SUB + j
+                        terms[kp].append(both * packs[device, at])
+                for kp in range(2):
+                    at = pl.multiple_of((group * 2 + kp) * SUB, SUB)
+                    coeffs[pl.ds(at, SUB), :] = row_sums(terms[kp])
             return carry
 
-        lax.fori_loop(0, groups_x // chunk, project, 0)
-
-        high, low = split_pair(coeffs[...])
-        coeffs[...] = mxu(high, ones) + mxu(low, ones)
-
-        def scatter(slab_at, carry):
-            for device, inner in slab_groups(slab_at):
+        lax.fori_loop(0, parts, project, 0)
+
+        high, low = split_pair(coeffs[: 2 * atoms, :])
+        coeffs[: 2 * atoms, :] = mxu(high, ones) + mxu(low, ones)
+
+        def scatter(part, carry):
+            for device, inner in part_groups(part):
                 group = device * per_device + inner
-                weights = [
-                    coeffs[pl.ds(pl.multiple_of((group * 2 + kp) * SUB, SUB), SUB), :]
-                    for kp in range(2)
-                ]
+                bases = [pl.multiple_of((group * 2 + kp) * SUB, SUB) for kp in range(2)]
                 for j in range(SUB):
                     atom = group * SUB + j
                     parts = [
-                        jnp.broadcast_to(weights[kp][j : j + 1], (SUB, LANE))
+                        spread_row(coeffs, bases[kp] + j)
                         * packs[device, SUB + (inner * 2 + kp) * SUB + j]
                         for kp in range(2)
                     ]
@@ -481,7 +472,7 @@
                     target[rows, :] = target[rows, :] + value
             return carry
 
-        lax.fori_loop(0, groups_x, scatter, 0)
+        lax.fori_loop(0, parts, scatter, 0)
 
         def combine(slab_at, carry):
             for tile in range(pairs_slab):
@@ -544,21 +535,91 @@
     lax.fori_loop(0, pairs, finish, 0)
 
 
-def packed_inputs(potential, projectors, extent, coupling):
+def pack_kernel(my_first, extent, coupling, potential, projectors, out):
     atoms = projectors.shape[0]
-    cells = jnp.arange(B, dtype=jnp.int32)
-    limit = extent[:, None, None, None]
-    inside = (
-        (cells[None, :, None, None] < limit)
-        & (cells[None, None, :, None] < limit)
-        & (cells[None, None, None, :] < limit)
-    )
-    masked = jnp.where(
-        inside.reshape(atoms, 1, B * B * B), projectors * jnp.sqrt(coupling)[:, :, None], 0.0
-    ).reshape(atoms // SUB, SUB, 2, 2, B * B, B)
-    masked = masked.transpose(0, 2, 1, 5, 3, 4).reshape(atoms // SUB * 2 * B, SUB, LANE)
-    shaped = potential.reshape(HALF, 2, HALF).transpose(2, 1, 0).reshape(SUB, SUB, LANE)
-    return jnp.concatenate([shaped, masked], axis=0)
+    f32, bf16 = jnp.float32, jnp.bfloat16
+    lane = lax.broadcasted_iota(jnp.int32, (SUB, LANE), 1)
+    row = lax.broadcasted_iota(jnp.int32, (SUB, LANE), 0)
+    lower = lane < HALF
+
+    flat = potential[...].reshape(HALF, LANE)
+    turned = jnp.concatenate([flat, flat], axis=0).T
+    low = lax.broadcasted_iota(jnp.int32, (HALF, LANE), 1) < HALF
+    out[:SUB] = jnp.where(low, turned[:HALF], turned[HALF:]).reshape(SUB, SUB, LANE)
+
+    cells = projectors.shape[2]
+    own_row = lax.broadcasted_iota(jnp.int32, (SUB, cells), 1) % B
+    own_row = own_row == lax.broadcasted_iota(jnp.int32, (SUB, cells), 0)
+    sides = []
+    for kh in range(2):
+        parts = []
+        for kp in range(2):
+            for atom in range(atoms):
+                line = projectors[atom, 2 * kp + kh : 2 * kp + kh + 1, :]
+                parts.append(jnp.where(own_row, jnp.broadcast_to(line, (SUB, cells)), 0.0))
+        sides.append(jnp.concatenate(parts, axis=0))
+    value = jnp.concatenate(sides, axis=1)
+    source = lax.broadcasted_iota(jnp.int32, (2 * cells, LANE), 0) // B
+    hot = source == lax.broadcasted_iota(jnp.int32, (2 * cells, LANE), 1)
+    hot = hot.astype(f32).astype(bf16)
+    high = value.astype(bf16)
+    rest = value - high.astype(f32)
+    mid = rest.astype(bf16)
+    small = (rest - mid.astype(f32)).astype(bf16)
+    moved = (mxu(high, hot) + mxu(mid, hot)) + mxu(small, hot)
+
+    reach = jnp.maximum(jnp.maximum((lane >> 3) & (B - 1), lane & (B - 1)), row)
+    for kp in range(2):
+        for atom in range(atoms):
+            at = my_first[0] + atom
+            scale = jnp.sqrt(
+                jnp.where(lower, coupling[2 * kp, at], coupling[2 * kp + 1, at])
+            )
+            number = kp * atoms + atom
+            part = moved[number * SUB : (number + 1) * SUB]
+            group, j = atom // SUB, atom % SUB
+            out[SUB + (group * 2 + kp) * SUB + j] = jnp.where(
+                reach < extent[at], part * scale, 0.0
+            )
+
+
+def packed_inputs(my_first, extent, coupling, potential, projectors, interpret=False):
+    vmem = pl.BlockSpec(memory_space=pltpu.VMEM)
+    smem = pl.BlockSpec(memory_space=pltpu.SMEM)
+    atoms = projectors.shape[0]
+    return pl.pallas_call(
+        pack_kernel,
+        out_shape=jax.ShapeDtypeStruct((SUB + 2 * atoms, SUB, LANE), jnp.float32),
+        in_specs=[smem] * 3 + [vmem] * 2,
+        out_specs=vmem,
+        compiler_params=pltpu.CompilerParams(vmem_limit_bytes=8 * 1024 * 1024),
+        interpret=interpret,
+    )(my_first, extent, coupling.T, potential, projectors)
+
+
+def weights_kernel(plane_in, depth_in, plane, depth, sems):
+    loads = [
+        pltpu.make_async_copy(plane_in, plane, sems.at[0]),
+        pltpu.make_async_copy(depth_in, depth, sems.at[1]),
+    ]
+    for load in loads:
+        load.start()
+    for load in loads:
+        load.wait()
+
+
+def weights_call(groups, interpret=False):
+    plane = jnp.asarray(plane_weights(groups[1]))
+    depth = jnp.asarray(depth_weights(groups[2]))
+    return pl.pallas_call(
+        weights_kernel,
+        out_shape=[jax.ShapeDtypeStruct(part.shape, part.dtype) for part in (plane, depth)],
+        in_specs=[pl.BlockSpec(memory_space=pl.ANY)] * 2,
+        out_specs=[pl.BlockSpec(memory_space=pltpu.VMEM)] * 2,
+        scratch_shapes=[pltpu.SemaphoreType.DMA((2,))],
+        compiler_params=pltpu.CompilerParams(vmem_limit_bytes=4 * 1024 * 1024),
+        interpret=interpret,
+    )(plane, depth)
 
 
 def box_places(groups, owner, anchor):
@@ -568,19 +629,13 @@
     return place, column % 2
 
 
-def weights_of(groups):
-    return jnp.asarray(plane_weights(groups[1])), jnp.asarray(depth_weights(groups[2]))
-
-
-def first_call(groups, field, interpret=False):
+def first_call(groups, field, plane, depth, interpret=False):
     groups_x, groups_y, groups_z = groups
     span = groups_z * LANE
     cells = (groups_x * groups_y // 2 * span, LANE)
     slabs = (groups_x * span, groups_y * HALF)
-    plane, depth = weights_of(groups)
     vmem = pl.BlockSpec(memory_space=pltpu.VMEM)
     anywhere = pl.BlockSpec(memory_space=pl.ANY)
-    in_hbm = pl.BlockSpec(memory_space=pltpu.HBM)
     work = 2 * slabs[0] * slabs[1] * (9 * slabs[1] + 3 * span)
     return pl.pallas_call(
         functools.partial(first_kernel, groups),
@@ -588,17 +643,15 @@
             jax.ShapeDtypeStruct(cells, jnp.float32),
             jax.ShapeDtypeStruct(cells, jnp.float32),
         ],
-        in_specs=[anywhere, in_hbm, in_hbm],
+        in_specs=[anywhere, vmem, vmem],
         out_specs=[vmem] * 2,
         scratch_shapes=[
             pltpu.VMEM(cells, jnp.float32),
             pltpu.VMEM(slabs, jnp.bfloat16),
             pltpu.VMEM(slabs, jnp.bfloat16),
-            pltpu.VMEM(plane.shape, plane.dtype),
-            pltpu.VMEM(depth.shape, depth.dtype),
-            pltpu.SemaphoreType.DMA((3,)),
+            pltpu.SemaphoreType.DMA((1,)),
         ],
-        compiler_params=pltpu.CompilerParams(vmem_limit_bytes=16 * 1024 * 1024),
+        compiler_params=pltpu.CompilerParams(vmem_limit_bytes=12 * 1024 * 1024),
         cost_estimate=pl.CostEstimate(
             flops=work, bytes_accessed=4 * field.size * 4, transcendentals=0
         ),
@@ -606,40 +659,38 @@
     )(field.reshape(cells), plane, depth)
 
 
-def filter_call(groups, place, half, my_place, field, near, packs, interpret=False):
+def filter_call(
+    groups, place, half, my_place, field, near, packs, plane, depth, interpret=False
+):
     groups_x, groups_y, groups_z = groups
     columns = groups_x * groups_y
     atoms = place.shape[0]
-    plane, depth = weights_of(groups)
     vmem = pl.BlockSpec(memory_space=pltpu.VMEM)
     anywhere = pl.BlockSpec(memory_space=pl.ANY)
     smem = pl.BlockSpec(memory_space=pltpu.SMEM)
     slabs = (groups_x * groups_z * LANE, groups_y * HALF)
     work = 2 * slabs[0] * slabs[1] * (9 * slabs[1] + 3 * groups_z * LANE)
-    in_hbm = pl.BlockSpec(memory_space=pltpu.HBM)
     out = pl.pallas_call(
         functools.partial(filter_kernel, groups, atoms),
         out_shape=jax.ShapeDtypeStruct(field.shape, jnp.float32),
-        in_specs=[smem] * 3 + [vmem] * 2 + [anywhere] * len(packs) + [in_hbm] * 2,
+        in_specs=[smem] * 3 + [vmem] * 2 + [anywhere] * len(packs) + [vmem] * 2,
         out_specs=anywhere,
         scratch_shapes=[
             pltpu.VMEM(field.shape, jnp.float32),
             pltpu.VMEM(field.shape, jnp.float32),
             pltpu.VMEM(field.shape, jnp.float32),
             pltpu.VMEM(field.shape, jnp.float32),
-            pltpu.VMEM((atoms * 2, LANE), jnp.float32),
+            pltpu.VMEM((atoms * 2 + SUB, LANE), jnp.float32),
             pltpu.VMEM(slabs, jnp.bfloat16),
             pltpu.VMEM(slabs, jnp.bfloat16),
             pltpu.VMEM(near.shape, jnp.float32),
             pltpu.VMEM((columns * groups_z,) + packs[0].shape[1:], jnp.float32),
-            pltpu.VMEM(plane.shape, plane.dtype),
-            pltpu.VMEM(depth.shape, depth.dtype),
-            pltpu.SemaphoreType.DMA((3,)),
+            pltpu.SemaphoreType.DMA((1,)),
             pltpu.SemaphoreType.DMA((columns * groups_z,)),
             pltpu.SemaphoreType.DMA((columns // 2,)),
         ]
         + [pltpu.VMEM(field.shape, jnp.float32) for _ in range(SPARES)],
-        compiler_params=pltpu.CompilerParams(vmem_limit_bytes=22 * 1024 * 1024),
+        compiler_params=pltpu.CompilerParams(vmem_limit_bytes=20 * 1024 * 1024),
         cost_estimate=pl.CostEstimate(
             flops=3 * work, bytes_accessed=8 * field.size * 4, transcendentals=0
         ),
@@ -664,17 +715,18 @@
     atoms_own = projectors.shape[0]
     my_place = jnp.stack([lax.axis_index(axis) for axis in axes])
     me = (my_place[0] * groups[1] + my_place[1]) * groups_z + my_place[2]
-    extent = lax.dynamic_slice(box_extent, (me * atoms_own,), (atoms_own,))
-    own = lax.dynamic_slice(coupling, (me * atoms_own, 0), (atoms_own, NPROJ))
-    pack = packed_inputs(potential, projectors, extent, own)
+    pack = packed_inputs((me * atoms_own)[None], box_extent, coupling, potential, projectors)
     line = jnp.stack(hops(pack, "gx"))
-    orbitals, line = lax.optimization_barrier((orbitals, line))
+    place, half = box_places(groups, owner_rank, box_anchor[2])
+    plane, depth = weights_call(groups)
+    orbitals, line, place, half, plane, depth = lax.optimization_barrier(
+        (orbitals, line, place, half, plane, depth)
+    )
     crossed = [hops(piece, "gz") for piece in hops(line, "gy")]
     packs = [crossed[hop_y][hop_z] for hop_z in range(groups_z) for hop_y in range(groups[1])]
     field = lax.all_to_all(orbitals, axes, split_axis=0, concat_axis=0, tiled=True)
-    field, near = first_call(groups, field)
-    place, half = box_places(groups, owner_rank, box_anchor[2])
-    result = filter_call(groups, place, half, my_place, field, near, packs)
+    field, near = first_call(groups, field, plane, depth)
+    result = filter_call(groups, place, half, my_place, field, near, packs, plane, depth)
     filtered = lax.all_to_all(result, axes, split_axis=0, concat_axis=0, tiled=True)
     states = filtered.shape[0]
     flattened = filtered.reshape(states, -1)

time: 129 us -> 128 us (level)
  Pallas kernels: 24.2 us -> 28.5 us
  waiting for transfers between devices: 32.1 us -> 29.1 us
  local copies, waits for them, and re-layouts: 8.58 us -> 7.24 us
    pallas_call x1, Pallas kernels: 21.3 us -> 24.6 us  [filter_call(): pl.pallas_call(functools.partial(filter_kernel, groups, atoms), out_shape...]
    ppermute x10, waiting for transfers between devices: 32.1 us -> 29.1 us  [hops(): lax.ppermute(value, axis, [(i, (i + hop) % count) for i in range(count)])]
    unnamed x20 -> x15, local copies, waits for them, and re-layouts: 4.9 us -> 5.37 us
  transfers between devices with their start and end apart: 11 -> 11, of which waited for: 5 -> 4; matrix products, arithmetic and copies ran while one was open for 1% -> 1% of each run, Pallas kernels for 2% -> 2%
where the time goes in v9:
time: 128 us
  blocking collectives  43 us (34%)
  waiting for transfers between devices  29.1 us (23%)
  Pallas kernels  28.5 us (22%)
  starting transfers between devices  17.8 us (14%)
  local copies, waits for them, and re-layouts  7.24 us (6%)
    all_to_all x1, blocking collectives, state_body(): lax.all_to_all(result, axes, split_axis=0, concat_axis=0, tiled=True)  31.3 us
    ppermute x10, waiting for transfers between devices, hops(): lax.ppermute(value, axis, [(i, (i + hop) % count) for i in range(count)])  29.1 us
    pallas_call x1, Pallas kernels, filter_call(): pl.pallas_call(functools.partial(filter_kernel, groups, atoms), out_shape...  24.6 us
    ppermute x10, starting transfers between devices, hops(): lax.ppermute(value, axis, [(i, (i + hop) % count) for i in range(count)])  11.9 us
    all_to_all x1, blocking collectives, state_body(): lax.all_to_all(jnp.broadcast_to(quarter[None], (domains,) + quarter.shape...  11.7 us
    all_to_all x1, starting transfers between devices, state_body(): lax.all_to_all(orbitals, axes, split_axis=0, concat_axis=0, tiled=True)  5.85 us
    unnamed x15, local copies, waits for them, and re-layouts  5.37 us
    pallas_call x1, Pallas kernels, first_call(): pl.pallas_call(functools.partial(first_kernel, groups), out_shape=[jax.Sh...  2.64 us
  transfers between devices with their start and end apart: 11, of which 4 were waited for; matrix products, arithmetic and copies ran while one was open for 1% of the time, Pallas kernels for 2%

profile of v9, /device:TPU:0, one launch (start us, length us, event | category | flops | bytes accessed | tf_op | source)
XLA Modules:
  0.0 127.6 jit_solution(9034920884048815361)
XLA Ops:
  0.6 0.0 copy-start.4
  0.7 0.0 copy-start.5
  0.7 0.7 copy-done.4
  1.3 0.0 copy-done.5
  1.3 0.0 copy-start.2
  1.3 0.8 copy-done.2
  2.2 0.0 copy-start.3
  2.2 0.8 copy-done.3
  2.9 0.0 copy-start.6
  2.9 1.0 shard_map.104
  4.0 3.1 %collective-permute-start = (f32[24,8,128]{2,1,0:T(8,128)S(1)}, f32[24,8,128]{2,1,0:T(8,128)S(1)}, u32[]{:S(2)}, u32[]{:S(2)}) collective-permute-start(f32[24,8,128]{2,1,0:T(8,128)S(1)} %shard_map.104), channel_id=1, source_target_pairs={{0,8},{8,16},{16,24},{24,0},{1,9},{9,17},{17,25},{25,1},{2,10},{10... | collective-permute-start | bytes 294920 | tf_op jit(solution)/shard_map/ppermute | solution.py:705
  7.0 2.6 %collective-permute-start.1 = (f32[24,8,128]{2,1,0:T(8,128)S(1)}, f32[24,8,128]{2,1,0:T(8,128)S(1)}, u32[]{:S(2)}, u32[]{:S(2)}) collective-permute-start(f32[24,8,128]{2,1,0:T(8,128)S(1)} %shard_map.104), channel_id=1, source_target_pairs={{0,16},{8,24},{16,0},{24,8},{1,17},{9,25},{17,1},{25,9},{2,18},{10... | collective-permute-start | bytes 294920 | tf_op jit(solution)/shard_map/ppermute | solution.py:705
  9.6 1.3 %collective-permute-start.2 = (f32[24,8,128]{2,1,0:T(8,128)S(1)}, f32[24,8,128]{2,1,0:T(8,128)S(1)}, u32[]{:S(2)}, u32[]{:S(2)}) collective-permute-start(f32[24,8,128]{2,1,0:T(8,128)S(1)} %shard_map.104), channel_id=1, source_target_pairs={{0,24},{8,0},{16,8},{24,16},{1,25},{9,1},{17,9},{25,17},{2,26},{10... | collective-permute-start | bytes 294920 | tf_op jit(solution)/shard_map/ppermute | solution.py:705
  11.0 0.0 copy-done.6
  11.0 0.7 slice.3
  11.7 0.0 copy-start
  11.7 1.1 copy-done
  12.8 0.0 copy-start.1
  12.8 1.0 copy-done.1
  13.8 0.3 shard_map.105
  14.1 0.0 collective-permute-done
  14.1 2.1 %collective-permute-done.1 = f32[24,8,128]{2,1,0:T(8,128)S(1)} collective-permute-done((f32[24,8,128]{2,1,0:T(8,128)S(1)}, f32[24,8,128]{2,1,0:T(8,128)S(1)}, u32[]{:S(2)}, u32[]{:S(2)}) %collective-permute-start.1) | collective-permute-done | bytes 98336 | tf_op jit(solution)/shard_map/ppermute | solution.py:705
  16.2 0.0 collective-permute-done.2
  16.3 5.8 %all-to-all-start = ((f32[32,8,8,128]{3,2,1,0:T(8,128)}), f32[32,8,8,128]{3,2,1,0:T(8,128)S(1)}, u32[]{:S(2)}, u32[]{:S(2)}) async-start(f32[32,8,8,128]{3,2,1,0:T(8,128)} %param.9), calls=%async_computation | async-start | bytes 2097152 | tf_op jit(solution)/shard_map/all_to_all | solution.py:727
  22.1 1.8 %collective-permute-start.3 = (f32[4,24,8,128]{3,2,1,0:T(8,128)S(1)}, f32[4,24,8,128]{3,2,1,0:T(8,128)S(1)}, u32[]{:S(2)}, u32[]{:S(2)}) collective-permute-start(f32[4,24,8,128]{3,2,1,0:T(8,128)S(1)} %pad_maximum_fusion.refs_2_), channel_id=1, source_target_pairs={{0,2},{2,4},{4,6},{6,0},{1,3},{3,5},{5,7},{7,1},{8,10},{10,12},{12... | collective-permute-start | bytes 1179656 | tf_op jit(solution)/shard_map/ppermute | solution.py:705
  24.0 1.5 %collective-permute-start.4 = (f32[4,24,8,128]{3,2,1,0:T(8,128)S(1)}, f32[4,24,8,128]{3,2,1,0:T(8,128)S(1)}, u32[]{:S(2)}, u32[]{:S(2)}) collective-permute-start(f32[4,24,8,128]{3,2,1,0:T(8,128)S(1)} %pad_maximum_fusion.refs_2_), channel_id=1, source_target_pairs={{0,4},{2,6},{4,0},{6,2},{1,5},{3,7},{5,1},{7,3},{8,12},{10,14},{12... | collective-permute-start | bytes 1179656 | tf_op jit(solution)/shard_map/ppermute | solution.py:705
  25.4 1.5 %collective-permute-start.5 = (f32[4,24,8,128]{3,2,1,0:T(8,128)S(1)}, f32[4,24,8,128]{3,2,1,0:T(8,128)}, u32[]{:S(2)}, u32[]{:S(2)}) collective-permute-start(f32[4,24,8,128]{3,2,1,0:T(8,128)S(1)} %pad_maximum_fusion.refs_2_), channel_id=1, source_target_pairs={{0,6},{2,0},{4,2},{6,4},{1,7},{3,1},{5,3},{7,5},{8,14},{10,8},{12,... | collective-permute-start | bytes 1179656 | tf_op jit(solution)/shard_map/ppermute | solution.py:705
  26.9 0.0 collective-permute-start.6
  26.9 18.6 %collective-permute-done.3.refs_3_ = f32[4,24,8,128]{3,2,1,0:T(8,128)S(1)} collective-permute-done((f32[4,24,8,128]{3,2,1,0:T(8,128)S(1)}, f32[4,24,8,128]{3,2,1,0:T(8,128)S(1)}, u32[]{:S(2)}, u32[]{:S(2)}) %collective-permute-start.3) | collective-permute-done | bytes 393248 | tf_op jit(solution)/shard_map/ppermute | solution.py:705
  45.5 0.0 collective-permute-start.7
  45.5 7.6 %collective-permute-done.4.refs_4_ = f32[4,24,8,128]{3,2,1,0:T(8,128)S(1)} collective-permute-done((f32[4,24,8,128]{3,2,1,0:T(8,128)S(1)}, f32[4,24,8,128]{3,2,1,0:T(8,128)S(1)}, u32[]{:S(2)}, u32[]{:S(2)}) %collective-permute-start.4) | collective-permute-done | bytes 393248 | tf_op jit(solution)/shard_map/ppermute | solution.py:705
  53.1 0.1 collective-permute-start.8
  53.2 0.7 collective-permute-done.5.refs_5_
  54.0 0.0 collective-permute-start.9
  54.0 0.1 pad_add_fusion.my_place
  54.1 0.0 all-to-all-done
  54.1 2.6 %shard_map.106 = (f32[2048,128]{1,0:T(8,128)S(1)}, f32[2048,128]{1,0:T(8,128)S(1)}) custom-call(f32[2048,128]{1,0:T(8,128)S(1)} %bitcast.24, bf16[1536,256]{1,0:T(8,128)(2,1)S(1)} %get-tuple-element.17.refs_1_.refs_10_, bf16[256,768]{1,0:T(8,128)(2,1)S(1)} %get-tuple-element.18.refs_2_.refs_11_), custom_call_target="tpu_custom_call" | custom-call | flops 1610612736 | bytes 4194304 | tf_op jit(solution)/shard_map/pallas_call | solution.py:640
  56.7 0.0 collective-permute-done.6.refs_6_
  56.7 0.0 collective-permute-done.7.refs_7_
  56.7 0.0 collective-permute-done.8.refs_8_
  56.7 0.0 collective-permute-done.9.refs_9_
  56.8 24.6 %shard_map.107 = f32[2048,128]{1,0:T(8,128)S(1)} custom-call(s32[256]{0:T(256)S(1)} %multiply_add_fusion.place, s32[256]{0:T(256)S(1)} %get-tuple-element.15.half, s32[3]{0:T(128)S(1)} %pad_add_fusion.my_place, f32[2048,128]{1,0:T(8,128)S(1)} %get-tuple-element.19.refs_0_, f32[2048,128]{1,0:T(8,128)S(1)} %get-tuple-element.20.refs_1_, ...), custom_call_target="tpu_custom_call" | custom-call | flops 4831838208 | bytes 8388608 | tf_op jit(solution)/shard_map/pallas_call | solution.py:673
  81.4 31.3 %all_to_all.15 = f32[32,8,8,128]{3,2,1,0:T(8,128)S(1)} all-to-all(f32[32,8,8,128]{3,2,1,0:T(8,128)S(1)} %bitcast.25), channel_id=1, replica_groups=mesh['gx'=4,'gy'=4,'gz'=2] {'gx','gy','gz'}, dimensions={0} | all-to-all | bytes 2097152 | tf_op jit(solution)/shard_map/all_to_all | solution.py:730
  112.7 0.2 dot_general.5
  112.9 0.2 reshape.26
  113.1 1.0 convolution_bitcast_fusion
  114.1 0.1 broadcast_in_dim.11
  114.2 11.7 %all_to_all.16 = f32[32,8,128]{2,1,0:T(8,128)S(1)} all-to-all(f32[32,8,128]{2,1,0:T(8,128)S(1)} %broadcast_in_dim.12), channel_id=1, replica_groups=mesh['gx'=4,'gy'=4,'gz'=2] {'gx','gy','gz'}, dimensions={0} | all-to-all | bytes 262144 | tf_op jit(solution)/shard_map/all_to_all | solution.py:735
  125.9 0.1 div.38
  126.0 0.6 copy.17
  126.6 1.0 copy.19
  (7 shorter events, 0.1 us)
Async XLA Ops:
  0.6 0.7 copy-start.4
  0.7 0.7 copy-start.5
  1.3 0.8 copy-start.2
  2.2 0.8 copy-start.3
  2.9 8.0 %copy-start.6 = (s32[256]{0:T(256)S(1)}, s32[256]{0:T(256)}, u32[]{:S(2)}) copy-start(s32[256]{0:T(256)} %param.12) | copy-start | bytes 3076
  4.0 10.1 %collective-permute-start = (f32[24,8,128]{2,1,0:T(8,128)S(1)}, f32[24,8,128]{2,1,0:T(8,128)S(1)}, u32[]{:S(2)}, u32[]{:S(2)}) collective-permute-start(f32[24,8,128]{2,1,0:T(8,128)S(1)} %shard_map.104), channel_id=1, source_target_pairs={{0,8},{8,16},{16,24},{24,0},{1,9},{9,17},{17,25},{25,1},{2,10},{10... | collective-permute-start | bytes 294920 | tf_op jit(solution)/shard_map/ppermute | solution.py:705
  7.0 9.2 %collective-permute-start.1 = (f32[24,8,128]{2,1,0:T(8,128)S(1)}, f32[24,8,128]{2,1,0:T(8,128)S(1)}, u32[]{:S(2)}, u32[]{:S(2)}) collective-permute-start(f32[24,8,128]{2,1,0:T(8,128)S(1)} %shard_map.104), channel_id=1, source_target_pairs={{0,16},{8,24},{16,0},{24,8},{1,17},{9,25},{17,1},{25,9},{2,18},{10... | collective-permute-start | bytes 294920 | tf_op jit(solution)/shard_map/ppermute | solution.py:705
  9.6 6.6 %collective-permute-start.2 = (f32[24,8,128]{2,1,0:T(8,128)S(1)}, f32[24,8,128]{2,1,0:T(8,128)S(1)}, u32[]{:S(2)}, u32[]{:S(2)}) collective-permute-start(f32[24,8,128]{2,1,0:T(8,128)S(1)} %shard_map.104), channel_id=1, source_target_pairs={{0,24},{8,0},{16,8},{24,16},{1,25},{9,1},{17,9},{25,17},{2,26},{10... | collective-permute-start | bytes 294920 | tf_op jit(solution)/shard_map/ppermute | solution.py:705
  11.7 1.1 copy-start
  12.8 1.0 copy-start.1
  16.3 37.8 %all-to-all-start = ((f32[32,8,8,128]{3,2,1,0:T(8,128)}), f32[32,8,8,128]{3,2,1,0:T(8,128)S(1)}, u32[]{:S(2)}, u32[]{:S(2)}) async-start(f32[32,8,8,128]{3,2,1,0:T(8,128)} %param.9), calls=%async_computation | async-start | bytes 2097152 | tf_op jit(solution)/shard_map/all_to_all | solution.py:727
  22.1 23.3 %collective-permute-start.3 = (f32[4,24,8,128]{3,2,1,0:T(8,128)S(1)}, f32[4,24,8,128]{3,2,1,0:T(8,128)S(1)}, u32[]{:S(2)}, u32[]{:S(2)}) collective-permute-start(f32[4,24,8,128]{3,2,1,0:T(8,128)S(1)} %pad_maximum_fusion.refs_2_), channel_id=1, source_target_pairs={{0,2},{2,4},{4,6},{6,0},{1,3},{3,5},{5,7},{7,1},{8,10},{10,12},{12... | collective-permute-start | bytes 1179656 | tf_op jit(solution)/shard_map/ppermute | solution.py:705
  24.0 29.1 %collective-permute-start.4 = (f32[4,24,8,128]{3,2,1,0:T(8,128)S(1)}, f32[4,24,8,128]{3,2,1,0:T(8,128)S(1)}, u32[]{:S(2)}, u32[]{:S(2)}) collective-permute-start(f32[4,24,8,128]{3,2,1,0:T(8,128)S(1)} %pad_maximum_fusion.refs_2_), channel_id=1, source_target_pairs={{0,4},{2,6},{4,0},{6,2},{1,5},{3,7},{5,1},{7,3},{8,12},{10,14},{12... | collective-permute-start | bytes 1179656 | tf_op jit(solution)/shard_map/ppermute | solution.py:705
  25.4 28.6 %collective-permute-start.5 = (f32[4,24,8,128]{3,2,1,0:T(8,128)S(1)}, f32[4,24,8,128]{3,2,1,0:T(8,128)}, u32[]{:S(2)}, u32[]{:S(2)}) collective-permute-start(f32[4,24,8,128]{3,2,1,0:T(8,128)S(1)} %pad_maximum_fusion.refs_2_), channel_id=1, source_target_pairs={{0,6},{2,0},{4,2},{6,4},{1,7},{3,1},{5,3},{7,5},{8,14},{10,8},{12,... | collective-permute-start | bytes 1179656 | tf_op jit(solution)/shard_map/ppermute | solution.py:705
  26.9 29.8 %collective-permute-start.6 = (f32[4,24,8,128]{3,2,1,0:T(8,128)S(1)}, f32[4,24,8,128]{3,2,1,0:T(8,128)}, u32[]{:S(2)}, u32[]{:S(2)}) collective-permute-start(f32[4,24,8,128]{3,2,1,0:T(8,128)S(1)} %pad_maximum_fusion.refs_2_), channel_id=1, source_target_pairs={{0,1},{1,0},{2,3},{3,2},{4,5},{5,4},{6,7},{7,6},{8,9},{9,8},{10,11... | collective-permute-start | bytes 1179656 | tf_op jit(solution)/shard_map/ppermute | solution.py:705
  45.5 11.3 %collective-permute-start.7 = (f32[4,24,8,128]{3,2,1,0:T(8,128)S(1)}, f32[4,24,8,128]{3,2,1,0:T(8,128)}, u32[]{:S(2)}, u32[]{:S(2)}) collective-permute-start(f32[4,24,8,128]{3,2,1,0:T(8,128)S(1)} %collective-permute-done.3.refs_3_), channel_id=1, source_target_pairs={{0,1},{1,0},{2,3},{3,2},{4,5},{5,4},{6,7},{7,6},{8,9},{9,8},{10,11... | collective-permute-start | bytes 1179656 | tf_op jit(solution)/shard_map/ppermute | solution.py:705
  53.1 3.6 %collective-permute-start.8 = (f32[4,24,8,128]{3,2,1,0:T(8,128)S(1)}, f32[4,24,8,128]{3,2,1,0:T(8,128)}, u32[]{:S(2)}, u32[]{:S(2)}) collective-permute-start(f32[4,24,8,128]{3,2,1,0:T(8,128)S(1)} %collective-permute-done.4.refs_4_), channel_id=1, source_target_pairs={{0,1},{1,0},{2,3},{3,2},{4,5},{5,4},{6,7},{7,6},{8,9},{9,8},{10,11... | collective-permute-start | bytes 1179656 | tf_op jit(solution)/shard_map/ppermute | solution.py:705
  54.0 2.8 %collective-permute-start.9 = (f32[4,24,8,128]{3,2,1,0:T(8,128)}, f32[4,24,8,128]{3,2,1,0:T(8,128)}, u32[]{:S(2)}, u32[]{:S(2)}) collective-permute-start(f32[4,24,8,128]{3,2,1,0:T(8,128)} %collective-permute-done.5.refs_5_), channel_id=1, source_target_pairs={{0,1},{1,0},{2,3},{3,2},{4,5},{5,4},{6,7},{7,6},{8,9},{9,8},{10,11... | collective-permute-start | bytes 1179656 | tf_op jit(solution)/shard_map/ppermute | solution.py:705

commit v10 on v9

--- a/solution.py
+++ b/solution.py
@@ -234,11 +234,7 @@
     return values[0]
 
 
-def spread_row(ref, at):
-    return ref[pl.ds(at, SUB, stride=0), :]
-
-
-SPARES = 3
+SPARES = 1
 TALL = 2 * SUB
 
 
@@ -415,25 +411,17 @@
         .astype(jnp.bfloat16)
     )
 
-    share = 4 if domains % 4 == 0 else 1
-    parts = domains // share
-
-    def part_groups(part):
+    def part_groups(part, share):
         for number in range(share):
             for inner in range(per_device):
                 yield part * share + number, inner
 
     def apply_step(cur, prev, new, alpha, beta, first, last):
-        def product(chunk_at, carry):
-            slabs = [chunk_at * chunk + number for number in range(chunk)]
-            lay_products(groups, high_buf, low_buf, plane, depth, slabs, near)
-            return carry
-
-        if not first:
-            lax.fori_loop(0, groups_x // chunk, product, 0)
-
         def project(part, carry):
-            for device, inner in part_groups(part):
+            if not first:
+                slabs = [part * chunk + number for number in range(chunk)]
+                lay_products(groups, high_buf, low_buf, plane, depth, slabs, near)
+            for device, inner in part_groups(part, domains // (groups_x // chunk)):
                 group = device * per_device + inner
                 terms = ([], [])
                 for j in range(SUB):
@@ -448,19 +436,22 @@
                     coeffs[pl.ds(at, SUB), :] = row_sums(terms[kp])
             return carry
 
-        lax.fori_loop(0, parts, project, 0)
-
-        high, low = split_pair(coeffs[: 2 * atoms, :])
-        coeffs[: 2 * atoms, :] = mxu(high, ones) + mxu(low, ones)
+        lax.fori_loop(0, groups_x // chunk, project, 0)
+
+        high, low = split_pair(coeffs[...])
+        coeffs[...] = mxu(high, ones) + mxu(low, ones)
 
         def scatter(part, carry):
-            for device, inner in part_groups(part):
+            for device, inner in part_groups(part, domains // groups_x):
                 group = device * per_device + inner
-                bases = [pl.multiple_of((group * 2 + kp) * SUB, SUB) for kp in range(2)]
+                weights = [
+                    coeffs[pl.ds(pl.multiple_of((group * 2 + kp) * SUB, SUB), SUB), :]
+                    for kp in range(2)
+                ]
                 for j in range(SUB):
                     atom = group * SUB + j
                     parts = [
-                        spread_row(coeffs, bases[kp] + j)
+                        jnp.broadcast_to(weights[kp][j : j + 1], (SUB, LANE))
                         * packs[device, SUB + (inner * 2 + kp) * SUB + j]
                         for kp in range(2)
                     ]
@@ -472,7 +463,7 @@
                     target[rows, :] = target[rows, :] + value
             return carry
 
-        lax.fori_loop(0, parts, scatter, 0)
+        lax.fori_loop(0, groups_x, scatter, 0)
 
         def combine(slab_at, carry):
             for tile in range(pairs_slab):
@@ -680,7 +671,7 @@
             pltpu.VMEM(field.shape, jnp.float32),
             pltpu.VMEM(field.shape, jnp.float32),
             pltpu.VMEM(field.shape, jnp.float32),
-            pltpu.VMEM((atoms * 2 + SUB, LANE), jnp.float32),
+            pltpu.VMEM((atoms * 2, LANE), jnp.float32),
             pltpu.VMEM(slabs, jnp.bfloat16),
             pltpu.VMEM(slabs, jnp.bfloat16),
             pltpu.VMEM(near.shape, jnp.float32),

time: 128 us -> 124 us (0.969)
  Pallas kernels: 28.5 us -> 24.3 us
    pallas_call x1, Pallas kernels: 24.6 us -> 20.4 us  [filter_call(): pl.pallas_call(functools.partial(filter_kernel, groups, atoms), out_shape...]
where the time goes in v10:
time: 124 us; the launch traced here: 123 us
  blocking collectives  43 us (35%)
  waiting for transfers between devices  29.1 us (23%)
  Pallas kernels  24.3 us (20%)
  starting transfers between devices  17.8 us (14%)
  local copies, waits for them, and re-layouts  7.24 us (6%)
    all_to_all x1, blocking collectives, state_body(): lax.all_to_all(result, axes, split_axis=0, concat_axis=0, tiled=True)  31.3 us
    ppermute x10, waiting for transfers between devices, hops(): lax.ppermute(value, axis, [(i, (i + hop) % count) for i in range(count)])  29.1 us
    pallas_call x1, Pallas kernels, filter_call(): pl.pallas_call(functools.partial(filter_kernel, groups, atoms), out_shape...  20.4 us
    ppermute x10, starting transfers between devices, hops(): lax.ppermute(value, axis, [(i, (i + hop) % count) for i in range(count)])  11.9 us
    all_to_all x1, blocking collectives, state_body(): lax.all_to_all(jnp.broadcast_to(quarter[None], (domains,) + quarter.shape...  11.7 us
    all_to_all x1, starting transfers between devices, state_body(): lax.all_to_all(orbitals, axes, split_axis=0, concat_axis=0, tiled=True)  5.85 us
    unnamed x15, local copies, waits for them, and re-layouts  5.37 us
    pallas_call x1, Pallas kernels, first_call(): pl.pallas_call(functools.partial(first_kernel, groups), out_shape=[jax.Sh...  2.64 us
  transfers between devices with their start and end apart: 11, of which 4 were waited for; matrix products, arithmetic and copies ran while one was open for 1% of the time, Pallas kernels for 2%

profile of v10, /device:TPU:0, one launch (start us, length us, event | category | flops | bytes accessed | tf_op | source)
XLA Modules:
  0.0 123.3 jit_solution(17583889183595108551)
XLA Ops:
  0.6 0.0 copy-start.4
  0.7 0.0 copy-start.5
  0.7 0.7 copy-done.4
  1.3 0.0 copy-done.5
  1.3 0.0 copy-start.2
  1.3 0.8 copy-done.2
  2.2 0.0 copy-start.3
  2.2 0.8 copy-done.3
  2.9 0.0 copy-start.6
  2.9 1.0 shard_map.104
  4.0 3.1 %collective-permute-start = (f32[24,8,128]{2,1,0:T(8,128)S(1)}, f32[24,8,128]{2,1,0:T(8,128)S(1)}, u32[]{:S(2)}, u32[]{:S(2)}) collective-permute-start(f32[24,8,128]{2,1,0:T(8,128)S(1)} %shard_map.104), channel_id=1, source_target_pairs={{0,8},{8,16},{16,24},{24,0},{1,9},{9,17},{17,25},{25,1},{2,10},{10... | collective-permute-start | bytes 294920 | tf_op jit(solution)/shard_map/ppermute | solution.py:696
  7.0 2.6 %collective-permute-start.1 = (f32[24,8,128]{2,1,0:T(8,128)S(1)}, f32[24,8,128]{2,1,0:T(8,128)S(1)}, u32[]{:S(2)}, u32[]{:S(2)}) collective-permute-start(f32[24,8,128]{2,1,0:T(8,128)S(1)} %shard_map.104), channel_id=1, source_target_pairs={{0,16},{8,24},{16,0},{24,8},{1,17},{9,25},{17,1},{25,9},{2,18},{10... | collective-permute-start | bytes 294920 | tf_op jit(solution)/shard_map/ppermute | solution.py:696
  9.6 1.3 %collective-permute-start.2 = (f32[24,8,128]{2,1,0:T(8,128)S(1)}, f32[24,8,128]{2,1,0:T(8,128)S(1)}, u32[]{:S(2)}, u32[]{:S(2)}) collective-permute-start(f32[24,8,128]{2,1,0:T(8,128)S(1)} %shard_map.104), channel_id=1, source_target_pairs={{0,24},{8,0},{16,8},{24,16},{1,25},{9,1},{17,9},{25,17},{2,26},{10... | collective-permute-start | bytes 294920 | tf_op jit(solution)/shard_map/ppermute | solution.py:696
  11.0 0.0 copy-done.6
  11.0 0.7 slice.3
  11.7 0.0 copy-start
  11.7 1.1 copy-done
  12.8 0.0 copy-start.1
  12.8 1.0 copy-done.1
  13.8 0.3 shard_map.105
  14.1 0.0 collective-permute-done
  14.1 2.1 %collective-permute-done.1 = f32[24,8,128]{2,1,0:T(8,128)S(1)} collective-permute-done((f32[24,8,128]{2,1,0:T(8,128)S(1)}, f32[24,8,128]{2,1,0:T(8,128)S(1)}, u32[]{:S(2)}, u32[]{:S(2)}) %collective-permute-start.1) | collective-permute-done | bytes 98336 | tf_op jit(solution)/shard_map/ppermute | solution.py:696
  16.2 0.0 collective-permute-done.2
  16.3 5.8 %all-to-all-start = ((f32[32,8,8,128]{3,2,1,0:T(8,128)}), f32[32,8,8,128]{3,2,1,0:T(8,128)S(1)}, u32[]{:S(2)}, u32[]{:S(2)}) async-start(f32[32,8,8,128]{3,2,1,0:T(8,128)} %param.9), calls=%async_computation | async-start | bytes 2097152 | tf_op jit(solution)/shard_map/all_to_all | solution.py:718
  22.1 1.8 %collective-permute-start.3 = (f32[4,24,8,128]{3,2,1,0:T(8,128)S(1)}, f32[4,24,8,128]{3,2,1,0:T(8,128)S(1)}, u32[]{:S(2)}, u32[]{:S(2)}) collective-permute-start(f32[4,24,8,128]{3,2,1,0:T(8,128)S(1)} %pad_maximum_fusion.refs_2_), channel_id=1, source_target_pairs={{0,2},{2,4},{4,6},{6,0},{1,3},{3,5},{5,7},{7,1},{8,10},{10,12},{12... | collective-permute-start | bytes 1179656 | tf_op jit(solution)/shard_map/ppermute | solution.py:696
  24.0 1.5 %collective-permute-start.4 = (f32[4,24,8,128]{3,2,1,0:T(8,128)S(1)}, f32[4,24,8,128]{3,2,1,0:T(8,128)S(1)}, u32[]{:S(2)}, u32[]{:S(2)}) collective-permute-start(f32[4,24,8,128]{3,2,1,0:T(8,128)S(1)} %pad_maximum_fusion.refs_2_), channel_id=1, source_target_pairs={{0,4},{2,6},{4,0},{6,2},{1,5},{3,7},{5,1},{7,3},{8,12},{10,14},{12... | collective-permute-start | bytes 1179656 | tf_op jit(solution)/shard_map/ppermute | solution.py:696
  25.4 1.5 %collective-permute-start.5 = (f32[4,24,8,128]{3,2,1,0:T(8,128)S(1)}, f32[4,24,8,128]{3,2,1,0:T(8,128)}, u32[]{:S(2)}, u32[]{:S(2)}) collective-permute-start(f32[4,24,8,128]{3,2,1,0:T(8,128)S(1)} %pad_maximum_fusion.refs_2_), channel_id=1, source_target_pairs={{0,6},{2,0},{4,2},{6,4},{1,7},{3,1},{5,3},{7,5},{8,14},{10,8},{12,... | collective-permute-start | bytes 1179656 | tf_op jit(solution)/shard_map/ppermute | solution.py:696
  26.9 0.0 collective-permute-start.6
  26.9 18.6 %collective-permute-done.3.refs_3_ = f32[4,24,8,128]{3,2,1,0:T(8,128)S(1)} collective-permute-done((f32[4,24,8,128]{3,2,1,0:T(8,128)S(1)}, f32[4,24,8,128]{3,2,1,0:T(8,128)S(1)}, u32[]{:S(2)}, u32[]{:S(2)}) %collective-permute-start.3) | collective-permute-done | bytes 393248 | tf_op jit(solution)/shard_map/ppermute | solution.py:696
  45.5 0.0 collective-permute-start.7
  45.5 7.6 %collective-permute-done.4.refs_4_ = f32[4,24,8,128]{3,2,1,0:T(8,128)S(1)} collective-permute-done((f32[4,24,8,128]{3,2,1,0:T(8,128)S(1)}, f32[4,24,8,128]{3,2,1,0:T(8,128)S(1)}, u32[]{:S(2)}, u32[]{:S(2)}) %collective-permute-start.4) | collective-permute-done | bytes 393248 | tf_op jit(solution)/shard_map/ppermute | solution.py:696
  53.1 0.1 collective-permute-start.8
  53.2 0.7 collective-permute-done.5.refs_5_
  54.0 0.0 collective-permute-start.9
  54.0 0.1 pad_add_fusion.my_place
  54.1 0.0 all-to-all-done
  54.1 2.6 %shard_map.106 = (f32[2048,128]{1,0:T(8,128)S(1)}, f32[2048,128]{1,0:T(8,128)S(1)}) custom-call(f32[2048,128]{1,0:T(8,128)S(1)} %bitcast.24, bf16[1536,256]{1,0:T(8,128)(2,1)S(1)} %get-tuple-element.17.refs_1_.refs_10_, bf16[256,768]{1,0:T(8,128)(2,1)S(1)} %get-tuple-element.18.refs_2_.refs_11_), custom_call_target="tpu_custom_call" | custom-call | flops 1610612736 | bytes 4194304 | tf_op jit(solution)/shard_map/pallas_call | solution.py:631
  56.7 0.0 collective-permute-done.6.refs_6_
  56.7 0.0 collective-permute-done.7.refs_7_
  56.7 0.0 collective-permute-done.8.refs_8_
  56.7 0.0 collective-permute-done.9.refs_9_
  56.8 20.4 %shard_map.107 = f32[2048,128]{1,0:T(8,128)S(1)} custom-call(s32[256]{0:T(256)S(1)} %multiply_add_fusion.place, s32[256]{0:T(256)S(1)} %get-tuple-element.15.half, s32[3]{0:T(128)S(1)} %pad_add_fusion.my_place, f32[2048,128]{1,0:T(8,128)S(1)} %get-tuple-element.19.refs_0_, f32[2048,128]{1,0:T(8,128)S(1)} %get-tuple-element.20.refs_1_, ...), custom_call_target="tpu_custom_call" | custom-call | flops 4831838208 | bytes 8388608 | tf_op jit(solution)/shard_map/pallas_call | solution.py:664
  77.2 31.3 %all_to_all.15 = f32[32,8,8,128]{3,2,1,0:T(8,128)S(1)} all-to-all(f32[32,8,8,128]{3,2,1,0:T(8,128)S(1)} %bitcast.25), channel_id=1, replica_groups=mesh['gx'=4,'gy'=4,'gz'=2] {'gx','gy','gz'}, dimensions={0} | all-to-all | bytes 2097152 | tf_op jit(solution)/shard_map/all_to_all | solution.py:721
  108.5 0.2 dot_general.5
  108.7 0.2 reshape.26
  108.9 1.0 convolution_bitcast_fusion
  109.9 0.1 broadcast_in_dim.11
  110.0 11.7 %all_to_all.16 = f32[32,8,128]{2,1,0:T(8,128)S(1)} all-to-all(f32[32,8,128]{2,1,0:T(8,128)S(1)} %broadcast_in_dim.12), channel_id=1, replica_groups=mesh['gx'=4,'gy'=4,'gz'=2] {'gx','gy','gz'}, dimensions={0} | all-to-all | bytes 262144 | tf_op jit(solution)/shard_map/all_to_all | solution.py:726
  121.7 0.1 div.38
  121.8 0.6 copy.17
  122.4 1.0 copy.19
  (7 shorter events, 0.1 us)
Async XLA Ops:
  0.6 0.7 copy-start.4
  0.7 0.7 copy-start.5
  1.3 0.8 copy-start.2
  2.2 0.8 copy-start.3
  2.9 8.0 %copy-start.6 = (s32[256]{0:T(256)S(1)}, s32[256]{0:T(256)}, u32[]{:S(2)}) copy-start(s32[256]{0:T(256)} %param.12) | copy-start | bytes 3076
  4.0 10.1 %collective-permute-start = (f32[24,8,128]{2,1,0:T(8,128)S(1)}, f32[24,8,128]{2,1,0:T(8,128)S(1)}, u32[]{:S(2)}, u32[]{:S(2)}) collective-permute-start(f32[24,8,128]{2,1,0:T(8,128)S(1)} %shard_map.104), channel_id=1, source_target_pairs={{0,8},{8,16},{16,24},{24,0},{1,9},{9,17},{17,25},{25,1},{2,10},{10... | collective-permute-start | bytes 294920 | tf_op jit(solution)/shard_map/ppermute | solution.py:696
  7.0 9.2 %collective-permute-start.1 = (f32[24,8,128]{2,1,0:T(8,128)S(1)}, f32[24,8,128]{2,1,0:T(8,128)S(1)}, u32[]{:S(2)}, u32[]{:S(2)}) collective-permute-start(f32[24,8,128]{2,1,0:T(8,128)S(1)} %shard_map.104), channel_id=1, source_target_pairs={{0,16},{8,24},{16,0},{24,8},{1,17},{9,25},{17,1},{25,9},{2,18},{10... | collective-permute-start | bytes 294920 | tf_op jit(solution)/shard_map/ppermute | solution.py:696
  9.6 6.6 %collective-permute-start.2 = (f32[24,8,128]{2,1,0:T(8,128)S(1)}, f32[24,8,128]{2,1,0:T(8,128)S(1)}, u32[]{:S(2)}, u32[]{:S(2)}) collective-permute-start(f32[24,8,128]{2,1,0:T(8,128)S(1)} %shard_map.104), channel_id=1, source_target_pairs={{0,24},{8,0},{16,8},{24,16},{1,25},{9,1},{17,9},{25,17},{2,26},{10... | collective-permute-start | bytes 294920 | tf_op jit(solution)/shard_map/ppermute | solution.py:696
  11.7 1.1 copy-start
  12.8 1.0 copy-start.1
  16.3 37.8 %all-to-all-start = ((f32[32,8,8,128]{3,2,1,0:T(8,128)}), f32[32,8,8,128]{3,2,1,0:T(8,128)S(1)}, u32[]{:S(2)}, u32[]{:S(2)}) async-start(f32[32,8,8,128]{3,2,1,0:T(8,128)} %param.9), calls=%async_computation | async-start | bytes 2097152 | tf_op jit(solution)/shard_map/all_to_all | solution.py:718
  22.1 23.3 %collective-permute-start.3 = (f32[4,24,8,128]{3,2,1,0:T(8,128)S(1)}, f32[4,24,8,128]{3,2,1,0:T(8,128)S(1)}, u32[]{:S(2)}, u32[]{:S(2)}) collective-permute-start(f32[4,24,8,128]{3,2,1,0:T(8,128)S(1)} %pad_maximum_fusion.refs_2_), channel_id=1, source_target_pairs={{0,2},{2,4},{4,6},{6,0},{1,3},{3,5},{5,7},{7,1},{8,10},{10,12},{12... | collective-permute-start | bytes 1179656 | tf_op jit(solution)/shard_map/ppermute | solution.py:696
  24.0 29.1 %collective-permute-start.4 = (f32[4,24,8,128]{3,2,1,0:T(8,128)S(1)}, f32[4,24,8,128]{3,2,1,0:T(8,128)S(1)}, u32[]{:S(2)}, u32[]{:S(2)}) collective-permute-start(f32[4,24,8,128]{3,2,1,0:T(8,128)S(1)} %pad_maximum_fusion.refs_2_), channel_id=1, source_target_pairs={{0,4},{2,6},{4,0},{6,2},{1,5},{3,7},{5,1},{7,3},{8,12},{10,14},{12... | collective-permute-start | bytes 1179656 | tf_op jit(solution)/shard_map/ppermute | solution.py:696
  25.4 28.6 %collective-permute-start.5 = (f32[4,24,8,128]{3,2,1,0:T(8,128)S(1)}, f32[4,24,8,128]{3,2,1,0:T(8,128)}, u32[]{:S(2)}, u32[]{:S(2)}) collective-permute-start(f32[4,24,8,128]{3,2,1,0:T(8,128)S(1)} %pad_maximum_fusion.refs_2_), channel_id=1, source_target_pairs={{0,6},{2,0},{4,2},{6,4},{1,7},{3,1},{5,3},{7,5},{8,14},{10,8},{12,... | collective-permute-start | bytes 1179656 | tf_op jit(solution)/shard_map/ppermute | solution.py:696
  26.9 29.8 %collective-permute-start.6 = (f32[4,24,8,128]{3,2,1,0:T(8,128)S(1)}, f32[4,24,8,128]{3,2,1,0:T(8,128)}, u32[]{:S(2)}, u32[]{:S(2)}) collective-permute-start(f32[4,24,8,128]{3,2,1,0:T(8,128)S(1)} %pad_maximum_fusion.refs_2_), channel_id=1, source_target_pairs={{0,1},{1,0},{2,3},{3,2},{4,5},{5,4},{6,7},{7,6},{8,9},{9,8},{10,11... | collective-permute-start | bytes 1179656 | tf_op jit(solution)/shard_map/ppermute | solution.py:696
  45.5 11.3 %collective-permute-start.7 = (f32[4,24,8,128]{3,2,1,0:T(8,128)S(1)}, f32[4,24,8,128]{3,2,1,0:T(8,128)}, u32[]{:S(2)}, u32[]{:S(2)}) collective-permute-start(f32[4,24,8,128]{3,2,1,0:T(8,128)S(1)} %collective-permute-done.3.refs_3_), channel_id=1, source_target_pairs={{0,1},{1,0},{2,3},{3,2},{4,5},{5,4},{6,7},{7,6},{8,9},{9,8},{10,11... | collective-permute-start | bytes 1179656 | tf_op jit(solution)/shard_map/ppermute | solution.py:696
  53.1 3.6 %collective-permute-start.8 = (f32[4,24,8,128]{3,2,1,0:T(8,128)S(1)}, f32[4,24,8,128]{3,2,1,0:T(8,128)}, u32[]{:S(2)}, u32[]{:S(2)}) collective-permute-start(f32[4,24,8,128]{3,2,1,0:T(8,128)S(1)} %collective-permute-done.4.refs_4_), channel_id=1, source_target_pairs={{0,1},{1,0},{2,3},{3,2},{4,5},{5,4},{6,7},{7,6},{8,9},{9,8},{10,11... | collective-permute-start | bytes 1179656 | tf_op jit(solution)/shard_map/ppermute | solution.py:696
  54.0 2.8 %collective-permute-start.9 = (f32[4,24,8,128]{3,2,1,0:T(8,128)}, f32[4,24,8,128]{3,2,1,0:T(8,128)}, u32[]{:S(2)}, u32[]{:S(2)}) collective-permute-start(f32[4,24,8,128]{3,2,1,0:T(8,128)} %collective-permute-done.5.refs_5_), channel_id=1, source_target_pairs={{0,1},{1,0},{2,3},{3,2},{4,5},{5,4},{6,7},{7,6},{8,9},{9,8},{10,11... | collective-permute-start | bytes 1179656 | tf_op jit(solution)/shard_map/ppermute | solution.py:696

commit v11 on v10

--- a/solution.py
+++ b/solution.py
@@ -292,13 +292,10 @@
 
 
 def first_kernel(groups, *refs):
-    field_in, plane, depth, field, near, raw, high_buf, low_buf, sems = refs
+    raw, plane, depth, field, near, high_buf, low_buf = refs
     groups_x, groups_y, groups_z = groups
     span = groups_z * LANE
     pairs_slab = groups_y // 2
-    load = pltpu.make_async_copy(field_in, raw, sems.at[0])
-    load.start()
-    load.wait()
 
     def lay_field(slab_at, carry):
         for tile in range(pairs_slab):
@@ -331,21 +328,8 @@
     field_a, near_a = refs[:2]
     packs_in = refs[2 : 2 + pieces]
     plane, depth, out = refs[2 + pieces : 5 + pieces]
-    (
-        field_b,
-        field_c,
-        turned_out,
-        local,
-        coeffs,
-        high_buf,
-        low_buf,
-        near,
-        packs,
-        in_sems,
-        pack_sems,
-        out_sems,
-    ) = refs[5 + pieces : 5 + pieces + 12]
-    spares = refs[5 + pieces + 12 :]
+    field_b, field_c, local, coeffs, high_buf, low_buf, near = refs[5 + pieces : 12 + pieces]
+    spares = refs[12 + pieces :]
     targets = (near,) + tuple(spares)
     columns = groups_x * groups_y
     domains = columns * groups_z
@@ -362,45 +346,31 @@
     side = lane // HALF
     f32 = jnp.float32
 
-    loads = [pltpu.make_async_copy(near_a, near, in_sems.at[0])]
-    pack_loads = []
-    for hop_z in range(groups_z):
-        for hop_y in range(groups_y):
-            source = packs_in[hop_z * groups_y + hop_y]
-            for hop_x in range(groups_x):
+    for target in targets:
+        target[...] = jnp.zeros(target.shape, f32)
+
+    def sources(hop_x):
+        for hop_z in range(groups_z):
+            for hop_y in range(groups_y):
                 from_x = lax.rem(my_place[0] + (groups_x - hop_x), groups_x)
                 from_y = lax.rem(my_place[1] + (groups_y - hop_y), groups_y)
                 from_z = lax.rem(my_place[2] + (groups_z - hop_z), groups_z)
-                device = (from_x * groups_y + from_y) * groups_z + from_z
-                number = (hop_z * groups_y + hop_y) * groups_x + hop_x
-                pack_loads.append(
-                    pltpu.make_async_copy(
-                        source.at[hop_x], packs.at[device], pack_sems.at[number]
-                    )
-                )
-    for load in pack_loads + loads:
-        load.start()
-    for spare in spares:
-        spare[...] = jnp.zeros(spare.shape, f32)
-    for load in pack_loads + loads:
-        load.wait()
-
-    def lay_potential(pair, carry):
-        for depth_at in range(groups_z):
-            for row in range(SUB):
-                first = packs[2 * pair * groups_z + depth_at, row]
-                second = packs[(2 * pair + 1) * groups_z + depth_at, row]
-                at = pl.multiple_of(pair * span + depth_at * LANE + row * SUB, SUB)
-                local[pl.ds(at, SUB), :] = diagonal + jnp.where(
-                    lower, first, pltpu.roll(second, HALF, 1)
-                )
-                at = pl.multiple_of(at + HALF, SUB)
-                local[pl.ds(at, SUB), :] = diagonal + jnp.where(
-                    lower, pltpu.roll(first, HALF, 1), second
-                )
+                yield packs_in[hop_z * groups_y + hop_y], from_x * groups_y + from_y, from_z
+
+    def lay_potential(hop_x, carry):
+        for piece, column, depth_at in sources(hop_x):
+            mine = side == column % 2
+            for tile in range(SUB):
+                value = diagonal + piece[hop_x, tile]
+                other = pltpu.roll(value, HALF, 1)
+                for upper in range(2):
+                    at = column // 2 * span + depth_at * LANE + upper * HALF + tile * SUB
+                    rows = pl.ds(pl.multiple_of(at, SUB), SUB)
+                    chosen = jnp.where(side == upper, value, other)
+                    local[rows, :] = jnp.where(mine, chosen, local[rows, :])
         return carry
 
-    lax.fori_loop(0, pairs, lay_potential, 0)
+    lax.fori_loop(0, groups_x, lay_potential, 0)
 
     ones = (
         (
@@ -413,26 +383,29 @@
 
     def part_groups(part, share):
         for number in range(share):
-            for inner in range(per_device):
-                yield part * share + number, inner
+            hop_x = part * share + number
+            for at, (piece, column, depth_at) in enumerate(sources(hop_x)):
+                for inner in range(per_device):
+                    stored = (hop_x * pieces + at) * per_device + inner
+                    atoms_at = ((column * groups_z + depth_at) * per_device + inner) * SUB
+                    yield piece, hop_x, inner, stored, atoms_at
 
     def apply_step(cur, prev, new, alpha, beta, first, last):
         def project(part, carry):
             if not first:
                 slabs = [part * chunk + number for number in range(chunk)]
                 lay_products(groups, high_buf, low_buf, plane, depth, slabs, near)
-            for device, inner in part_groups(part, domains // (groups_x // chunk)):
-                group = device * per_device + inner
+            for piece, hop_x, inner, stored, atoms_at in part_groups(part, chunk):
                 terms = ([], [])
                 for j in range(SUB):
-                    atom = group * SUB + j
+                    atom = atoms_at + j
                     value = cur[pl.ds(place[atom], SUB), :]
                     both = jnp.where(side == half[atom], value, pltpu.roll(value, HALF, 1))
                     for kp in range(2):
                         at = SUB + (inner * 2 + kp) * SUB + j
-                        terms[kp].append(both * packs[device, at])
+                        terms[kp].append(both * piece[hop_x, at])
                 for kp in range(2):
-                    at = pl.multiple_of((group * 2 + kp) * SUB, SUB)
+                    at = pl.multiple_of((stored * 2 + kp) * SUB, SUB)
                     coeffs[pl.ds(at, SUB), :] = row_sums(terms[kp])
             return carry
 
@@ -442,17 +415,16 @@
         coeffs[...] = mxu(high, ones) + mxu(low, ones)
 
         def scatter(part, carry):
-            for device, inner in part_groups(part, domains // groups_x):
-                group = device * per_device + inner
+            for piece, hop_x, inner, stored, atoms_at in part_groups(part, 1):
                 weights = [
-                    coeffs[pl.ds(pl.multiple_of((group * 2 + kp) * SUB, SUB), SUB), :]
+                    coeffs[pl.ds(pl.multiple_of((stored * 2 + kp) * SUB, SUB), SUB), :]
                     for kp in range(2)
                 ]
                 for j in range(SUB):
-                    atom = group * SUB + j
+                    atom = atoms_at + j
                     parts = [
                         jnp.broadcast_to(weights[kp][j : j + 1], (SUB, LANE))
-                        * packs[device, SUB + (inner * 2 + kp) * SUB + j]
+                        * piece[hop_x, SUB + (inner * 2 + kp) * SUB + j]
                         for kp in range(2)
                     ]
                     value = parts[0] + parts[1]
@@ -473,6 +445,8 @@
                     rows = pl.ds(pl.multiple_of(pair * span + at_row, TALL), TALL)
                     slab_at_row = pl.ds(pl.multiple_of(slab_at * span + at_row, TALL), TALL)
                     total = local[rows, :] * cur[rows, :]
+                    if first:
+                        total = total + near_a[rows, :]
                     for target in targets:
                         total = total + target[rows, :]
                     if not last:
@@ -488,12 +462,8 @@
                     for depth_at in range(groups_z):
                         at = pl.multiple_of(pair * span + depth_at * LANE, LANE)
                         turned = new[pl.ds(at, LANE), :].T
-                        turned_out[block_rows(groups_z, pair, 0, depth_at), :] = turned[:HALF]
-                        turned_out[block_rows(groups_z, pair, 1, depth_at), :] = turned[HALF:]
-                    rows = pl.ds(pl.multiple_of(pair * span, span), span)
-                    pltpu.make_async_copy(
-                        turned_out.at[rows], out.at[rows], out_sems.at[pair]
-                    ).start()
+                        out[block_rows(groups_z, pair, 0, depth_at), :] = turned[:HALF]
+                        out[block_rows(groups_z, pair, 1, depth_at), :] = turned[HALF:]
             return carry
 
         lax.fori_loop(0, groups_x, combine, 0)
@@ -517,13 +487,6 @@
         )
         prev, cur = cur, target
         sigma_now = sigma_next
-
-    def finish(pair, carry):
-        rows = pl.ds(pl.multiple_of(pair * span, span), span)
-        pltpu.make_async_copy(turned_out.at[rows], out.at[rows], out_sems.at[pair]).wait()
-        return carry
-
-    lax.fori_loop(0, pairs, finish, 0)
 
 
 def pack_kernel(my_first, extent, coupling, potential, projectors, out):
@@ -626,7 +589,6 @@
     cells = (groups_x * groups_y // 2 * span, LANE)
     slabs = (groups_x * span, groups_y * HALF)
     vmem = pl.BlockSpec(memory_space=pltpu.VMEM)
-    anywhere = pl.BlockSpec(memory_space=pl.ANY)
     work = 2 * slabs[0] * slabs[1] * (9 * slabs[1] + 3 * span)
     return pl.pallas_call(
         functools.partial(first_kernel, groups),
@@ -634,13 +596,11 @@
             jax.ShapeDtypeStruct(cells, jnp.float32),
             jax.ShapeDtypeStruct(cells, jnp.float32),
         ],
-        in_specs=[anywhere, vmem, vmem],
+        in_specs=[vmem] * 3,
         out_specs=[vmem] * 2,
         scratch_shapes=[
-            pltpu.VMEM(cells, jnp.float32),
             pltpu.VMEM(slabs, jnp.bfloat16),
             pltpu.VMEM(slabs, jnp.bfloat16),
-            pltpu.SemaphoreType.DMA((1,)),
         ],
         compiler_params=pltpu.CompilerParams(vmem_limit_bytes=12 * 1024 * 1024),
         cost_estimate=pl.CostEstimate(
@@ -657,31 +617,24 @@
     columns = groups_x * groups_y
     atoms = place.shape[0]
     vmem = pl.BlockSpec(memory_space=pltpu.VMEM)
-    anywhere = pl.BlockSpec(memory_space=pl.ANY)
     smem = pl.BlockSpec(memory_space=pltpu.SMEM)
     slabs = (groups_x * groups_z * LANE, groups_y * HALF)
     work = 2 * slabs[0] * slabs[1] * (9 * slabs[1] + 3 * groups_z * LANE)
     out = pl.pallas_call(
         functools.partial(filter_kernel, groups, atoms),
         out_shape=jax.ShapeDtypeStruct(field.shape, jnp.float32),
-        in_specs=[smem] * 3 + [vmem] * 2 + [anywhere] * len(packs) + [vmem] * 2,
-        out_specs=anywhere,
+        in_specs=[smem] * 3 + [vmem] * (len(packs) + 4),
+        out_specs=vmem,
         scratch_shapes=[
-            pltpu.VMEM(field.shape, jnp.float32),
             pltpu.VMEM(field.shape, jnp.float32),
             pltpu.VMEM(field.shape, jnp.float32),
             pltpu.VMEM(field.shape, jnp.float32),
             pltpu.VMEM((atoms * 2, LANE), jnp.float32),
             pltpu.VMEM(slabs, jnp.bfloat16),
             pltpu.VMEM(slabs, jnp.bfloat16),
-            pltpu.VMEM(near.shape, jnp.float32),
-            pltpu.VMEM((columns * groups_z,) + packs[0].shape[1:], jnp.float32),
-            pltpu.SemaphoreType.DMA((1,)),
-            pltpu.SemaphoreType.DMA((columns * groups_z,)),
-            pltpu.SemaphoreType.DMA((columns // 2,)),
         ]
-        + [pltpu.VMEM(field.shape, jnp.float32) for _ in range(SPARES)],
-        compiler_params=pltpu.CompilerParams(vmem_limit_bytes=20 * 1024 * 1024),
+        + [pltpu.VMEM(field.shape, jnp.float32) for _ in range(1 + SPARES)],
+        compiler_params=pltpu.CompilerParams(vmem_limit_bytes=22 * 1024 * 1024),
         cost_estimate=pl.CostEstimate(
             flops=3 * work, bytes_accessed=8 * field.size * 4, transcendentals=0
         ),

time: 124 us -> 120 us (0.968)
  Pallas kernels: 24.3 us -> 20.4 us
    pallas_call x1, Pallas kernels: 20.4 us -> 16.5 us  [filter_call(): pl.pallas_call(functools.partial(filter_kernel, groups, atoms), out_shape...]
where the time goes in v11:
time: 120 us; the launch traced here: 119 us
  blocking collectives  43 us (36%)
  waiting for transfers between devices  29.1 us (24%)
  Pallas kernels  20.4 us (17%)
  starting transfers between devices  17.8 us (15%)
  local copies, waits for them, and re-layouts  7.24 us (6%)
    all_to_all x1, blocking collectives, state_body(): lax.all_to_all(result, axes, split_axis=0, concat_axis=0, tiled=True)  31.3 us
    ppermute x10, waiting for transfers between devices, hops(): lax.ppermute(value, axis, [(i, (i + hop) % count) for i in range(count)])  29.1 us
    pallas_call x1, Pallas kernels, filter_call(): pl.pallas_call(functools.partial(filter_kernel, groups, atoms), out_shape...  16.5 us
    ppermute x10, starting transfers between devices, hops(): lax.ppermute(value, axis, [(i, (i + hop) % count) for i in range(count)])  11.9 us
    all_to_all x1, blocking collectives, state_body(): lax.all_to_all(jnp.broadcast_to(quarter[None], (domains,) + quarter.shape...  11.7 us
    all_to_all x1, starting transfers between devices, state_body(): lax.all_to_all(orbitals, axes, split_axis=0, concat_axis=0, tiled=True)  5.85 us
    unnamed x15, local copies, waits for them, and re-layouts  5.37 us
    pallas_call x1, Pallas kernels, first_call(): pl.pallas_call(functools.partial(first_kernel, groups), out_shape=[jax.Sh...  2.55 us
  transfers between devices with their start and end apart: 11, of which 4 were waited for; matrix products, arithmetic and copies ran while one was open for 1% of the time, Pallas kernels for 2%

profile of v11, /device:TPU:0, one launch (start us, length us, event | category | flops | bytes accessed | tf_op | source)
XLA Modules:
  0.0 119.4 jit_solution(15327608035832337673)
XLA Ops:
  0.6 0.0 copy-start.4
  0.7 0.0 copy-start.5
  0.7 0.7 copy-done.4
  1.3 0.0 copy-done.5
  1.3 0.0 copy-start.2
  1.3 0.8 copy-done.2
  2.2 0.0 copy-start.3
  2.2 0.8 copy-done.3
  2.9 0.0 copy-start.6
  2.9 1.0 shard_map.104
  4.0 3.1 %collective-permute-start = (f32[24,8,128]{2,1,0:T(8,128)S(1)}, f32[24,8,128]{2,1,0:T(8,128)S(1)}, u32[]{:S(2)}, u32[]{:S(2)}) collective-permute-start(f32[24,8,128]{2,1,0:T(8,128)S(1)} %shard_map.104), channel_id=1, source_target_pairs={{0,8},{8,16},{16,24},{24,0},{1,9},{9,17},{17,25},{25,1},{2,10},{10... | collective-permute-start | bytes 294920 | tf_op jit(solution)/shard_map/ppermute | solution.py:649
  7.0 2.6 %collective-permute-start.1 = (f32[24,8,128]{2,1,0:T(8,128)S(1)}, f32[24,8,128]{2,1,0:T(8,128)S(1)}, u32[]{:S(2)}, u32[]{:S(2)}) collective-permute-start(f32[24,8,128]{2,1,0:T(8,128)S(1)} %shard_map.104), channel_id=1, source_target_pairs={{0,16},{8,24},{16,0},{24,8},{1,17},{9,25},{17,1},{25,9},{2,18},{10... | collective-permute-start | bytes 294920 | tf_op jit(solution)/shard_map/ppermute | solution.py:649
  9.6 1.3 %collective-permute-start.2 = (f32[24,8,128]{2,1,0:T(8,128)S(1)}, f32[24,8,128]{2,1,0:T(8,128)S(1)}, u32[]{:S(2)}, u32[]{:S(2)}) collective-permute-start(f32[24,8,128]{2,1,0:T(8,128)S(1)} %shard_map.104), channel_id=1, source_target_pairs={{0,24},{8,0},{16,8},{24,16},{1,25},{9,1},{17,9},{25,17},{2,26},{10... | collective-permute-start | bytes 294920 | tf_op jit(solution)/shard_map/ppermute | solution.py:649
  11.0 0.0 copy-done.6
  11.0 0.7 slice.3
  11.7 0.0 copy-start
  11.7 1.1 copy-done
  12.8 0.0 copy-start.1
  12.8 1.0 copy-done.1
  13.8 0.3 shard_map.105
  14.1 0.0 collective-permute-done
  14.1 2.1 %collective-permute-done.1 = f32[24,8,128]{2,1,0:T(8,128)S(1)} collective-permute-done((f32[24,8,128]{2,1,0:T(8,128)S(1)}, f32[24,8,128]{2,1,0:T(8,128)S(1)}, u32[]{:S(2)}, u32[]{:S(2)}) %collective-permute-start.1) | collective-permute-done | bytes 98336 | tf_op jit(solution)/shard_map/ppermute | solution.py:649
  16.2 0.0 collective-permute-done.2
  16.3 5.8 %all-to-all-start = ((f32[32,8,8,128]{3,2,1,0:T(8,128)}), f32[32,8,8,128]{3,2,1,0:T(8,128)S(1)}, u32[]{:S(2)}, u32[]{:S(2)}) async-start(f32[32,8,8,128]{3,2,1,0:T(8,128)} %param.9), calls=%async_computation | async-start | bytes 2097152 | tf_op jit(solution)/shard_map/all_to_all | solution.py:671
  22.1 1.8 %collective-permute-start.3 = (f32[4,24,8,128]{3,2,1,0:T(8,128)S(1)}, f32[4,24,8,128]{3,2,1,0:T(8,128)S(1)}, u32[]{:S(2)}, u32[]{:S(2)}) collective-permute-start(f32[4,24,8,128]{3,2,1,0:T(8,128)S(1)} %pad_maximum_fusion.refs_2_), channel_id=1, source_target_pairs={{0,2},{2,4},{4,6},{6,0},{1,3},{3,5},{5,7},{7,1},{8,10},{10,12},{12... | collective-permute-start | bytes 1179656 | tf_op jit(solution)/shard_map/ppermute | solution.py:649
  24.0 1.5 %collective-permute-start.4 = (f32[4,24,8,128]{3,2,1,0:T(8,128)S(1)}, f32[4,24,8,128]{3,2,1,0:T(8,128)S(1)}, u32[]{:S(2)}, u32[]{:S(2)}) collective-permute-start(f32[4,24,8,128]{3,2,1,0:T(8,128)S(1)} %pad_maximum_fusion.refs_2_), channel_id=1, source_target_pairs={{0,4},{2,6},{4,0},{6,2},{1,5},{3,7},{5,1},{7,3},{8,12},{10,14},{12... | collective-permute-start | bytes 1179656 | tf_op jit(solution)/shard_map/ppermute | solution.py:649
  25.4 1.5 %collective-permute-start.5 = (f32[4,24,8,128]{3,2,1,0:T(8,128)S(1)}, f32[4,24,8,128]{3,2,1,0:T(8,128)}, u32[]{:S(2)}, u32[]{:S(2)}) collective-permute-start(f32[4,24,8,128]{3,2,1,0:T(8,128)S(1)} %pad_maximum_fusion.refs_2_), channel_id=1, source_target_pairs={{0,6},{2,0},{4,2},{6,4},{1,7},{3,1},{5,3},{7,5},{8,14},{10,8},{12,... | collective-permute-start | bytes 1179656 | tf_op jit(solution)/shard_map/ppermute | solution.py:649
  26.9 0.0 collective-permute-start.6
  26.9 18.6 %collective-permute-done.3.refs_3_ = f32[4,24,8,128]{3,2,1,0:T(8,128)S(1)} collective-permute-done((f32[4,24,8,128]{3,2,1,0:T(8,128)S(1)}, f32[4,24,8,128]{3,2,1,0:T(8,128)S(1)}, u32[]{:S(2)}, u32[]{:S(2)}) %collective-permute-start.3) | collective-permute-done | bytes 393248 | tf_op jit(solution)/shard_map/ppermute | solution.py:649
  45.5 0.0 collective-permute-start.7
  45.5 7.6 %collective-permute-done.4.refs_4_ = f32[4,24,8,128]{3,2,1,0:T(8,128)S(1)} collective-permute-done((f32[4,24,8,128]{3,2,1,0:T(8,128)S(1)}, f32[4,24,8,128]{3,2,1,0:T(8,128)S(1)}, u32[]{:S(2)}, u32[]{:S(2)}) %collective-permute-start.4) | collective-permute-done | bytes 393248 | tf_op jit(solution)/shard_map/ppermute | solution.py:649
  53.1 0.1 collective-permute-start.8
  53.2 0.7 collective-permute-done.5.refs_5_
  54.0 0.0 collective-permute-start.9
  54.0 0.1 pad_add_fusion.my_place
  54.1 0.0 all-to-all-done
  54.1 2.5 %shard_map.106 = (f32[2048,128]{1,0:T(8,128)S(1)}, f32[2048,128]{1,0:T(8,128)S(1)}) custom-call(f32[2048,128]{1,0:T(8,128)S(1)} %bitcast.24, bf16[1536,256]{1,0:T(8,128)(2,1)S(1)} %get-tuple-element.17.refs_1_.refs_10_, bf16[256,768]{1,0:T(8,128)(2,1)S(1)} %get-tuple-element.18.refs_2_.refs_11_), custom_call_target="tpu_custom_call" | custom-call | flops 1610612736 | bytes 4194304 | tf_op jit(solution)/shard_map/pallas_call | solution.py:593
  56.6 0.0 collective-permute-done.6.refs_6_
  56.6 0.0 collective-permute-done.7.refs_7_
  56.7 0.0 collective-permute-done.8.refs_8_
  56.7 0.0 collective-permute-done.9.refs_9_
  56.7 16.5 %shard_map.107 = f32[2048,128]{1,0:T(8,128)S(1)} custom-call(s32[256]{0:T(256)S(1)} %multiply_add_fusion.place, s32[256]{0:T(256)S(1)} %get-tuple-element.15.half, s32[3]{0:T(128)S(1)} %pad_add_fusion.my_place, f32[2048,128]{1,0:T(8,128)S(1)} %get-tuple-element.19.refs_0_, f32[2048,128]{1,0:T(8,128)S(1)} %get-tuple-element.20.refs_1_, ...), custom_call_target="tpu_custom_call" | custom-call | flops 4831838208 | bytes 8388608 | tf_op jit(solution)/shard_map/pallas_call | solution.py:623
  73.2 31.3 %all_to_all.15 = f32[32,8,8,128]{3,2,1,0:T(8,128)S(1)} all-to-all(f32[32,8,8,128]{3,2,1,0:T(8,128)S(1)} %bitcast.25), channel_id=1, replica_groups=mesh['gx'=4,'gy'=4,'gz'=2] {'gx','gy','gz'}, dimensions={0} | all-to-all | bytes 2097152 | tf_op jit(solution)/shard_map/all_to_all | solution.py:674
  104.6 0.2 dot_general.5
  104.7 0.2 reshape.26
  104.9 1.0 convolution_bitcast_fusion
  105.9 0.1 broadcast_in_dim.11
  106.0 11.7 %all_to_all.16 = f32[32,8,128]{2,1,0:T(8,128)S(1)} all-to-all(f32[32,8,128]{2,1,0:T(8,128)S(1)} %broadcast_in_dim.12), channel_id=1, replica_groups=mesh['gx'=4,'gy'=4,'gz'=2] {'gx','gy','gz'}, dimensions={0} | all-to-all | bytes 262144 | tf_op jit(solution)/shard_map/all_to_all | solution.py:679
  117.7 0.1 div.38
  117.8 0.6 copy.17
  118.4 1.0 copy.19
  (7 shorter events, 0.1 us)
Async XLA Ops:
  0.6 0.7 copy-start.4
  0.7 0.7 copy-start.5
  1.3 0.8 copy-start.2
  2.2 0.8 copy-start.3
  2.9 8.0 %copy-start.6 = (s32[256]{0:T(256)S(1)}, s32[256]{0:T(256)}, u32[]{:S(2)}) copy-start(s32[256]{0:T(256)} %param.12) | copy-start | bytes 3076
  4.0 10.1 %collective-permute-start = (f32[24,8,128]{2,1,0:T(8,128)S(1)}, f32[24,8,128]{2,1,0:T(8,128)S(1)}, u32[]{:S(2)}, u32[]{:S(2)}) collective-permute-start(f32[24,8,128]{2,1,0:T(8,128)S(1)} %shard_map.104), channel_id=1, source_target_pairs={{0,8},{8,16},{16,24},{24,0},{1,9},{9,17},{17,25},{25,1},{2,10},{10... | collective-permute-start | bytes 294920 | tf_op jit(solution)/shard_map/ppermute | solution.py:649
  7.0 9.2 %collective-permute-start.1 = (f32[24,8,128]{2,1,0:T(8,128)S(1)}, f32[24,8,128]{2,1,0:T(8,128)S(1)}, u32[]{:S(2)}, u32[]{:S(2)}) collective-permute-start(f32[24,8,128]{2,1,0:T(8,128)S(1)} %shard_map.104), channel_id=1, source_target_pairs={{0,16},{8,24},{16,0},{24,8},{1,17},{9,25},{17,1},{25,9},{2,18},{10... | collective-permute-start | bytes 294920 | tf_op jit(solution)/shard_map/ppermute | solution.py:649
  9.6 6.6 %collective-permute-start.2 = (f32[24,8,128]{2,1,0:T(8,128)S(1)}, f32[24,8,128]{2,1,0:T(8,128)S(1)}, u32[]{:S(2)}, u32[]{:S(2)}) collective-permute-start(f32[24,8,128]{2,1,0:T(8,128)S(1)} %shard_map.104), channel_id=1, source_target_pairs={{0,24},{8,0},{16,8},{24,16},{1,25},{9,1},{17,9},{25,17},{2,26},{10... | collective-permute-start | bytes 294920 | tf_op jit(solution)/shard_map/ppermute | solution.py:649
  11.7 1.1 copy-start
  12.8 1.0 copy-start.1
  16.3 37.8 %all-to-all-start = ((f32[32,8,8,128]{3,2,1,0:T(8,128)}), f32[32,8,8,128]{3,2,1,0:T(8,128)S(1)}, u32[]{:S(2)}, u32[]{:S(2)}) async-start(f32[32,8,8,128]{3,2,1,0:T(8,128)} %param.9), calls=%async_computation | async-start | bytes 2097152 | tf_op jit(solution)/shard_map/all_to_all | solution.py:671
  22.1 23.3 %collective-permute-start.3 = (f32[4,24,8,128]{3,2,1,0:T(8,128)S(1)}, f32[4,24,8,128]{3,2,1,0:T(8,128)S(1)}, u32[]{:S(2)}, u32[]{:S(2)}) collective-permute-start(f32[4,24,8,128]{3,2,1,0:T(8,128)S(1)} %pad_maximum_fusion.refs_2_), channel_id=1, source_target_pairs={{0,2},{2,4},{4,6},{6,0},{1,3},{3,5},{5,7},{7,1},{8,10},{10,12},{12... | collective-permute-start | bytes 1179656 | tf_op jit(solution)/shard_map/ppermute | solution.py:649
  24.0 29.1 %collective-permute-start.4 = (f32[4,24,8,128]{3,2,1,0:T(8,128)S(1)}, f32[4,24,8,128]{3,2,1,0:T(8,128)S(1)}, u32[]{:S(2)}, u32[]{:S(2)}) collective-permute-start(f32[4,24,8,128]{3,2,1,0:T(8,128)S(1)} %pad_maximum_fusion.refs_2_), channel_id=1, source_target_pairs={{0,4},{2,6},{4,0},{6,2},{1,5},{3,7},{5,1},{7,3},{8,12},{10,14},{12... | collective-permute-start | bytes 1179656 | tf_op jit(solution)/shard_map/ppermute | solution.py:649
  25.4 28.6 %collective-permute-start.5 = (f32[4,24,8,128]{3,2,1,0:T(8,128)S(1)}, f32[4,24,8,128]{3,2,1,0:T(8,128)}, u32[]{:S(2)}, u32[]{:S(2)}) collective-permute-start(f32[4,24,8,128]{3,2,1,0:T(8,128)S(1)} %pad_maximum_fusion.refs_2_), channel_id=1, source_target_pairs={{0,6},{2,0},{4,2},{6,4},{1,7},{3,1},{5,3},{7,5},{8,14},{10,8},{12,... | collective-permute-start | bytes 1179656 | tf_op jit(solution)/shard_map/ppermute | solution.py:649
  26.9 29.7 %collective-permute-start.6 = (f32[4,24,8,128]{3,2,1,0:T(8,128)S(1)}, f32[4,24,8,128]{3,2,1,0:T(8,128)}, u32[]{:S(2)}, u32[]{:S(2)}) collective-permute-start(f32[4,24,8,128]{3,2,1,0:T(8,128)S(1)} %pad_maximum_fusion.refs_2_), channel_id=1, source_target_pairs={{0,1},{1,0},{2,3},{3,2},{4,5},{5,4},{6,7},{7,6},{8,9},{9,8},{10,11... | collective-permute-start | bytes 1179656 | tf_op jit(solution)/shard_map/ppermute | solution.py:649
  45.5 11.2 %collective-permute-start.7 = (f32[4,24,8,128]{3,2,1,0:T(8,128)S(1)}, f32[4,24,8,128]{3,2,1,0:T(8,128)}, u32[]{:S(2)}, u32[]{:S(2)}) collective-permute-start(f32[4,24,8,128]{3,2,1,0:T(8,128)S(1)} %collective-permute-done.3.refs_3_), channel_id=1, source_target_pairs={{0,1},{1,0},{2,3},{3,2},{4,5},{5,4},{6,7},{7,6},{8,9},{9,8},{10,11... | collective-permute-start | bytes 1179656 | tf_op jit(solution)/shard_map/ppermute | solution.py:649
  53.1 3.6 %collective-permute-start.8 = (f32[4,24,8,128]{3,2,1,0:T(8,128)S(1)}, f32[4,24,8,128]{3,2,1,0:T(8,128)}, u32[]{:S(2)}, u32[]{:S(2)}) collective-permute-start(f32[4,24,8,128]{3,2,1,0:T(8,128)S(1)} %collective-permute-done.4.refs_4_), channel_id=1, source_target_pairs={{0,1},{1,0},{2,3},{3,2},{4,5},{5,4},{6,7},{7,6},{8,9},{9,8},{10,11... | collective-permute-start | bytes 1179656 | tf_op jit(solution)/shard_map/ppermute | solution.py:649
  54.0 2.7 %collective-permute-start.9 = (f32[4,24,8,128]{3,2,1,0:T(8,128)}, f32[4,24,8,128]{3,2,1,0:T(8,128)}, u32[]{:S(2)}, u32[]{:S(2)}) collective-permute-start(f32[4,24,8,128]{3,2,1,0:T(8,128)} %collective-permute-done.5.refs_5_), channel_id=1, source_target_pairs={{0,1},{1,0},{2,3},{3,2},{4,5},{5,4},{6,7},{7,6},{8,9},{9,8},{10,11... | collective-permute-start | bytes 1179656 | tf_op jit(solution)/shard_map/ppermute | solution.py:649

commit v12 on v11

--- a/solution.py
+++ b/solution.py
@@ -322,13 +322,46 @@
     lax.fori_loop(0, groups_x // chunk, product, 0)
 
 
+def pieces_from(groups, my_place, packs_in, hop_x):
+    groups_x, groups_y, groups_z = groups
+    for hop_z in range(groups_z):
+        for hop_y in range(groups_y):
+            from_x = lax.rem(my_place[0] + (groups_x - hop_x), groups_x)
+            from_y = lax.rem(my_place[1] + (groups_y - hop_y), groups_y)
+            from_z = lax.rem(my_place[2] + (groups_z - hop_z), groups_z)
+            yield packs_in[hop_z * groups_y + hop_y], from_x * groups_y + from_y, from_z
+
+
+def potential_kernel(groups, my_place, *refs):
+    packs_in, local = refs[:-1], refs[-1]
+    span = groups[2] * LANE
+    side = lax.broadcasted_iota(jnp.int32, (SUB, LANE), 1) // HALF
+    middle = (UPPER + CUTOFF) / 2.0
+    diagonal = -0.5 * 3.0 * STENCIL[0] / (SPACING * SPACING) - middle
+
+    def lay_potential(hop_x, carry):
+        for piece, column, depth_at in pieces_from(groups, my_place, packs_in, hop_x):
+            mine = side == column % 2
+            for tile in range(SUB):
+                value = diagonal + piece[hop_x, tile]
+                other = pltpu.roll(value, HALF, 1)
+                for upper in range(2):
+                    at = column // 2 * span + depth_at * LANE + upper * HALF + tile * SUB
+                    rows = pl.ds(pl.multiple_of(at, SUB), SUB)
+                    chosen = jnp.where(side == upper, value, other)
+                    local[rows, :] = jnp.where(mine, chosen, local[rows, :])
+        return carry
+
+    lax.fori_loop(0, groups[0], lay_potential, 0)
+
+
 def filter_kernel(groups, atoms, place, half, my_place, *refs):
     groups_x, groups_y, groups_z = groups
     pieces = groups_y * groups_z
-    field_a, near_a = refs[:2]
-    packs_in = refs[2 : 2 + pieces]
-    plane, depth, out = refs[2 + pieces : 5 + pieces]
-    field_b, field_c, local, coeffs, high_buf, low_buf, near = refs[5 + pieces : 12 + pieces]
+    field_a, near_a, local = refs[:3]
+    packs_in = refs[3 : 3 + pieces]
+    plane, depth, out = refs[3 + pieces : 6 + pieces]
+    field_b, field_c, coeffs, high_buf, low_buf, near = refs[6 + pieces : 12 + pieces]
     spares = refs[12 + pieces :]
     targets = (near,) + tuple(spares)
     columns = groups_x * groups_y
@@ -350,27 +383,7 @@
         target[...] = jnp.zeros(target.shape, f32)
 
     def sources(hop_x):
-        for hop_z in range(groups_z):
-            for hop_y in range(groups_y):
-                from_x = lax.rem(my_place[0] + (groups_x - hop_x), groups_x)
-                from_y = lax.rem(my_place[1] + (groups_y - hop_y), groups_y)
-                from_z = lax.rem(my_place[2] + (groups_z - hop_z), groups_z)
-                yield packs_in[hop_z * groups_y + hop_y], from_x * groups_y + from_y, from_z
-
-    def lay_potential(hop_x, carry):
-        for piece, column, depth_at in sources(hop_x):
-            mine = side == column % 2
-            for tile in range(SUB):
-                value = diagonal + piece[hop_x, tile]
-                other = pltpu.roll(value, HALF, 1)
-                for upper in range(2):
-                    at = column // 2 * span + depth_at * LANE + upper * HALF + tile * SUB
-                    rows = pl.ds(pl.multiple_of(at, SUB), SUB)
-                    chosen = jnp.where(side == upper, value, other)
-                    local[rows, :] = jnp.where(mine, chosen, local[rows, :])
-        return carry
-
-    lax.fori_loop(0, groups_x, lay_potential, 0)
+        return pieces_from(groups, my_place, packs_in, hop_x)
 
     ones = (
         (
@@ -395,6 +408,7 @@
             if not first:
                 slabs = [part * chunk + number for number in range(chunk)]
                 lay_products(groups, high_buf, low_buf, plane, depth, slabs, near)
+            sums = []
             for piece, hop_x, inner, stored, atoms_at in part_groups(part, chunk):
                 terms = ([], [])
                 for j in range(SUB):
@@ -404,15 +418,14 @@
                     for kp in range(2):
                         at = SUB + (inner * 2 + kp) * SUB + j
                         terms[kp].append(both * piece[hop_x, at])
-                for kp in range(2):
-                    at = pl.multiple_of((stored * 2 + kp) * SUB, SUB)
-                    coeffs[pl.ds(at, SUB), :] = row_sums(terms[kp])
+                sums += [row_sums(terms[0]), row_sums(terms[1])]
+            high, low = split_pair(jnp.concatenate(sums, axis=0))
+            rows = len(sums) * SUB
+            at = pl.multiple_of(part * rows, rows)
+            coeffs[pl.ds(at, rows), :] = mxu(high, ones) + mxu(low, ones)
             return carry
 
         lax.fori_loop(0, groups_x // chunk, project, 0)
-
-        high, low = split_pair(coeffs[...])
-        coeffs[...] = mxu(high, ones) + mxu(low, ones)
 
         def scatter(part, carry):
             for piece, hop_x, inner, stored, atoms_at in part_groups(part, 1):
@@ -610,8 +623,25 @@
     )(field.reshape(cells), plane, depth)
 
 
+def potential_call(groups, my_place, packs, interpret=False):
+    groups_x, groups_y, groups_z = groups
+    cells = (groups_x * groups_y // 2 * groups_z * LANE, LANE)
+    vmem = pl.BlockSpec(memory_space=pltpu.VMEM)
+    return pl.pallas_call(
+        functools.partial(potential_kernel, groups),
+        out_shape=jax.ShapeDtypeStruct(cells, jnp.float32),
+        in_specs=[pl.BlockSpec(memory_space=pltpu.SMEM)] + [vmem] * len(packs),
+        out_specs=vmem,
+        compiler_params=pltpu.CompilerParams(vmem_limit_bytes=8 * 1024 * 1024),
+        cost_estimate=pl.CostEstimate(
+            flops=0, bytes_accessed=160 * cells[0] * LANE, transcendentals=0
+        ),
+        interpret=interpret,
+    )(my_place, *packs)
+
+
 def filter_call(
-    groups, place, half, my_place, field, near, packs, plane, depth, interpret=False
+    groups, place, half, my_place, field, near, local, packs, plane, depth, interpret=False
 ):
     groups_x, groups_y, groups_z = groups
     columns = groups_x * groups_y
@@ -623,10 +653,9 @@
     out = pl.pallas_call(
         functools.partial(filter_kernel, groups, atoms),
         out_shape=jax.ShapeDtypeStruct(field.shape, jnp.float32),
-        in_specs=[smem] * 3 + [vmem] * (len(packs) + 4),
+        in_specs=[smem] * 3 + [vmem] * (len(packs) + 5),
         out_specs=vmem,
         scratch_shapes=[
-            pltpu.VMEM(field.shape, jnp.float32),
             pltpu.VMEM(field.shape, jnp.float32),
             pltpu.VMEM(field.shape, jnp.float32),
             pltpu.VMEM((atoms * 2, LANE), jnp.float32),
@@ -639,7 +668,7 @@
             flops=3 * work, bytes_accessed=8 * field.size * 4, transcendentals=0
         ),
         interpret=interpret,
-    )(place, half, my_place, field, near, *packs, plane, depth)
+    )(place, half, my_place, field, near, local, *packs, plane, depth)
     return out.reshape(columns * groups_z, SUB, SUB, LANE)
 
 
@@ -670,7 +699,8 @@
     packs = [crossed[hop_y][hop_z] for hop_z in range(groups_z) for hop_y in range(groups[1])]
     field = lax.all_to_all(orbitals, axes, split_axis=0, concat_axis=0, tiled=True)
     field, near = first_call(groups, field, plane, depth)
-    result = filter_call(groups, place, half, my_place, field, near, packs, plane, depth)
+    local = potential_call(groups, my_place, packs)
+    result = filter_call(groups, place, half, my_place, field, near, local, packs, plane, depth)
     filtered = lax.all_to_all(result, axes, split_axis=0, concat_axis=0, tiled=True)
     states = filtered.shape[0]
     flattened = filtered.reshape(states, -1)

time: 120 us -> 126 us (1.050)
  local copies, waits for them, and re-layouts: 7.24 us -> 14.8 us
  waiting for transfers between devices: 29.1 us -> 31.6 us
  starting transfers between devices: 17.8 us -> 15.4 us
    unnamed x15 -> x47, local copies, waits for them, and re-layouts: 5.37 us -> 12.9 us
    ppermute x10, waiting for transfers between devices: 29.1 us -> 31.6 us  [hops(): lax.ppermute(value, axis, [(i, (i + hop) % count) for i in range(count)])]
    pallas_call x1, Pallas kernels: 16.5 us -> 14.3 us  [filter_call(): pl.pallas_call(functools.partial(filter_kernel, groups, atoms), out_shape...]
    all_to_all x1, starting transfers between devices: 5.85 us -> 4.53 us  [state_body(): lax.all_to_all(orbitals, axes, split_axis=0, concat_axis=0, tiled=True)]
  transfers between devices with their start and end apart: 11 -> 11, of which waited for: 4 -> 6; matrix products, arithmetic and copies ran while one was open for 1% -> 1% of each run, Pallas kernels for 2% -> 1%
where the time goes in v12:
time: 126 us
  blocking collectives  42.9 us (34%)
  waiting for transfers between devices  31.6 us (25%)
  Pallas kernels  19.3 us (15%)
  starting transfers between devices  15.4 us (12%)
  local copies, waits for them, and re-layouts  14.8 us (12%)
    ppermute x10, waiting for transfers between devices, hops(): lax.ppermute(value, axis, [(i, (i + hop) % count) for i in range(count)])  31.6 us
    all_to_all x1, blocking collectives, state_body(): lax.all_to_all(result, axes, split_axis=0, concat_axis=0, tiled=True)  31.2 us
    pallas_call x1, Pallas kernels, filter_call(): pl.pallas_call(functools.partial(filter_kernel, groups, atoms), out_shape...  14.3 us
    unnamed x47, local copies, waits for them, and re-layouts  12.9 us
    all_to_all x1, blocking collectives, state_body(): lax.all_to_all(jnp.broadcast_to(quarter[None], (domains,) + quarter.shape...  11.7 us
    ppermute x10, starting transfers between devices, hops(): lax.ppermute(value, axis, [(i, (i + hop) % count) for i in range(count)])  10.9 us
    all_to_all x1, starting transfers between devices, state_body(): lax.all_to_all(orbitals, axes, split_axis=0, concat_axis=0, tiled=True)  4.53 us
    pallas_call x1, Pallas kernels, first_call(): pl.pallas_call(functools.partial(first_kernel, groups), out_shape=[jax.Sh...  2.54 us
  transfers between devices with their start and end apart: 11, of which 6 were waited for; matrix products, arithmetic and copies ran while one was open for 1% of the time, Pallas kernels for 1%

profile of v12, /device:TPU:0, one launch (start us, length us, event | category | flops | bytes accessed | tf_op | source)
XLA Modules:
  0.0 125.9 jit_solution(17022995324777738381)
XLA Ops:
  0.6 0.0 copy-start.14
  0.7 0.0 copy-start.15
  0.7 0.7 copy-done.14
  1.3 0.0 copy-done.15
  1.3 0.8 copy-done.12
  2.2 0.8 copy-done.13
  2.9 1.0 shard_map.104
  4.0 0.0 copy-start.22
  4.0 5.1 %collective-permute-start.2 = (f32[24,8,128]{2,1,0:T(8,128)S(1)}, f32[24,8,128]{2,1,0:T(8,128)S(1)}, u32[]{:S(2)}, u32[]{:S(2)}) collective-permute-start(f32[24,8,128]{2,1,0:T(8,128)S(1)} %shard_map.104), channel_id=1, source_target_pairs={{0,24},{8,0},{16,8},{24,16},{1,25},{9,1},{17,9},{25,17},{2,26},{10... | collective-permute-start | bytes 294920 | tf_op jit(solution)/shard_map/ppermute | solution.py:678
  9.1 0.0 collective-permute-start.1
  9.1 1.0 collective-permute-start
  10.1 0.7 slice.3
  10.8 0.0 copy-done.22
  10.8 0.0 copy-start
  10.8 1.1 copy-done
  12.0 1.0 copy-done.11
  13.0 0.3 shard_map.105
  13.2 0.0 copy-start.16
  13.2 0.9 copy-done.16
  14.1 0.7 copy-done.19
  14.8 0.0 collective-permute-done.2
  14.9 3.0 %collective-permute-done.1 = f32[24,8,128]{2,1,0:T(8,128)S(1)} collective-permute-done((f32[24,8,128]{2,1,0:T(8,128)S(1)}, f32[24,8,128]{2,1,0:T(8,128)S(1)}, u32[]{:S(2)}, u32[]{:S(2)}) %collective-permute-start.1) | collective-permute-done | bytes 98336 | tf_op jit(solution)/shard_map/ppermute | solution.py:678
  17.8 0.0 collective-permute-done
  17.9 4.5 %all-to-all-start = ((f32[32,8,8,128]{3,2,1,0:T(8,128)}), f32[32,8,8,128]{3,2,1,0:T(8,128)S(1)}, u32[]{:S(2)}, u32[]{:S(2)}) async-start(f32[32,8,8,128]{3,2,1,0:T(8,128)} %param.9), calls=%async_computation | async-start | bytes 2097152 | tf_op jit(solution)/shard_map/all_to_all | solution.py:700
  22.4 1.8 %collective-permute-start.3 = (f32[4,24,8,128]{3,2,1,0:T(8,128)S(1)}, f32[4,24,8,128]{3,2,1,0:T(8,128)S(1)}, u32[]{:S(2)}, u32[]{:S(2)}) collective-permute-start(f32[4,24,8,128]{3,2,1,0:T(8,128)S(1)} %pad_maximum_fusion.refs_0_.refs_3_), channel_id=1, source_target_pairs={{0,2},{2,4},{4,6},{6,0},{1,3},{3,5},{5,7},{7,1},{8,10},{10,12},{12... | collective-permute-start | bytes 1179656 | tf_op jit(solution)/shard_map/ppermute | solution.py:678
  24.2 1.5 %collective-permute-start.4 = (f32[4,24,8,128]{3,2,1,0:T(8,128)S(1)}, f32[4,24,8,128]{3,2,1,0:T(8,128)S(1)}, u32[]{:S(2)}, u32[]{:S(2)}) collective-permute-start(f32[4,24,8,128]{3,2,1,0:T(8,128)S(1)} %pad_maximum_fusion.refs_0_.refs_3_), channel_id=1, source_target_pairs={{0,4},{2,6},{4,0},{6,2},{1,5},{3,7},{5,1},{7,3},{8,12},{10,14},{12... | collective-permute-start | bytes 1179656 | tf_op jit(solution)/shard_map/ppermute | solution.py:678
  25.7 1.5 %collective-permute-start.5 = (f32[4,24,8,128]{3,2,1,0:T(8,128)S(1)}, f32[4,24,8,128]{3,2,1,0:T(8,128)S(1)}, u32[]{:S(2)}, u32[]{:S(2)}) collective-permute-start(f32[4,24,8,128]{3,2,1,0:T(8,128)S(1)} %pad_maximum_fusion.refs_0_.refs_3_), channel_id=1, source_target_pairs={{0,6},{2,0},{4,2},{6,4},{1,7},{3,1},{5,3},{7,5},{8,14},{10,8},{12,... | collective-permute-start | bytes 1179656 | tf_op jit(solution)/shard_map/ppermute | solution.py:678
  27.1 0.0 collective-permute-start.6
  27.1 18.6 %collective-permute-done.3.refs_1_.refs_4_ = f32[4,24,8,128]{3,2,1,0:T(8,128)S(1)} collective-permute-done((f32[4,24,8,128]{3,2,1,0:T(8,128)S(1)}, f32[4,24,8,128]{3,2,1,0:T(8,128)S(1)}, u32[]{:S(2)}, u32[]{:S(2)}) %collective-permute-start.3) | collective-permute-done | bytes 393248 | tf_op jit(solution)/shard_map/ppermute | solution.py:678
  45.7 0.0 collective-permute-start.7
  45.7 7.6 %collective-permute-done.4.refs_2_.refs_5_ = f32[4,24,8,128]{3,2,1,0:T(8,128)S(1)} collective-permute-done((f32[4,24,8,128]{3,2,1,0:T(8,128)S(1)}, f32[4,24,8,128]{3,2,1,0:T(8,128)S(1)}, u32[]{:S(2)}, u32[]{:S(2)}) %collective-permute-start.4) | collective-permute-done | bytes 393248 | tf_op jit(solution)/shard_map/ppermute | solution.py:678
  53.3 0.0 collective-permute-start.8
  53.4 0.7 collective-permute-done.5.refs_3_.refs_6_
  54.1 0.0 collective-permute-start.9
  54.1 0.1 pad_add_fusion.my_place
  54.2 0.0 collective-permute-done.6.refs_4_.refs_7_
  54.2 0.0 collective-permute-done.7.refs_5_.refs_8_
  54.2 0.8 collective-permute-done.8.refs_6_.refs_9_
  55.1 0.8 collective-permute-done.9.refs_7_.refs_10_
  55.9 1.1 shard_map.107.refs_2_
  57.0 0.0 copy-start.1
  57.0 0.7 copy-done.1
  57.7 0.8 copy-done.3
  58.5 0.7 copy-done.5
  59.2 0.7 copy-done.7
  60.0 0.7 copy-done.9
  60.7 0.0 all-to-all-done
  60.7 1.1 copy-done.17
  61.9 1.0 copy-done.20
  62.9 0.0 copy-start.10
  62.9 0.0 copy-start.18
  62.9 0.0 copy-start.21
  62.9 2.5 %shard_map.106 = (f32[2048,128]{1,0:T(8,128)S(1)}, f32[2048,128]{1,0:T(8,128)S(1)}) custom-call(f32[2048,128]{1,0:T(8,128)S(1)} %bitcast.24, bf16[1536,256]{1,0:T(8,128)(2,1)S(1)} %copy-done.17, bf16[256,768]{1,0:T(8,128)(2,1)S(1)} %copy-done.20), custom_call_target="tpu_custom_call" | custom-call | flops 1610612736 | bytes 4194304 | tf_op jit(solution)/shard_map/pallas_call | solution.py:606
  65.4 0.0 copy-done.2
  65.5 14.3 %shard_map.108 = f32[2048,128]{1,0:T(8,128)S(1)} custom-call(s32[256]{0:T(256)S(1)} %multiply_add_fusion.place, s32[256]{0:T(256)S(1)} %get-tuple-element.15.half, s32[3]{0:T(128)S(1)} %pad_add_fusion.my_place, f32[2048,128]{1,0:T(8,128)S(1)} %get-tuple-element.19.refs_0_, f32[2048,128]{1,0:T(8,128)S(1)} %get-tuple-element.20.refs_1_, ...), custom_call_target="tpu_custom_call" | custom-call | flops 4831838208 | bytes 8388608 | tf_op jit(solution)/shard_map/pallas_call | solution.py:653
  79.9 31.2 %all_to_all.15 = f32[32,8,8,128]{3,2,1,0:T(8,128)S(1)} all-to-all(f32[32,8,8,128]{3,2,1,0:T(8,128)S(1)} %bitcast.25), channel_id=1, replica_groups=mesh['gx'=4,'gy'=4,'gz'=2] {'gx','gy','gz'}, dimensions={0} | all-to-all | bytes 2097152 | tf_op jit(solution)/shard_map/all_to_all | solution.py:704
  111.1 0.2 dot_general.5
  111.3 0.2 reshape.26
  111.5 1.0 convolution_bitcast_fusion
  112.5 0.1 broadcast_in_dim.11
  112.6 11.7 %all_to_all.16 = f32[32,8,128]{2,1,0:T(8,128)S(1)} all-to-all(f32[32,8,128]{2,1,0:T(8,128)S(1)} %broadcast_in_dim.12), channel_id=1, replica_groups=mesh['gx'=4,'gy'=4,'gz'=2] {'gx','gy','gz'}, dimensions={0} | all-to-all | bytes 262144 | tf_op jit(solution)/shard_map/all_to_all | solution.py:709
  124.3 0.1 div.38
  124.3 0.6 copy.17
  125.0 1.0 copy.19
  (27 shorter events, 0.2 us)
Async XLA Ops:
  0.6 0.7 copy-start.14
  0.7 0.7 copy-start.15
  1.3 0.8 copy-start.12
  2.2 0.8 copy-start.13
  4.0 6.8 %copy-start.22 = (s32[256]{0:T(256)S(1)}, s32[256]{0:T(256)}, u32[]{:S(2)}) copy-start(s32[256]{0:T(256)} %param.12) | copy-start | bytes 3076
  4.0 10.9 %collective-permute-start.2 = (f32[24,8,128]{2,1,0:T(8,128)S(1)}, f32[24,8,128]{2,1,0:T(8,128)S(1)}, u32[]{:S(2)}, u32[]{:S(2)}) collective-permute-start(f32[24,8,128]{2,1,0:T(8,128)S(1)} %shard_map.104), channel_id=1, source_target_pairs={{0,24},{8,0},{16,8},{24,16},{1,25},{9,1},{17,9},{25,17},{2,26},{10... | collective-permute-start | bytes 294920 | tf_op jit(solution)/shard_map/ppermute | solution.py:678
  9.1 8.7 %collective-permute-start.1 = (f32[24,8,128]{2,1,0:T(8,128)S(1)}, f32[24,8,128]{2,1,0:T(8,128)S(1)}, u32[]{:S(2)}, u32[]{:S(2)}) collective-permute-start(f32[24,8,128]{2,1,0:T(8,128)S(1)} %shard_map.104), channel_id=1, source_target_pairs={{0,16},{8,24},{16,0},{24,8},{1,17},{9,25},{17,1},{25,9},{2,18},{10... | collective-permute-start | bytes 294920 | tf_op jit(solution)/shard_map/ppermute | solution.py:678
  9.1 8.7 %collective-permute-start = (f32[24,8,128]{2,1,0:T(8,128)S(1)}, f32[24,8,128]{2,1,0:T(8,128)S(1)}, u32[]{:S(2)}, u32[]{:S(2)}) collective-permute-start(f32[24,8,128]{2,1,0:T(8,128)S(1)} %shard_map.104), channel_id=1, source_target_pairs={{0,8},{8,16},{16,24},{24,0},{1,9},{9,17},{17,25},{25,1},{2,10},{10... | collective-permute-start | bytes 294920 | tf_op jit(solution)/shard_map/ppermute | solution.py:678
  10.8 1.1 copy-start
  12.0 1.0 copy-start.11
  13.2 0.9 copy-start.16
  14.1 0.7 copy-start.19
  17.9 42.9 %all-to-all-start = ((f32[32,8,8,128]{3,2,1,0:T(8,128)}), f32[32,8,8,128]{3,2,1,0:T(8,128)S(1)}, u32[]{:S(2)}, u32[]{:S(2)}) async-start(f32[32,8,8,128]{3,2,1,0:T(8,128)} %param.9), calls=%async_computation | async-start | bytes 2097152 | tf_op jit(solution)/shard_map/all_to_all | solution.py:700
  22.4 23.3 %collective-permute-start.3 = (f32[4,24,8,128]{3,2,1,0:T(8,128)S(1)}, f32[4,24,8,128]{3,2,1,0:T(8,128)S(1)}, u32[]{:S(2)}, u32[]{:S(2)}) collective-permute-start(f32[4,24,8,128]{3,2,1,0:T(8,128)S(1)} %pad_maximum_fusion.refs_0_.refs_3_), channel_id=1, source_target_pairs={{0,2},{2,4},{4,6},{6,0},{1,3},{3,5},{5,7},{7,1},{8,10},{10,12},{12... | collective-permute-start | bytes 1179656 | tf_op jit(solution)/shard_map/ppermute | solution.py:678
  24.2 29.1 %collective-permute-start.4 = (f32[4,24,8,128]{3,2,1,0:T(8,128)S(1)}, f32[4,24,8,128]{3,2,1,0:T(8,128)S(1)}, u32[]{:S(2)}, u32[]{:S(2)}) collective-permute-start(f32[4,24,8,128]{3,2,1,0:T(8,128)S(1)} %pad_maximum_fusion.refs_0_.refs_3_), channel_id=1, source_target_pairs={{0,4},{2,6},{4,0},{6,2},{1,5},{3,7},{5,1},{7,3},{8,12},{10,14},{12... | collective-permute-start | bytes 1179656 | tf_op jit(solution)/shard_map/ppermute | solution.py:678
  25.7 28.5 %collective-permute-start.5 = (f32[4,24,8,128]{3,2,1,0:T(8,128)S(1)}, f32[4,24,8,128]{3,2,1,0:T(8,128)S(1)}, u32[]{:S(2)}, u32[]{:S(2)}) collective-permute-start(f32[4,24,8,128]{3,2,1,0:T(8,128)S(1)} %pad_maximum_fusion.refs_0_.refs_3_), channel_id=1, source_target_pairs={{0,6},{2,0},{4,2},{6,4},{1,7},{3,1},{5,3},{7,5},{8,14},{10,8},{12,... | collective-permute-start | bytes 1179656 | tf_op jit(solution)/shard_map/ppermute | solution.py:678
  27.1 27.1 %collective-permute-start.6 = (f32[4,24,8,128]{3,2,1,0:T(8,128)S(1)}, f32[4,24,8,128]{3,2,1,0:T(8,128)S(1)}, u32[]{:S(2)}, u32[]{:S(2)}) collective-permute-start(f32[4,24,8,128]{3,2,1,0:T(8,128)S(1)} %pad_maximum_fusion.refs_0_.refs_3_), channel_id=1, source_target_pairs={{0,1},{1,0},{2,3},{3,2},{4,5},{5,4},{6,7},{7,6},{8,9},{9,8},{10,11... | collective-permute-start | bytes 1179656 | tf_op jit(solution)/shard_map/ppermute | solution.py:678
  45.7 8.5 %collective-permute-start.7 = (f32[4,24,8,128]{3,2,1,0:T(8,128)S(1)}, f32[4,24,8,128]{3,2,1,0:T(8,128)S(1)}, u32[]{:S(2)}, u32[]{:S(2)}) collective-permute-start(f32[4,24,8,128]{3,2,1,0:T(8,128)S(1)} %collective-permute-done.3.refs_1_.refs_4_), channel_id=1, source_target_pairs={{0,1},{1,0},{2,3},{3,2},{4,5},{5,4},{6,7},{7,6},{8,9},{9,8},{10,11... | collective-permute-start | bytes 1179656 | tf_op jit(solution)/shard_map/ppermute | solution.py:678
  53.3 1.7 %collective-permute-start.8 = (f32[4,24,8,128]{3,2,1,0:T(8,128)S(1)}, f32[4,24,8,128]{3,2,1,0:T(8,128)S(1)}, u32[]{:S(2)}, u32[]{:S(2)}) collective-permute-start(f32[4,24,8,128]{3,2,1,0:T(8,128)S(1)} %collective-permute-done.4.refs_2_.refs_5_), channel_id=1, source_target_pairs={{0,1},{1,0},{2,3},{3,2},{4,5},{5,4},{6,7},{7,6},{8,9},{9,8},{10,11... | collective-permute-start | bytes 1179656 | tf_op jit(solution)/shard_map/ppermute | solution.py:678
  54.1 1.7 %collective-permute-start.9 = (f32[4,24,8,128]{3,2,1,0:T(8,128)S(1)}, f32[4,24,8,128]{3,2,1,0:T(8,128)S(1)}, u32[]{:S(2)}, u32[]{:S(2)}) collective-permute-start(f32[4,24,8,128]{3,2,1,0:T(8,128)S(1)} %collective-permute-done.5.refs_3_.refs_6_), channel_id=1, source_target_pairs={{0,1},{1,0},{2,3},{3,2},{4,5},{5,4},{6,7},{7,6},{8,9},{9,8},{10,11... | collective-permute-start | bytes 1179656 | tf_op jit(solution)/shard_map/ppermute | solution.py:678
  57.0 0.8 copy-start.1
  57.7 0.8 copy-start.3
  58.5 0.7 copy-start.5
  59.2 0.7 copy-start.7
  60.0 0.7 copy-start.9
  60.7 1.1 copy-start.17
  61.9 1.0 copy-start.20
  62.9 2.6 %copy-start.2 = (f32[4,24,8,128]{3,2,1,0:T(8,128)S(1)}, f32[4,24,8,128]{3,2,1,0:T(8,128)}, u32[]{:S(2)}) copy-start(f32[4,24,8,128]{3,2,1,0:T(8,128)} %copy-done.1) | copy-start | bytes 1179652
  62.9 2.6 %copy-start.4 = (f32[4,24,8,128]{3,2,1,0:T(8,128)S(1)}, f32[4,24,8,128]{3,2,1,0:T(8,128)}, u32[]{:S(2)}) copy-start(f32[4,24,8,128]{3,2,1,0:T(8,128)} %copy-done.3) | copy-start | bytes 1179652
  62.9 2.6 %copy-start.6 = (f32[4,24,8,128]{3,2,1,0:T(8,128)S(1)}, f32[4,24,8,128]{3,2,1,0:T(8,128)}, u32[]{:S(2)}) copy-start(f32[4,24,8,128]{3,2,1,0:T(8,128)} %copy-done.5) | copy-start | bytes 1179652
  62.9 2.6 %copy-start.8 = (f32[4,24,8,128]{3,2,1,0:T(8,128)S(1)}, f32[4,24,8,128]{3,2,1,0:T(8,128)}, u32[]{:S(2)}) copy-start(f32[4,24,8,128]{3,2,1,0:T(8,128)} %copy-done.7) | copy-start | bytes 1179652
  62.9 2.6 %copy-start.10 = (f32[4,24,8,128]{3,2,1,0:T(8,128)S(1)}, f32[4,24,8,128]{3,2,1,0:T(8,128)}, u32[]{:S(2)}) copy-start(f32[4,24,8,128]{3,2,1,0:T(8,128)} %copy-done.9) | copy-start | bytes 1179652
  62.9 2.6 %copy-start.18 = (bf16[1536,256]{1,0:T(8,128)(2,1)S(1)}, bf16[1536,256]{1,0:T(8,128)(2,1)}, u32[]{:S(2)}) copy-start(bf16[1536,256]{1,0:T(8,128)(2,1)} %copy-done.16) | copy-start | bytes 2359300
  62.9 2.6 %copy-start.21 = (bf16[256,768]{1,0:T(8,128)(2,1)S(1)}, bf16[256,768]{1,0:T(8,128)(2,1)}, u32[]{:S(2)}) copy-start(bf16[256,768]{1,0:T(8,128)(2,1)} %copy-done.19) | copy-start | bytes 1179652

commit v13 on v11

--- a/solution.py
+++ b/solution.py
@@ -395,6 +395,7 @@
             if not first:
                 slabs = [part * chunk + number for number in range(chunk)]
                 lay_products(groups, high_buf, low_buf, plane, depth, slabs, near)
+            sums = []
             for piece, hop_x, inner, stored, atoms_at in part_groups(part, chunk):
                 terms = ([], [])
                 for j in range(SUB):
@@ -404,15 +405,14 @@
                     for kp in range(2):
                         at = SUB + (inner * 2 + kp) * SUB + j
                         terms[kp].append(both * piece[hop_x, at])
-                for kp in range(2):
-                    at = pl.multiple_of((stored * 2 + kp) * SUB, SUB)
-                    coeffs[pl.ds(at, SUB), :] = row_sums(terms[kp])
+                sums += [row_sums(terms[0]), row_sums(terms[1])]
+            high, low = split_pair(jnp.concatenate(sums, axis=0))
+            rows = len(sums) * SUB
+            at = pl.multiple_of(part * rows, rows)
+            coeffs[pl.ds(at, rows), :] = mxu(high, ones) + mxu(low, ones)
             return carry
 
         lax.fori_loop(0, groups_x // chunk, project, 0)
-
-        high, low = split_pair(coeffs[...])
-        coeffs[...] = mxu(high, ones) + mxu(low, ones)
 
         def scatter(part, carry):
             for piece, hop_x, inner, stored, atoms_at in part_groups(part, 1):

time: 120 us -> 119 us (level)
  no operation moved by 1% of the time
where the time goes in v13:
time: 119 us
  blocking collectives  43 us (36%)
  waiting for transfers between devices  29.1 us (24%)
  Pallas kernels  19.7 us (17%)
  starting transfers between devices  17.8 us (15%)
  local copies, waits for them, and re-layouts  7.24 us (6%)
    all_to_all x1, blocking collectives, state_body(): lax.all_to_all(result, axes, split_axis=0, concat_axis=0, tiled=True)  31.3 us
    ppermute x10, waiting for transfers between devices, hops(): lax.ppermute(value, axis, [(i, (i + hop) % count) for i in range(count)])  29.1 us
    pallas_call x1, Pallas kernels, filter_call(): pl.pallas_call(functools.partial(filter_kernel, groups, atoms), out_shape...  15.9 us
    ppermute x10, starting transfers between devices, hops(): lax.ppermute(value, axis, [(i, (i + hop) % count) for i in range(count)])  11.9 us
    all_to_all x1, blocking collectives, state_body(): lax.all_to_all(jnp.broadcast_to(quarter[None], (domains,) + quarter.shape...  11.7 us
    all_to_all x1, starting transfers between devices, state_body(): lax.all_to_all(orbitals, axes, split_axis=0, concat_axis=0, tiled=True)  5.85 us
    unnamed x15, local copies, waits for them, and re-layouts  5.37 us
    pallas_call x1, Pallas kernels, first_call(): pl.pallas_call(functools.partial(first_kernel, groups), out_shape=[jax.Sh...  2.55 us
  transfers between devices with their start and end apart: 11, of which 4 were waited for; matrix products, arithmetic and copies ran while one was open for 1% of the time, Pallas kernels for 2%

profile of v13, /device:TPU:0, one launch (start us, length us, event | category | flops | bytes accessed | tf_op | source)
XLA Modules:
  0.0 118.7 jit_solution(4861226360822378680)
XLA Ops:
  0.6 0.0 copy-start.4
  0.7 0.0 copy-start.5
  0.7 0.7 copy-done.4
  1.3 0.0 copy-done.5
  1.3 0.0 copy-start.2
  1.3 0.8 copy-done.2
  2.2 0.0 copy-start.3
  2.2 0.8 copy-done.3
  2.9 0.0 copy-start.6
  2.9 1.0 shard_map.104
  4.0 3.1 %collective-permute-start = (f32[24,8,128]{2,1,0:T(8,128)S(1)}, f32[24,8,128]{2,1,0:T(8,128)S(1)}, u32[]{:S(2)}, u32[]{:S(2)}) collective-permute-start(f32[24,8,128]{2,1,0:T(8,128)S(1)} %shard_map.104), channel_id=1, source_target_pairs={{0,8},{8,16},{16,24},{24,0},{1,9},{9,17},{17,25},{25,1},{2,10},{10... | collective-permute-start | bytes 294920 | tf_op jit(solution)/shard_map/ppermute | solution.py:649
  7.0 2.6 %collective-permute-start.1 = (f32[24,8,128]{2,1,0:T(8,128)S(1)}, f32[24,8,128]{2,1,0:T(8,128)S(1)}, u32[]{:S(2)}, u32[]{:S(2)}) collective-permute-start(f32[24,8,128]{2,1,0:T(8,128)S(1)} %shard_map.104), channel_id=1, source_target_pairs={{0,16},{8,24},{16,0},{24,8},{1,17},{9,25},{17,1},{25,9},{2,18},{10... | collective-permute-start | bytes 294920 | tf_op jit(solution)/shard_map/ppermute | solution.py:649
  9.6 1.3 %collective-permute-start.2 = (f32[24,8,128]{2,1,0:T(8,128)S(1)}, f32[24,8,128]{2,1,0:T(8,128)S(1)}, u32[]{:S(2)}, u32[]{:S(2)}) collective-permute-start(f32[24,8,128]{2,1,0:T(8,128)S(1)} %shard_map.104), channel_id=1, source_target_pairs={{0,24},{8,0},{16,8},{24,16},{1,25},{9,1},{17,9},{25,17},{2,26},{10... | collective-permute-start | bytes 294920 | tf_op jit(solution)/shard_map/ppermute | solution.py:649
  11.0 0.0 copy-done.6
  11.0 0.7 slice.3
  11.7 0.0 copy-start
  11.7 1.1 copy-done
  12.8 0.0 copy-start.1
  12.8 1.0 copy-done.1
  13.8 0.3 shard_map.105
  14.1 0.0 collective-permute-done
  14.1 2.1 %collective-permute-done.1 = f32[24,8,128]{2,1,0:T(8,128)S(1)} collective-permute-done((f32[24,8,128]{2,1,0:T(8,128)S(1)}, f32[24,8,128]{2,1,0:T(8,128)S(1)}, u32[]{:S(2)}, u32[]{:S(2)}) %collective-permute-start.1) | collective-permute-done | bytes 98336 | tf_op jit(solution)/shard_map/ppermute | solution.py:649
  16.2 0.0 collective-permute-done.2
  16.3 5.8 %all-to-all-start = ((f32[32,8,8,128]{3,2,1,0:T(8,128)}), f32[32,8,8,128]{3,2,1,0:T(8,128)S(1)}, u32[]{:S(2)}, u32[]{:S(2)}) async-start(f32[32,8,8,128]{3,2,1,0:T(8,128)} %param.9), calls=%async_computation | async-start | bytes 2097152 | tf_op jit(solution)/shard_map/all_to_all | solution.py:671
  22.1 1.8 %collective-permute-start.3 = (f32[4,24,8,128]{3,2,1,0:T(8,128)S(1)}, f32[4,24,8,128]{3,2,1,0:T(8,128)S(1)}, u32[]{:S(2)}, u32[]{:S(2)}) collective-permute-start(f32[4,24,8,128]{3,2,1,0:T(8,128)S(1)} %pad_maximum_fusion.refs_2_), channel_id=1, source_target_pairs={{0,2},{2,4},{4,6},{6,0},{1,3},{3,5},{5,7},{7,1},{8,10},{10,12},{12... | collective-permute-start | bytes 1179656 | tf_op jit(solution)/shard_map/ppermute | solution.py:649
  24.0 1.5 %collective-permute-start.4 = (f32[4,24,8,128]{3,2,1,0:T(8,128)S(1)}, f32[4,24,8,128]{3,2,1,0:T(8,128)S(1)}, u32[]{:S(2)}, u32[]{:S(2)}) collective-permute-start(f32[4,24,8,128]{3,2,1,0:T(8,128)S(1)} %pad_maximum_fusion.refs_2_), channel_id=1, source_target_pairs={{0,4},{2,6},{4,0},{6,2},{1,5},{3,7},{5,1},{7,3},{8,12},{10,14},{12... | collective-permute-start | bytes 1179656 | tf_op jit(solution)/shard_map/ppermute | solution.py:649
  25.4 1.5 %collective-permute-start.5 = (f32[4,24,8,128]{3,2,1,0:T(8,128)S(1)}, f32[4,24,8,128]{3,2,1,0:T(8,128)}, u32[]{:S(2)}, u32[]{:S(2)}) collective-permute-start(f32[4,24,8,128]{3,2,1,0:T(8,128)S(1)} %pad_maximum_fusion.refs_2_), channel_id=1, source_target_pairs={{0,6},{2,0},{4,2},{6,4},{1,7},{3,1},{5,3},{7,5},{8,14},{10,8},{12,... | collective-permute-start | bytes 1179656 | tf_op jit(solution)/shard_map/ppermute | solution.py:649
  26.9 0.0 collective-permute-start.6
  26.9 18.6 %collective-permute-done.3.refs_3_ = f32[4,24,8,128]{3,2,1,0:T(8,128)S(1)} collective-permute-done((f32[4,24,8,128]{3,2,1,0:T(8,128)S(1)}, f32[4,24,8,128]{3,2,1,0:T(8,128)S(1)}, u32[]{:S(2)}, u32[]{:S(2)}) %collective-permute-start.3) | collective-permute-done | bytes 393248 | tf_op jit(solution)/shard_map/ppermute | solution.py:649
  45.5 0.0 collective-permute-start.7
  45.5 7.6 %collective-permute-done.4.refs_4_ = f32[4,24,8,128]{3,2,1,0:T(8,128)S(1)} collective-permute-done((f32[4,24,8,128]{3,2,1,0:T(8,128)S(1)}, f32[4,24,8,128]{3,2,1,0:T(8,128)S(1)}, u32[]{:S(2)}, u32[]{:S(2)}) %collective-permute-start.4) | collective-permute-done | bytes 393248 | tf_op jit(solution)/shard_map/ppermute | solution.py:649
  53.1 0.1 collective-permute-start.8
  53.2 0.7 collective-permute-done.5.refs_5_
  54.0 0.0 collective-permute-start.9
  54.0 0.1 pad_add_fusion.my_place
  54.1 0.0 all-to-all-done
  54.1 2.5 %shard_map.106 = (f32[2048,128]{1,0:T(8,128)S(1)}, f32[2048,128]{1,0:T(8,128)S(1)}) custom-call(f32[2048,128]{1,0:T(8,128)S(1)} %bitcast.24, bf16[1536,256]{1,0:T(8,128)(2,1)S(1)} %get-tuple-element.17.refs_1_.refs_10_, bf16[256,768]{1,0:T(8,128)(2,1)S(1)} %get-tuple-element.18.refs_2_.refs_11_), custom_call_target="tpu_custom_call" | custom-call | flops 1610612736 | bytes 4194304 | tf_op jit(solution)/shard_map/pallas_call | solution.py:593
  56.6 0.0 collective-permute-done.6.refs_6_
  56.6 0.0 collective-permute-done.7.refs_7_
  56.7 0.0 collective-permute-done.8.refs_8_
  56.7 0.0 collective-permute-done.9.refs_9_
  56.7 15.9 %shard_map.107 = f32[2048,128]{1,0:T(8,128)S(1)} custom-call(s32[256]{0:T(256)S(1)} %multiply_add_fusion.place, s32[256]{0:T(256)S(1)} %get-tuple-element.15.half, s32[3]{0:T(128)S(1)} %pad_add_fusion.my_place, f32[2048,128]{1,0:T(8,128)S(1)} %get-tuple-element.19.refs_0_, f32[2048,128]{1,0:T(8,128)S(1)} %get-tuple-element.20.refs_1_, ...), custom_call_target="tpu_custom_call" | custom-call | flops 4831838208 | bytes 8388608 | tf_op jit(solution)/shard_map/pallas_call | solution.py:623
  72.6 31.3 %all_to_all.15 = f32[32,8,8,128]{3,2,1,0:T(8,128)S(1)} all-to-all(f32[32,8,8,128]{3,2,1,0:T(8,128)S(1)} %bitcast.25), channel_id=1, replica_groups=mesh['gx'=4,'gy'=4,'gz'=2] {'gx','gy','gz'}, dimensions={0} | all-to-all | bytes 2097152 | tf_op jit(solution)/shard_map/all_to_all | solution.py:674
  103.9 0.2 dot_general.5
  104.1 0.2 reshape.26
  104.3 1.0 convolution_bitcast_fusion
  105.3 0.1 broadcast_in_dim.11
  105.4 11.7 %all_to_all.16 = f32[32,8,128]{2,1,0:T(8,128)S(1)} all-to-all(f32[32,8,128]{2,1,0:T(8,128)S(1)} %broadcast_in_dim.12), channel_id=1, replica_groups=mesh['gx'=4,'gy'=4,'gz'=2] {'gx','gy','gz'}, dimensions={0} | all-to-all | bytes 262144 | tf_op jit(solution)/shard_map/all_to_all | solution.py:679
  117.1 0.1 div.38
  117.2 0.6 copy.17
  117.8 1.0 copy.19
  (7 shorter events, 0.1 us)
Async XLA Ops:
  0.6 0.7 copy-start.4
  0.7 0.7 copy-start.5
  1.3 0.8 copy-start.2
  2.2 0.8 copy-start.3
  2.9 8.0 %copy-start.6 = (s32[256]{0:T(256)S(1)}, s32[256]{0:T(256)}, u32[]{:S(2)}) copy-start(s32[256]{0:T(256)} %param.12) | copy-start | bytes 3076
  4.0 10.1 %collective-permute-start = (f32[24,8,128]{2,1,0:T(8,128)S(1)}, f32[24,8,128]{2,1,0:T(8,128)S(1)}, u32[]{:S(2)}, u32[]{:S(2)}) collective-permute-start(f32[24,8,128]{2,1,0:T(8,128)S(1)} %shard_map.104), channel_id=1, source_target_pairs={{0,8},{8,16},{16,24},{24,0},{1,9},{9,17},{17,25},{25,1},{2,10},{10... | collective-permute-start | bytes 294920 | tf_op jit(solution)/shard_map/ppermute | solution.py:649
  7.0 9.2 %collective-permute-start.1 = (f32[24,8,128]{2,1,0:T(8,128)S(1)}, f32[24,8,128]{2,1,0:T(8,128)S(1)}, u32[]{:S(2)}, u32[]{:S(2)}) collective-permute-start(f32[24,8,128]{2,1,0:T(8,128)S(1)} %shard_map.104), channel_id=1, source_target_pairs={{0,16},{8,24},{16,0},{24,8},{1,17},{9,25},{17,1},{25,9},{2,18},{10... | collective-permute-start | bytes 294920 | tf_op jit(solution)/shard_map/ppermute | solution.py:649
  9.6 6.6 %collective-permute-start.2 = (f32[24,8,128]{2,1,0:T(8,128)S(1)}, f32[24,8,128]{2,1,0:T(8,128)S(1)}, u32[]{:S(2)}, u32[]{:S(2)}) collective-permute-start(f32[24,8,128]{2,1,0:T(8,128)S(1)} %shard_map.104), channel_id=1, source_target_pairs={{0,24},{8,0},{16,8},{24,16},{1,25},{9,1},{17,9},{25,17},{2,26},{10... | collective-permute-start | bytes 294920 | tf_op jit(solution)/shard_map/ppermute | solution.py:649
  11.7 1.1 copy-start
  12.8 1.0 copy-start.1
  16.3 37.8 %all-to-all-start = ((f32[32,8,8,128]{3,2,1,0:T(8,128)}), f32[32,8,8,128]{3,2,1,0:T(8,128)S(1)}, u32[]{:S(2)}, u32[]{:S(2)}) async-start(f32[32,8,8,128]{3,2,1,0:T(8,128)} %param.9), calls=%async_computation | async-start | bytes 2097152 | tf_op jit(solution)/shard_map/all_to_all | solution.py:671
  22.1 23.3 %collective-permute-start.3 = (f32[4,24,8,128]{3,2,1,0:T(8,128)S(1)}, f32[4,24,8,128]{3,2,1,0:T(8,128)S(1)}, u32[]{:S(2)}, u32[]{:S(2)}) collective-permute-start(f32[4,24,8,128]{3,2,1,0:T(8,128)S(1)} %pad_maximum_fusion.refs_2_), channel_id=1, source_target_pairs={{0,2},{2,4},{4,6},{6,0},{1,3},{3,5},{5,7},{7,1},{8,10},{10,12},{12... | collective-permute-start | bytes 1179656 | tf_op jit(solution)/shard_map/ppermute | solution.py:649
  24.0 29.1 %collective-permute-start.4 = (f32[4,24,8,128]{3,2,1,0:T(8,128)S(1)}, f32[4,24,8,128]{3,2,1,0:T(8,128)S(1)}, u32[]{:S(2)}, u32[]{:S(2)}) collective-permute-start(f32[4,24,8,128]{3,2,1,0:T(8,128)S(1)} %pad_maximum_fusion.refs_2_), channel_id=1, source_target_pairs={{0,4},{2,6},{4,0},{6,2},{1,5},{3,7},{5,1},{7,3},{8,12},{10,14},{12... | collective-permute-start | bytes 1179656 | tf_op jit(solution)/shard_map/ppermute | solution.py:649
  25.4 28.6 %collective-permute-start.5 = (f32[4,24,8,128]{3,2,1,0:T(8,128)S(1)}, f32[4,24,8,128]{3,2,1,0:T(8,128)}, u32[]{:S(2)}, u32[]{:S(2)}) collective-permute-start(f32[4,24,8,128]{3,2,1,0:T(8,128)S(1)} %pad_maximum_fusion.refs_2_), channel_id=1, source_target_pairs={{0,6},{2,0},{4,2},{6,4},{1,7},{3,1},{5,3},{7,5},{8,14},{10,8},{12,... | collective-permute-start | bytes 1179656 | tf_op jit(solution)/shard_map/ppermute | solution.py:649
  26.9 29.7 %collective-permute-start.6 = (f32[4,24,8,128]{3,2,1,0:T(8,128)S(1)}, f32[4,24,8,128]{3,2,1,0:T(8,128)}, u32[]{:S(2)}, u32[]{:S(2)}) collective-permute-start(f32[4,24,8,128]{3,2,1,0:T(8,128)S(1)} %pad_maximum_fusion.refs_2_), channel_id=1, source_target_pairs={{0,1},{1,0},{2,3},{3,2},{4,5},{5,4},{6,7},{7,6},{8,9},{9,8},{10,11... | collective-permute-start | bytes 1179656 | tf_op jit(solution)/shard_map/ppermute | solution.py:649
  45.5 11.2 %collective-permute-start.7 = (f32[4,24,8,128]{3,2,1,0:T(8,128)S(1)}, f32[4,24,8,128]{3,2,1,0:T(8,128)}, u32[]{:S(2)}, u32[]{:S(2)}) collective-permute-start(f32[4,24,8,128]{3,2,1,0:T(8,128)S(1)} %collective-permute-done.3.refs_3_), channel_id=1, source_target_pairs={{0,1},{1,0},{2,3},{3,2},{4,5},{5,4},{6,7},{7,6},{8,9},{9,8},{10,11... | collective-permute-start | bytes 1179656 | tf_op jit(solution)/shard_map/ppermute | solution.py:649
  53.1 3.6 %collective-permute-start.8 = (f32[4,24,8,128]{3,2,1,0:T(8,128)S(1)}, f32[4,24,8,128]{3,2,1,0:T(8,128)}, u32[]{:S(2)}, u32[]{:S(2)}) collective-permute-start(f32[4,24,8,128]{3,2,1,0:T(8,128)S(1)} %collective-permute-done.4.refs_4_), channel_id=1, source_target_pairs={{0,1},{1,0},{2,3},{3,2},{4,5},{5,4},{6,7},{7,6},{8,9},{9,8},{10,11... | collective-permute-start | bytes 1179656 | tf_op jit(solution)/shard_map/ppermute | solution.py:649
  54.0 2.7 %collective-permute-start.9 = (f32[4,24,8,128]{3,2,1,0:T(8,128)}, f32[4,24,8,128]{3,2,1,0:T(8,128)}, u32[]{:S(2)}, u32[]{:S(2)}) collective-permute-start(f32[4,24,8,128]{3,2,1,0:T(8,128)} %collective-permute-done.5.refs_5_), channel_id=1, source_target_pairs={{0,1},{1,0},{2,3},{3,2},{4,5},{5,4},{6,7},{7,6},{8,9},{9,8},{10,11... | collective-permute-start | bytes 1179656 | tf_op jit(solution)/shard_map/ppermute | solution.py:649

commit v14 on v13

--- a/solution.py
+++ b/solution.py
@@ -322,14 +322,21 @@
     lax.fori_loop(0, groups_x // chunk, product, 0)
 
 
+def hops_apart(count):
+    near = sorted({0, 1 % count, count - 1})
+    return near, [hop for hop in range(count) if hop not in near]
+
+
 def filter_kernel(groups, atoms, place, half, my_place, *refs):
     groups_x, groups_y, groups_z = groups
     pieces = groups_y * groups_z
     field_a, near_a = refs[:2]
-    packs_in = refs[2 : 2 + pieces]
-    plane, depth, out = refs[2 + pieces : 5 + pieces]
-    field_b, field_c, local, coeffs, high_buf, low_buf, near = refs[5 + pieces : 12 + pieces]
-    spares = refs[12 + pieces :]
+    kinds = hops_apart(groups_x)
+    arrays = pieces * sum(1 for hops_of in kinds if hops_of)
+    packs_in = refs[2 : 2 + arrays]
+    plane, depth, out = refs[2 + arrays : 5 + arrays]
+    field_b, field_c, local, coeffs, high_buf, low_buf, near = refs[5 + arrays : 12 + arrays]
+    spares = refs[12 + arrays :]
     targets = (near,) + tuple(spares)
     columns = groups_x * groups_y
     domains = columns * groups_z
@@ -349,16 +356,28 @@
     for target in targets:
         target[...] = jnp.zeros(target.shape, f32)
 
-    def sources(hop_x):
+    def sources(kind, index):
+        hop_x = index + 2 if kind else jnp.where(index < 2, index, groups_x - 1)
         for hop_z in range(groups_z):
             for hop_y in range(groups_y):
                 from_x = lax.rem(my_place[0] + (groups_x - hop_x), groups_x)
                 from_y = lax.rem(my_place[1] + (groups_y - hop_y), groups_y)
                 from_z = lax.rem(my_place[2] + (groups_z - hop_z), groups_z)
-                yield packs_in[hop_z * groups_y + hop_y], from_x * groups_y + from_y, from_z
-
-    def lay_potential(hop_x, carry):
-        for piece, column, depth_at in sources(hop_x):
+                piece = packs_in[kind * pieces + hop_z * groups_y + hop_y]
+                yield piece, from_x * groups_y + from_y, from_z
+
+    def each_hop(visit):
+        for kind, hops_of in enumerate(kinds):
+            if hops_of:
+
+                def step(index, carry, kind=kind):
+                    visit(kind, index)
+                    return carry
+
+                lax.fori_loop(0, len(hops_of), step, 0)
+
+    def lay_potential(kind, hop_x):
+        for piece, column, depth_at in sources(kind, hop_x):
             mine = side == column % 2
             for tile in range(SUB):
                 value = diagonal + piece[hop_x, tile]
@@ -368,9 +387,8 @@
                     rows = pl.ds(pl.multiple_of(at, SUB), SUB)
                     chosen = jnp.where(side == upper, value, other)
                     local[rows, :] = jnp.where(mine, chosen, local[rows, :])
-        return carry
-
-    lax.fori_loop(0, groups_x, lay_potential, 0)
+
+    each_hop(lay_potential)
 
     ones = (
         (
@@ -381,22 +399,28 @@
         .astype(jnp.bfloat16)
     )
 
-    def part_groups(part, share):
-        for number in range(share):
-            hop_x = part * share + number
-            for at, (piece, column, depth_at) in enumerate(sources(hop_x)):
-                for inner in range(per_device):
-                    stored = (hop_x * pieces + at) * per_device + inner
-                    atoms_at = ((column * groups_z + depth_at) * per_device + inner) * SUB
-                    yield piece, hop_x, inner, stored, atoms_at
+    blocks = [(kind, index) for kind, hops_of in enumerate(kinds) for index in range(len(hops_of))]
+
+    def hop_groups(kind, index):
+        block = index + kind * len(kinds[0])
+        for at, (piece, column, depth_at) in enumerate(sources(kind, index)):
+            for inner in range(per_device):
+                stored = (block * pieces + at) * per_device + inner
+                atoms_at = ((column * groups_z + depth_at) * per_device + inner) * SUB
+                yield piece, index, inner, stored, atoms_at
 
     def apply_step(cur, prev, new, alpha, beta, first, last):
-        def project(part, carry):
+        def project(part):
             if not first:
                 slabs = [part * chunk + number for number in range(chunk)]
                 lay_products(groups, high_buf, low_buf, plane, depth, slabs, near)
             sums = []
-            for piece, hop_x, inner, stored, atoms_at in part_groups(part, chunk):
+            held = [
+                group
+                for kind, index in blocks[part * chunk : (part + 1) * chunk]
+                for group in hop_groups(kind, index)
+            ]
+            for piece, hop_x, inner, stored, atoms_at in held:
                 terms = ([], [])
                 for j in range(SUB):
                     atom = atoms_at + j
@@ -408,14 +432,13 @@
                 sums += [row_sums(terms[0]), row_sums(terms[1])]
             high, low = split_pair(jnp.concatenate(sums, axis=0))
             rows = len(sums) * SUB
-            at = pl.multiple_of(part * rows, rows)
-            coeffs[pl.ds(at, rows), :] = mxu(high, ones) + mxu(low, ones)
-            return carry
-
-        lax.fori_loop(0, groups_x // chunk, project, 0)
-
-        def scatter(part, carry):
-            for piece, hop_x, inner, stored, atoms_at in part_groups(part, 1):
+            coeffs[part * rows : (part + 1) * rows, :] = mxu(high, ones) + mxu(low, ones)
+
+        for part in range(groups_x // chunk):
+            project(part)
+
+        def scatter(kind, index):
+            for piece, hop_x, inner, stored, atoms_at in hop_groups(kind, index):
                 weights = [
                     coeffs[pl.ds(pl.multiple_of((stored * 2 + kp) * SUB, SUB), SUB), :]
                     for kp in range(2)
@@ -433,9 +456,8 @@
                     rows = pl.ds(place[atom], SUB)
                     target = targets[j % len(targets)]
                     target[rows, :] = target[rows, :] + value
-            return carry
-
-        lax.fori_loop(0, groups_x, scatter, 0)
+
+        each_hop(scatter)
 
         def combine(slab_at, carry):
             for tile in range(pairs_slab):
@@ -643,12 +665,15 @@
     return out.reshape(columns * groups_z, SUB, SUB, LANE)
 
 
+def moved(value, axis, hop):
+    count = lax.axis_size(axis)
+    if hop == 0:
+        return value
+    return lax.ppermute(value, axis, [(i, (i + hop) % count) for i in range(count)])
+
+
 def hops(value, axis):
-    count = lax.axis_size(axis)
-    return [value] + [
-        lax.ppermute(value, axis, [(i, (i + hop) % count) for i in range(count)])
-        for hop in range(1, count)
-    ]
+    return [moved(value, axis, hop) for hop in range(lax.axis_size(axis))]
 
 
 def state_body(orbitals, potential, projectors, owner_rank, box_anchor, box_extent, coupling):
@@ -660,14 +685,20 @@
     my_place = jnp.stack([lax.axis_index(axis) for axis in axes])
     me = (my_place[0] * groups[1] + my_place[1]) * groups_z + my_place[2]
     pack = packed_inputs((me * atoms_own)[None], box_extent, coupling, potential, projectors)
-    line = jnp.stack(hops(pack, "gx"))
+    near_hops, far_hops = hops_apart(groups[0])
+    near_line = jnp.stack([moved(pack, "gx", hop) for hop in near_hops])
     place, half = box_places(groups, owner_rank, box_anchor[2])
     plane, depth = weights_call(groups)
-    orbitals, line, place, half, plane, depth = lax.optimization_barrier(
-        (orbitals, line, place, half, plane, depth)
-    )
-    crossed = [hops(piece, "gz") for piece in hops(line, "gy")]
-    packs = [crossed[hop_y][hop_z] for hop_z in range(groups_z) for hop_y in range(groups[1])]
+    orbitals, near_line, place, half, plane, depth = lax.optimization_barrier(
+        (orbitals, near_line, place, half, plane, depth)
+    )
+    lines = [near_line]
+    if far_hops:
+        lines.append(jnp.stack([moved(pack, "gx", hop) for hop in far_hops]))
+    packs = []
+    for line in lines:
+        crossed = [hops(piece, "gz") for piece in hops(line, "gy")]
+        packs += [crossed[hop_y][hop_z] for hop_z in range(groups_z) for hop_y in range(groups[1])]
     field = lax.all_to_all(orbitals, axes, split_axis=0, concat_axis=0, tiled=True)
     field, near = first_call(groups, field, plane, depth)
     result = filter_call(groups, place, half, my_place, field, near, packs, plane, depth)

time: 119 us -> 127 us (1.067)
  starting transfers between devices: 17.8 us -> 23.3 us
  local copies, waits for them, and re-layouts: 7.24 us -> 11.1 us
  blocking collectives: 43 us -> 41.4 us
    ppermute x10 -> x17, starting transfers between devices: 11.9 us -> 18.6 us  [moved(): lax.ppermute(value, axis, [(i, (i + hop) % count) for i in range(count)])]
    unnamed x15 -> x39, local copies, waits for them, and re-layouts: 5.37 us -> 9.21 us
    all_to_all x1, blocking collectives: 31.3 us -> 29.8 us  [state_body(): lax.all_to_all(result, axes, split_axis=0, concat_axis=0, tiled=True)]
    ppermute x10 -> x17, waiting for transfers between devices: 29.1 us -> 30 us  [moved(): lax.ppermute(value, axis, [(i, (i + hop) % count) for i in range(count)])]
  transfers between devices with their start and end apart: 11 -> 18, of which waited for: 4 -> 7; matrix products, arithmetic and copies ran while one was open for 1% -> 1% of each run, Pallas kernels for 2% -> 2%
where the time goes in v14:
time: 127 us
  blocking collectives  41.4 us (33%)
  waiting for transfers between devices  30 us (24%)
  starting transfers between devices  23.3 us (18%)
  Pallas kernels  19.1 us (15%)
  local copies, waits for them, and re-layouts  11.1 us (9%)
    ppermute x17, waiting for transfers between devices, moved(): lax.ppermute(value, axis, [(i, (i + hop) % count) for i in range(count)])  30 us
    all_to_all x1, blocking collectives, state_body(): lax.all_to_all(result, axes, split_axis=0, concat_axis=0, tiled=True)  29.8 us
    ppermute x17, starting transfers between devices, moved(): lax.ppermute(value, axis, [(i, (i + hop) % count) for i in range(count)])  18.6 us
    pallas_call x1, Pallas kernels, filter_call(): pl.pallas_call(functools.partial(filter_kernel, groups, atoms), out_shape...  15.3 us
    all_to_all x1, blocking collectives, state_body(): lax.all_to_all(jnp.broadcast_to(quarter[None], (domains,) + quarter.shape...  11.7 us
    unnamed x39, local copies, waits for them, and re-layouts  9.21 us
    all_to_all x1, starting transfers between devices, state_body(): lax.all_to_all(orbitals, axes, split_axis=0, concat_axis=0, tiled=True)  4.65 us
  transfers between devices with their start and end apart: 18, of which 7 were waited for; matrix products, arithmetic and copies ran while one was open for 1% of the time, Pallas kernels for 2%

profile of v14, /device:TPU:0, one launch (start us, length us, event | category | flops | bytes accessed | tf_op | source)
XLA Modules:
  0.0 126.9 jit_solution(10993770177731702086)
XLA Ops:
  0.7 0.7 copy-done.4
  1.3 0.0 copy-done.5
  1.3 0.8 copy-done.2
  2.2 0.8 copy-done.3
  2.9 1.0 shard_map.104
  4.0 3.1 %collective-permute-start = (f32[24,8,128]{2,1,0:T(8,128)S(1)}, f32[24,8,128]{2,1,0:T(8,128)S(1)}, u32[]{:S(2)}, u32[]{:S(2)}) collective-permute-start(f32[24,8,128]{2,1,0:T(8,128)S(1)} %shard_map.104), channel_id=1, source_target_pairs={{0,8},{8,16},{16,24},{24,0},{1,9},{9,17},{17,25},{25,1},{2,10},{10... | collective-permute-start | bytes 294920 | tf_op jit(solution)/shard_map/ppermute | solution.py:672
  7.0 2.1 %collective-permute-start.1 = (f32[24,8,128]{2,1,0:T(8,128)S(1)}, f32[24,8,128]{2,1,0:T(8,128)S(1)}, u32[]{:S(2)}, u32[]{:S(2)}) collective-permute-start(f32[24,8,128]{2,1,0:T(8,128)S(1)} %shard_map.104), channel_id=1, source_target_pairs={{0,24},{8,0},{16,8},{24,16},{1,25},{9,1},{17,9},{25,17},{2,26},{10... | collective-permute-start | bytes 294920 | tf_op jit(solution)/shard_map/ppermute | solution.py:672
  9.2 0.7 slice.3
  9.9 0.0 copy-start
  9.9 1.1 copy-done
  11.0 1.0 copy-done.1
  12.0 0.3 shard_map.105
  12.3 0.3 collective-permute-done
  12.6 0.8 collective-permute-done.1
  13.4 4.6 %all-to-all-start = ((f32[32,8,8,128]{3,2,1,0:T(8,128)}), f32[32,8,8,128]{3,2,1,0:T(8,128)S(1)}, u32[]{:S(2)}, u32[]{:S(2)}) async-start(f32[32,8,8,128]{3,2,1,0:T(8,128)} %param.9), calls=%async_computation | async-start | bytes 2097152 | tf_op jit(solution)/shard_map/all_to_all | solution.py:702
  18.1 2.7 %collective-permute-start.9 = (f32[24,8,128]{2,1,0:T(8,128)S(1)}, f32[24,8,128]{2,1,0:T(8,128)S(1)}, u32[]{:S(2)}, u32[]{:S(2)}) collective-permute-start(f32[24,8,128]{2,1,0:T(8,128)S(1)} %shard_map.104), channel_id=1, source_target_pairs={{0,16},{8,24},{16,0},{24,8},{1,17},{9,25},{17,1},{25,9},{2,18},{10... | collective-permute-start | bytes 294920 | tf_op jit(solution)/shard_map/ppermute | solution.py:672
  20.8 1.5 %collective-permute-start.2 = (f32[3,24,8,128]{3,2,1,0:T(8,128)S(1)}, f32[3,24,8,128]{3,2,1,0:T(8,128)S(1)}, u32[]{:S(2)}, u32[]{:S(2)}) collective-permute-start(f32[3,24,8,128]{3,2,1,0:T(8,128)S(1)} %pad_maximum_fusion.refs_2_), channel_id=1, source_target_pairs={{0,2},{2,4},{4,6},{6,0},{1,3},{3,5},{5,7},{7,1},{8,10},{10,12},{12... | collective-permute-start | bytes 884744 | tf_op jit(solution)/shard_map/ppermute | solution.py:672
  22.3 1.5 %collective-permute-start.3 = (f32[3,24,8,128]{3,2,1,0:T(8,128)S(1)}, f32[3,24,8,128]{3,2,1,0:T(8,128)S(1)}, u32[]{:S(2)}, u32[]{:S(2)}) collective-permute-start(f32[3,24,8,128]{3,2,1,0:T(8,128)S(1)} %pad_maximum_fusion.refs_2_), channel_id=1, source_target_pairs={{0,4},{2,6},{4,0},{6,2},{1,5},{3,7},{5,1},{7,3},{8,12},{10,14},{12... | collective-permute-start | bytes 884744 | tf_op jit(solution)/shard_map/ppermute | solution.py:672
  23.8 1.4 %collective-permute-start.4 = (f32[3,24,8,128]{3,2,1,0:T(8,128)S(1)}, f32[3,24,8,128]{3,2,1,0:T(8,128)S(1)}, u32[]{:S(2)}, u32[]{:S(2)}) collective-permute-start(f32[3,24,8,128]{3,2,1,0:T(8,128)S(1)} %pad_maximum_fusion.refs_2_), channel_id=1, source_target_pairs={{0,6},{2,0},{4,2},{6,4},{1,7},{3,1},{5,3},{7,5},{8,14},{10,8},{12,... | collective-permute-start | bytes 884744 | tf_op jit(solution)/shard_map/ppermute | solution.py:672
  25.2 23.3 %collective-permute-done.9 = f32[24,8,128]{2,1,0:T(8,128)S(1)} collective-permute-done((f32[24,8,128]{2,1,0:T(8,128)S(1)}, f32[24,8,128]{2,1,0:T(8,128)S(1)}, u32[]{:S(2)}, u32[]{:S(2)}) %collective-permute-start.9) | collective-permute-done | bytes 98336 | tf_op jit(solution)/shard_map/ppermute | solution.py:672
  48.5 1.5 %collective-permute-start.10 = (f32[1,24,8,128]{3,2,1,0:T(8,128)S(1)}, f32[1,24,8,128]{3,2,1,0:T(8,128)S(1)}, u32[]{:S(2)}, u32[]{:S(2)}) collective-permute-start(f32[1,24,8,128]{3,2,1,0:T(8,128)S(1)} %bitcast.28), channel_id=1, source_target_pairs={{0,2},{2,4},{4,6},{6,0},{1,3},{3,5},{5,7},{7,1},{8,10},{10,12},{12... | collective-permute-start | bytes 294920 | tf_op jit(solution)/shard_map/ppermute | solution.py:672
  50.0 1.5 %collective-permute-start.11 = (f32[1,24,8,128]{3,2,1,0:T(8,128)S(1)}, f32[1,24,8,128]{3,2,1,0:T(8,128)S(1)}, u32[]{:S(2)}, u32[]{:S(2)}) collective-permute-start(f32[1,24,8,128]{3,2,1,0:T(8,128)S(1)} %bitcast.29), channel_id=1, source_target_pairs={{0,4},{2,6},{4,0},{6,2},{1,5},{3,7},{5,1},{7,3},{8,12},{10,14},{12... | collective-permute-start | bytes 294920 | tf_op jit(solution)/shard_map/ppermute | solution.py:672
  51.5 2.6 %collective-permute-done.10.refs_11_ = f32[1,24,8,128]{3,2,1,0:T(8,128)S(1)} collective-permute-done((f32[1,24,8,128]{3,2,1,0:T(8,128)S(1)}, f32[1,24,8,128]{3,2,1,0:T(8,128)S(1)}, u32[]{:S(2)}, u32[]{:S(2)}) %collective-permute-start.10) | collective-permute-done | bytes 98336 | tf_op jit(solution)/shard_map/ppermute | solution.py:672
  54.1 1.4 %collective-permute-start.12 = (f32[1,24,8,128]{3,2,1,0:T(8,128)S(1)}, f32[1,24,8,128]{3,2,1,0:T(8,128)}, u32[]{:S(2)}, u32[]{:S(2)}) collective-permute-start(f32[1,24,8,128]{3,2,1,0:T(8,128)S(1)} %bitcast.30), channel_id=1, source_target_pairs={{0,6},{2,0},{4,2},{6,4},{1,7},{3,1},{5,3},{7,5},{8,14},{10,8},{12,... | collective-permute-start | bytes 294920 | tf_op jit(solution)/shard_map/ppermute | solution.py:672
  55.5 0.3 collective-permute-done.11.refs_12_
  55.9 0.0 collective-permute-start.13
  55.9 0.6 copy-done.6
  56.5 2.3 %collective-permute-done.12.refs_13_ = f32[1,24,8,128]{3,2,1,0:T(8,128)} collective-permute-done((f32[1,24,8,128]{3,2,1,0:T(8,128)S(1)}, f32[1,24,8,128]{3,2,1,0:T(8,128)}, u32[]{:S(2)}, u32[]{:S(2)}) %collective-permute-start.12) | collective-permute-done | bytes 98336 | tf_op jit(solution)/shard_map/ppermute | solution.py:672
  58.8 0.0 collective-permute-start.14
  58.8 0.6 copy-done.8
  59.5 0.0 collective-permute-done.13.refs_14_
  59.5 0.6 copy-done.12
  60.1 0.5 collective-permute-start.5
  60.6 0.0 collective-permute-done.2.refs_3_
  60.6 0.0 collective-permute-start.6
  60.6 0.0 collective-permute-done.3.refs_4_
  60.6 0.5 collective-permute-start.7
  61.1 0.0 collective-permute-done.4.refs_5_
  61.1 0.1 collective-permute-start.8
  61.2 0.0 collective-permute-done.14.refs_15_
  61.2 0.6 copy-done.14
  61.8 0.4 collective-permute-start.15
  62.3 0.6 copy-done.10
  62.9 0.1 pad_add_fusion.my_place
  63.0 0.2 collective-permute-done.15.refs_16_
  63.2 0.6 copy-done.16
  63.9 0.4 collective-permute-start.16
  64.2 0.0 all-to-all-done
  64.3 2.5 %shard_map.106 = (f32[2048,128]{1,0:T(8,128)S(1)}, f32[2048,128]{1,0:T(8,128)S(1)}) custom-call(f32[2048,128]{1,0:T(8,128)S(1)} %bitcast.24, bf16[1536,256]{1,0:T(8,128)(2,1)S(1)} %get-tuple-element.17.refs_1_.refs_18_, bf16[256,768]{1,0:T(8,128)(2,1)S(1)} %get-tuple-element.18.refs_2_.refs_19_), custom_call_target="tpu_custom_call" | custom-call | flops 1610612736 | bytes 4194304 | tf_op jit(solution)/shard_map/pallas_call | solution.py:615
  66.8 0.0 collective-permute-done.16.refs_17_
  66.8 0.0 collective-permute-done.5.refs_6_
  66.9 0.0 collective-permute-done.6.refs_7_
  66.9 0.0 collective-permute-done.7.refs_8_
  66.9 0.0 collective-permute-done.8.refs_9_
  66.9 15.3 %shard_map.107 = f32[2048,128]{1,0:T(8,128)S(1)} custom-call(s32[256]{0:T(256)S(1)} %multiply_add_fusion.place, s32[256]{0:T(256)S(1)} %get-tuple-element.15.half, s32[3]{0:T(128)S(1)} %pad_add_fusion.my_place, f32[2048,128]{1,0:T(8,128)S(1)} %get-tuple-element.19.refs_0_, f32[2048,128]{1,0:T(8,128)S(1)} %get-tuple-element.20.refs_1_, ...), custom_call_target="tpu_custom_call" | custom-call | flops 4831838208 | bytes 8388608 | tf_op jit(solution)/shard_map/pallas_call | solution.py:645
  82.3 29.8 %all_to_all.15 = f32[32,8,8,128]{3,2,1,0:T(8,128)S(1)} all-to-all(f32[32,8,8,128]{3,2,1,0:T(8,128)S(1)} %bitcast.25), channel_id=1, replica_groups=mesh['gx'=4,'gy'=4,'gz'=2] {'gx','gy','gz'}, dimensions={0} | all-to-all | bytes 2097152 | tf_op jit(solution)/shard_map/all_to_all | solution.py:705
  112.1 0.2 dot_general.5
  112.2 0.2 reshape.26
  112.4 1.0 convolution_bitcast_fusion
  113.4 0.1 broadcast_in_dim.11
  113.5 11.7 %all_to_all.16 = f32[32,8,128]{2,1,0:T(8,128)S(1)} all-to-all(f32[32,8,128]{2,1,0:T(8,128)S(1)} %broadcast_in_dim.12), channel_id=1, replica_groups=mesh['gx'=4,'gy'=4,'gz'=2] {'gx','gy','gz'}, dimensions={0} | all-to-all | bytes 262144 | tf_op jit(solution)/shard_map/all_to_all | solution.py:710
  125.2 0.1 div.38
  125.3 0.6 copy.17
  125.9 1.0 copy.19
  (32 shorter events, 0.2 us)
Async XLA Ops:
  0.6 0.7 copy-start.4
  0.7 0.7 copy-start.5
  1.3 0.8 copy-start.2
  2.2 0.8 copy-start.3
  2.9 6.2 %copy-start.18 = (s32[256]{0:T(256)S(1)}, s32[256]{0:T(256)}, u32[]{:S(2)}) copy-start(s32[256]{0:T(256)} %param.12) | copy-start | bytes 3076
  4.0 8.6 %collective-permute-start = (f32[24,8,128]{2,1,0:T(8,128)S(1)}, f32[24,8,128]{2,1,0:T(8,128)S(1)}, u32[]{:S(2)}, u32[]{:S(2)}) collective-permute-start(f32[24,8,128]{2,1,0:T(8,128)S(1)} %shard_map.104), channel_id=1, source_target_pairs={{0,8},{8,16},{16,24},{24,0},{1,9},{9,17},{17,25},{25,1},{2,10},{10... | collective-permute-start | bytes 294920 | tf_op jit(solution)/shard_map/ppermute | solution.py:672
  7.0 6.4 %collective-permute-start.1 = (f32[24,8,128]{2,1,0:T(8,128)S(1)}, f32[24,8,128]{2,1,0:T(8,128)S(1)}, u32[]{:S(2)}, u32[]{:S(2)}) collective-permute-start(f32[24,8,128]{2,1,0:T(8,128)S(1)} %shard_map.104), channel_id=1, source_target_pairs={{0,24},{8,0},{16,8},{24,16},{1,25},{9,1},{17,9},{25,17},{2,26},{10... | collective-permute-start | bytes 294920 | tf_op jit(solution)/shard_map/ppermute | solution.py:672
  9.9 1.1 copy-start
  11.0 1.0 copy-start.1
  13.4 50.8 %all-to-all-start = ((f32[32,8,8,128]{3,2,1,0:T(8,128)}), f32[32,8,8,128]{3,2,1,0:T(8,128)S(1)}, u32[]{:S(2)}, u32[]{:S(2)}) async-start(f32[32,8,8,128]{3,2,1,0:T(8,128)} %param.9), calls=%async_computation | async-start | bytes 2097152 | tf_op jit(solution)/shard_map/all_to_all | solution.py:702
  18.1 30.4 %collective-permute-start.9 = (f32[24,8,128]{2,1,0:T(8,128)S(1)}, f32[24,8,128]{2,1,0:T(8,128)S(1)}, u32[]{:S(2)}, u32[]{:S(2)}) collective-permute-start(f32[24,8,128]{2,1,0:T(8,128)S(1)} %shard_map.104), channel_id=1, source_target_pairs={{0,16},{8,24},{16,0},{24,8},{1,17},{9,25},{17,1},{25,9},{2,18},{10... | collective-permute-start | bytes 294920 | tf_op jit(solution)/shard_map/ppermute | solution.py:672
  20.8 39.8 %collective-permute-start.2 = (f32[3,24,8,128]{3,2,1,0:T(8,128)S(1)}, f32[3,24,8,128]{3,2,1,0:T(8,128)S(1)}, u32[]{:S(2)}, u32[]{:S(2)}) collective-permute-start(f32[3,24,8,128]{3,2,1,0:T(8,128)S(1)} %pad_maximum_fusion.refs_2_), channel_id=1, source_target_pairs={{0,2},{2,4},{4,6},{6,0},{1,3},{3,5},{5,7},{7,1},{8,10},{10,12},{12... | collective-permute-start | bytes 884744 | tf_op jit(solution)/shard_map/ppermute | solution.py:672
  22.3 38.3 %collective-permute-start.3 = (f32[3,24,8,128]{3,2,1,0:T(8,128)S(1)}, f32[3,24,8,128]{3,2,1,0:T(8,128)S(1)}, u32[]{:S(2)}, u32[]{:S(2)}) collective-permute-start(f32[3,24,8,128]{3,2,1,0:T(8,128)S(1)} %pad_maximum_fusion.refs_2_), channel_id=1, source_target_pairs={{0,4},{2,6},{4,0},{6,2},{1,5},{3,7},{5,1},{7,3},{8,12},{10,14},{12... | collective-permute-start | bytes 884744 | tf_op jit(solution)/shard_map/ppermute | solution.py:672
  23.8 37.4 %collective-permute-start.4 = (f32[3,24,8,128]{3,2,1,0:T(8,128)S(1)}, f32[3,24,8,128]{3,2,1,0:T(8,128)S(1)}, u32[]{:S(2)}, u32[]{:S(2)}) collective-permute-start(f32[3,24,8,128]{3,2,1,0:T(8,128)S(1)} %pad_maximum_fusion.refs_2_), channel_id=1, source_target_pairs={{0,6},{2,0},{4,2},{6,4},{1,7},{3,1},{5,3},{7,5},{8,14},{10,8},{12,... | collective-permute-start | bytes 884744 | tf_op jit(solution)/shard_map/ppermute | solution.py:672
  48.5 5.6 %collective-permute-start.10 = (f32[1,24,8,128]{3,2,1,0:T(8,128)S(1)}, f32[1,24,8,128]{3,2,1,0:T(8,128)S(1)}, u32[]{:S(2)}, u32[]{:S(2)}) collective-permute-start(f32[1,24,8,128]{3,2,1,0:T(8,128)S(1)} %bitcast.28), channel_id=1, source_target_pairs={{0,2},{2,4},{4,6},{6,0},{1,3},{3,5},{5,7},{7,1},{8,10},{10,12},{12... | collective-permute-start | bytes 294920 | tf_op jit(solution)/shard_map/ppermute | solution.py:672
  50.0 5.9 %collective-permute-start.11 = (f32[1,24,8,128]{3,2,1,0:T(8,128)S(1)}, f32[1,24,8,128]{3,2,1,0:T(8,128)S(1)}, u32[]{:S(2)}, u32[]{:S(2)}) collective-permute-start(f32[1,24,8,128]{3,2,1,0:T(8,128)S(1)} %bitcast.29), channel_id=1, source_target_pairs={{0,4},{2,6},{4,0},{6,2},{1,5},{3,7},{5,1},{7,3},{8,12},{10,14},{12... | collective-permute-start | bytes 294920 | tf_op jit(solution)/shard_map/ppermute | solution.py:672
  54.1 4.7 %collective-permute-start.12 = (f32[1,24,8,128]{3,2,1,0:T(8,128)S(1)}, f32[1,24,8,128]{3,2,1,0:T(8,128)}, u32[]{:S(2)}, u32[]{:S(2)}) collective-permute-start(f32[1,24,8,128]{3,2,1,0:T(8,128)S(1)} %bitcast.30), channel_id=1, source_target_pairs={{0,6},{2,0},{4,2},{6,4},{1,7},{3,1},{5,3},{7,5},{8,14},{10,8},{12,... | collective-permute-start | bytes 294920 | tf_op jit(solution)/shard_map/ppermute | solution.py:672
  55.9 3.6 %collective-permute-start.13 = (f32[1,24,8,128]{3,2,1,0:T(8,128)S(1)}, f32[1,24,8,128]{3,2,1,0:T(8,128)S(1)}, u32[]{:S(2)}, u32[]{:S(2)}) collective-permute-start(f32[1,24,8,128]{3,2,1,0:T(8,128)S(1)} %bitcast.31), channel_id=1, source_target_pairs={{0,1},{1,0},{2,3},{3,2},{4,5},{5,4},{6,7},{7,6},{8,9},{9,8},{10,11... | collective-permute-start | bytes 294920 | tf_op jit(solution)/shard_map/ppermute | solution.py:672
  55.9 0.6 copy-start.6
  58.8 2.4 %collective-permute-start.14 = (f32[1,24,8,128]{3,2,1,0:T(8,128)S(1)}, f32[1,24,8,128]{3,2,1,0:T(8,128)S(1)}, u32[]{:S(2)}, u32[]{:S(2)}) collective-permute-start(f32[1,24,8,128]{3,2,1,0:T(8,128)S(1)} %collective-permute-done.10.refs_11_), channel_id=1, source_target_pairs={{0,1},{1,0},{2,3},{3,2},{4,5},{5,4},{6,7},{7,6},{8,9},{9,8},{10,11... | collective-permute-start | bytes 294920 | tf_op jit(solution)/shard_map/ppermute | solution.py:672
  58.8 0.6 copy-start.8
  59.5 0.6 copy-start.12
  60.1 6.7 %collective-permute-start.5 = (f32[3,24,8,128]{3,2,1,0:T(8,128)S(1)}, f32[3,24,8,128]{3,2,1,0:T(8,128)}, u32[]{:S(2)}, u32[]{:S(2)}) collective-permute-start(f32[3,24,8,128]{3,2,1,0:T(8,128)S(1)} %pad_maximum_fusion.refs_2_), channel_id=1, source_target_pairs={{0,1},{1,0},{2,3},{3,2},{4,5},{5,4},{6,7},{7,6},{8,9},{9,8},{10,11... | collective-permute-start | bytes 884744 | tf_op jit(solution)/shard_map/ppermute | solution.py:672
  60.6 6.2 %collective-permute-start.6 = (f32[3,24,8,128]{3,2,1,0:T(8,128)S(1)}, f32[3,24,8,128]{3,2,1,0:T(8,128)}, u32[]{:S(2)}, u32[]{:S(2)}) collective-permute-start(f32[3,24,8,128]{3,2,1,0:T(8,128)S(1)} %collective-permute-done.2.refs_3_), channel_id=1, source_target_pairs={{0,1},{1,0},{2,3},{3,2},{4,5},{5,4},{6,7},{7,6},{8,9},{9,8},{10,11... | collective-permute-start | bytes 884744 | tf_op jit(solution)/shard_map/ppermute | solution.py:672
  60.6 6.2 %collective-permute-start.7 = (f32[3,24,8,128]{3,2,1,0:T(8,128)S(1)}, f32[3,24,8,128]{3,2,1,0:T(8,128)}, u32[]{:S(2)}, u32[]{:S(2)}) collective-permute-start(f32[3,24,8,128]{3,2,1,0:T(8,128)S(1)} %collective-permute-done.3.refs_4_), channel_id=1, source_target_pairs={{0,1},{1,0},{2,3},{3,2},{4,5},{5,4},{6,7},{7,6},{8,9},{9,8},{10,11... | collective-permute-start | bytes 884744 | tf_op jit(solution)/shard_map/ppermute | solution.py:672
  61.1 5.7 %collective-permute-start.8 = (f32[3,24,8,128]{3,2,1,0:T(8,128)S(1)}, f32[3,24,8,128]{3,2,1,0:T(8,128)}, u32[]{:S(2)}, u32[]{:S(2)}) collective-permute-start(f32[3,24,8,128]{3,2,1,0:T(8,128)S(1)} %collective-permute-done.4.refs_5_), channel_id=1, source_target_pairs={{0,1},{1,0},{2,3},{3,2},{4,5},{5,4},{6,7},{7,6},{8,9},{9,8},{10,11... | collective-permute-start | bytes 884744 | tf_op jit(solution)/shard_map/ppermute | solution.py:672
  61.2 0.6 copy-start.14
  61.8 1.4 %collective-permute-start.15 = (f32[1,24,8,128]{3,2,1,0:T(8,128)S(1)}, f32[1,24,8,128]{3,2,1,0:T(8,128)S(1)}, u32[]{:S(2)}, u32[]{:S(2)}) collective-permute-start(f32[1,24,8,128]{3,2,1,0:T(8,128)S(1)} %collective-permute-done.11.refs_12_), channel_id=1, source_target_pairs={{0,1},{1,0},{2,3},{3,2},{4,5},{5,4},{6,7},{7,6},{8,9},{9,8},{10,11... | collective-permute-start | bytes 294920 | tf_op jit(solution)/shard_map/ppermute | solution.py:672
  62.3 0.6 copy-start.10
  63.2 0.6 copy-start.16
  63.9 3.0 %collective-permute-start.16 = (f32[1,24,8,128]{3,2,1,0:T(8,128)}, f32[1,24,8,128]{3,2,1,0:T(8,128)}, u32[]{:S(2)}, u32[]{:S(2)}) collective-permute-start(f32[1,24,8,128]{3,2,1,0:T(8,128)} %collective-permute-done.12.refs_13_), channel_id=1, source_target_pairs={{0,1},{1,0},{2,3},{3,2},{4,5},{5,4},{6,7},{7,6},{8,9},{9,8},{10,11... | collective-permute-start | bytes 294920 | tf_op jit(solution)/shard_map/ppermute | solution.py:672
  64.2 2.6 %copy-start.7 = (f32[24,8,128]{2,1,0:T(8,128)S(1)}, f32[24,8,128]{2,1,0:T(8,128)}, u32[]{:S(2)}) copy-start(f32[24,8,128]{2,1,0:T(8,128)} %copy-done.6) | copy-start | bytes 294916
  64.2 2.6 %copy-start.9 = (f32[1,24,8,128]{3,2,1,0:T(8,128)S(1)}, f32[1,24,8,128]{3,2,1,0:T(8,128)}, u32[]{:S(2)}) copy-start(f32[1,24,8,128]{3,2,1,0:T(8,128)} %copy-done.8) | copy-start | bytes 294916
  64.3 2.7 %copy-start.11 = (f32[1,24,8,128]{3,2,1,0:T(8,128)S(1)}, f32[1,24,8,128]{3,2,1,0:T(8,128)}, u32[]{:S(2)}) copy-start(f32[1,24,8,128]{3,2,1,0:T(8,128)} %copy-done.10) | copy-start | bytes 294916
  64.3 2.7 %copy-start.13 = (f32[1,24,8,128]{3,2,1,0:T(8,128)S(1)}, f32[1,24,8,128]{3,2,1,0:T(8,128)}, u32[]{:S(2)}) copy-start(f32[1,24,8,128]{3,2,1,0:T(8,128)} %copy-done.12) | copy-start | bytes 294916
  64.3 2.7 %copy-start.15 = (f32[1,24,8,128]{3,2,1,0:T(8,128)S(1)}, f32[1,24,8,128]{3,2,1,0:T(8,128)}, u32[]{:S(2)}) copy-start(f32[1,24,8,128]{3,2,1,0:T(8,128)} %copy-done.14) | copy-start | bytes 294916
  64.3 2.7 %copy-start.17 = (f32[1,24,8,128]{3,2,1,0:T(8,128)S(1)}, f32[1,24,8,128]{3,2,1,0:T(8,128)}, u32[]{:S(2)}) copy-start(f32[1,24,8,128]{3,2,1,0:T(8,128)} %copy-done.16) | copy-start | bytes 294916

commit v15 on v13

--- a/solution.py
+++ b/solution.py
@@ -415,7 +415,7 @@
         lax.fori_loop(0, groups_x // chunk, project, 0)
 
         def scatter(part, carry):
-            for piece, hop_x, inner, stored, atoms_at in part_groups(part, 1):
+            for piece, hop_x, inner, stored, atoms_at in part_groups(part, chunk):
                 weights = [
                     coeffs[pl.ds(pl.multiple_of((stored * 2 + kp) * SUB, SUB), SUB), :]
                     for kp in range(2)
@@ -435,7 +435,7 @@
                     target[rows, :] = target[rows, :] + value
             return carry
 
-        lax.fori_loop(0, groups_x, scatter, 0)
+        lax.fori_loop(0, groups_x // chunk, scatter, 0)
 
         def combine(slab_at, carry):
             for tile in range(pairs_slab):

time: 119 us -> 119 us (level)
  no operation moved by 1% of the time
where the time goes in v15:
time: 119 us; the launch traced here: 118 us
  blocking collectives  43 us (36%)
  waiting for transfers between devices  29.1 us (24%)
  Pallas kernels  19.2 us (16%)
  starting transfers between devices  17.8 us (15%)
  local copies, waits for them, and re-layouts  7.24 us (6%)
    all_to_all x1, blocking collectives, state_body(): lax.all_to_all(result, axes, split_axis=0, concat_axis=0, tiled=True)  31.3 us
    ppermute x10, waiting for transfers between devices, hops(): lax.ppermute(value, axis, [(i, (i + hop) % count) for i in range(count)])  29.1 us
    pallas_call x1, Pallas kernels, filter_call(): pl.pallas_call(functools.partial(filter_kernel, groups, atoms), out_shape...  15.4 us
    ppermute x10, starting transfers between devices, hops(): lax.ppermute(value, axis, [(i, (i + hop) % count) for i in range(count)])  11.9 us
    all_to_all x1, blocking collectives, state_body(): lax.all_to_all(jnp.broadcast_to(quarter[None], (domains,) + quarter.shape...  11.7 us
    all_to_all x1, starting transfers between devices, state_body(): lax.all_to_all(orbitals, axes, split_axis=0, concat_axis=0, tiled=True)  5.85 us
    unnamed x15, local copies, waits for them, and re-layouts  5.37 us
    pallas_call x1, Pallas kernels, first_call(): pl.pallas_call(functools.partial(first_kernel, groups), out_shape=[jax.Sh...  2.55 us
  transfers between devices with their start and end apart: 11, of which 4 were waited for; matrix products, arithmetic and copies ran while one was open for 1% of the time, Pallas kernels for 2%

profile of v15, /device:TPU:0, one launch (start us, length us, event | category | flops | bytes accessed | tf_op | source)
XLA Modules:
  0.0 118.3 jit_solution(14122128988922195450)
XLA Ops:
  0.6 0.0 copy-start.4
  0.7 0.0 copy-start.5
  0.7 0.7 copy-done.4
  1.3 0.0 copy-done.5
  1.3 0.0 copy-start.2
  1.3 0.8 copy-done.2
  2.2 0.0 copy-start.3
  2.2 0.8 copy-done.3
  2.9 0.0 copy-start.6
  2.9 1.0 shard_map.104
  4.0 3.1 %collective-permute-start = (f32[24,8,128]{2,1,0:T(8,128)S(1)}, f32[24,8,128]{2,1,0:T(8,128)S(1)}, u32[]{:S(2)}, u32[]{:S(2)}) collective-permute-start(f32[24,8,128]{2,1,0:T(8,128)S(1)} %shard_map.104), channel_id=1, source_target_pairs={{0,8},{8,16},{16,24},{24,0},{1,9},{9,17},{17,25},{25,1},{2,10},{10... | collective-permute-start | bytes 294920 | tf_op jit(solution)/shard_map/ppermute | solution.py:649
  7.0 2.6 %collective-permute-start.1 = (f32[24,8,128]{2,1,0:T(8,128)S(1)}, f32[24,8,128]{2,1,0:T(8,128)S(1)}, u32[]{:S(2)}, u32[]{:S(2)}) collective-permute-start(f32[24,8,128]{2,1,0:T(8,128)S(1)} %shard_map.104), channel_id=1, source_target_pairs={{0,16},{8,24},{16,0},{24,8},{1,17},{9,25},{17,1},{25,9},{2,18},{10... | collective-permute-start | bytes 294920 | tf_op jit(solution)/shard_map/ppermute | solution.py:649
  9.6 1.3 %collective-permute-start.2 = (f32[24,8,128]{2,1,0:T(8,128)S(1)}, f32[24,8,128]{2,1,0:T(8,128)S(1)}, u32[]{:S(2)}, u32[]{:S(2)}) collective-permute-start(f32[24,8,128]{2,1,0:T(8,128)S(1)} %shard_map.104), channel_id=1, source_target_pairs={{0,24},{8,0},{16,8},{24,16},{1,25},{9,1},{17,9},{25,17},{2,26},{10... | collective-permute-start | bytes 294920 | tf_op jit(solution)/shard_map/ppermute | solution.py:649
  11.0 0.0 copy-done.6
  11.0 0.7 slice.3
  11.7 0.0 copy-start
  11.7 1.1 copy-done
  12.8 0.0 copy-start.1
  12.8 1.0 copy-done.1
  13.8 0.3 shard_map.105
  14.1 0.0 collective-permute-done
  14.1 2.1 %collective-permute-done.1 = f32[24,8,128]{2,1,0:T(8,128)S(1)} collective-permute-done((f32[24,8,128]{2,1,0:T(8,128)S(1)}, f32[24,8,128]{2,1,0:T(8,128)S(1)}, u32[]{:S(2)}, u32[]{:S(2)}) %collective-permute-start.1) | collective-permute-done | bytes 98336 | tf_op jit(solution)/shard_map/ppermute | solution.py:649
  16.2 0.0 collective-permute-done.2
  16.3 5.8 %all-to-all-start = ((f32[32,8,8,128]{3,2,1,0:T(8,128)}), f32[32,8,8,128]{3,2,1,0:T(8,128)S(1)}, u32[]{:S(2)}, u32[]{:S(2)}) async-start(f32[32,8,8,128]{3,2,1,0:T(8,128)} %param.9), calls=%async_computation | async-start | bytes 2097152 | tf_op jit(solution)/shard_map/all_to_all | solution.py:671
  22.1 1.8 %collective-permute-start.3 = (f32[4,24,8,128]{3,2,1,0:T(8,128)S(1)}, f32[4,24,8,128]{3,2,1,0:T(8,128)S(1)}, u32[]{:S(2)}, u32[]{:S(2)}) collective-permute-start(f32[4,24,8,128]{3,2,1,0:T(8,128)S(1)} %pad_maximum_fusion.refs_2_), channel_id=1, source_target_pairs={{0,2},{2,4},{4,6},{6,0},{1,3},{3,5},{5,7},{7,1},{8,10},{10,12},{12... | collective-permute-start | bytes 1179656 | tf_op jit(solution)/shard_map/ppermute | solution.py:649
  24.0 1.5 %collective-permute-start.4 = (f32[4,24,8,128]{3,2,1,0:T(8,128)S(1)}, f32[4,24,8,128]{3,2,1,0:T(8,128)S(1)}, u32[]{:S(2)}, u32[]{:S(2)}) collective-permute-start(f32[4,24,8,128]{3,2,1,0:T(8,128)S(1)} %pad_maximum_fusion.refs_2_), channel_id=1, source_target_pairs={{0,4},{2,6},{4,0},{6,2},{1,5},{3,7},{5,1},{7,3},{8,12},{10,14},{12... | collective-permute-start | bytes 1179656 | tf_op jit(solution)/shard_map/ppermute | solution.py:649
  25.4 1.5 %collective-permute-start.5 = (f32[4,24,8,128]{3,2,1,0:T(8,128)S(1)}, f32[4,24,8,128]{3,2,1,0:T(8,128)}, u32[]{:S(2)}, u32[]{:S(2)}) collective-permute-start(f32[4,24,8,128]{3,2,1,0:T(8,128)S(1)} %pad_maximum_fusion.refs_2_), channel_id=1, source_target_pairs={{0,6},{2,0},{4,2},{6,4},{1,7},{3,1},{5,3},{7,5},{8,14},{10,8},{12,... | collective-permute-start | bytes 1179656 | tf_op jit(solution)/shard_map/ppermute | solution.py:649
  26.9 0.0 collective-permute-start.6
  26.9 18.6 %collective-permute-done.3.refs_3_ = f32[4,24,8,128]{3,2,1,0:T(8,128)S(1)} collective-permute-done((f32[4,24,8,128]{3,2,1,0:T(8,128)S(1)}, f32[4,24,8,128]{3,2,1,0:T(8,128)S(1)}, u32[]{:S(2)}, u32[]{:S(2)}) %collective-permute-start.3) | collective-permute-done | bytes 393248 | tf_op jit(solution)/shard_map/ppermute | solution.py:649
  45.5 0.0 collective-permute-start.7
  45.5 7.6 %collective-permute-done.4.refs_4_ = f32[4,24,8,128]{3,2,1,0:T(8,128)S(1)} collective-permute-done((f32[4,24,8,128]{3,2,1,0:T(8,128)S(1)}, f32[4,24,8,128]{3,2,1,0:T(8,128)S(1)}, u32[]{:S(2)}, u32[]{:S(2)}) %collective-permute-start.4) | collective-permute-done | bytes 393248 | tf_op jit(solution)/shard_map/ppermute | solution.py:649
  53.1 0.1 collective-permute-start.8
  53.2 0.7 collective-permute-done.5.refs_5_
  54.0 0.0 collective-permute-start.9
  54.0 0.1 pad_add_fusion.my_place
  54.1 0.0 all-to-all-done
  54.1 2.5 %shard_map.106 = (f32[2048,128]{1,0:T(8,128)S(1)}, f32[2048,128]{1,0:T(8,128)S(1)}) custom-call(f32[2048,128]{1,0:T(8,128)S(1)} %bitcast.24, bf16[1536,256]{1,0:T(8,128)(2,1)S(1)} %get-tuple-element.17.refs_1_.refs_10_, bf16[256,768]{1,0:T(8,128)(2,1)S(1)} %get-tuple-element.18.refs_2_.refs_11_), custom_call_target="tpu_custom_call" | custom-call | flops 1610612736 | bytes 4194304 | tf_op jit(solution)/shard_map/pallas_call | solution.py:593
  56.6 0.0 collective-permute-done.6.refs_6_
  56.6 0.0 collective-permute-done.7.refs_7_
  56.7 0.0 collective-permute-done.8.refs_8_
  56.7 0.0 collective-permute-done.9.refs_9_
  56.7 15.4 %shard_map.107 = f32[2048,128]{1,0:T(8,128)S(1)} custom-call(s32[256]{0:T(256)S(1)} %multiply_add_fusion.place, s32[256]{0:T(256)S(1)} %get-tuple-element.15.half, s32[3]{0:T(128)S(1)} %pad_add_fusion.my_place, f32[2048,128]{1,0:T(8,128)S(1)} %get-tuple-element.19.refs_0_, f32[2048,128]{1,0:T(8,128)S(1)} %get-tuple-element.20.refs_1_, ...), custom_call_target="tpu_custom_call" | custom-call | flops 4831838208 | bytes 8388608 | tf_op jit(solution)/shard_map/pallas_call | solution.py:623
  72.1 31.3 %all_to_all.15 = f32[32,8,8,128]{3,2,1,0:T(8,128)S(1)} all-to-all(f32[32,8,8,128]{3,2,1,0:T(8,128)S(1)} %bitcast.25), channel_id=1, replica_groups=mesh['gx'=4,'gy'=4,'gz'=2] {'gx','gy','gz'}, dimensions={0} | all-to-all | bytes 2097152 | tf_op jit(solution)/shard_map/all_to_all | solution.py:674
  103.4 0.2 dot_general.5
  103.6 0.2 reshape.26
  103.8 1.0 convolution_bitcast_fusion
  104.8 0.1 broadcast_in_dim.11
  104.9 11.7 %all_to_all.16 = f32[32,8,128]{2,1,0:T(8,128)S(1)} all-to-all(f32[32,8,128]{2,1,0:T(8,128)S(1)} %broadcast_in_dim.12), channel_id=1, replica_groups=mesh['gx'=4,'gy'=4,'gz'=2] {'gx','gy','gz'}, dimensions={0} | all-to-all | bytes 262144 | tf_op jit(solution)/shard_map/all_to_all | solution.py:679
  116.6 0.1 div.38
  116.7 0.6 copy.17
  117.3 1.0 copy.19
  (7 shorter events, 0.1 us)
Async XLA Ops:
  0.6 0.7 copy-start.4
  0.7 0.7 copy-start.5
  1.3 0.8 copy-start.2
  2.2 0.8 copy-start.3
  2.9 8.0 %copy-start.6 = (s32[256]{0:T(256)S(1)}, s32[256]{0:T(256)}, u32[]{:S(2)}) copy-start(s32[256]{0:T(256)} %param.12) | copy-start | bytes 3076
  4.0 10.1 %collective-permute-start = (f32[24,8,128]{2,1,0:T(8,128)S(1)}, f32[24,8,128]{2,1,0:T(8,128)S(1)}, u32[]{:S(2)}, u32[]{:S(2)}) collective-permute-start(f32[24,8,128]{2,1,0:T(8,128)S(1)} %shard_map.104), channel_id=1, source_target_pairs={{0,8},{8,16},{16,24},{24,0},{1,9},{9,17},{17,25},{25,1},{2,10},{10... | collective-permute-start | bytes 294920 | tf_op jit(solution)/shard_map/ppermute | solution.py:649
  7.0 9.2 %collective-permute-start.1 = (f32[24,8,128]{2,1,0:T(8,128)S(1)}, f32[24,8,128]{2,1,0:T(8,128)S(1)}, u32[]{:S(2)}, u32[]{:S(2)}) collective-permute-start(f32[24,8,128]{2,1,0:T(8,128)S(1)} %shard_map.104), channel_id=1, source_target_pairs={{0,16},{8,24},{16,0},{24,8},{1,17},{9,25},{17,1},{25,9},{2,18},{10... | collective-permute-start | bytes 294920 | tf_op jit(solution)/shard_map/ppermute | solution.py:649
  9.6 6.6 %collective-permute-start.2 = (f32[24,8,128]{2,1,0:T(8,128)S(1)}, f32[24,8,128]{2,1,0:T(8,128)S(1)}, u32[]{:S(2)}, u32[]{:S(2)}) collective-permute-start(f32[24,8,128]{2,1,0:T(8,128)S(1)} %shard_map.104), channel_id=1, source_target_pairs={{0,24},{8,0},{16,8},{24,16},{1,25},{9,1},{17,9},{25,17},{2,26},{10... | collective-permute-start | bytes 294920 | tf_op jit(solution)/shard_map/ppermute | solution.py:649
  11.7 1.1 copy-start
  12.8 1.0 copy-start.1
  16.3 37.8 %all-to-all-start = ((f32[32,8,8,128]{3,2,1,0:T(8,128)}), f32[32,8,8,128]{3,2,1,0:T(8,128)S(1)}, u32[]{:S(2)}, u32[]{:S(2)}) async-start(f32[32,8,8,128]{3,2,1,0:T(8,128)} %param.9), calls=%async_computation | async-start | bytes 2097152 | tf_op jit(solution)/shard_map/all_to_all | solution.py:671
  22.1 23.3 %collective-permute-start.3 = (f32[4,24,8,128]{3,2,1,0:T(8,128)S(1)}, f32[4,24,8,128]{3,2,1,0:T(8,128)S(1)}, u32[]{:S(2)}, u32[]{:S(2)}) collective-permute-start(f32[4,24,8,128]{3,2,1,0:T(8,128)S(1)} %pad_maximum_fusion.refs_2_), channel_id=1, source_target_pairs={{0,2},{2,4},{4,6},{6,0},{1,3},{3,5},{5,7},{7,1},{8,10},{10,12},{12... | collective-permute-start | bytes 1179656 | tf_op jit(solution)/shard_map/ppermute | solution.py:649
  24.0 29.1 %collective-permute-start.4 = (f32[4,24,8,128]{3,2,1,0:T(8,128)S(1)}, f32[4,24,8,128]{3,2,1,0:T(8,128)S(1)}, u32[]{:S(2)}, u32[]{:S(2)}) collective-permute-start(f32[4,24,8,128]{3,2,1,0:T(8,128)S(1)} %pad_maximum_fusion.refs_2_), channel_id=1, source_target_pairs={{0,4},{2,6},{4,0},{6,2},{1,5},{3,7},{5,1},{7,3},{8,12},{10,14},{12... | collective-permute-start | bytes 1179656 | tf_op jit(solution)/shard_map/ppermute | solution.py:649
  25.4 28.6 %collective-permute-start.5 = (f32[4,24,8,128]{3,2,1,0:T(8,128)S(1)}, f32[4,24,8,128]{3,2,1,0:T(8,128)}, u32[]{:S(2)}, u32[]{:S(2)}) collective-permute-start(f32[4,24,8,128]{3,2,1,0:T(8,128)S(1)} %pad_maximum_fusion.refs_2_), channel_id=1, source_target_pairs={{0,6},{2,0},{4,2},{6,4},{1,7},{3,1},{5,3},{7,5},{8,14},{10,8},{12,... | collective-permute-start | bytes 1179656 | tf_op jit(solution)/shard_map/ppermute | solution.py:649
  26.9 29.7 %collective-permute-start.6 = (f32[4,24,8,128]{3,2,1,0:T(8,128)S(1)}, f32[4,24,8,128]{3,2,1,0:T(8,128)}, u32[]{:S(2)}, u32[]{:S(2)}) collective-permute-start(f32[4,24,8,128]{3,2,1,0:T(8,128)S(1)} %pad_maximum_fusion.refs_2_), channel_id=1, source_target_pairs={{0,1},{1,0},{2,3},{3,2},{4,5},{5,4},{6,7},{7,6},{8,9},{9,8},{10,11... | collective-permute-start | bytes 1179656 | tf_op jit(solution)/shard_map/ppermute | solution.py:649
  45.5 11.2 %collective-permute-start.7 = (f32[4,24,8,128]{3,2,1,0:T(8,128)S(1)}, f32[4,24,8,128]{3,2,1,0:T(8,128)}, u32[]{:S(2)}, u32[]{:S(2)}) collective-permute-start(f32[4,24,8,128]{3,2,1,0:T(8,128)S(1)} %collective-permute-done.3.refs_3_), channel_id=1, source_target_pairs={{0,1},{1,0},{2,3},{3,2},{4,5},{5,4},{6,7},{7,6},{8,9},{9,8},{10,11... | collective-permute-start | bytes 1179656 | tf_op jit(solution)/shard_map/ppermute | solution.py:649
  53.1 3.6 %collective-permute-start.8 = (f32[4,24,8,128]{3,2,1,0:T(8,128)S(1)}, f32[4,24,8,128]{3,2,1,0:T(8,128)}, u32[]{:S(2)}, u32[]{:S(2)}) collective-permute-start(f32[4,24,8,128]{3,2,1,0:T(8,128)S(1)} %collective-permute-done.4.refs_4_), channel_id=1, source_target_pairs={{0,1},{1,0},{2,3},{3,2},{4,5},{5,4},{6,7},{7,6},{8,9},{9,8},{10,11... | collective-permute-start | bytes 1179656 | tf_op jit(solution)/shard_map/ppermute | solution.py:649
  54.0 2.7 %collective-permute-start.9 = (f32[4,24,8,128]{3,2,1,0:T(8,128)}, f32[4,24,8,128]{3,2,1,0:T(8,128)}, u32[]{:S(2)}, u32[]{:S(2)}) collective-permute-start(f32[4,24,8,128]{3,2,1,0:T(8,128)} %collective-permute-done.5.refs_5_), channel_id=1, source_target_pairs={{0,1},{1,0},{2,3},{3,2},{4,5},{5,4},{6,7},{7,6},{8,9},{9,8},{10,11... | collective-permute-start | bytes 1179656 | tf_op jit(solution)/shard_map/ppermute | solution.py:649
